TPU v7x, 32 devices: a whole 2x2x4 slice. The times are simulated.
32 devices in a mesh: sa: 4 (over z), sb: 4 (over y, x), noise: 2 (over core).
Axes of the slice: x: 2, y: 2, z: 4, core: 2. Of those that a mesh axis runs over, the one named last changes fastest.
Arguments:
- base: bfloat16 [512, 1536], P(('sa', 'sb')), may hold values from -6 to 6
- noise: bfloat16 [4, 512, 1536], P('noise', ('sa', 'sb')), may hold values from -3 to 3
- cot: bfloat16 [512, 1536], P(('sa', 'sb')), may hold values from -6 to 6
- convolution_weight: bfloat16 [3, 1536, 384], P(None, 'sa'), may hold values from -0.15625 to 0.15625
- mix_w: bfloat16 [384, 1536], P('sa'), may hold values from -0.625 to 0.625
- norm_gain: float32 [1536], replicated, may hold values from 0.1 to 1.9
- qkv_w: bfloat16 [1536, 896], P('sa'), may hold values from -1 to 1
- out_w: bfloat16 [384, 1536], P('sa'), may hold values from -1.25 to 1.25
- band_width: int32 [4], replicated, may hold values from 1 to 32, as said below
- pairs: int32 [16, 2], replicated, may hold values from 0 to 3, as said below
Outputs:
- saliency: float32 [512, 1536], P(('sa', 'sb'))
Inputs may be any that keep to these rules, and one draw needn't show every extreme that they name: `band_width`: one head has band half-width exactly 32. Tile t holds bins t * 128 to (t + 1) * 128 - 1; both tiles of a pair lie in the same stretch of 128 bins that starts at a multiple of 128; pairs may repeat.
All inputs are finite; a program needn't handle non-finite values.
Results may differ from a plain program's by a relative error of at most 0.018.
Values may be sent and summed in bfloat16 or wider, within the bound.
No kernel may reach another device: no remote copies, remote signals or barrier semaphores. Data moves between devices by JAX's collectives and lax.ppermute only.
A program may use at most 64 MiB of HBM per device.

v0:
```python
import jax
import jax.numpy as jnp
from jax import lax
from jax.sharding import PartitionSpec as P

HID = 384
HEADS = 4
KEY = 64
VAL = 96
DILATION_BINS = 16
BAND = 32
TILE = 128


ROOT_TWO_PI = 0.7978845608
CUBIC = 0.044715


def extended(value, sides, width):
    for axis, dim in sides:
        peers, length = (lax.axis_size(axis), value.shape[dim])
        up = [(i, (i + 1) % peers) for i in range(peers - 1)]
        down = [(j, i) for i, j in up]
        last = lax.slice_in_dim(value, length - width, length, axis=dim)
        leading = lax.slice_in_dim(value, 0, width, axis=dim)
        before = lax.ppermute(last, axis, up)
        after = lax.ppermute(leading, axis, down)
        value = jnp.concatenate([before, value, after], axis=dim)
    return value


def from_behind(block, axis, distance):
    devices = range(lax.axis_size(axis))
    route = [(i - distance, i) for i in devices if i - distance in devices]
    return lax.ppermute(block, axis, route)


def gelu_tanh(values):
    inner = ROOT_TWO_PI * (values + CUBIC * values * values * values)
    return 0.5 * values * (1.0 + jnp.tanh(inner))


def gelu_slope(values):
    tangent = jnp.tanh(ROOT_TWO_PI * (values + CUBIC * values * values * values))
    return 0.5 * (1.0 + tangent) + 0.5 * values * (1.0 - tangent * tangent) * ROOT_TWO_PI * (
        1.0 + 3.0 * CUBIC * values * values
    )


def shards(base, noise, cot, convolution_weight, mix_w, norm_gain, qkv_w, out_w, band_width, pairs):
    conv_full, mix_full, qkv_full, out_full = (
        lax.all_gather(convolution_weight, "sa", axis=1, tiled=True),
        lax.all_gather(mix_w, "sa", axis=0, tiled=True),
        lax.all_gather(qkv_w, "sa", axis=0, tiled=True),
        lax.all_gather(out_w, "sa", axis=0, tiled=True),
    )
    sequence_bins = base.shape[0]
    samples_dev = noise.shape[0]
    stretch = sequence_bins * lax.axis_size("sb")
    sequence_length = stretch * lax.axis_size("sa")
    heads_key = HEADS * KEY
    heads_val = HEADS * VAL
    width = sequence_bins + 2 * BAND
    scale = KEY ** (-0.5)
    stretch_first = lax.axis_index("sa") * stretch
    first_row = stretch_first + lax.axis_index("sb") * sequence_bins
    row_pos = first_row + jnp.arange(sequence_bins, dtype=jnp.int32)
    ext_pos = first_row - BAND + jnp.arange(width, dtype=jnp.int32)
    stretch_pos = stretch_first + jnp.arange(stretch, dtype=jnp.int32)
    tiles = sequence_length // TILE
    tile_ids = jnp.arange(tiles, dtype=jnp.int32)
    pick_query = (pairs[:, 0][:, None] == tile_ids[None, :]).astype(jnp.float32)
    pick_key = (pairs[:, 1][:, None] == tile_ids[None, :]).astype(jnp.float32)
    table = jnp.dot(pick_query.T, pick_key)
    own_select = ((row_pos // TILE)[:, None] == tile_ids[None, :]).astype(jnp.float32)
    stretch_select = ((stretch_pos // TILE)[:, None] == tile_ids[None, :]).astype(jnp.float32)
    pair_own_rows = jnp.dot(jnp.dot(own_select, table), stretch_select.T) > 0.5
    pair_own_keys = jnp.dot(jnp.dot(stretch_select, table), own_select.T) > 0.5
    inside = (ext_pos >= 0) & (ext_pos < sequence_length)
    band_mask = inside[None, None, :] & (
        jnp.abs(row_pos[:, None] - ext_pos[None, :])[None] <= band_width[:, None, None]
    )
    far_rows = jnp.abs(row_pos[:, None] - stretch_pos[None, :])[None] > band_width[:, None, None]
    pair_mask = pair_own_rows[None] & far_rows
    key_mask = pair_own_keys[None] & jnp.transpose(far_rows, (0, 2, 1))
    noisy = base.astype(jnp.float32)[None] + noise.astype(jnp.float32)
    gelu_input = gelu_tanh(noisy).astype(jnp.bfloat16)
    gelu_extended = extended(gelu_input, ((("sa", "sb"), 1),), DILATION_BINS)
    hidden_state = jnp.zeros((samples_dev, sequence_bins, HID), jnp.float32)
    for tap_index in range(3):
        hidden_state = hidden_state + jnp.einsum(
            "nbd,dc->nbc",
            gelu_extended[:, tap_index * DILATION_BINS : tap_index * DILATION_BINS + sequence_bins],
            conv_full[tap_index],
            preferred_element_type=jnp.float32,
        )
    act = gelu_tanh(hidden_state).astype(jnp.bfloat16)
    resid = noisy + jnp.einsum("nbc,cd->nbd", act, mix_full, preferred_element_type=jnp.float32)
    inv_rms = lax.rsqrt(jnp.mean(resid * resid, axis=-1, keepdims=True) + 1e-06)
    normed = (resid * inv_rms * norm_gain).astype(jnp.bfloat16)
    proj = jnp.einsum("nbd,dc->nbc", normed, qkv_full, preferred_element_type=jnp.float32).astype(
        jnp.bfloat16
    )
    queries = proj[..., :heads_key].reshape(samples_dev, sequence_bins, HEADS, KEY)
    key_vals = proj[..., heads_key:]
    kv_ext = extended(key_vals, ((("sa", "sb"), 1),), BAND)
    kv_all = lax.all_gather(key_vals, "sb", axis=1, tiled=True)
    keys_ext = kv_ext[..., :heads_key].reshape(samples_dev, width, HEADS, KEY)
    vals_ext = kv_ext[..., heads_key:].reshape(samples_dev, width, HEADS, VAL)
    keys_all = kv_all[..., :heads_key].reshape(samples_dev, stretch, HEADS, KEY)
    vals_all = kv_all[..., heads_key:].reshape(samples_dev, stretch, HEADS, VAL)
    score_band = (
        jnp.einsum("nihd,njhd->nhij", queries, keys_ext, preferred_element_type=jnp.float32) * scale
    )
    score_band = jnp.where(band_mask[None], score_band, -1e30)
    raw_pair = jnp.einsum("nihd,njhd->nhij", queries, keys_all, preferred_element_type=jnp.float32)
    score_pair = jnp.where(pair_mask[None], raw_pair * scale, -1e30)
    top = jnp.maximum(jnp.max(score_band, axis=-1), jnp.max(score_pair, axis=-1))
    total = jnp.sum(jnp.where(band_mask[None], jnp.exp(score_band - top[..., None]), 0.0), axis=-1)
    total = total + jnp.sum(
        jnp.where(pair_mask[None], jnp.exp(score_pair - top[..., None]), 0.0), axis=-1
    )
    lse = top + jnp.log(total)
    prob_band = jnp.where(band_mask[None], jnp.exp(score_band - lse[..., None]), 0.0)
    prob_pair = jnp.where(pair_mask[None], jnp.exp(score_pair - lse[..., None]), 0.0)
    band_b = prob_band.astype(jnp.bfloat16)
    pair_b = prob_pair.astype(jnp.bfloat16)
    attn = jnp.einsum("nhij,njhe->nihe", band_b, vals_ext, preferred_element_type=jnp.float32)
    attn = attn + jnp.einsum(
        "nhij,njhe->nihe", pair_b, vals_all, preferred_element_type=jnp.float32
    )
    d_att = jnp.dot(cot, out_full.T, preferred_element_type=jnp.float32).astype(jnp.bfloat16)
    d_att_heads = d_att.reshape(sequence_bins, HEADS, VAL)
    delta = jnp.transpose(jnp.sum(d_att_heads.astype(jnp.float32)[None] * attn, axis=-1), (0, 2, 1))
    d_prob_band = jnp.einsum(
        "ihe,njhe->nhij", d_att_heads, vals_ext, preferred_element_type=jnp.float32
    )
    d_prob_pair = jnp.einsum(
        "ihe,njhe->nhij", d_att_heads, vals_all, preferred_element_type=jnp.float32
    )
    d_score_band = (prob_band * (d_prob_band - delta[..., None]) * scale).astype(jnp.bfloat16)
    d_score_pair = (prob_pair * (d_prob_pair - delta[..., None]) * scale).astype(jnp.bfloat16)
    d_query = jnp.einsum(
        "nhij,njhd->nihd", d_score_band, keys_ext, preferred_element_type=jnp.float32
    )
    d_query = d_query + jnp.einsum(
        "nhij,njhd->nihd", d_score_pair, keys_all, preferred_element_type=jnp.float32
    )
    d_key_ext = jnp.einsum(
        "nhij,nihd->njhd", d_score_band, queries, preferred_element_type=jnp.float32
    )
    d_val_ext = jnp.einsum(
        "nhij,ihe->njhe", band_b, d_att_heads, preferred_element_type=jnp.float32
    )
    d_kv_ext = jnp.concatenate(
        [
            d_key_ext.reshape(samples_dev, width, heads_key),
            d_val_ext.reshape(samples_dev, width, heads_val),
        ],
        axis=2,
    )
    from_right = from_behind(d_kv_ext[:, :BAND].astype(jnp.bfloat16), ("sa", "sb"), -1).astype(
        jnp.float32
    )
    from_left = from_behind(
        d_kv_ext[:, BAND + sequence_bins :].astype(jnp.bfloat16), ("sa", "sb"), 1
    ).astype(jnp.float32)
    d_key_vals = d_kv_ext[:, BAND : BAND + sequence_bins]
    d_key_vals = d_key_vals + from_left
    d_key_vals = d_key_vals + from_right
    statistics = jnp.stack([lse, delta], axis=1)
    query_rows = proj[..., :heads_key]
    queries_all, d_att_all = (
        lax.all_gather(query_rows, "sb", axis=1, tiled=True),
        lax.all_gather(d_att, "sb", axis=0, tiled=True),
    )
    stats_all = lax.all_gather(statistics, "sb", axis=3, tiled=True)
    queries_all = queries_all.reshape(samples_dev, stretch, HEADS, KEY)
    d_att_all = d_att_all.reshape(stretch, HEADS, VAL)
    keys_own = key_vals[..., :heads_key].reshape(samples_dev, sequence_bins, HEADS, KEY)
    vals_own = key_vals[..., heads_key:].reshape(samples_dev, sequence_bins, HEADS, VAL)
    score_key = (
        jnp.einsum("nihd,njhd->nhij", queries_all, keys_own, preferred_element_type=jnp.float32)
        * scale
    )
    prob_key = jnp.where(key_mask[None], jnp.exp(score_key - stats_all[:, 0][..., None]), 0.0)
    d_val_pair = jnp.einsum(
        "nhij,ihe->njhe",
        prob_key.astype(jnp.bfloat16),
        d_att_all,
        preferred_element_type=jnp.float32,
    )
    d_prob_key = jnp.einsum(
        "ihe,njhe->nhij", d_att_all, vals_own, preferred_element_type=jnp.float32
    )
    d_score_key = (prob_key * (d_prob_key - stats_all[:, 1][..., None]) * scale).astype(
        jnp.bfloat16
    )
    d_key_pair = jnp.einsum(
        "nhij,nihd->njhd", d_score_key, queries_all, preferred_element_type=jnp.float32
    )
    d_key_vals = d_key_vals + jnp.concatenate(
        [
            d_key_pair.reshape(samples_dev, sequence_bins, heads_key),
            d_val_pair.reshape(samples_dev, sequence_bins, heads_val),
        ],
        axis=2,
    )
    d_proj = jnp.concatenate(
        [d_query.reshape(samples_dev, sequence_bins, heads_key), d_key_vals], axis=2
    ).astype(jnp.bfloat16)
    d_normed = jnp.einsum("nbc,dc->nbd", d_proj, qkv_full, preferred_element_type=jnp.float32)
    gained = norm_gain * d_normed
    d_resid = (
        cot.astype(jnp.float32)[None]
        + inv_rms * gained
        - resid * inv_rms * inv_rms * inv_rms * jnp.mean(resid * gained, axis=-1, keepdims=True)
    )
    d_act = jnp.einsum(
        "nbd,cd->nbc", d_resid.astype(jnp.bfloat16), mix_full, preferred_element_type=jnp.float32
    )
    hidden_gradient = (d_act * gelu_slope(hidden_state)).astype(jnp.bfloat16)
    gradient_extended = extended(hidden_gradient, ((("sa", "sb"), 1),), DILATION_BINS)
    d_gelu_in = jnp.zeros((samples_dev, sequence_bins, base.shape[1]), jnp.float32)
    for tap_index in range(3):
        start_offset = (2 - tap_index) * DILATION_BINS
        d_gelu_in = d_gelu_in + jnp.einsum(
            "nbc,dc->nbd",
            gradient_extended[:, start_offset : start_offset + sequence_bins],
            conv_full[tap_index],
            preferred_element_type=jnp.float32,
        )
    grads = d_resid + d_gelu_in * gelu_slope(noisy)
    summed = lax.psum(jnp.sum(grads, axis=0).astype(jnp.bfloat16), "noise").astype(jnp.float32)
    return summed / (samples_dev * lax.axis_size("noise"))


def solution(mesh):
    return jax.shard_map(
        shards,
        mesh=mesh,
        in_specs=(
            P(("sa", "sb"), None),
            P("noise", ("sa", "sb"), None),
            P(("sa", "sb"), None),
            P(None, "sa", None),
            P("sa", None),
            P(),
            P("sa", None),
            P("sa", None),
            P(),
            P(),
        ),
        out_specs=P(("sa", "sb"), None),
        check_vma=False,
    )
```

profile of v0, /device:TPU:8, one launch (start us, length us, event | category | flops | bytes accessed | tf_op | source)
XLA Modules:
  0.0 303.7 jit_solution(13062586746198982350)
XLA Ops:
  6.5 0.7 all-gather.11.cloned.1.call-update
  7.3 0.7 all-gather.5.cloned.1.call-update
  8.1 0.7 all-gather.7.cloned.1.call-update
  9.1 3.4 %collective-permute-start = (bf16[2,16,1536]{2,1,0:T(8,128)(2,1)S(1)}, bf16[2,16,1536]{2,1,0:T(8,128)(2,1)S(1)}, u32[]{:S(2)}, u32[]{:S(2)}) collective-permute-start(bf16[2,16,1536]{2,1,0:T(8,128)(2,1)S(1)} %get-tuple-element.9), channel_id=1, source_target_pairs={{0,2},{2,4},{4,6},{6,8},{8,10},{10,12},{12,14},{14,16},{16,18},{18... | collective-permute-start | bytes 294920 | tf_op jit(solution)/shard_map/ppermute | solution.py:26
  12.5 4.2 %collective-permute-start.1 = (bf16[2,16,1536]{2,1,0:T(8,128)(2,1)S(1)}, bf16[2,16,1536]{2,1,0:T(8,128)(2,1)S(1)}, u32[]{:S(2)}, u32[]{:S(2)}) collective-permute-start(bf16[2,16,1536]{2,1,0:T(8,128)(2,1)S(1)} %get-tuple-element.10), channel_id=1, source_target_pairs={{2,0},{4,2},{6,4},{8,6},{10,8},{12,10},{14,12},{16,14},{18,16},{20... | collective-permute-start | bytes 294920 | tf_op jit(solution)/shard_map/ppermute | solution.py:27
  16.8 0.7 convert_element_type.74
  19.0 21.4 %all-gather.11.cloned.1.call-done = bf16[384,1536]{1,0:T(8,128)(2,1)} async-done(((bf16[96,1536]{1,0:T(8,128)(2,1)}), bf16[384,1536]{1,0:T(8,128)(2,1)}) %all-gather.11.cloned.1.call-update) | async-done | bytes 1179664 | tf_op jit(solution)/shard_map/all_gather | solution.py:55
  40.5 1.7 convolution_convert_fusion
  42.3 8.3 %all_gather.31 = bf16[128,384]{1,0:T(8,128)(2,1)S(1)} all-gather(bf16[32,384]{1,0:T(8,128)(2,1)S(1)} %convolution_convert_fusion), channel_id=1, replica_groups=mesh['sa'=4,'sb'=4,'noise'=2] {'sb'}, dimensions={0}, use_global_device_ids=true | all-gather | bytes 122880 | tf_op jit(solution)/shard_map/all_gather | solution.py:175
  50.6 0.8 copy.133
  51.4 57.5 %all-gather.5.cloned.1.call-done = bf16[3,1536,384]{2,1,0:T(8,128)(2,1)} async-done(((bf16[3,384,384]{2,1,0:T(8,128)(2,1)}), bf16[3,1536,384]{2,1,0:T(8,128)(2,1)}) %all-gather.5.cloned.1.call-update) | async-done | bytes 3538960 | tf_op jit(solution)/shard_map/all_gather | solution.py:52
  108.9 1.6 fusion.52
  110.5 1.6 fusion.54
  112.1 1.6 fusion.36
  113.7 28.0 %all-gather.7.cloned.1.call-done = bf16[384,1536]{1,0:T(8,128)(2,1)} async-done(((bf16[96,1536]{1,0:T(8,128)(2,1)}), bf16[384,1536]{1,0:T(8,128)(2,1)}) %all-gather.7.cloned.1.call-update) | async-done | bytes 1179664 | tf_op jit(solution)/shard_map/all_gather | solution.py:53
  141.7 1.7 multiply_reduce_fusion.1
  143.4 54.4 %all-gather.9.cloned.1.call-done = bf16[1536,896]{1,0:T(8,128)(2,1)} async-done(((bf16[384,896]{1,0:T(8,128)(2,1)}), bf16[1536,896]{1,0:T(8,128)(2,1)}) %all-gather.9.cloned.1.call-update) | async-done | bytes 2752528 | tf_op jit(solution)/shard_map/all_gather | solution.py:54
  197.7 2.4 fusion.14
  200.2 6.2 %collective-permute-start.3 = (bf16[2,32,640]{2,1,0:T(8,128)(2,1)S(1)}, bf16[2,32,640]{2,1,0:T(8,128)(2,1)S(1)}, u32[]{:S(2)}, u32[]{:S(2)}) collective-permute-start(bf16[2,32,640]{2,1,0:T(8,128)(2,1)S(1)} %slice.121), channel_id=1, source_target_pairs={{2,0},{4,2},{6,4},{8,6},{10,8},{12,10},{14,12},{16,14},{18,16},{20... | collective-permute-start | bytes 245768 | tf_op jit(solution)/shard_map/ppermute | solution.py:27
  206.4 1.9 collective-permute-start.2
  208.4 9.1 %all_gather.27 = bf16[2,128,640]{2,1,0:T(8,128)(2,1)S(1)} all-gather(bf16[2,32,640]{2,1,0:T(8,128)(2,1)S(1)} %slice.121), channel_id=1, replica_groups=mesh['sa'=4,'sb'=4,'noise'=2] {'sb'}, dimensions={1}, use_global_device_ids=true | all-gather | bytes 409600 | tf_op jit(solution)/shard_map/all_gather | solution.py:107
  218.0 0.7 reshape.250
  218.9 9.3 %all_gather.29 = bf16[2,128,256]{2,1,0:T(8,128)(2,1)S(1)} all-gather(bf16[2,32,256]{2,1,0:T(8,128)(2,1)S(1)} %get-tuple-element.12), channel_id=1, replica_groups=mesh['sa'=4,'sb'=4,'noise'=2] {'sb'}, dimensions={1}, use_global_device_ids=true | all-gather | bytes 163840 | tf_op jit(solution)/shard_map/all_gather | solution.py:174
  231.0 0.8 fusion.45
  232.1 7.9 %all_gather.30 = f32[2,2,4,128]{2,1,0,3:T(2,128)S(1)} all-gather(f32[2,2,4,32]{2,1,0,3:T(2,128)S(1)} %copy.131), channel_id=1, replica_groups=mesh['sa'=4,'sb'=4,'noise'=2] {'sb'}, dimensions={3}, use_global_device_ids=true | all-gather | bytes 10240 | tf_op jit(solution)/shard_map/all_gather | solution.py:177
  241.1 0.7 fusion.142
  241.9 3.5 %collective-permute-start.4 = (bf16[2,32,640]{2,1,0:T(8,128)(2,1)}, bf16[2,32,640]{2,1,0:T(8,128)(2,1)}, u32[]{:S(2)}, u32[]{:S(2)}) collective-permute-start(bf16[2,32,640]{2,1,0:T(8,128)(2,1)} %get-tuple-element.7), channel_id=1, source_target_pairs={{0,2},{2,4},{4,6},{6,8},{8,10},{10,12},{12,14},{14,16},{16,18},{18... | collective-permute-start | bytes 245768 | tf_op jit(solution)/shard_map/ppermute | solution.py:35
  245.4 4.1 %collective-permute-start.5 = (bf16[2,32,640]{2,1,0:T(8,128)(2,1)}, bf16[2,32,640]{2,1,0:T(8,128)(2,1)}, u32[]{:S(2)}, u32[]{:S(2)}) collective-permute-start(bf16[2,32,640]{2,1,0:T(8,128)(2,1)} %get-tuple-element.8), channel_id=1, source_target_pairs={{2,0},{4,2},{6,4},{8,6},{10,8},{12,10},{14,12},{16,14},{18,16},{20... | collective-permute-start | bytes 245768 | tf_op jit(solution)/shard_map/ppermute | solution.py:35
  249.5 0.9 fusion.148
  250.4 2.2 convolution_bitcast_fusion.3
  252.5 1.7 convolution_bitcast_fusion.2
  254.3 1.5 copy.123
  255.7 1.6 reshape.245
  257.3 1.6 copy.138
  258.9 1.7 reshape.253
  260.6 1.6 copy.136
  262.3 1.7 reshape.252
  263.9 1.1 fusion.74
  265.1 2.0 multiply_reduce_fusion
  267.1 0.5 fusion.41
  267.6 2.2 collective-permute-start.6
  269.8 3.7 %collective-permute-start.7 = (bf16[2,16,384]{2,1,0:T(8,128)(2,1)S(1)}, bf16[2,16,384]{2,1,0:T(8,128)(2,1)S(1)}, u32[]{:S(2)}, u32[]{:S(2)}) collective-permute-start(bf16[2,16,384]{2,1,0:T(8,128)(2,1)S(1)} %get-tuple-element.14), channel_id=1, source_target_pairs={{0,2},{2,4},{4,6},{6,8},{8,10},{10,12},{12,14},{14,16},{16,18},{18... | collective-permute-start | bytes 73736 | tf_op jit(solution)/shard_map/ppermute | solution.py:26
  273.5 0.5 fusion.51
  274.0 3.3 %collective-permute-done.7 = bf16[2,16,384]{2,1,0:T(8,128)(2,1)S(1)} collective-permute-done((bf16[2,16,384]{2,1,0:T(8,128)(2,1)S(1)}, bf16[2,16,384]{2,1,0:T(8,128)(2,1)S(1)}, u32[]{:S(2)}, u32[]{:S(2)}) %collective-permute-start.7) | collective-permute-done | bytes 24608 | tf_op jit(solution)/shard_map/ppermute | solution.py:26
  277.3 0.5 fusion.53
  277.9 1.3 fusion.13
  279.2 16.4 %all-reduce.2.cloned.1.call-done = bf16[32,1536]{1,0:T(8,128)(2,1)} async-done(((bf16[32,1536]{1,0:T(8,128)(2,1)}), bf16[32,1536]{1,0:T(8,128)(2,1)}) %all-reduce.2.cloned.1.call-update) | async-done | bytes 98320 | tf_op jit(solution)/shard_map/psum | solution.py:234
  295.6 1.6 convert_multiply_fusion
  (101 shorter events, 6.7 us)
Async XLA Ops:
  6.5 2.3 copy-start.12
  6.5 2.3 copy-start.7
  6.5 33.9 %all-gather.11.cloned.1.call-start = ((), (), s32[]{:S(2)}) async-start(), calls=%async_computation.3 | async-start | bytes 1474560 | tf_op jit(solution)/shard_map/all_gather | solution.py:55
  7.3 101.6 %all-gather.5.cloned.1.call-start = ((), (), s32[]{:S(2)}) async-start(), calls=%async_computation | async-start | bytes 4423680 | tf_op jit(solution)/shard_map/all_gather | solution.py:52
  8.0 8.8 %copy-start.10 = (bf16[32,1536]{1,0:T(8,128)(2,1)S(1)}, bf16[32,1536]{1,0:T(8,128)(2,1)}, u32[]{:S(2)}) copy-start(bf16[32,1536]{1,0:T(8,128)(2,1)} %param.12) | copy-start | bytes 294916
  8.0 133.6 %all-gather.7.cloned.1.call-start = ((), (), s32[]{:S(2)}) async-start(), calls=%async_computation.1 | async-start | bytes 1474560 | tf_op jit(solution)/shard_map/all_gather | solution.py:53
  8.8 8.8 %copy-start.14 = (s32[16,2]{0,1:T(2,128)S(1)}, s32[16,2]{0,1:T(2,128)}, u32[]{:S(2)}) copy-start(s32[16,2]{0,1:T(2,128)} %param.19) | copy-start | bytes 388
  8.8 189.0 %all-gather.9.cloned.1.call-start = ((), (), s32[]{:S(2)}) async-start(), calls=%async_computation.2 | async-start | bytes 3440640 | tf_op jit(solution)/shard_map/all_gather | solution.py:54
  8.9 132.8 %copy-start.3 = (f32[32,1536]{1,0:T(8,128)}, f32[32,1536]{1,0:T(8,128)S(1)}, u32[]{:S(2)}) copy-start(f32[32,1536]{1,0:T(8,128)S(1)} %convert_element_type.75) | copy-start | bytes 589828
  8.9 9.9 %copy-start.13 = (s32[4]{0:T(128)S(1)}, s32[4]{0:T(128)}, u32[]{:S(2)}) copy-start(s32[4]{0:T(128)} %param.18) | copy-start | bytes 52
  9.1 103.0 %collective-permute-start = (bf16[2,16,1536]{2,1,0:T(8,128)(2,1)S(1)}, bf16[2,16,1536]{2,1,0:T(8,128)(2,1)S(1)}, u32[]{:S(2)}, u32[]{:S(2)}) collective-permute-start(bf16[2,16,1536]{2,1,0:T(8,128)(2,1)S(1)} %get-tuple-element.9), channel_id=1, source_target_pairs={{0,2},{2,4},{4,6},{6,8},{8,10},{10,12},{12,14},{14,16},{16,18},{18... | collective-permute-start | bytes 294920 | tf_op jit(solution)/shard_map/ppermute | solution.py:26
  12.5 98.0 %collective-permute-start.1 = (bf16[2,16,1536]{2,1,0:T(8,128)(2,1)S(1)}, bf16[2,16,1536]{2,1,0:T(8,128)(2,1)S(1)}, u32[]{:S(2)}, u32[]{:S(2)}) collective-permute-start(bf16[2,16,1536]{2,1,0:T(8,128)(2,1)S(1)} %get-tuple-element.10), channel_id=1, source_target_pairs={{2,0},{4,2},{6,4},{8,6},{10,8},{12,10},{14,12},{16,14},{18,16},{20... | collective-permute-start | bytes 294920 | tf_op jit(solution)/shard_map/ppermute | solution.py:27
  16.7 278.9 %all-reduce.2.cloned.1.call-start = ((), (), s32[]{:S(2)}) async-start(), calls=%async_computation.4 | async-start | bytes 196608 | tf_op jit(solution)/shard_map/psum | solution.py:234
  113.7 84.1 %copy-start.11 = (f32[1536]{0:T(1024)S(1)}, f32[1536]{0:T(1024)}, u32[]{:S(2)}) copy-start(f32[1536]{0:T(1024)} %param.15) | copy-start | bytes 18436
  200.2 28.3 %collective-permute-start.3 = (bf16[2,32,640]{2,1,0:T(8,128)(2,1)S(1)}, bf16[2,32,640]{2,1,0:T(8,128)(2,1)S(1)}, u32[]{:S(2)}, u32[]{:S(2)}) collective-permute-start(bf16[2,32,640]{2,1,0:T(8,128)(2,1)S(1)} %slice.121), channel_id=1, source_target_pairs={{2,0},{4,2},{6,4},{8,6},{10,8},{12,10},{14,12},{16,14},{18,16},{20... | collective-permute-start | bytes 245768 | tf_op jit(solution)/shard_map/ppermute | solution.py:27
  206.4 22.1 %collective-permute-start.2 = (bf16[2,32,640]{2,1,0:T(8,128)(2,1)S(1)}, bf16[2,32,640]{2,1,0:T(8,128)(2,1)S(1)}, u32[]{:S(2)}, u32[]{:S(2)}) collective-permute-start(bf16[2,32,640]{2,1,0:T(8,128)(2,1)S(1)} %slice.121), channel_id=1, source_target_pairs={{0,2},{2,4},{4,6},{6,8},{8,10},{10,12},{12,14},{14,16},{16,18},{18... | collective-permute-start | bytes 245768 | tf_op jit(solution)/shard_map/ppermute | solution.py:26
  228.3 21.2 %copy-start.6 = (bf16[2,128,256]{1,2,0:T(8,128)(2,1)}, bf16[2,128,256]{1,2,0:T(8,128)(2,1)S(1)}, u32[]{:S(2)}) copy-start(bf16[2,128,256]{1,2,0:T(8,128)(2,1)S(1)} %copy.129) | copy-start | bytes 393220
  232.0 9.1 %copy-start.5 = (f32[2,96,256]{2,1,0:T(8,128)}, f32[2,96,256]{2,1,0:T(8,128)S(1)}, u32[]{:S(2)}) copy-start(f32[2,96,256]{2,1,0:T(8,128)S(1)} %copy.128) | copy-start | bytes 589828
  241.9 22.1 %collective-permute-start.4 = (bf16[2,32,640]{2,1,0:T(8,128)(2,1)}, bf16[2,32,640]{2,1,0:T(8,128)(2,1)}, u32[]{:S(2)}, u32[]{:S(2)}) collective-permute-start(bf16[2,32,640]{2,1,0:T(8,128)(2,1)} %get-tuple-element.7), channel_id=1, source_target_pairs={{0,2},{2,4},{4,6},{6,8},{8,10},{10,12},{12,14},{14,16},{16,18},{18... | collective-permute-start | bytes 245768 | tf_op jit(solution)/shard_map/ppermute | solution.py:35
  245.4 18.5 %collective-permute-start.5 = (bf16[2,32,640]{2,1,0:T(8,128)(2,1)}, bf16[2,32,640]{2,1,0:T(8,128)(2,1)}, u32[]{:S(2)}, u32[]{:S(2)}) collective-permute-start(bf16[2,32,640]{2,1,0:T(8,128)(2,1)} %get-tuple-element.8), channel_id=1, source_target_pairs={{2,0},{4,2},{6,4},{8,6},{10,8},{12,10},{14,12},{16,14},{18,16},{20... | collective-permute-start | bytes 245768 | tf_op jit(solution)/shard_map/ppermute | solution.py:35
  250.4 14.7 %copy-start = (bf16[1536,896]{1,0:T(8,128)(2,1)S(1)}, bf16[1536,896]{1,0:T(8,128)(2,1)}, u32[]{:S(2)}) copy-start(bf16[1536,896]{1,0:T(8,128)(2,1)} %all-gather.9.cloned.1.call-done) | copy-start | bytes 8257540
  263.9 3.1 %copy-start.9 = (f32[32,1536]{1,0:T(8,128)S(1)}, f32[32,1536]{1,0:T(8,128)}, u32[]{:S(2)}) copy-start(f32[32,1536]{1,0:T(8,128)} %convert_element_type.74) | copy-start | bytes 589828
  265.1 2.0 copy-start.1
  265.1 8.4 %copy-start.2 = (bf16[3,1536,384]{2,1,0:T(8,128)(2,1)S(1)}, bf16[3,1536,384]{2,1,0:T(8,128)(2,1)}, u32[]{:S(2)}) copy-start(bf16[3,1536,384]{2,1,0:T(8,128)(2,1)} %all-gather.5.cloned.1.call-done) | copy-start | bytes 10616836
  267.6 10.2 %collective-permute-start.6 = (bf16[2,16,384]{2,1,0:T(8,128)(2,1)S(1)}, bf16[2,16,384]{2,1,0:T(8,128)(2,1)S(1)}, u32[]{:S(2)}, u32[]{:S(2)}) collective-permute-start(bf16[2,16,384]{2,1,0:T(8,128)(2,1)S(1)} %get-tuple-element.13), channel_id=1, source_target_pairs={{2,0},{4,2},{6,4},{8,6},{10,8},{12,10},{14,12},{16,14},{18,16},{20... | collective-permute-start | bytes 73736 | tf_op jit(solution)/shard_map/ppermute | solution.py:27
  269.8 7.5 %collective-permute-start.7 = (bf16[2,16,384]{2,1,0:T(8,128)(2,1)S(1)}, bf16[2,16,384]{2,1,0:T(8,128)(2,1)S(1)}, u32[]{:S(2)}, u32[]{:S(2)}) collective-permute-start(bf16[2,16,384]{2,1,0:T(8,128)(2,1)S(1)} %get-tuple-element.14), channel_id=1, source_target_pairs={{0,2},{2,4},{4,6},{6,8},{8,10},{10,12},{12,14},{14,16},{16,18},{18... | collective-permute-start | bytes 73736 | tf_op jit(solution)/shard_map/ppermute | solution.py:26
  274.0 3.8 %copy-start.4 = (f32[32,1536]{1,0:T(8,128)S(1)}, f32[32,1536]{1,0:T(8,128)}, u32[]{:S(2)}) copy-start(f32[32,1536]{1,0:T(8,128)} %copy-done.3) | copy-start | bytes 589828
  274.0 3.8 %copy-start.8 = (bf16[2,32,1536]{2,1,0:T(8,128)(2,1)S(1)}, bf16[2,32,1536]{2,1,0:T(8,128)(2,1)}, u32[]{:S(2)}) copy-start(bf16[2,32,1536]{2,1,0:T(8,128)(2,1)} %param.11) | copy-start | bytes 589828
Sparse Core Ops, SparseCore 0:
  8.9 31.4 all-gather.10
  42.0 66.7 all-gather.4
  110.4 31.1 all-gather.6
  143.1 54.6 all-gather.8
  279.3 16.2 all-reduce.1
where the time goes:
time: 306 us; the launch traced here: 304 us
  waiting for transfers between devices  183 us (60%)
  blocking collectives  34.7 us (11%)
  starting transfers between devices  29.4 us (10%)
  matrix products  24.1 us (8%)
  local copies, waits for them, and re-layouts  14 us (5%)
  between operations  13.8 us (5%)
  other arithmetic  4.55 us (1%)
    all_gather x1, waiting for transfers between devices, shards(): lax.all_gather(convolution_weight, 'sa', axis=1, tiled=True)  57.5 us
    all_gather x1, waiting for transfers between devices, shards(): lax.all_gather(qkv_w, 'sa', axis=0, tiled=True)  54.4 us
    all_gather x1, waiting for transfers between devices, shards(): lax.all_gather(mix_w, 'sa', axis=0, tiled=True)  28 us
    all_gather x1, waiting for transfers between devices, shards(): lax.all_gather(out_w, 'sa', axis=0, tiled=True)  21.4 us
    psum x1, waiting for transfers between devices, shards(): lax.psum(jnp.sum(grads, axis=0).astype(jnp.bfloat16), 'noise')  16.4 us
    ppermute x3, starting transfers between devices, extended(): after = lax.ppermute(leading, axis, down)  12.7 us
    all_gather x1, blocking collectives, shards(): lax.all_gather(query_rows, 'sb', axis=1, tiled=True)  9.34 us
    all_gather x1, blocking collectives, shards(): kv_all = lax.all_gather(key_vals, 'sb', axis=1, tiled=True)  9.13 us
  transfers between devices with their start and end apart: 13, of which 6 were waited for; matrix products, arithmetic and copies ran while one was open for 9% of the time, Pallas kernels for 0%

commit v1 on v0

--- a/solution.py
+++ b/solution.py
@@ -47,13 +47,30 @@
     )
 
 
+def gathered_weights(convolution_weight, mix_w, qkv_w, out_w):
+    n_sa, n_sb, n_noise = (lax.axis_size("sa"), lax.axis_size("sb"), lax.axis_size("noise"))
+    parts = n_sb * n_noise
+    part = lax.axis_index("sb") * n_noise + lax.axis_index("noise")
+    arrays = (convolution_weight, mix_w, qkv_w, out_w)
+    flat = [a.reshape(parts, -1) for a in arrays]
+    sizes = [f.shape[1] for f in flat]
+    mine = jnp.concatenate(
+        [lax.dynamic_index_in_dim(f, part, 0, keepdims=False).reshape(-1, 128) for f in flat], axis=0
+    )
+    everything = lax.all_gather(mine, ("sa", "sb", "noise"), axis=0, tiled=False)
+    everything = everything.reshape(n_sa, parts, -1, 128)
+    full, first = [], 0
+    for a, size in zip(arrays, sizes):
+        rows = size // 128
+        full.append(everything[:, :, first : first + rows].reshape((n_sa,) + a.shape))
+        first += rows
+    conv, mix, qkv, out = full
+    conv = jnp.transpose(conv, (1, 0, 2, 3)).reshape(conv.shape[1], -1, conv.shape[3])
+    return conv, mix.reshape(-1, mix.shape[2]), qkv.reshape(-1, qkv.shape[2]), out.reshape(-1, out.shape[2])
+
+
 def shards(base, noise, cot, convolution_weight, mix_w, norm_gain, qkv_w, out_w, band_width, pairs):
-    conv_full, mix_full, qkv_full, out_full = (
-        lax.all_gather(convolution_weight, "sa", axis=1, tiled=True),
-        lax.all_gather(mix_w, "sa", axis=0, tiled=True),
-        lax.all_gather(qkv_w, "sa", axis=0, tiled=True),
-        lax.all_gather(out_w, "sa", axis=0, tiled=True),
-    )
+    conv_full, mix_full, qkv_full, out_full = gathered_weights(convolution_weight, mix_w, qkv_w, out_w)
     sequence_bins = base.shape[0]
     samples_dev = noise.shape[0]
     stretch = sequence_bins * lax.axis_size("sb")
@@ -231,7 +248,13 @@
             preferred_element_type=jnp.float32,
         )
     grads = d_resid + d_gelu_in * gelu_slope(noisy)
-    summed = lax.psum(jnp.sum(grads, axis=0).astype(jnp.bfloat16), "noise").astype(jnp.float32)
+    own = jnp.sum(grads, axis=0)
+    n_noise = lax.axis_size("noise")
+    passing = own.astype(jnp.bfloat16)
+    summed = passing.astype(jnp.float32)
+    for _ in range(n_noise - 1):
+        passing = lax.ppermute(passing, "noise", [(i, (i + 1) % n_noise) for i in range(n_noise)])
+        summed = summed + passing.astype(jnp.float32)
     return summed / (samples_dev * lax.axis_size("noise"))
 
 

time: 306 us -> 265 us (0.87)
  waiting for transfers between devices: 183 us -> 69 us
  local copies, waits for them, and re-layouts: 14 us -> 70.2 us
  other arithmetic: 4.55 us -> 11.4 us
  matrix products: 24.1 us -> 30 us
    all_gather x4 -> x1, waiting for transfers between devices: 161 us -> 66.7 us  [gathered_weights(): lax.all_gather(mine, ('sa', 'sb', 'noise'), axis=0, tiled=False)]
    psum x1 -> x0, waiting for transfers between devices: 16.4 us -> none  [shards(): lax.psum(jnp.sum(grads, axis=0).astype(jnp.bfloat16), 'noise')]
    slice x0 -> x4, local copies, waits for them, and re-layouts: none -> 12.3 us  [the longest x3 10.8 us: gathered_weights(): full.append(everything[:, :, first:first + rows].reshape((n_sa,) + a.shape))]
    another operation x0 -> x3, local copies, waits for them, and re-layouts: none -> 10.8 us  [the longest x1 4.99 us: gathered_weights(): qkv.reshape(-1, qkv.shape[2])]
    reshape x0 -> x5, local copies, waits for them, and re-layouts: none -> 8.85 us  [the longest x1 5.11 us: gathered_weights(): full.append(everything[:, :, first:first + rows].reshape((n_sa,) + a.shape))]
    ppermute x3, waiting for transfers between devices: 3.33 us -> 0.01 us  [extended(): before = lax.ppermute(last, axis, up)]
  transfers between devices with their start and end apart: 13 -> 10, of which waited for: 6 -> 3; matrix products, arithmetic and copies ran while one was open for 9% -> 26% of each run, Pallas kernels for 0% -> 0%
where the time goes in v1:
time: 265 us; the launch traced here: 261 us
  local copies, waits for them, and re-layouts  70.2 us (26%)
  waiting for transfers between devices  69 us (26%)
  blocking collectives  37.1 us (14%)
  matrix products  30 us (11%)
  starting transfers between devices  29.1 us (11%)
  between operations  14.2 us (5%)
  other arithmetic  11.4 us (4%)
    all_gather x1, waiting for transfers between devices, gathered_weights(): lax.all_gather(mine, ('sa', 'sb', 'noise'), axis=0, tiled=False)  66.7 us
    ppermute x3, starting transfers between devices, extended(): after = lax.ppermute(leading, axis, down)  13.4 us
    slice x3, local copies, waits for them, and re-layouts, gathered_weights(): full.append(everything[:, :, first:first + rows].reshape((n_sa,) + a.shape))  10.8 us
    all_gather x1, blocking collectives, shards(): kv_all = lax.all_gather(key_vals, 'sb', axis=1, tiled=True)  10.1 us
    all_gather x1, blocking collectives, shards(): lax.all_gather(d_att, 'sb', axis=0, tiled=True)  9.14 us
    all_gather x1, blocking collectives, shards(): lax.all_gather(query_rows, 'sb', axis=1, tiled=True)  9.1 us
    all_gather x1, blocking collectives, shards(): stats_all = lax.all_gather(statistics, 'sb', axis=3, tiled=True)  8.77 us
    ppermute x3, starting transfers between devices, extended(): before = lax.ppermute(last, axis, up)  7.96 us
  transfers between devices with their start and end apart: 10, of which 3 were waited for; matrix products, arithmetic and copies ran while one was open for 26% of the time, Pallas kernels for 0%

profile of v1, /device:TPU:8, one launch (start us, length us, event | category | flops | bytes accessed | tf_op | source)
XLA Modules:
  0.0 261.0 jit_solution(9661752335281715874)
XLA Ops:
  6.5 1.6 reshape.282
  8.1 1.5 reshape.286
  14.4 3.4 %collective-permute-start = (bf16[2,16,1536]{2,1,0:T(8,128)(2,1)}, bf16[2,16,1536]{2,1,0:T(8,128)(2,1)}, u32[]{:S(2)}, u32[]{:S(2)}) collective-permute-start(bf16[2,16,1536]{2,1,0:T(8,128)(2,1)} %get-tuple-element.14), channel_id=1, source_target_pairs={{0,2},{2,4},{4,6},{6,8},{8,10},{10,12},{12,14},{14,16},{16,18},{18... | collective-permute-start | bytes 294920 | tf_op jit(solution)/shard_map/ppermute | solution.py:26
  17.8 4.2 %collective-permute-start.1 = (bf16[2,16,1536]{2,1,0:T(8,128)(2,1)}, bf16[2,16,1536]{2,1,0:T(8,128)(2,1)}, u32[]{:S(2)}, u32[]{:S(2)}) collective-permute-start(bf16[2,16,1536]{2,1,0:T(8,128)(2,1)} %get-tuple-element.15), channel_id=1, source_target_pairs={{2,0},{4,2},{6,4},{8,6},{10,8},{12,10},{14,12},{16,14},{18,16},{20... | collective-permute-start | bytes 294920 | tf_op jit(solution)/shard_map/ppermute | solution.py:27
  26.1 66.7 %all-gather.3.cloned.1.call-done = bf16[33792,128]{1,0:T(8,128)(2,1)} async-done(((bf16[1056,128]{1,0:T(8,128)(2,1)}), bf16[33792,128]{1,0:T(8,128)(2,1)}) %all-gather.3.cloned.1.call-update) | async-done | bytes 8650768 | tf_op jit(solution)/shard_map/all_gather | solution.py:60
  92.8 3.2 %fusion.122 = (bf16[4,8,144,128]{3,2,1,0:T(8,128)(2,1)}, bf16[4,8,144,128]{3,2,1,0:T(8,128)(2,1)}) fusion(bf16[4,8,1056,128]{3,2,1,0:T(8,128)(2,1)} %bitcast.141), kind=kLoop, calls=%fused_computation.193 | loop fusion | bytes 4718592 | tf_op jit(solution)/shard_map/slice | solution.py:65
  96.0 4.0 %slice.136 = bf16[4,8,432,128]{3,2,1,0:T(8,128)(2,1)} slice(bf16[4,8,1056,128]{3,2,1,0:T(8,128)(2,1)} %bitcast.142), slice={[0:4], [0:8], [0:432], [0:128]} | slice | bytes 7077888 | tf_op jit(solution)/shard_map/slice | solution.py:65
  100.0 5.1 %reshape.289 = bf16[4,3,384,384]{3,2,1,0:T(8,128)(2,1)S(1)} reshape(bf16[4,8,432,128]{3,2,1,0:T(8,128)(2,1)} %slice.136) | data formatting | bytes 7077888 | tf_op jit(solution)/shard_map/reshape | solution.py:65
  105.1 1.5 fusion.123
  108.3 3.6 %slice.142 = bf16[4,8,336,128]{3,2,1,0:T(8,128)(2,1)} slice(bf16[4,8,1056,128]{3,2,1,0:T(8,128)(2,1)} %bitcast.143), slice={[0:4], [0:8], [576:912], [0:128]} | slice | bytes 5505024 | tf_op jit(solution)/shard_map/slice | solution.py:65
  111.9 2.2 reshape.310
  114.1 5.0 %reshape.311 = bf16[1536,896,1]{1,0,2:T(8,128)(2,1)S(1)} reshape(bf16[4,8,336,128]{3,2,1,0:T(8,128)(2,1)} %slice.142) | data formatting | bytes 5505024 | tf_op jit(solution)/shard_map/reshape;reshape | solution.py:69
  119.1 1.8 fusion.20
  123.0 3.3 %collective-permute-start.3 = (bf16[2,32,640]{2,1,0:T(8,128)(2,1)S(1)}, bf16[2,32,640]{2,1,0:T(8,128)(2,1)}, u32[]{:S(2)}, u32[]{:S(2)}) collective-permute-start(bf16[2,32,640]{2,1,0:T(8,128)(2,1)S(1)} %slice.143), channel_id=1, source_target_pairs={{2,0},{4,2},{6,4},{8,6},{10,8},{12,10},{14,12},{16,14},{18,16},{20... | collective-permute-start | bytes 245768 | tf_op jit(solution)/shard_map/ppermute | solution.py:27
  126.4 2.5 collective-permute-start.2
  128.9 10.1 %all_gather.20 = bf16[2,128,640]{2,1,0:T(8,128)(2,1)S(1)} all-gather(bf16[2,32,640]{2,1,0:T(8,128)(2,1)S(1)} %slice.143), channel_id=1, replica_groups=mesh['sa'=4,'sb'=4,'noise'=2] {'sb'}, dimensions={1}, use_global_device_ids=true | all-gather | bytes 409600 | tf_op jit(solution)/shard_map/all_gather | solution.py:124
  139.0 3.6 %reshape_reshape.11 = bf16[384,1536]{1,0:T(8,128)(2,1)} reshape(bf16[4,8,144,128]{3,2,1,0:T(8,128)(2,1)} %get-tuple-element.5) | data formatting | bytes 2359296 | tf_op jit(solution)/shard_map/reshape;reshape | solution.py:69
  142.6 2.4 fusion.29
  144.9 1.5 reshape.291
  147.1 1.7 copy.115
  148.8 1.7 fusion.130
  151.9 1.4 reshape.294
  154.8 9.1 %all_gather.23 = bf16[128,384]{1,0:T(8,128)(2,1)} all-gather(bf16[32,384]{1,0:T(8,128)(2,1)} %fusion.29), channel_id=1, replica_groups=mesh['sa'=4,'sb'=4,'noise'=2] {'sb'}, dimensions={0}, use_global_device_ids=true | all-gather | bytes 122880 | tf_op jit(solution)/shard_map/all_gather | solution.py:192
  163.9 1.6 copy.133
  165.5 1.5 reshape.301
  167.1 1.5 reshape.300
  168.5 9.1 %all_gather.21 = bf16[2,128,256]{2,1,0:T(8,128)(2,1)} all-gather(bf16[2,32,256]{2,1,0:T(8,128)(2,1)} %get-tuple-element.17), channel_id=1, replica_groups=mesh['sa'=4,'sb'=4,'noise'=2] {'sb'}, dimensions={1}, use_global_device_ids=true | all-gather | bytes 163840 | tf_op jit(solution)/shard_map/all_gather | solution.py:191
  177.6 1.7 copy.129
  181.7 1.5 pad_maximum_fusion.6
  183.2 1.8 reshape.293
  190.9 1.9 fusion.28
  194.0 1.8 fusion.82
  195.8 1.8 fusion.27
  197.7 1.8 copy.128
  199.4 8.8 %all_gather.22 = f32[2,2,4,128]{2,1,0,3:T(2,128)S(1)} all-gather(f32[2,2,4,32]{2,1,0,3:T(2,128)S(1)} %copy.131), channel_id=1, replica_groups=mesh['sa'=4,'sb'=4,'noise'=2] {'sb'}, dimensions={3}, use_global_device_ids=true | all-gather | bytes 10240 | tf_op jit(solution)/shard_map/all_gather | solution.py:194
  209.1 1.6 copy.135
  212.4 1.9 copy.127
  217.1 2.6 %collective-permute-start.4 = (bf16[2,32,640]{2,1,0:T(8,128)(2,1)}, bf16[2,32,640]{2,1,0:T(8,128)(2,1)}, u32[]{:S(2)}, u32[]{:S(2)}) collective-permute-start(bf16[2,32,640]{2,1,0:T(8,128)(2,1)} %get-tuple-element.12), channel_id=1, source_target_pairs={{0,2},{2,4},{4,6},{6,8},{8,10},{10,12},{12,14},{14,16},{16,18},{18... | collective-permute-start | bytes 245768 | tf_op jit(solution)/shard_map/ppermute | solution.py:35
  219.8 5.0 %collective-permute-start.5 = (bf16[2,32,640]{2,1,0:T(8,128)(2,1)}, bf16[2,32,640]{2,1,0:T(8,128)(2,1)}, u32[]{:S(2)}, u32[]{:S(2)}) collective-permute-start(bf16[2,32,640]{2,1,0:T(8,128)(2,1)} %get-tuple-element.13), channel_id=1, source_target_pairs={{2,0},{4,2},{6,4},{8,6},{10,8},{12,10},{14,12},{16,14},{18,16},{20... | collective-permute-start | bytes 245768 | tf_op jit(solution)/shard_map/ppermute | solution.py:35
  224.8 1.8 fusion.131
  226.6 2.0 convolution_bitcast_fusion.3
  228.6 1.7 convolution_bitcast_fusion.2
  231.8 1.6 copy.138
  234.5 1.6 copy.136
  236.2 1.7 reshape.303
  238.9 1.9 multiply_reduce_fusion
  241.5 2.1 collective-permute-start.7
  244.0 5.8 %collective-permute-start.6 = (bf16[2,16,384]{2,1,0:T(8,128)(2,1)S(1)}, bf16[2,16,384]{2,1,0:T(8,128)(2,1)S(1)}, u32[]{:S(2)}, u32[]{:S(2)}) collective-permute-start(bf16[2,16,384]{2,1,0:T(8,128)(2,1)S(1)} %get-tuple-element.18), channel_id=1, source_target_pairs={{2,0},{4,2},{6,4},{8,6},{10,8},{12,10},{14,12},{16,14},{18,16},{20... | collective-permute-start | bytes 73736 | tf_op jit(solution)/shard_map/ppermute | solution.py:27
  (162 shorter events, 39.9 us)
Async XLA Ops:
  6.5 3.0 %copy-start.26 = (bf16[384,896]{1,0:T(8,128)(2,1)S(1)}, bf16[384,896]{1,0:T(8,128)(2,1)}, u32[]{:S(2)}) copy-start(bf16[384,896]{1,0:T(8,128)(2,1)} %param.16) | copy-start | bytes 2064388
  6.5 86.3 %all-gather.3.cloned.1.call-start = ((), (), s32[]{:S(2)}) async-start(), calls=%async_computation | async-start | bytes 8921088 | tf_op jit(solution)/shard_map/all_gather | solution.py:60
  6.5 3.4 %copy-start.18 = (bf16[3,384,384]{2,1,0:T(8,128)(2,1)S(1)}, bf16[3,384,384]{2,1,0:T(8,128)(2,1)}, u32[]{:S(2)}) copy-start(bf16[3,384,384]{2,1,0:T(8,128)(2,1)} %param.13) | copy-start | bytes 2654212
  10.3 2.5 copy-start.35
  10.3 2.5 copy-start.21
  11.6 10.5 %copy-start.29 = (bf16[32,1536]{1,0:T(8,128)(2,1)S(1)}, bf16[32,1536]{1,0:T(8,128)(2,1)}, u32[]{:S(2)}) copy-start(bf16[32,1536]{1,0:T(8,128)(2,1)} %param.12) | copy-start | bytes 294916
  12.0 10.8 %copy-start.41 = (s32[16,2]{0,1:T(2,128)S(1)}, s32[16,2]{0,1:T(2,128)}, u32[]{:S(2)}) copy-start(s32[16,2]{0,1:T(2,128)} %param.19) | copy-start | bytes 388
  12.8 11.3 %copy-start.40 = (s32[4]{0:T(128)S(1)}, s32[4]{0:T(128)}, u32[]{:S(2)}) copy-start(s32[4]{0:T(128)} %param.18) | copy-start | bytes 52
  12.9 1.5 copy-start.11
  14.4 104.7 %collective-permute-start = (bf16[2,16,1536]{2,1,0:T(8,128)(2,1)}, bf16[2,16,1536]{2,1,0:T(8,128)(2,1)}, u32[]{:S(2)}, u32[]{:S(2)}) collective-permute-start(bf16[2,16,1536]{2,1,0:T(8,128)(2,1)} %get-tuple-element.14), channel_id=1, source_target_pairs={{0,2},{2,4},{4,6},{6,8},{8,10},{10,12},{12,14},{14,16},{16,18},{18... | collective-permute-start | bytes 294920 | tf_op jit(solution)/shard_map/ppermute | solution.py:26
  17.8 89.1 %collective-permute-start.1 = (bf16[2,16,1536]{2,1,0:T(8,128)(2,1)}, bf16[2,16,1536]{2,1,0:T(8,128)(2,1)}, u32[]{:S(2)}, u32[]{:S(2)}) collective-permute-start(bf16[2,16,1536]{2,1,0:T(8,128)(2,1)} %get-tuple-element.15), channel_id=1, source_target_pairs={{2,0},{4,2},{6,4},{8,6},{10,8},{12,10},{14,12},{16,14},{18,16},{20... | collective-permute-start | bytes 294920 | tf_op jit(solution)/shard_map/ppermute | solution.py:27
  106.6 1.7 copy-start
  106.6 1.7 copy-start.2
  108.3 3.6 %copy-start.10 = (bf16[4,8,144,128]{3,2,1,0:T(8,128)(2,1)S(1)}, bf16[4,8,144,128]{3,2,1,0:T(8,128)(2,1)}, u32[]{:S(2)}) copy-start(bf16[4,8,144,128]{3,2,1,0:T(8,128)(2,1)} %get-tuple-element.6) | copy-start | bytes 3538948
  114.1 5.0 %copy-start.8 = (bf16[2,32,1536]{2,1,0:T(8,128)(2,1)S(1)}, bf16[2,32,1536]{2,1,0:T(8,128)(2,1)}, u32[]{:S(2)}) copy-start(bf16[2,32,1536]{2,1,0:T(8,128)(2,1)} %copy-done.6) | copy-start | bytes 589828
  119.1 1.8 copy-start.4
  119.1 1.8 copy-start.12
  119.1 1.8 copy-start.22
  122.3 4.0 %copy-start.20 = (bf16[2,32,896]{2,1,0:T(8,128)(2,1)}, bf16[2,32,896]{2,1,0:T(8,128)(2,1)S(1)}, u32[]{:S(2)}) copy-start(bf16[2,32,896]{2,1,0:T(8,128)(2,1)S(1)} %convolution_convert_fusion) | copy-start | bytes 344068
  123.0 57.1 %collective-permute-start.3 = (bf16[2,32,640]{2,1,0:T(8,128)(2,1)S(1)}, bf16[2,32,640]{2,1,0:T(8,128)(2,1)}, u32[]{:S(2)}, u32[]{:S(2)}) collective-permute-start(bf16[2,32,640]{2,1,0:T(8,128)(2,1)S(1)} %slice.143), channel_id=1, source_target_pairs={{2,0},{4,2},{6,4},{8,6},{10,8},{12,10},{14,12},{16,14},{18,16},{20... | collective-permute-start | bytes 245768 | tf_op jit(solution)/shard_map/ppermute | solution.py:27
  126.4 53.8 %collective-permute-start.2 = (bf16[2,32,640]{2,1,0:T(8,128)(2,1)S(1)}, bf16[2,32,640]{2,1,0:T(8,128)(2,1)}, u32[]{:S(2)}, u32[]{:S(2)}) collective-permute-start(bf16[2,32,640]{2,1,0:T(8,128)(2,1)S(1)} %slice.143), channel_id=1, source_target_pairs={{0,2},{2,4},{4,6},{6,8},{8,10},{10,12},{12,14},{14,16},{16,18},{18... | collective-permute-start | bytes 245768 | tf_op jit(solution)/shard_map/ppermute | solution.py:26
  139.0 7.4 %copy-start.14 = (bf16[2,128,640]{2,1,0:T(8,128)(2,1)}, bf16[2,128,640]{2,1,0:T(8,128)(2,1)S(1)}, u32[]{:S(2)}) copy-start(bf16[2,128,640]{2,1,0:T(8,128)(2,1)S(1)} %all_gather.20) | copy-start | bytes 983044
  147.1 32.2 %slice-start = ((bf16[2,128,640]{2,1,0:T(8,128)(2,1)}), bf16[2,128,384]{2,1,0:T(8,128)(2,1)S(1)}, s32[]{:S(2)}) async-start(bf16[2,128,640]{2,1,0:T(8,128)(2,1)} %copy-done.14), calls=%async_computation.1 | async-start | bytes 393216 | tf_op jit(solution)/shard_map/slice | solution.py:128
  183.2 6.7 %copy-start.28 = (pred[4,32,96]{2,1,0:T(8,128)(4,1)S(1)}, pred[4,32,96]{2,1,0:T(8,128)(4,1)}, u32[]{:S(2)}) copy-start(pred[4,32,96]{2,1,0:T(8,128)(4,1)} %compare_and_fusion.2) | copy-start | bytes 36868
  183.2 7.7 %copy-start.15 = (bf16[2,128,256]{1,2,0:T(8,128)(2,1)S(1)}, bf16[2,128,256]{1,2,0:T(8,128)(2,1)}, u32[]{:S(2)}) copy-start(bf16[2,128,256]{1,2,0:T(8,128)(2,1)} %copy.115) | copy-start | bytes 393220
  185.0 4.9 %copy-start.24 = (bf16[2,96,4,96]{3,2,1,0:T(4,128)(2,1)S(1)}, bf16[2,96,4,96]{3,2,1,0:T(4,128)(2,1)}, u32[]{:S(2)}) copy-start(bf16[2,96,4,96]{3,2,1,0:T(4,128)(2,1)} %reshape.293) | copy-start | bytes 442372
  185.0 5.0 %copy-start.30 = (f32[32,4,96]{2,0,1:T(8,128)S(1)}, f32[32,4,96]{2,0,1:T(8,128)}, u32[]{:S(2)}) copy-start(f32[32,4,96]{2,0,1:T(8,128)} %copy.119) | copy-start | bytes 147460
  188.7 2.2 copy-start.31
  192.8 4.8 %copy-start.32 = (f32[1,8,32]{2,1,0:T(8,128)S(1)}, f32[1,8,32]{2,1,0:T(8,128)}, u32[]{:S(2)}) copy-start(f32[1,8,32]{2,1,0:T(8,128)} %copy-done.31) | copy-start | bytes 3076
  192.8 4.8 %copy-start.37 = (f32[2,32,4]{1,2,0:T(4,128)S(1)}, f32[2,32,4]{1,2,0:T(4,128)}, u32[]{:S(2)}) copy-start(f32[2,32,4]{1,2,0:T(4,128)} %fusion.26) | copy-start | bytes 3076
  194.0 17.3 %copy-start.27 = (bf16[32,4,96]{2,1,0:T(4,128)(2,1)S(1)}, bf16[32,4,96]{2,1,0:T(4,128)(2,1)}, u32[]{:S(2)}) copy-start(bf16[32,4,96]{2,1,0:T(4,128)(2,1)} %reshape.294) | copy-start | bytes 73732
  212.4 12.4 %copy-start.36 = (pred[4,128,32]{1,2,0:T(8,128)(4,1)S(1)}, pred[4,128,32]{1,2,0:T(8,128)(4,1)}, u32[]{:S(2)}) copy-start(pred[4,128,32]{1,2,0:T(8,128)(4,1)} %compare_and_fusion) | copy-start | bytes 49156
  214.3 12.3 %copy-start.19 = (bf16[128,384]{0,1:T(8,128)(2,1)S(1)}, bf16[128,384]{0,1:T(8,128)(2,1)}, u32[]{:S(2)}) copy-start(bf16[128,384]{0,1:T(8,128)(2,1)} %copy.133) | copy-start | bytes 294916
  217.1 20.7 %collective-permute-start.4 = (bf16[2,32,640]{2,1,0:T(8,128)(2,1)}, bf16[2,32,640]{2,1,0:T(8,128)(2,1)}, u32[]{:S(2)}, u32[]{:S(2)}) collective-permute-start(bf16[2,32,640]{2,1,0:T(8,128)(2,1)} %get-tuple-element.12), channel_id=1, source_target_pairs={{0,2},{2,4},{4,6},{6,8},{8,10},{10,12},{12,14},{14,16},{16,18},{18... | collective-permute-start | bytes 245768 | tf_op jit(solution)/shard_map/ppermute | solution.py:35
  219.8 18.1 %collective-permute-start.5 = (bf16[2,32,640]{2,1,0:T(8,128)(2,1)}, bf16[2,32,640]{2,1,0:T(8,128)(2,1)}, u32[]{:S(2)}, u32[]{:S(2)}) collective-permute-start(bf16[2,32,640]{2,1,0:T(8,128)(2,1)} %get-tuple-element.13), channel_id=1, source_target_pairs={{2,0},{4,2},{6,4},{8,6},{10,8},{12,10},{14,12},{16,14},{18,16},{20... | collective-permute-start | bytes 245768 | tf_op jit(solution)/shard_map/ppermute | solution.py:35
  228.6 10.3 %copy-start.34 = (f32[1536]{0:T(1024)S(1)}, f32[1536]{0:T(1024)}, u32[]{:S(2)}) copy-start(f32[1536]{0:T(1024)} %param.15) | copy-start | bytes 18436
  238.9 2.0 copy-start.5
  238.9 2.0 copy-start.17
  238.9 2.0 copy-start.25
  238.9 2.0 copy-start.39
  240.9 2.6 %copy-start.3 = (bf16[1,4,384,384]{3,2,0,1:T(8,128)(2,1)S(1)}, bf16[1,4,384,384]{3,2,0,1:T(8,128)(2,1)}, u32[]{:S(2)}) copy-start(bf16[1,4,384,384]{3,2,0,1:T(8,128)(2,1)} %copy-done.2) | copy-start | bytes 3538948
  241.4 8.5 %copy-start.1 = (bf16[1,4,384,384]{3,2,0,1:T(8,128)(2,1)S(1)}, bf16[1,4,384,384]{3,2,0,1:T(8,128)(2,1)}, u32[]{:S(2)}) copy-start(bf16[1,4,384,384]{3,2,0,1:T(8,128)(2,1)} %copy-done) | copy-start | bytes 3538948
  241.5 8.5 %collective-permute-start.7 = (bf16[2,16,384]{2,1,0:T(8,128)(2,1)S(1)}, bf16[2,16,384]{2,1,0:T(8,128)(2,1)S(1)}, u32[]{:S(2)}, u32[]{:S(2)}) collective-permute-start(bf16[2,16,384]{2,1,0:T(8,128)(2,1)S(1)} %get-tuple-element.19), channel_id=1, source_target_pairs={{0,2},{2,4},{4,6},{6,8},{8,10},{10,12},{12,14},{14,16},{16,18},{18... | collective-permute-start | bytes 73736 | tf_op jit(solution)/shard_map/ppermute | solution.py:26
  244.0 7.4 %copy-start.9 = (bf16[1,4,384,384]{3,2,0,1:T(8,128)(2,1)S(1)}, bf16[1,4,384,384]{3,2,0,1:T(8,128)(2,1)}, u32[]{:S(2)}) copy-start(bf16[1,4,384,384]{3,2,0,1:T(8,128)(2,1)} %get-tuple-element.7) | copy-start | bytes 3538948
  244.0 7.4 %copy-start.13 = (f32[32,1536]{1,0:T(8,128)S(1)}, f32[32,1536]{1,0:T(8,128)}, u32[]{:S(2)}) copy-start(f32[32,1536]{1,0:T(8,128)} %copy-done.11) | copy-start | bytes 589828
  244.0 7.4 %copy-start.23 = (bf16[2,32,1536]{2,1,0:T(8,128)(2,1)S(1)}, bf16[2,32,1536]{2,1,0:T(8,128)(2,1)}, u32[]{:S(2)}) copy-start(bf16[2,32,1536]{2,1,0:T(8,128)(2,1)} %param.11) | copy-start | bytes 589828
  244.0 7.4 %collective-permute-start.6 = (bf16[2,16,384]{2,1,0:T(8,128)(2,1)S(1)}, bf16[2,16,384]{2,1,0:T(8,128)(2,1)S(1)}, u32[]{:S(2)}, u32[]{:S(2)}) collective-permute-start(bf16[2,16,384]{2,1,0:T(8,128)(2,1)S(1)} %get-tuple-element.18), channel_id=1, source_target_pairs={{2,0},{4,2},{6,4},{8,6},{10,8},{12,10},{14,12},{16,14},{18,16},{20... | collective-permute-start | bytes 73736 | tf_op jit(solution)/shard_map/ppermute | solution.py:27
  252.1 1.4 collective-permute-start.8
  (5 other events, 4.3 us)
Sparse Core Ops, SparseCore 0:
  12.9 79.8 all-gather.2

commit v2 on v0

--- a/solution.py
+++ b/solution.py
@@ -1,6 +1,8 @@
 import jax
 import jax.numpy as jnp
 from jax import lax
+from jax.experimental import pallas as pl
+from jax.experimental.pallas import tpu as pltpu
 from jax.sharding import PartitionSpec as P
 
 HID = 384
@@ -235,9 +237,375 @@
     return summed / (samples_dev * lax.axis_size("noise"))
 
 
+def permuted(value, pairs):
+    return lax.ppermute(value, ("sa", "sb", "noise"), pairs)
+
+
+def routes(n_sa, route):
+    flat = lambda z, y, x, c: ((z * 2 + y) * 2 + x) * 2 + c
+    pairs = []
+    for z in range(n_sa):
+        for y in range(2):
+            for x in range(2):
+                for c in range(2):
+                    target = route(z, y, x, c)
+                    if target is not None and 0 <= target[0] < n_sa:
+                        pairs.append((flat(z, y, x, c), flat(*target)))
+    return pairs
+
+
+def pack_kernel(info, conv, mix, qkv, out, packed, sems):
+    b, n = info[1], info[2]
+    part = b * 2 + n
+    rows = pl.ds(pl.multiple_of(part * 48, 16), 48)
+    half = pl.ds(pl.multiple_of(n * 48, 16), 48)
+    columns = pl.ds(pl.multiple_of(b * 384, 128), 384)
+    copies = [(conv.at[t, rows, :], packed.at[pl.ds(48 * t, 48), :]) for t in range(3)]
+    copies.append((mix.at[half, columns], packed.at[pl.ds(144, 48), :]))
+    copies.append((out.at[half, columns], packed.at[pl.ds(192, 48), :]))
+    for k in range(2):
+        copies.append((qkv.at[rows, pl.ds(384 * k, 384)], packed.at[pl.ds(240 + 48 * k, 48), :]))
+    for k in range(3):
+        third = pl.ds(pl.multiple_of(part * 48 + 16 * k, 16), 16)
+        copies.append((qkv.at[third, pl.ds(768, 128)], packed.at[pl.ds(336, 16), pl.ds(128 * k, 128)]))
+    started = [pltpu.make_async_copy(s, d, sems.at[i]) for i, (s, d) in enumerate(copies)]
+    for copy in started:
+        copy.start()
+    for copy in started:
+        copy.wait()
+
+
+def nt(a, b):
+    return lax.dot_general(a, b, (((1,), (1,)), ((), ())), preferred_element_type=jnp.float32)
+
+
+def tn(a, b):
+    return lax.dot_general(a, b, (((0,), (0,)), ((), ())), preferred_element_type=jnp.float32)
+
+
+def nn(a, b):
+    return jnp.dot(a, b, preferred_element_type=jnp.float32)
+
+
+CHUNK = 384
+
+
+def chunk(c):
+    return pl.ds(pl.multiple_of(c * CHUNK, 128), CHUNK)
+
+
+def forward_kernel(
+    info, band, noise, base, cot, gathered, gain,
+    d_q_out, d_kv_out, send, resid_out, inv_out, hidden_out, conv_out, mix_out, qkv_out,
+    conv, mix, qkv, out, noisy, gelu_in, sems,
+):
+    length = info[5]
+    first = info[0] * 128
+    pair_flag = info[4]
+
+    def unpack(i, _):
+        part = lax.rem(i, 8)
+        z = i // 8
+        b, n = part // 2, lax.rem(part, 2)
+        rows = pl.ds(pl.multiple_of(z * 384 + part * 48, 16), 48)
+        half = pl.ds(pl.multiple_of(z * 96 + n * 48, 16), 48)
+        columns = pl.ds(pl.multiple_of(b * 384, 128), 384)
+        for t in range(3):
+            conv[t, rows, :] = gathered[i, pl.ds(48 * t, 48), :]
+        mix[half, columns] = gathered[i, pl.ds(144, 48), :]
+        out[half, columns] = gathered[i, pl.ds(192, 48), :]
+        for k in range(2):
+            qkv[rows, pl.ds(384 * k, 384)] = gathered[i, pl.ds(240 + 48 * k, 48), :]
+        for k in range(3):
+            third = pl.ds(pl.multiple_of(z * 384 + part * 48 + 16 * k, 16), 16)
+            qkv[third, pl.ds(768, 128)] = gathered[i, pl.ds(336, 16), pl.ds(128 * k, 128)]
+        return 0
+
+    lax.fori_loop(0, gathered.shape[0], unpack, 0)
+    copies = [
+        pltpu.make_async_copy(s, d, sems.at[i])
+        for i, (s, d) in enumerate(((conv, conv_out), (mix, mix_out), (qkv, qkv_out)))
+    ]
+    for copy in copies:
+        copy.start()
+
+    def activate(c, _):
+        values = base[:, chunk(c)].astype(jnp.float32) + noise[:, chunk(c)].astype(jnp.float32)
+        noisy[:, chunk(c)] = values
+        gelu_in[:, chunk(c)] = gelu_tanh(values).astype(jnp.bfloat16)
+        return 0
+
+    lax.fori_loop(0, 4, activate, 0)
+
+    def convolve(c, total):
+        for t in range(3):
+            total = total + nn(gelu_in[pl.ds(16 * t, 192), chunk(c)], conv[t, chunk(c), :])
+        return total
+
+    hidden = lax.fori_loop(0, 4, convolve, jnp.zeros((192, HID), jnp.float32))
+    hidden_out[...] = hidden[32:160]
+    act = gelu_tanh(hidden).astype(jnp.bfloat16)
+
+    def mixing(c, squares):
+        resid = noisy[pl.ds(16, 192), chunk(c)] + nn(act, mix[:, chunk(c)])
+        noisy[pl.ds(16, 192), chunk(c)] = resid
+        resid_out[:, chunk(c)] = resid[32:160]
+        return squares + jnp.sum(resid * resid, axis=1, keepdims=True)
+
+    squares = lax.fori_loop(0, 4, mixing, jnp.zeros((192, 1), jnp.float32))
+    inv_rms = lax.rsqrt(squares * (1.0 / 1536) + 1e-06)
+    inv_out[...] = inv_rms[32:160]
+
+    def project(c, total):
+        normed = (noisy[pl.ds(16, 192), chunk(c)] * inv_rms * gain[:, chunk(c)]).astype(jnp.bfloat16)
+        return total + nn(normed, qkv[chunk(c), :])
+
+    proj = lax.fori_loop(0, 4, project, jnp.zeros((192, 896), jnp.float32)).astype(jnp.bfloat16)
+
+    def attended(c, total):
+        return total + nt(cot[:, chunk(c)], out[:, chunk(c)])
+
+    d_att = lax.fori_loop(0, 4, attended, jnp.zeros((128, HEADS * VAL), jnp.float32)).astype(jnp.bfloat16)
+
+    row = lax.broadcasted_iota(jnp.int32, (128, 192), 0)
+    column = lax.broadcasted_iota(jnp.int32, (128, 192), 1) - 32
+    inside = (column + first >= 0) & (column + first < length)
+    paired = (column >= 0) & (column < 128) & (pair_flag > 0)
+    apart = jnp.abs(row - column)
+    scale = KEY ** (-0.5)
+    d_queries, d_keys, d_values = [], [], []
+    for h in range(HEADS):
+        q = proj[32:160, KEY * h : KEY * (h + 1)]
+        k = proj[:, HEADS * KEY + KEY * h : HEADS * KEY + KEY * (h + 1)]
+        v = proj[:, 2 * HEADS * KEY + VAL * h : 2 * HEADS * KEY + VAL * (h + 1)]
+        d_att_h = d_att[:, VAL * h : VAL * (h + 1)]
+        allowed = inside & (paired | (apart <= band[h]))
+        score = jnp.where(allowed, nt(q, k) * scale, -1e30)
+        top = jnp.max(score, axis=1, keepdims=True)
+        raised = jnp.where(allowed, jnp.exp(score - top), 0.0)
+        prob = raised / jnp.sum(raised, axis=1, keepdims=True)
+        prob_b = prob.astype(jnp.bfloat16)
+        attn = nn(prob_b, v)
+        delta = jnp.sum(d_att_h.astype(jnp.float32) * attn, axis=1, keepdims=True)
+        d_score = (prob * (nt(d_att_h, v) - delta) * scale).astype(jnp.bfloat16)
+        d_queries.append(nn(d_score, k))
+        d_keys.append(tn(d_score, q))
+        d_values.append(tn(prob_b, d_att_h))
+    d_q_out[...] = jnp.concatenate(d_queries, axis=1)
+    d_kv = jnp.concatenate(d_keys + d_values, axis=1)
+    d_kv_out[...] = d_kv[32:160]
+
+    @pl.when(info[2] == 0)
+    def _():
+        send[...] = d_kv[:32].astype(jnp.bfloat16)
+
+    @pl.when(info[2] == 1)
+    def _():
+        send[...] = d_kv[160:].astype(jnp.bfloat16)
+
+    for copy in copies:
+        copy.wait()
+
+
+def norm_kernel(
+    info, d_q, d_kv, received, resid, inv_rms_ref, hidden, cot, gain, mix, qkv,
+    d_hidden_out, d_resid_out, send, total_kv, gained, d_resid_all,
+):
+    n = info[2]
+    total_kv[...] = d_kv[...]
+    edge = pl.ds(pl.multiple_of(n * 96, 32), 32)
+    total_kv[edge, :] = total_kv[edge, :] + received[...].astype(jnp.float32)
+    d_proj = jnp.concatenate([d_q[...], total_kv[...]], axis=1).astype(jnp.bfloat16)
+    inv_rms = inv_rms_ref[...]
+
+    def back(c, mean):
+        part = gain[:, chunk(c)] * nt(d_proj, qkv[chunk(c), :])
+        gained[:, chunk(c)] = part
+        return mean + jnp.sum(resid[:, chunk(c)] * part, axis=1, keepdims=True)
+
+    mean = lax.fori_loop(0, 4, back, jnp.zeros((128, 1), jnp.float32)) * (1.0 / 1536)
+    cubed = inv_rms * inv_rms * inv_rms * mean
+
+    def residual(c, total):
+        d_resid = (
+            cot[:, chunk(c)].astype(jnp.float32)
+            + inv_rms * gained[:, chunk(c)]
+            - resid[:, chunk(c)] * cubed
+        )
+        d_resid_all[:, chunk(c)] = d_resid
+        return total + nt(d_resid.astype(jnp.bfloat16), mix[:, chunk(c)])
+
+    d_act = lax.fori_loop(0, 4, residual, jnp.zeros((128, HID), jnp.float32))
+    d_hidden = (d_act * gelu_slope(hidden[...])).astype(jnp.bfloat16)
+    d_hidden_out[...] = d_hidden
+    d_resid_out[...] = d_resid_all[pl.ds(pl.multiple_of(n * 64, 64), 64), :]
+
+    @pl.when(n == 0)
+    def _():
+        send[...] = d_hidden[:16]
+
+    @pl.when(n == 1)
+    def _():
+        send[...] = d_hidden[112:]
+
+
+def taps_kernel(info, d_hidden, received, d_resid, noise, base, conv, keep, send, extended_ref, grads):
+    n, x = info[2], info[3]
+
+    @pl.when(n == 0)
+    def _():
+        extended_ref[pl.ds(0, 16), :] = received[...]
+        extended_ref[pl.ds(16, 80), :] = d_hidden[pl.ds(0, 80), :]
+
+    @pl.when(n == 1)
+    def _():
+        extended_ref[pl.ds(0, 80), :] = d_hidden[pl.ds(48, 80), :]
+        extended_ref[pl.ds(80, 16), :] = received[...]
+
+    rows = pl.ds(pl.multiple_of(48 + 64 * n, 16), 64)
+
+    def taps(c, _):
+        noisy = base[rows, chunk(c)].astype(jnp.float32) + noise[rows, chunk(c)].astype(jnp.float32)
+        total = nt(extended_ref[pl.ds(32, 64), :], conv[0, chunk(c), :])
+        total = total + nt(extended_ref[pl.ds(16, 64), :], conv[1, chunk(c), :])
+        total = total + nt(extended_ref[pl.ds(0, 64), :], conv[2, chunk(c), :])
+        grads[:, chunk(c)] = d_resid[:, chunk(c)] + total * gelu_slope(noisy)
+        return 0
+
+    lax.fori_loop(0, 4, taps, 0)
+    keep[...] = grads[pl.ds(pl.multiple_of(32 * x, 32), 32), :]
+    send[...] = grads[pl.ds(pl.multiple_of(32 - 32 * x, 32), 32), :].astype(jnp.bfloat16)
+
+
+def vmem(count):
+    return [pl.BlockSpec(memory_space=pltpu.VMEM)] * count
+
+
+def smem(count):
+    return [pl.BlockSpec(memory_space=pltpu.SMEM)] * count
+
+
+def hbm(count):
+    return [pl.BlockSpec(memory_space=pl.ANY)] * count
+
+
+LIMIT = pltpu.CompilerParams(vmem_limit_bytes=56 * 1024 * 1024)
+f32, bf16 = (jnp.float32, jnp.bfloat16)
+
+
+def shaped(*shape, dtype=jnp.float32):
+    return jax.ShapeDtypeStruct(shape, dtype)
+
+
+def stretch_shards(
+    base, noise, cot, convolution_weight, mix_w, norm_gain, qkv_w, out_w, band_width, pairs
+):
+    n_sa = lax.axis_size("sa")
+    z, b, n = (lax.axis_index("sa"), lax.axis_index("sb"), lax.axis_index("noise"))
+    y, x = (b >> 1, b & 1)
+    flag = jnp.any((pairs[:, 0] == z) & (pairs[:, 1] == z)).astype(jnp.int32)
+    info = jnp.stack([z, b, n, x, flag, jnp.int32(n_sa * 128)]).astype(jnp.int32)
+    features = base.shape[1]
+
+    packed = pl.pallas_call(
+        pack_kernel,
+        out_shape=shaped(352, CHUNK, dtype=bf16),
+        in_specs=smem(1) + hbm(4),
+        out_specs=pl.BlockSpec(memory_space=pl.ANY),
+        scratch_shapes=[pltpu.SemaphoreType.DMA((10,))],
+    )(info, convolution_weight, mix_w, qkv_w, out_w)
+    gathered = lax.all_gather(packed, ("sa", "sb", "noise"), axis=0, tiled=False)
+    gathered = gathered.reshape(-1, 352, CHUNK)
+
+    def to_sample(shift):
+        return routes(n_sa, lambda z, y, x, c: (z, c, (x + shift) % 2, y))
+
+    got = [
+        permuted(jnp.where(x == shift, noise[0], noise[1]), to_sample(shift))
+        for shift in range(2)
+    ]
+    even = x == 0
+    noise_half = jnp.concatenate([jnp.where(even, got[0], got[1]), jnp.where(even, got[1], got[0])], axis=0)
+    both = jnp.stack([base, cot])
+    across = permuted(both, routes(n_sa, lambda z, y, x, c: (z, 1 - y, x, 1 - c) if y != c else None))
+    current = jnp.where(y == n, both, across)
+    beside = permuted(current, routes(n_sa, lambda z, y, x, c: (z, y, 1 - x, c)))
+    halves = jnp.concatenate([jnp.where(even, current, beside), jnp.where(even, beside, current)], axis=1)
+    edge_route = routes(n_sa, lambda z, y, x, c: (z - 1, y, x, 1) if c == 0 else (z + 1, y, x, 0))
+    core_route = routes(n_sa, lambda z, y, x, c: (z, y, x, 1 - c))
+    mine = jnp.stack([noise_half, halves[0]])
+    edge = permuted(jnp.where(n == 0, mine[:, :48], mine[:, 16:]), edge_route)
+    wide = jnp.concatenate([jnp.where(n == 0, edge, mine[:, :48])] + [jnp.where(n == 0, mine, jnp.concatenate([mine[:, 48:], edge], axis=1))], axis=1)
+    swap = permuted(jnp.concatenate([wide.reshape(224, features), halves[1]], axis=0), core_route)
+    wide_other = swap[:224].reshape(2, 112, features)
+    whole = jnp.concatenate([jnp.where(n == 0, wide, wide_other), jnp.where(n == 0, wide_other, wide)], axis=1)
+    noise_rows, base_rows = whole[0], whole[1]
+    cot_rows = jnp.concatenate(
+        [jnp.where(n == 0, halves[1], swap[224:]), jnp.where(n == 0, swap[224:], halves[1])], axis=0
+    )
+    gain = norm_gain.reshape(1, features)
+
+    d_q, d_kv, send, resid, inv_rms, hidden, conv, mix, qkv = pl.pallas_call(
+        forward_kernel,
+        out_shape=(
+            shaped(128, 256), shaped(128, 640), shaped(32, 640, dtype=bf16), shaped(128, features),
+            shaped(128, 1), shaped(128, HID), shaped(3, features, HID, dtype=bf16),
+            shaped(HID, features, dtype=bf16), shaped(features, 896, dtype=bf16),
+        ),
+        in_specs=smem(2) + vmem(5),
+        out_specs=tuple(vmem(6) + hbm(3)),
+        scratch_shapes=[
+            pltpu.VMEM((3, features, HID), bf16), pltpu.VMEM((HID, features), bf16),
+            pltpu.VMEM((features, 896), bf16), pltpu.VMEM((HEADS * VAL, features), bf16),
+            pltpu.VMEM((224, features), f32), pltpu.VMEM((224, features), bf16),
+            pltpu.SemaphoreType.DMA((3,)),
+        ],
+        compiler_params=LIMIT,
+    )(info, band_width, noise_rows, base_rows, cot_rows, gathered, gain)
+
+    received = permuted(send, edge_route)
+    d_hidden, d_resid, send = pl.pallas_call(
+        norm_kernel,
+        out_shape=(shaped(128, HID, dtype=bf16), shaped(64, features), shaped(16, HID, dtype=bf16)),
+        in_specs=smem(1) + vmem(10),
+        out_specs=tuple(vmem(3)),
+        scratch_shapes=[
+            pltpu.VMEM((128, 640), f32), pltpu.VMEM((128, features), f32), pltpu.VMEM((128, features), f32),
+        ],
+        compiler_params=LIMIT,
+    )(info, d_q, d_kv, received, resid, inv_rms, hidden, cot_rows, gain, mix, qkv)
+
+    received = permuted(send, edge_route)
+    keep, send = pl.pallas_call(
+        taps_kernel,
+        out_shape=(shaped(32, features), shaped(32, features, dtype=bf16)),
+        in_specs=smem(1) + vmem(6),
+        out_specs=tuple(vmem(2)),
+        scratch_shapes=[pltpu.VMEM((96, HID), bf16), pltpu.VMEM((64, features), f32)],
+        compiler_params=LIMIT,
+    )(info, d_hidden, received, d_resid, noise_rows, base_rows, conv)
+
+    received = permuted(send, routes(n_sa, lambda z, y, x, c: (z, y, 1 - x, c)))
+    partial = (keep + received.astype(f32)).astype(bf16)
+    first_sum = permuted(
+        partial, routes(n_sa, lambda z, y, x, c: (z, c, x, c) if y != c else (z, y, x, 1 - c))
+    )
+    second_sum = permuted(partial, routes(n_sa, lambda z, y, x, c: (z, c, x, 1 - c) if y != c else None))
+    other = jnp.where(y == n, partial, second_sum)
+    return (first_sum.astype(f32) + other.astype(f32)) * 0.25
+
+
 def solution(mesh):
+    fits = mesh.shape["sb"] == 4 and mesh.shape["noise"] == 2 and HEADS == 4
+
+    def body(*arrays):
+        if fits and arrays[0].shape[0] == 32 and arrays[1].shape[0] == 2 and TILE == 128:
+            if arrays[0].shape[1] == 1536 and mesh.shape["sa"] == 4:
+                return stretch_shards(*arrays)
+        return shards(*arrays)
+
     return jax.shard_map(
-        shards,
+        body,
         mesh=mesh,
         in_specs=(
             P(("sa", "sb"), None),

time: 306 us -> 161 us (0.53)
  waiting for transfers between devices: 183 us -> 77.4 us
  Pallas kernels: 0 us -> 37.9 us
  blocking collectives: 34.7 us -> 0 us
  matrix products: 24.1 us -> 0 us
  local copies, waits for them, and re-layouts: 14 us -> 2.44 us
  starting transfers between devices: 29.4 us -> 21.9 us
    all_gather x4 -> x1, waiting for transfers between devices: 161 us -> 50.2 us  [stretch_shards(): lax.all_gather(packed, ('sa', 'sb', 'noise'), axis=0, tiled=False)]
    pallas_call x0 -> x4, Pallas kernels: none -> 37.9 us  [the longest x1 15.9 us: stretch_shards(): pl.pallas_call(forward_kernel, out_shape=(shaped(128, 256), shaped(128, 6...]
    all_gather x4 -> x0, blocking collectives: 34.7 us -> none  [the longest x1 9.34 us: shards(): lax.all_gather(query_rows, 'sb', axis=1, tiled=True)]
    dot_general x26 -> x0, matrix products: 24.1 us -> none  [the longest x3 4.76 us: shards(): jnp.einsum('nbd,dc->nbc', gelu_extended[:, tap_index * DILATION_BINS:tap_...]
    ppermute x8 -> x11, waiting for transfers between devices: 3.34 us -> 27.1 us  [permuted(): return lax.ppermute(value, ('sa', 'sb', 'noise'), pairs)]
    psum x1 -> x0, waiting for transfers between devices: 16.4 us -> none  [shards(): lax.psum(jnp.sum(grads, axis=0).astype(jnp.bfloat16), 'noise')]
    ppermute x8 -> x11, starting transfers between devices: 29.3 us -> 21.9 us  [permuted(): return lax.ppermute(value, ('sa', 'sb', 'noise'), pairs)]
    reshape x10 -> x1, local copies, waits for them, and re-layouts: 6.42 us -> 0.6 us  [stretch_shards(): gain = norm_gain.reshape(1, features)]
  transfers between devices with their start and end apart: 13 -> 12, of which waited for: 6 -> 9; matrix products, arithmetic and copies ran while one was open for 9% -> 2% of each run, Pallas kernels for 0% -> 0%
where the time goes in v2:
time: 161 us; the launch traced here: 160 us
  waiting for transfers between devices  77.4 us (48%)
  Pallas kernels  37.9 us (24%)
  starting transfers between devices  21.9 us (14%)
  between operations  14.3 us (9%)
  other arithmetic  5.87 us (4%)
  local copies, waits for them, and re-layouts  2.44 us (2%)
    all_gather x1, waiting for transfers between devices, stretch_shards(): lax.all_gather(packed, ('sa', 'sb', 'noise'), axis=0, tiled=False)  50.2 us
    ppermute x11, waiting for transfers between devices, permuted(): return lax.ppermute(value, ('sa', 'sb', 'noise'), pairs)  27.1 us
    ppermute x11, starting transfers between devices, permuted(): return lax.ppermute(value, ('sa', 'sb', 'noise'), pairs)  21.9 us
    pallas_call x1, Pallas kernels, stretch_shards(): pl.pallas_call(forward_kernel, out_shape=(shaped(128, 256), shaped(128, 6...  15.9 us
    pallas_call x1, Pallas kernels, stretch_shards(): pl.pallas_call(pack_kernel, out_shape=shaped(352, CHUNK, dtype=bf16), in_...  10.2 us
    pallas_call x1, Pallas kernels, stretch_shards(): pl.pallas_call(norm_kernel, out_shape=(shaped(128, HID, dtype=bf16), shap...  6.71 us
    pallas_call x1, Pallas kernels, stretch_shards(): pl.pallas_call(taps_kernel, out_shape=(shaped(32, features), shaped(32, f...  5.08 us
  transfers between devices with their start and end apart: 12, of which 9 were waited for; matrix products, arithmetic and copies ran while one was open for 2% of the time, Pallas kernels for 0%

profile of v2, /device:TPU:8, one launch (start us, length us, event | category | flops | bytes accessed | tf_op | source)
XLA Modules:
  0.0 159.8 jit_solution(15424421773103912941)
XLA Ops:
  6.5 0.0 copy-start.2
  6.5 0.0 all-gather.3.cloned.1.call-start
  6.5 1.5 and_reduce_fusion
  8.7 0.6 stack.42.info
  9.3 10.2 %shard_map.100 = bf16[352,384]{1,0:T(8,128)(2,1)} custom-call(s32[6]{0:T(128)} %stack.42.info, bf16[3,384,384]{2,1,0:T(8,128)(2,1)} %conv.1, bf16[96,1536]{1,0:T(8,128)(2,1)} %mix.1, bf16[384,896]{1,0:T(8,128)(2,1)} %qkv.1, bf16[96,1536]{1,0:T(8,128)(2,1)} %out.1), custom_call_target="tpu_custom_call" | custom-call | tf_op jit(solution)/shard_map/pallas_call | solution.py:510
  19.5 0.0 all-gather.3.cloned.1.call-update
  19.5 0.0 copy-done.2
  19.5 0.7 collective-permute-start
  20.2 1.6 collective-permute-start.1
  21.8 0.0 copy-done
  21.8 0.0 copy-done.1
  21.8 0.7 collective-permute-start.2
  22.5 0.0 collective-permute-done
  22.5 2.4 %collective-permute-done.1 = bf16[32,1536]{1,0:T(8,128)(2,1)S(1)} collective-permute-done((bf16[32,1536]{1,0:T(8,128)(2,1)S(1)}, bf16[32,1536]{1,0:T(8,128)(2,1)S(1)}, u32[]{:S(2)}, u32[]{:S(2)}) %collective-permute-start.1) | collective-permute-done | bytes 98336 | tf_op jit(solution)/shard_map/ppermute | solution.py:241
  24.9 0.0 collective-permute-done.2
  25.0 1.6 collective-permute-start.3
  26.5 4.2 %collective-permute-done.3 = bf16[2,32,1536]{2,1,0:T(8,128)(2,1)S(1)} collective-permute-done((bf16[2,32,1536]{2,1,0:T(8,128)(2,1)S(1)}, bf16[2,32,1536]{2,1,0:T(8,128)(2,1)S(1)}, u32[]{:S(2)}, u32[]{:S(2)}) %collective-permute-start.3) | collective-permute-done | bytes 196640 | tf_op jit(solution)/shard_map/ppermute | solution.py:241
  30.7 0.1 broadcast_select_fusion.7
  30.8 7.3 %collective-permute-start.4 = (bf16[2,48,1536]{2,1,0:T(8,128)(2,1)S(1)}, bf16[2,48,1536]{2,1,0:T(8,128)(2,1)S(1)}, u32[]{:S(2)}, u32[]{:S(2)}) collective-permute-start(bf16[2,48,1536]{2,1,0:T(8,128)(2,1)S(1)} %fusion.6), channel_id=1, source_target_pairs={{1,8},{3,10},{5,12},{7,14},{8,1},{9,16},{10,3},{11,18},{12,5},{13,... | collective-permute-start | bytes 884744 | tf_op jit(solution)/shard_map/ppermute | solution.py:241
  38.1 5.6 %collective-permute-done.4 = bf16[2,48,1536]{2,1,0:T(8,128)(2,1)S(1)} collective-permute-done((bf16[2,48,1536]{2,1,0:T(8,128)(2,1)S(1)}, bf16[2,48,1536]{2,1,0:T(8,128)(2,1)S(1)}, u32[]{:S(2)}, u32[]{:S(2)}) %collective-permute-start.4) | collective-permute-done | bytes 294944 | tf_op jit(solution)/shard_map/ppermute | solution.py:241
  43.8 0.1 fusion.3
  43.9 0.0 copy-start.5
  44.0 0.1 pad_maximum_fusion
  44.1 0.8 collective-permute-start.5
  44.8 0.0 copy-done.5
  44.8 0.6 reshape.20.gain
  45.4 1.5 collective-permute-done.5
  47.0 0.8 pad_maximum_fusion.4.cot
  47.7 0.2 broadcast_select_fusion
  48.0 1.2 fusion.2
  49.2 50.2 %all-gather.3.cloned.1.call-done = bf16[11264,384]{1,0:T(8,128)(2,1)} async-done(((bf16[352,384]{1,0:T(8,128)(2,1)}), bf16[11264,384]{1,0:T(8,128)(2,1)}) %all-gather.3.cloned.1.call-update) | async-done | bytes 8650768 | tf_op jit(solution)/shard_map/all_gather | solution.py:517
  99.4 15.9 %shard_map.101 = (f32[128,256]{1,0:T(8,128)}, f32[128,640]{1,0:T(8,128)}, bf16[32,640]{1,0:T(8,128)(2,1)}, f32[128,1536]{1,0:T(8,128)}, f32[128,1]{1,0:T(8,128)}...) custom-call(s32[6]{0:T(128)} %stack.42.info, ...), custom_call_target="tpu_custom_call" | custom-call | tf_op jit(solution)/shard_map/pallas_call | solution.py:548
  115.4 2.3 %collective-permute-start.6 = (bf16[32,640]{1,0:T(8,128)(2,1)}, bf16[32,640]{1,0:T(8,128)(2,1)S(1)}, u32[]{:S(2)}, u32[]{:S(2)}) collective-permute-start(bf16[32,640]{1,0:T(8,128)(2,1)} %get-tuple-element.21), channel_id=1, source_target_pairs={{1,8},{3,10},{5,12},{7,14},{8,1},{9,16},{10,3},{11,18},{12,5},{13,... | collective-permute-start | bytes 122888 | tf_op jit(solution)/shard_map/ppermute | solution.py:241
  117.6 3.3 %collective-permute-done.6.received = bf16[32,640]{1,0:T(8,128)(2,1)S(1)} collective-permute-done((bf16[32,640]{1,0:T(8,128)(2,1)}, bf16[32,640]{1,0:T(8,128)(2,1)S(1)}, u32[]{:S(2)}, u32[]{:S(2)}) %collective-permute-start.6) | collective-permute-done | bytes 40992 | tf_op jit(solution)/shard_map/ppermute | solution.py:241
  120.9 0.6 copy-done.3
  121.5 6.7 %shard_map.102 = (bf16[128,384]{1,0:T(8,128)(2,1)}, f32[64,1536]{1,0:T(8,128)}, bf16[16,384]{1,0:T(8,128)(2,1)}) custom-call(s32[6]{0:T(128)} %stack.42.info, f32[128,256]{1,0:T(8,128)} %get-tuple-element.19.d_q, f32[128,640]{1,0:T(8,128)} %get-tuple-element.20.d_kv, bf16[32,640]{1,0:T(8,128)(2,1)} %copy-done.3, f32[128,1536]{1,0:T(8,128)} %get-tuple-element.22.resid, ...), custom_call_target="tpu_custom_call" | custom-call | tf_op jit(solution)/shard_map/pallas_call | solution.py:567
  128.2 2.2 %collective-permute-start.7 = (bf16[16,384]{1,0:T(8,128)(2,1)}, bf16[16,384]{1,0:T(8,128)(2,1)S(1)}, u32[]{:S(2)}, u32[]{:S(2)}) collective-permute-start(bf16[16,384]{1,0:T(8,128)(2,1)} %get-tuple-element.28), channel_id=1, source_target_pairs={{1,8},{3,10},{5,12},{7,14},{8,1},{9,16},{10,3},{11,18},{12,5},{13,... | collective-permute-start | bytes 36872 | tf_op jit(solution)/shard_map/ppermute | solution.py:241
  130.5 3.0 %collective-permute-done.7.received = bf16[16,384]{1,0:T(8,128)(2,1)S(1)} collective-permute-done((bf16[16,384]{1,0:T(8,128)(2,1)}, bf16[16,384]{1,0:T(8,128)(2,1)S(1)}, u32[]{:S(2)}, u32[]{:S(2)}) %collective-permute-start.7) | collective-permute-done | bytes 12320 | tf_op jit(solution)/shard_map/ppermute | solution.py:241
  133.5 0.6 copy-done.4
  134.0 5.1 %shard_map.103 = (f32[32,1536]{1,0:T(8,128)}, bf16[32,1536]{1,0:T(8,128)(2,1)}) custom-call(s32[6]{0:T(128)} %stack.42.info, bf16[128,384]{1,0:T(8,128)(2,1)} %get-tuple-element.27.d_hidden, bf16[16,384]{1,0:T(8,128)(2,1)} %copy-done.4, f32[64,1536]{1,0:T(8,128)} %get-tuple-element.29.d_resid, bf16[224,1536]{1,0:T(8,128)(2,1)} %get-tuple-element.34.noise, ...), custom_call_target="tpu_custom_call" | custom-call | tf_op jit(solution)/shard_map/pallas_call | solution.py:579
  139.1 1.4 collective-permute-start.8
  140.5 3.7 %collective-permute-done.8 = bf16[32,1536]{1,0:T(8,128)(2,1)S(1)} collective-permute-done((bf16[32,1536]{1,0:T(8,128)(2,1)}, bf16[32,1536]{1,0:T(8,128)(2,1)S(1)}, u32[]{:S(2)}, u32[]{:S(2)}) %collective-permute-start.8) | collective-permute-done | bytes 98336 | tf_op jit(solution)/shard_map/ppermute | solution.py:241
  144.3 1.0 add_convert_fusion
  145.2 0.7 collective-permute-start.10
  145.9 2.8 %collective-permute-start.9 = (bf16[32,1536]{1,0:T(8,128)(2,1)S(1)}, bf16[32,1536]{1,0:T(8,128)(2,1)S(1)}, u32[]{:S(2)}, u32[]{:S(2)}) collective-permute-start(bf16[32,1536]{1,0:T(8,128)(2,1)S(1)} %add_convert_fusion), channel_id=1, source_target_pairs={{0,1},{1,5},{2,3},{3,7},{4,0},{5,4},{6,2},{7,6},{8,9},{9,13},{10,1... | collective-permute-start | bytes 294920 | tf_op jit(solution)/shard_map/ppermute | solution.py:241
  148.7 0.0 collective-permute-done.10
  148.7 3.5 %collective-permute-done.9 = bf16[32,1536]{1,0:T(8,128)(2,1)S(1)} collective-permute-done((bf16[32,1536]{1,0:T(8,128)(2,1)S(1)}, bf16[32,1536]{1,0:T(8,128)(2,1)S(1)}, u32[]{:S(2)}, u32[]{:S(2)}) %collective-permute-start.9) | collective-permute-done | bytes 98336 | tf_op jit(solution)/shard_map/ppermute | solution.py:241
  152.2 0.7 add_multiply_fusion
  (16 shorter events, 0.3 us)
Async XLA Ops:
  6.5 13.0 %copy-start.2 = (bf16[2,32,1536]{2,1,0:T(8,128)(2,1)S(1)}, bf16[2,32,1536]{2,1,0:T(8,128)(2,1)}, u32[]{:S(2)}) copy-start(bf16[2,32,1536]{2,1,0:T(8,128)(2,1)} %param.11) | copy-start | bytes 589828
  6.5 92.9 %all-gather.3.cloned.1.call-start = ((), (), s32[]{:S(2)}) async-start(), calls=%async_computation | async-start | bytes 8921088 | tf_op jit(solution)/shard_map/all_gather | solution.py:517
  9.3 12.5 %copy-start = (bf16[32,1536]{1,0:T(8,128)(2,1)S(1)}, bf16[32,1536]{1,0:T(8,128)(2,1)}, u32[]{:S(2)}) copy-start(bf16[32,1536]{1,0:T(8,128)(2,1)} %param.12) | copy-start | bytes 294916
  9.3 12.5 %copy-start.1 = (bf16[32,1536]{1,0:T(8,128)(2,1)S(1)}, bf16[32,1536]{1,0:T(8,128)(2,1)}, u32[]{:S(2)}) copy-start(bf16[32,1536]{1,0:T(8,128)(2,1)} %param.10) | copy-start | bytes 294916
  19.5 3.0 %collective-permute-start = (bf16[32,1536]{1,0:T(8,128)(2,1)S(1)}, bf16[32,1536]{1,0:T(8,128)(2,1)S(1)}, u32[]{:S(2)}, u32[]{:S(2)}) collective-permute-start(bf16[32,1536]{1,0:T(8,128)(2,1)S(1)} %get-tuple-element.45), channel_id=1, source_target_pairs={{0,0},{1,4},{2,2},{3,6},{4,1},{5,5},{6,3},{7,7},{8,8},{9,12},{10,1... | collective-permute-start | bytes 294920 | tf_op jit(solution)/shard_map/ppermute | solution.py:241
  20.2 4.7 %collective-permute-start.1 = (bf16[32,1536]{1,0:T(8,128)(2,1)S(1)}, bf16[32,1536]{1,0:T(8,128)(2,1)S(1)}, u32[]{:S(2)}, u32[]{:S(2)}) collective-permute-start(bf16[32,1536]{1,0:T(8,128)(2,1)S(1)} %get-tuple-element.46), channel_id=1, source_target_pairs={{0,2},{1,6},{2,0},{3,4},{4,3},{5,7},{6,1},{7,5},{8,10},{9,14},{10,... | collective-permute-start | bytes 294920 | tf_op jit(solution)/shard_map/ppermute | solution.py:241
  21.8 3.1 %collective-permute-start.2 = (bf16[2,32,1536]{2,1,0:T(8,128)(2,1)S(1)}, bf16[2,32,1536]{2,1,0:T(8,128)(2,1)S(1)}, u32[]{:S(2)}, u32[]{:S(2)}) collective-permute-start(bf16[2,32,1536]{2,1,0:T(8,128)(2,1)S(1)} %pad_maximum_fusion.6), channel_id=1, source_target_pairs={{1,4},{3,6},{4,1},{6,3},{9,12},{11,14},{12,9},{14,11},{17,20},{19,... | collective-permute-start | bytes 589832 | tf_op jit(solution)/shard_map/ppermute | solution.py:241
  25.0 5.7 %collective-permute-start.3 = (bf16[2,32,1536]{2,1,0:T(8,128)(2,1)S(1)}, bf16[2,32,1536]{2,1,0:T(8,128)(2,1)S(1)}, u32[]{:S(2)}, u32[]{:S(2)}) collective-permute-start(bf16[2,32,1536]{2,1,0:T(8,128)(2,1)S(1)} %broadcast_select_fusion.5), channel_id=1, source_target_pairs={{0,2},{1,3},{2,0},{3,1},{4,6},{5,7},{6,4},{7,5},{8,10},{9,11},{10,... | collective-permute-start | bytes 589832 | tf_op jit(solution)/shard_map/ppermute | solution.py:241
  30.8 12.9 %collective-permute-start.4 = (bf16[2,48,1536]{2,1,0:T(8,128)(2,1)S(1)}, bf16[2,48,1536]{2,1,0:T(8,128)(2,1)S(1)}, u32[]{:S(2)}, u32[]{:S(2)}) collective-permute-start(bf16[2,48,1536]{2,1,0:T(8,128)(2,1)S(1)} %fusion.6), channel_id=1, source_target_pairs={{1,8},{3,10},{5,12},{7,14},{8,1},{9,16},{10,3},{11,18},{12,5},{13,... | collective-permute-start | bytes 884744 | tf_op jit(solution)/shard_map/ppermute | solution.py:241
  43.9 0.9 copy-start.5
  44.1 2.8 %collective-permute-start.5 = (bf16[288,1536]{1,0:T(8,128)(2,1)S(1)}, bf16[288,1536]{1,0:T(8,128)(2,1)S(1)}, u32[]{:S(2)}, u32[]{:S(2)}) collective-permute-start(bf16[288,1536]{1,0:T(8,128)(2,1)S(1)} %pad_maximum_fusion), channel_id=1, source_target_pairs={{0,1},{1,0},{2,3},{3,2},{4,5},{5,4},{6,7},{7,6},{8,9},{9,8},{10,11... | collective-permute-start | bytes 2654216 | tf_op jit(solution)/shard_map/ppermute | solution.py:241
  115.4 5.5 %collective-permute-start.6 = (bf16[32,640]{1,0:T(8,128)(2,1)}, bf16[32,640]{1,0:T(8,128)(2,1)S(1)}, u32[]{:S(2)}, u32[]{:S(2)}) collective-permute-start(bf16[32,640]{1,0:T(8,128)(2,1)} %get-tuple-element.21), channel_id=1, source_target_pairs={{1,8},{3,10},{5,12},{7,14},{8,1},{9,16},{10,3},{11,18},{12,5},{13,... | collective-permute-start | bytes 122888 | tf_op jit(solution)/shard_map/ppermute | solution.py:241
  120.9 0.6 copy-start.3
  128.2 5.2 %collective-permute-start.7 = (bf16[16,384]{1,0:T(8,128)(2,1)}, bf16[16,384]{1,0:T(8,128)(2,1)S(1)}, u32[]{:S(2)}, u32[]{:S(2)}) collective-permute-start(bf16[16,384]{1,0:T(8,128)(2,1)} %get-tuple-element.28), channel_id=1, source_target_pairs={{1,8},{3,10},{5,12},{7,14},{8,1},{9,16},{10,3},{11,18},{12,5},{13,... | collective-permute-start | bytes 36872 | tf_op jit(solution)/shard_map/ppermute | solution.py:241
  133.4 0.6 copy-start.4
  139.1 5.1 %collective-permute-start.8 = (bf16[32,1536]{1,0:T(8,128)(2,1)}, bf16[32,1536]{1,0:T(8,128)(2,1)S(1)}, u32[]{:S(2)}, u32[]{:S(2)}) collective-permute-start(bf16[32,1536]{1,0:T(8,128)(2,1)} %get-tuple-element.32), channel_id=1, source_target_pairs={{0,2},{1,3},{2,0},{3,1},{4,6},{5,7},{6,4},{7,5},{8,10},{9,11},{10,... | collective-permute-start | bytes 294920 | tf_op jit(solution)/shard_map/ppermute | solution.py:241
  145.2 3.5 %collective-permute-start.10 = (bf16[32,1536]{1,0:T(8,128)(2,1)S(1)}, bf16[32,1536]{1,0:T(8,128)(2,1)S(1)}, u32[]{:S(2)}, u32[]{:S(2)}) collective-permute-start(bf16[32,1536]{1,0:T(8,128)(2,1)S(1)} %add_convert_fusion), channel_id=1, source_target_pairs={{1,4},{3,6},{4,1},{6,3},{9,12},{11,14},{12,9},{14,11},{17,20},{19,... | collective-permute-start | bytes 294920 | tf_op jit(solution)/shard_map/ppermute | solution.py:241
  145.9 6.3 %collective-permute-start.9 = (bf16[32,1536]{1,0:T(8,128)(2,1)S(1)}, bf16[32,1536]{1,0:T(8,128)(2,1)S(1)}, u32[]{:S(2)}, u32[]{:S(2)}) collective-permute-start(bf16[32,1536]{1,0:T(8,128)(2,1)S(1)} %add_convert_fusion), channel_id=1, source_target_pairs={{0,1},{1,5},{2,3},{3,7},{4,0},{5,4},{6,2},{7,6},{8,9},{9,13},{10,1... | collective-permute-start | bytes 294920 | tf_op jit(solution)/shard_map/ppermute | solution.py:241
Sparse Core Ops, SparseCore 0:
  19.6 79.7 all-gather.2

commit v3 on v2

--- a/solution.py
+++ b/solution.py
@@ -254,25 +254,27 @@
     return pairs
 
 
-def pack_kernel(info, conv, mix, qkv, out, packed, sems):
-    b, n = info[1], info[2]
+def position():
+    b = lax.axis_index("sb")
+    return lax.axis_index("sa"), b // 2, lax.rem(b, 2), lax.axis_index("noise")
+
+
+def pack_kernel(conv, mix, qkv, out, early, late):
+    z, y, x, n = position()
+    b = 2 * y + x
     part = b * 2 + n
     rows = pl.ds(pl.multiple_of(part * 48, 16), 48)
     half = pl.ds(pl.multiple_of(n * 48, 16), 48)
     columns = pl.ds(pl.multiple_of(b * 384, 128), 384)
-    copies = [(conv.at[t, rows, :], packed.at[pl.ds(48 * t, 48), :]) for t in range(3)]
-    copies.append((mix.at[half, columns], packed.at[pl.ds(144, 48), :]))
-    copies.append((out.at[half, columns], packed.at[pl.ds(192, 48), :]))
+    for t in range(3):
+        early[pl.ds(48 * t, 48), :] = conv[t, rows, :]
+    early[pl.ds(144, 48), :] = mix[half, columns]
+    late[pl.ds(0, 48), :] = out[half, columns]
     for k in range(2):
-        copies.append((qkv.at[rows, pl.ds(384 * k, 384)], packed.at[pl.ds(240 + 48 * k, 48), :]))
+        late[pl.ds(48 + 48 * k, 48), :] = qkv[rows, pl.ds(384 * k, 384)]
     for k in range(3):
         third = pl.ds(pl.multiple_of(part * 48 + 16 * k, 16), 16)
-        copies.append((qkv.at[third, pl.ds(768, 128)], packed.at[pl.ds(336, 16), pl.ds(128 * k, 128)]))
-    started = [pltpu.make_async_copy(s, d, sems.at[i]) for i, (s, d) in enumerate(copies)]
-    for copy in started:
-        copy.start()
-    for copy in started:
-        copy.wait()
+        late[pl.ds(144, 16), pl.ds(128 * k, 128)] = qkv[third, pl.ds(768, 128)]
 
 
 def nt(a, b):
@@ -294,37 +296,31 @@
     return pl.ds(pl.multiple_of(c * CHUNK, 128), CHUNK)
 
 
+def pieces(mine, other, n, i):
+    first, second = mine[i], other[i]
+    return jnp.where(n == 0, first, second), jnp.where(n == 0, second, first)
+
+
 def forward_kernel(
-    info, band, noise, base, cot, gathered, gain,
-    d_q_out, d_kv_out, send, resid_out, inv_out, hidden_out, conv_out, mix_out, qkv_out,
-    conv, mix, qkv, out, noisy, gelu_in, sems,
+    noise, base, mine, other, gain, normed_out, resid_out, inv_out, hidden_out, conv_out, mix_out,
+    conv, mix, noisy, gelu_in, sems,
 ):
-    length = info[5]
-    first = info[0] * 128
-    pair_flag = info[4]
+    z, y, x, n = position()
 
     def unpack(i, _):
-        part = lax.rem(i, 8)
-        z = i // 8
-        b, n = part // 2, lax.rem(part, 2)
-        rows = pl.ds(pl.multiple_of(z * 384 + part * 48, 16), 48)
-        half = pl.ds(pl.multiple_of(z * 96 + n * 48, 16), 48)
-        columns = pl.ds(pl.multiple_of(b * 384, 128), 384)
-        for t in range(3):
-            conv[t, rows, :] = gathered[i, pl.ds(48 * t, 48), :]
-        mix[half, columns] = gathered[i, pl.ds(144, 48), :]
-        out[half, columns] = gathered[i, pl.ds(192, 48), :]
-        for k in range(2):
-            qkv[rows, pl.ds(384 * k, 384)] = gathered[i, pl.ds(240 + 48 * k, 48), :]
-        for k in range(3):
-            third = pl.ds(pl.multiple_of(z * 384 + part * 48 + 16 * k, 16), 16)
-            qkv[third, pl.ds(768, 128)] = gathered[i, pl.ds(336, 16), pl.ds(128 * k, 128)]
+        source, b = i // 4, lax.rem(i, 4)
+        for core, piece in enumerate(pieces(mine, other, n, i)):
+            rows = pl.ds(pl.multiple_of(source * 384 + (b * 2 + core) * 48, 16), 48)
+            half = pl.ds(pl.multiple_of(source * 96 + core * 48, 16), 48)
+            columns = pl.ds(pl.multiple_of(b * 384, 128), 384)
+            for t in range(3):
+                conv[t, rows, :] = piece[48 * t : 48 * t + 48]
+            mix[half, columns] = piece[144:192]
         return 0
 
-    lax.fori_loop(0, gathered.shape[0], unpack, 0)
+    lax.fori_loop(0, mine.shape[0], unpack, 0)
     copies = [
-        pltpu.make_async_copy(s, d, sems.at[i])
-        for i, (s, d) in enumerate(((conv, conv_out), (mix, mix_out), (qkv, qkv_out)))
+        pltpu.make_async_copy(s, d, sems.at[i]) for i, (s, d) in enumerate(((conv, conv_out), (mix, mix_out)))
     ]
     for copy in copies:
         copy.start()
@@ -356,16 +352,42 @@
     inv_rms = lax.rsqrt(squares * (1.0 / 1536) + 1e-06)
     inv_out[...] = inv_rms[32:160]
 
-    def project(c, total):
-        normed = (noisy[pl.ds(16, 192), chunk(c)] * inv_rms * gain[:, chunk(c)]).astype(jnp.bfloat16)
-        return total + nn(normed, qkv[chunk(c), :])
-
-    proj = lax.fori_loop(0, 4, project, jnp.zeros((192, 896), jnp.float32)).astype(jnp.bfloat16)
-
-    def attended(c, total):
-        return total + nt(cot[:, chunk(c)], out[:, chunk(c)])
-
-    d_att = lax.fori_loop(0, 4, attended, jnp.zeros((128, HEADS * VAL), jnp.float32)).astype(jnp.bfloat16)
+    def normalise(c, _):
+        normed = noisy[pl.ds(16, 192), chunk(c)] * inv_rms * gain[:, chunk(c)]
+        normed_out[:, chunk(c)] = normed.astype(jnp.bfloat16)
+        return 0
+
+    lax.fori_loop(0, 4, normalise, 0)
+    for copy in copies:
+        copy.wait()
+
+
+def attention_kernel(
+    band, pairs, normed, cot, mine, other, d_q_out, d_kv_out, send, qkv_out, qkv, out, sems,
+):
+    z, y, x, n = position()
+    length = lax.axis_size("sa") * 128
+    first = z * 128
+    pair_flag = jnp.int32(0)
+    for i in range(pairs.shape[0]):
+        pair_flag = pair_flag | ((pairs[i, 0] == z) & (pairs[i, 1] == z)).astype(jnp.int32)
+
+    proj = jnp.zeros((192, 896), jnp.float32)
+    for source in range(4):
+        for b in range(4):
+            for core, piece in enumerate(pieces(mine, other, n, 4 * source + b)):
+                row = source * 384 + (b * 2 + core) * 48
+                out[pl.ds(source * 96 + core * 48, 48), pl.ds(b * 384, 384)] = piece[:48]
+                for k in range(2):
+                    qkv[pl.ds(row, 48), pl.ds(384 * k, 384)] = piece[48 + 48 * k : 96 + 48 * k]
+                for k in range(3):
+                    qkv[pl.ds(row + 16 * k, 16), pl.ds(768, 128)] = piece[144:160, 128 * k : 128 * k + 128]
+        rows = pl.ds(source * 384, 384)
+        proj = proj + nn(normed[:, rows], qkv[rows, :])
+    proj = proj.astype(jnp.bfloat16)
+    copy = pltpu.make_async_copy(qkv, qkv_out, sems.at[0])
+    copy.start()
+    d_att = nt(cot[...], out[...]).astype(jnp.bfloat16)
 
     row = lax.broadcasted_iota(jnp.int32, (128, 192), 0)
     column = lax.broadcasted_iota(jnp.int32, (128, 192), 1) - 32
@@ -394,24 +416,15 @@
     d_q_out[...] = jnp.concatenate(d_queries, axis=1)
     d_kv = jnp.concatenate(d_keys + d_values, axis=1)
     d_kv_out[...] = d_kv[32:160]
-
-    @pl.when(info[2] == 0)
-    def _():
-        send[...] = d_kv[:32].astype(jnp.bfloat16)
-
-    @pl.when(info[2] == 1)
-    def _():
-        send[...] = d_kv[160:].astype(jnp.bfloat16)
-
-    for copy in copies:
-        copy.wait()
+    send[...] = jnp.where(n == 0, d_kv[:32], d_kv[160:]).astype(jnp.bfloat16)
+    copy.wait()
 
 
 def norm_kernel(
-    info, d_q, d_kv, received, resid, inv_rms_ref, hidden, cot, gain, mix, qkv,
+    d_q, d_kv, received, resid, inv_rms_ref, hidden, cot, gain, mix, qkv,
     d_hidden_out, d_resid_out, send, total_kv, gained, d_resid_all,
 ):
-    n = info[2]
+    z, y, x, n = position()
     total_kv[...] = d_kv[...]
     edge = pl.ds(pl.multiple_of(n * 96, 32), 32)
     total_kv[edge, :] = total_kv[edge, :] + received[...].astype(jnp.float32)
@@ -449,8 +462,8 @@
         send[...] = d_hidden[112:]
 
 
-def taps_kernel(info, d_hidden, received, d_resid, noise, base, conv, keep, send, extended_ref, grads):
-    n, x = info[2], info[3]
+def taps_kernel(d_hidden, received, d_resid, noise, base, conv, keep, send, extended_ref, grads):
+    z, y, x, n = position()
 
     @pl.when(n == 0)
     def _():
@@ -489,7 +502,10 @@
     return [pl.BlockSpec(memory_space=pl.ANY)] * count
 
 
-LIMIT = pltpu.CompilerParams(vmem_limit_bytes=56 * 1024 * 1024)
+def limit(mebibytes):
+    return pltpu.CompilerParams(vmem_limit_bytes=mebibytes * 1024 * 1024)
+
+
 f32, bf16 = (jnp.float32, jnp.bfloat16)
 
 
@@ -503,19 +519,17 @@
     n_sa = lax.axis_size("sa")
     z, b, n = (lax.axis_index("sa"), lax.axis_index("sb"), lax.axis_index("noise"))
     y, x = (b >> 1, b & 1)
-    flag = jnp.any((pairs[:, 0] == z) & (pairs[:, 1] == z)).astype(jnp.int32)
-    info = jnp.stack([z, b, n, x, flag, jnp.int32(n_sa * 128)]).astype(jnp.int32)
     features = base.shape[1]
 
-    packed = pl.pallas_call(
+    early, late = pl.pallas_call(
         pack_kernel,
-        out_shape=shaped(352, CHUNK, dtype=bf16),
-        in_specs=smem(1) + hbm(4),
-        out_specs=pl.BlockSpec(memory_space=pl.ANY),
-        scratch_shapes=[pltpu.SemaphoreType.DMA((10,))],
-    )(info, convolution_weight, mix_w, qkv_w, out_w)
-    gathered = lax.all_gather(packed, ("sa", "sb", "noise"), axis=0, tiled=False)
-    gathered = gathered.reshape(-1, 352, CHUNK)
+        out_shape=(shaped(192, CHUNK, dtype=bf16), shaped(160, CHUNK, dtype=bf16)),
+        in_specs=vmem(4),
+        out_specs=tuple(vmem(2)),
+        compiler_params=limit(8),
+    )(convolution_weight, mix_w, qkv_w, out_w)
+    early = lax.all_gather(early, ("sa", "sb"), axis=0, tiled=False)
+    late = lax.all_gather(late, ("sa", "sb"), axis=0, tiled=False)
 
     def to_sample(shift):
         return routes(n_sa, lambda z, y, x, c: (z, c, (x + shift) % 2, y))
@@ -545,45 +559,58 @@
     )
     gain = norm_gain.reshape(1, features)
 
-    d_q, d_kv, send, resid, inv_rms, hidden, conv, mix, qkv = pl.pallas_call(
+    early_other = permuted(early, core_route)
+    normed, resid, inv_rms, hidden, conv, mix = pl.pallas_call(
         forward_kernel,
         out_shape=(
-            shaped(128, 256), shaped(128, 640), shaped(32, 640, dtype=bf16), shaped(128, features),
-            shaped(128, 1), shaped(128, HID), shaped(3, features, HID, dtype=bf16),
-            shaped(HID, features, dtype=bf16), shaped(features, 896, dtype=bf16),
+            shaped(192, features, dtype=bf16), shaped(128, features), shaped(128, 1), shaped(128, HID),
+            shaped(3, features, HID, dtype=bf16), shaped(HID, features, dtype=bf16),
         ),
-        in_specs=smem(2) + vmem(5),
-        out_specs=tuple(vmem(6) + hbm(3)),
+        in_specs=vmem(5),
+        out_specs=tuple(vmem(4) + hbm(2)),
         scratch_shapes=[
             pltpu.VMEM((3, features, HID), bf16), pltpu.VMEM((HID, features), bf16),
+            pltpu.VMEM((224, features), f32), pltpu.VMEM((224, features), bf16),
+            pltpu.SemaphoreType.DMA((2,)),
+        ],
+        compiler_params=limit(28),
+    )(noise_rows, base_rows, early, early_other, gain)
+    late_other = permuted(late, core_route)
+    d_q, d_kv, send, qkv = pl.pallas_call(
+        attention_kernel,
+        out_shape=(
+            shaped(128, 256), shaped(128, 640), shaped(32, 640, dtype=bf16), shaped(features, 896, dtype=bf16)
+        ),
+        in_specs=smem(2) + vmem(4),
+        out_specs=tuple(vmem(3) + hbm(1)),
+        scratch_shapes=[
             pltpu.VMEM((features, 896), bf16), pltpu.VMEM((HEADS * VAL, features), bf16),
-            pltpu.VMEM((224, features), f32), pltpu.VMEM((224, features), bf16),
-            pltpu.SemaphoreType.DMA((3,)),
+            pltpu.SemaphoreType.DMA((1,)),
         ],
-        compiler_params=LIMIT,
-    )(info, band_width, noise_rows, base_rows, cot_rows, gathered, gain)
+        compiler_params=limit(24),
+    )(band_width, pairs, normed, cot_rows, late, late_other)
 
     received = permuted(send, edge_route)
     d_hidden, d_resid, send = pl.pallas_call(
         norm_kernel,
         out_shape=(shaped(128, HID, dtype=bf16), shaped(64, features), shaped(16, HID, dtype=bf16)),
-        in_specs=smem(1) + vmem(10),
+        in_specs=vmem(10),
         out_specs=tuple(vmem(3)),
         scratch_shapes=[
             pltpu.VMEM((128, 640), f32), pltpu.VMEM((128, features), f32), pltpu.VMEM((128, features), f32),
         ],
-        compiler_params=LIMIT,
-    )(info, d_q, d_kv, received, resid, inv_rms, hidden, cot_rows, gain, mix, qkv)
+        compiler_params=limit(16),
+    )(d_q, d_kv, received, resid, inv_rms, hidden, cot_rows, gain, mix, qkv)
 
     received = permuted(send, edge_route)
     keep, send = pl.pallas_call(
         taps_kernel,
         out_shape=(shaped(32, features), shaped(32, features, dtype=bf16)),
-        in_specs=smem(1) + vmem(6),
+        in_specs=vmem(6),
         out_specs=tuple(vmem(2)),
         scratch_shapes=[pltpu.VMEM((96, HID), bf16), pltpu.VMEM((64, features), f32)],
-        compiler_params=LIMIT,
-    )(info, d_hidden, received, d_resid, noise_rows, base_rows, conv)
+        compiler_params=limit(16),
+    )(d_hidden, received, d_resid, noise_rows, base_rows, conv)
 
     received = permuted(send, routes(n_sa, lambda z, y, x, c: (z, y, 1 - x, c)))
     partial = (keep + received.astype(f32)).astype(bf16)

time: 161 us -> 188 us (1.17)
  waiting for transfers between devices: 77.4 us -> 122 us
  Pallas kernels: 37.9 us -> 17.3 us
  local copies, waits for them, and re-layouts: 2.44 us -> 7.19 us
  other arithmetic: 5.87 us -> 3.45 us
    all_gather x1 -> x2, waiting for transfers between devices: 50.2 us -> 98.4 us  [the longest x1 61.1 us: stretch_shards(): late = lax.all_gather(late, ('sa', 'sb'), axis=0, tiled=False)]
    pallas_call x2 -> x3, Pallas kernels: 26.1 us -> 12.4 us  [the longest x1 6.42 us: stretch_shards(): pl.pallas_call(attention_kernel, out_shape=(shaped(128, 256), shaped(128,...]
    unnamed x12 -> x25, local copies, waits for them, and re-layouts: 1.22 us -> 6.04 us
    pallas_call x1, Pallas kernels: 6.71 us -> 3.12 us  [stretch_shards(): pl.pallas_call(norm_kernel, out_shape=(shaped(128, HID, dtype=bf16), shap...]
    pallas_call x1, Pallas kernels: 5.08 us -> 1.77 us  [stretch_shards(): pl.pallas_call(taps_kernel, out_shape=(shaped(32, features), shaped(32, f...]
    ppermute x11 -> x13, waiting for transfers between devices: 27.1 us -> 23.8 us  [permuted(): return lax.ppermute(value, ('sa', 'sb', 'noise'), pairs)]
    ppermute x11 -> x13, starting transfers between devices: 21.9 us -> 21.3 us  [permuted(): return lax.ppermute(value, ('sa', 'sb', 'noise'), pairs)]
  transfers between devices with their start and end apart: 12 -> 15, of which waited for: 9 -> 9; matrix products, arithmetic and copies ran while one was open for 2% -> 2% of each run, Pallas kernels for 0% -> 3%
where the time goes in v3:
time: 188 us; the launch traced here: 185 us
  waiting for transfers between devices  122 us (65%)
  starting transfers between devices  21.3 us (11%)
  Pallas kernels  17.3 us (9%)
  between operations  13.7 us (7%)
  local copies, waits for them, and re-layouts  7.19 us (4%)
  other arithmetic  3.45 us (2%)
    all_gather x1, waiting for transfers between devices, stretch_shards(): late = lax.all_gather(late, ('sa', 'sb'), axis=0, tiled=False)  61.1 us
    all_gather x1, waiting for transfers between devices, stretch_shards(): early = lax.all_gather(early, ('sa', 'sb'), axis=0, tiled=False)  37.4 us
    ppermute x13, waiting for transfers between devices, permuted(): return lax.ppermute(value, ('sa', 'sb', 'noise'), pairs)  23.8 us
    ppermute x13, starting transfers between devices, permuted(): return lax.ppermute(value, ('sa', 'sb', 'noise'), pairs)  21.3 us
    pallas_call x1, Pallas kernels, stretch_shards(): pl.pallas_call(attention_kernel, out_shape=(shaped(128, 256), shaped(128,...  6.42 us
    unnamed x25, local copies, waits for them, and re-layouts  6.04 us
    pallas_call x1, Pallas kernels, stretch_shards(): pl.pallas_call(forward_kernel, out_shape=(shaped(192, features, dtype=bf1...  5.27 us
  transfers between devices with their start and end apart: 15, of which 9 were waited for; matrix products, arithmetic and copies ran while one was open for 2% of the time, Pallas kernels for 3%

profile of v3, /device:TPU:8, one launch (start us, length us, event | category | flops | bytes accessed | tf_op | source)
XLA Modules:
  0.0 185.2 jit_solution(16849480960906541418)
XLA Ops:
  6.5 1.2 copy-done.2
  7.7 1.1 copy-done.3
  8.8 1.0 copy-done.4
  9.8 1.0 copy-done.5
  10.7 0.7 shard_map.100
  11.5 0.0 all-gather.5.cloned.1.call-update
  11.5 0.0 all-gather.7.cloned.1.call-start
  11.5 0.2 copy-done.9
  11.8 0.7 collective-permute-start
  12.5 1.6 collective-permute-start.1
  14.0 0.7 collective-permute-start.2
  14.7 0.0 all-gather.7.cloned.1.call-update
  14.8 0.0 collective-permute-done
  14.8 2.4 %collective-permute-done.1 = bf16[32,1536]{1,0:T(8,128)(2,1)S(1)} collective-permute-done((bf16[32,1536]{1,0:T(8,128)(2,1)S(1)}, bf16[32,1536]{1,0:T(8,128)(2,1)S(1)}, u32[]{:S(2)}, u32[]{:S(2)}) %collective-permute-start.1) | collective-permute-done | bytes 98336 | tf_op jit(solution)/shard_map/ppermute | solution.py:241
  17.2 1.6 collective-permute-start.3
  18.8 4.2 %collective-permute-done.3 = bf16[2,32,1536]{2,1,0:T(8,128)(2,1)S(1)} collective-permute-done((bf16[2,32,1536]{2,1,0:T(8,128)(2,1)S(1)}, bf16[2,32,1536]{2,1,0:T(8,128)(2,1)S(1)}, u32[]{:S(2)}, u32[]{:S(2)}) %collective-permute-start.3) | collective-permute-done | bytes 196640 | tf_op jit(solution)/shard_map/ppermute | solution.py:241
  22.9 0.1 broadcast_select_fusion.7
  23.1 7.2 %collective-permute-start.4 = (bf16[2,48,1536]{2,1,0:T(8,128)(2,1)S(1)}, bf16[2,48,1536]{2,1,0:T(8,128)(2,1)S(1)}, u32[]{:S(2)}, u32[]{:S(2)}) collective-permute-start(bf16[2,48,1536]{2,1,0:T(8,128)(2,1)S(1)} %fusion.6), channel_id=1, source_target_pairs={{1,8},{3,10},{5,12},{7,14},{8,1},{9,16},{10,3},{11,18},{12,5},{13,... | collective-permute-start | bytes 884744 | tf_op jit(solution)/shard_map/ppermute | solution.py:241
  30.3 4.8 %collective-permute-done.4 = bf16[2,48,1536]{2,1,0:T(8,128)(2,1)S(1)} collective-permute-done((bf16[2,48,1536]{2,1,0:T(8,128)(2,1)S(1)}, bf16[2,48,1536]{2,1,0:T(8,128)(2,1)S(1)}, u32[]{:S(2)}, u32[]{:S(2)}) %collective-permute-start.4) | collective-permute-done | bytes 294944 | tf_op jit(solution)/shard_map/ppermute | solution.py:241
  35.1 0.1 fusion.3
  35.3 0.0 copy-start.10
  35.3 0.0 copy-start.11
  35.3 1.0 pad_maximum_fusion
  36.3 1.8 collective-permute-start.5
  38.1 37.4 %all-gather.5.cloned.1.call-done = bf16[3072,384]{1,0:T(8,128)(2,1)} async-done(((bf16[192,384]{1,0:T(8,128)(2,1)}), bf16[3072,384]{1,0:T(8,128)(2,1)}) %all-gather.5.cloned.1.call-update) | async-done | bytes 2359312 | tf_op jit(solution)/shard_map/all_gather | solution.py:531
  75.5 0.0 collective-permute-start.6
  75.5 61.1 %all-gather.7.cloned.1.call-done = bf16[2560,384]{1,0:T(8,128)(2,1)} async-done(((bf16[160,384]{1,0:T(8,128)(2,1)}), bf16[2560,384]{1,0:T(8,128)(2,1)}) %all-gather.7.cloned.1.call-update) | async-done | bytes 1966096 | tf_op jit(solution)/shard_map/all_gather | solution.py:532
  136.6 0.0 collective-permute-start.7
  136.6 0.1 copy.11.pairs
  136.7 1.1 slice.58
  137.8 1.0 broadcast_select_fusion.4
  138.8 0.2 broadcast_select_fusion
  139.1 0.1 fusion.2
  139.2 1.5 copy-done
  140.8 5.3 %shard_map.101 = (bf16[192,1536]{1,0:T(8,128)(2,1)S(1)}, f32[128,1536]{1,0:T(8,128)S(1)}, f32[128,1]{1,0:T(8,128)S(1)}, f32[128,384]{1,0:T(8,128)S(1)}, bf16[3,1...) custom-call(bf16[224,1536]{1,0:T(8,128)(2,1)S(1)} %get-tuple-element.40.noise, ...), custom_call_target="tpu_custom_call" | custom-call | tf_op jit(solution)/shard_map/pallas_call | solution.py:563
  146.1 6.4 %shard_map.102 = (f32[128,256]{1,0:T(8,128)S(1)}, f32[128,640]{1,0:T(8,128)S(1)}, bf16[32,640]{1,0:T(8,128)(2,1)S(1)}, bf16[1536,896]{1,0:T(8,128)(2,1)S(1)}) custom-call(s32[4]{0:T(128)S(1)} %copy-done.6, s32[16,2]{1,0:T(8,128)S(1)} %copy.11.pairs, bf16[192,1536]{1,0:T(8,128)(2,1)S(1)} %get-tuple-element.23.normed, ...), custom_call_target="tpu_custom_call" | custom-call | tf_op jit(solution)/shard_map/pallas_call | solution.py:579
  152.5 2.8 %collective-permute-start.8 = (bf16[32,640]{1,0:T(8,128)(2,1)S(1)}, bf16[32,640]{1,0:T(8,128)(2,1)S(1)}, u32[]{:S(2)}, u32[]{:S(2)}) collective-permute-start(bf16[32,640]{1,0:T(8,128)(2,1)S(1)} %get-tuple-element.27), channel_id=1, source_target_pairs={{1,8},{3,10},{5,12},{7,14},{8,1},{9,16},{10,3},{11,18},{12,5},{13,... | collective-permute-start | bytes 122888 | tf_op jit(solution)/shard_map/ppermute | solution.py:241
  155.3 2.5 %collective-permute-done.8.received = bf16[32,640]{1,0:T(8,128)(2,1)S(1)} collective-permute-done((bf16[32,640]{1,0:T(8,128)(2,1)S(1)}, bf16[32,640]{1,0:T(8,128)(2,1)S(1)}, u32[]{:S(2)}, u32[]{:S(2)}) %collective-permute-start.8) | collective-permute-done | bytes 40992 | tf_op jit(solution)/shard_map/ppermute | solution.py:241
  157.8 3.1 %shard_map.103 = (bf16[128,384]{1,0:T(8,128)(2,1)S(1)}, f32[64,1536]{1,0:T(8,128)S(1)}, bf16[16,384]{1,0:T(8,128)(2,1)S(1)}) custom-call(f32[128,256]{1,0:T(8,128)S(1)} %get-tuple-element.25.d_q, f32[128,640]{1,0:T(8,128)S(1)} %get-tuple-element.26.d_kv, bf16[32,640]{1,0:T(8,128)(2,1)S(1)} %collective-permute-done.8.received, ...), custom_call_target="tpu_custom_call" | custom-call | tf_op jit(solution)/shard_map/pallas_call | solution.py:594
  160.9 2.8 %collective-permute-start.9 = (bf16[16,384]{1,0:T(8,128)(2,1)S(1)}, bf16[16,384]{1,0:T(8,128)(2,1)S(1)}, u32[]{:S(2)}, u32[]{:S(2)}) collective-permute-start(bf16[16,384]{1,0:T(8,128)(2,1)S(1)} %get-tuple-element.34), channel_id=1, source_target_pairs={{1,8},{3,10},{5,12},{7,14},{8,1},{9,16},{10,3},{11,18},{12,5},{13,... | collective-permute-start | bytes 36872 | tf_op jit(solution)/shard_map/ppermute | solution.py:241
  163.7 2.2 %collective-permute-done.9.received = bf16[16,384]{1,0:T(8,128)(2,1)S(1)} collective-permute-done((bf16[16,384]{1,0:T(8,128)(2,1)S(1)}, bf16[16,384]{1,0:T(8,128)(2,1)S(1)}, u32[]{:S(2)}, u32[]{:S(2)}) %collective-permute-start.9) | collective-permute-done | bytes 12320 | tf_op jit(solution)/shard_map/ppermute | solution.py:241
  165.9 1.8 shard_map.104
  167.7 1.5 collective-permute-start.10
  169.2 3.8 %collective-permute-done.10 = bf16[32,1536]{1,0:T(8,128)(2,1)S(1)} collective-permute-done((bf16[32,1536]{1,0:T(8,128)(2,1)S(1)}, bf16[32,1536]{1,0:T(8,128)(2,1)S(1)}, u32[]{:S(2)}, u32[]{:S(2)}) %collective-permute-start.10) | collective-permute-done | bytes 98336 | tf_op jit(solution)/shard_map/ppermute | solution.py:241
  173.0 0.0 collective-permute-start.11
  173.1 0.7 collective-permute-start.12
  173.7 3.9 %collective-permute-done.11 = bf16[32,1536]{1,0:T(8,128)(2,1)S(1)} collective-permute-done((bf16[32,1536]{1,0:T(8,128)(2,1)S(1)}, bf16[32,1536]{1,0:T(8,128)(2,1)S(1)}, u32[]{:S(2)}, u32[]{:S(2)}) %collective-permute-start.11) | collective-permute-done | bytes 98336 | tf_op jit(solution)/shard_map/ppermute | solution.py:241
  177.7 0.7 add_multiply_fusion
  (35 shorter events, 0.4 us)
Async XLA Ops:
  6.5 69.0 %all-gather.5.cloned.1.call-start = ((), (), s32[]{:S(2)}) async-start(), calls=%async_computation | async-start | bytes 2506752 | tf_op jit(solution)/shard_map/all_gather | solution.py:531
  6.5 1.2 copy-start.2
  7.7 1.1 copy-start.3
  8.8 1.0 copy-start.4
  9.8 1.0 copy-start.5
  10.7 1.0 copy-start.9
  10.7 3.3 %copy-start.7 = (bf16[32,1536]{1,0:T(8,128)(2,1)S(1)}, bf16[32,1536]{1,0:T(8,128)(2,1)}, u32[]{:S(2)}) copy-start(bf16[32,1536]{1,0:T(8,128)(2,1)} %param.12) | copy-start | bytes 294916
  10.7 3.3 %copy-start.8 = (bf16[32,1536]{1,0:T(8,128)(2,1)S(1)}, bf16[32,1536]{1,0:T(8,128)(2,1)}, u32[]{:S(2)}) copy-start(bf16[32,1536]{1,0:T(8,128)(2,1)} %param.10) | copy-start | bytes 294916
  11.5 125.1 %all-gather.7.cloned.1.call-start = ((), (), s32[]{:S(2)}) async-start(), calls=%async_computation.1 | async-start | bytes 2088960 | tf_op jit(solution)/shard_map/all_gather | solution.py:532
  11.8 3.0 %collective-permute-start = (bf16[32,1536]{1,0:T(8,128)(2,1)S(1)}, bf16[32,1536]{1,0:T(8,128)(2,1)S(1)}, u32[]{:S(2)}, u32[]{:S(2)}) collective-permute-start(bf16[32,1536]{1,0:T(8,128)(2,1)S(1)} %get-tuple-element.51), channel_id=1, source_target_pairs={{0,0},{1,4},{2,2},{3,6},{4,1},{5,5},{6,3},{7,7},{8,8},{9,12},{10,1... | collective-permute-start | bytes 294920 | tf_op jit(solution)/shard_map/ppermute | solution.py:241
  12.5 4.7 %collective-permute-start.1 = (bf16[32,1536]{1,0:T(8,128)(2,1)S(1)}, bf16[32,1536]{1,0:T(8,128)(2,1)S(1)}, u32[]{:S(2)}, u32[]{:S(2)}) collective-permute-start(bf16[32,1536]{1,0:T(8,128)(2,1)S(1)} %get-tuple-element.52), channel_id=1, source_target_pairs={{0,2},{1,6},{2,0},{3,4},{4,3},{5,7},{6,1},{7,5},{8,10},{9,14},{10,... | collective-permute-start | bytes 294920 | tf_op jit(solution)/shard_map/ppermute | solution.py:241
  14.0 3.1 %collective-permute-start.2 = (bf16[2,32,1536]{2,1,0:T(8,128)(2,1)S(1)}, bf16[2,32,1536]{2,1,0:T(8,128)(2,1)S(1)}, u32[]{:S(2)}, u32[]{:S(2)}) collective-permute-start(bf16[2,32,1536]{2,1,0:T(8,128)(2,1)S(1)} %pad_maximum_fusion.6), channel_id=1, source_target_pairs={{1,4},{3,6},{4,1},{6,3},{9,12},{11,14},{12,9},{14,11},{17,20},{19,... | collective-permute-start | bytes 589832 | tf_op jit(solution)/shard_map/ppermute | solution.py:241
  17.2 5.7 %collective-permute-start.3 = (bf16[2,32,1536]{2,1,0:T(8,128)(2,1)S(1)}, bf16[2,32,1536]{2,1,0:T(8,128)(2,1)S(1)}, u32[]{:S(2)}, u32[]{:S(2)}) collective-permute-start(bf16[2,32,1536]{2,1,0:T(8,128)(2,1)S(1)} %broadcast_select_fusion.5), channel_id=1, source_target_pairs={{0,2},{1,3},{2,0},{3,1},{4,6},{5,7},{6,4},{7,5},{8,10},{9,11},{10,... | collective-permute-start | bytes 589832 | tf_op jit(solution)/shard_map/ppermute | solution.py:241
  23.1 12.0 %collective-permute-start.4 = (bf16[2,48,1536]{2,1,0:T(8,128)(2,1)S(1)}, bf16[2,48,1536]{2,1,0:T(8,128)(2,1)S(1)}, u32[]{:S(2)}, u32[]{:S(2)}) collective-permute-start(bf16[2,48,1536]{2,1,0:T(8,128)(2,1)S(1)} %fusion.6), channel_id=1, source_target_pairs={{1,8},{3,10},{5,12},{7,14},{8,1},{9,16},{10,3},{11,18},{12,5},{13,... | collective-permute-start | bytes 884744 | tf_op jit(solution)/shard_map/ppermute | solution.py:241
  35.3 101.3 %copy-start.10 = (f32[1536]{0:T(1024)S(1)}, f32[1536]{0:T(1024)}, u32[]{:S(2)}) copy-start(f32[1536]{0:T(1024)} %param.15) | copy-start | bytes 18436
  35.3 101.3 %copy-start.11 = (s32[16,2]{0,1:T(2,128)S(1)}, s32[16,2]{0,1:T(2,128)}, u32[]{:S(2)}) copy-start(s32[16,2]{0,1:T(2,128)} %param.19) | copy-start | bytes 388
  36.3 100.4 %collective-permute-start.5 = (bf16[288,1536]{1,0:T(8,128)(2,1)}, bf16[288,1536]{1,0:T(8,128)(2,1)}, u32[]{:S(2)}, u32[]{:S(2)}) collective-permute-start(bf16[288,1536]{1,0:T(8,128)(2,1)} %pad_maximum_fusion), channel_id=1, source_target_pairs={{0,1},{1,0},{2,3},{3,2},{4,5},{5,4},{6,7},{7,6},{8,9},{9,8},{10,11... | collective-permute-start | bytes 2654216 | tf_op jit(solution)/shard_map/ppermute | solution.py:241
  75.5 63.7 %collective-permute-start.6 = (bf16[16,192,384]{2,1,0:T(8,128)(2,1)}, bf16[16,192,384]{2,1,0:T(8,128)(2,1)S(1)}, u32[]{:S(2)}, u32[]{:S(2)}) collective-permute-start(bf16[16,192,384]{2,1,0:T(8,128)(2,1)} %bitcast.18), channel_id=1, source_target_pairs={{0,1},{1,0},{2,3},{3,2},{4,5},{5,4},{6,7},{7,6},{8,9},{9,8},{10,11... | collective-permute-start | bytes 7077896 | tf_op jit(solution)/shard_map/ppermute | solution.py:241
  136.6 9.5 %collective-permute-start.7 = (bf16[16,160,384]{2,1,0:T(8,128)(2,1)}, bf16[16,160,384]{2,1,0:T(8,128)(2,1)}, u32[]{:S(2)}, u32[]{:S(2)}) collective-permute-start(bf16[16,160,384]{2,1,0:T(8,128)(2,1)} %bitcast.20), channel_id=1, source_target_pairs={{0,1},{1,0},{2,3},{3,2},{4,5},{5,4},{6,7},{7,6},{8,9},{9,8},{10,11... | collective-permute-start | bytes 5898248 | tf_op jit(solution)/shard_map/ppermute | solution.py:241
  139.1 1.7 copy-start
  140.7 5.3 %copy-start.1 = (bf16[2560,384]{1,0:T(8,128)(2,1)S(1)}, bf16[2560,384]{1,0:T(8,128)(2,1)}, u32[]{:S(2)}) copy-start(bf16[2560,384]{1,0:T(8,128)(2,1)} %all-gather.7.cloned.1.call-done) | copy-start | bytes 5898244
  140.8 5.3 %copy-start.6 = (s32[4]{0:T(128)S(1)}, s32[4]{0:T(128)}, u32[]{:S(2)}) copy-start(s32[4]{0:T(128)} %band.1) | copy-start | bytes 52
  152.5 5.3 %collective-permute-start.8 = (bf16[32,640]{1,0:T(8,128)(2,1)S(1)}, bf16[32,640]{1,0:T(8,128)(2,1)S(1)}, u32[]{:S(2)}, u32[]{:S(2)}) collective-permute-start(bf16[32,640]{1,0:T(8,128)(2,1)S(1)} %get-tuple-element.27), channel_id=1, source_target_pairs={{1,8},{3,10},{5,12},{7,14},{8,1},{9,16},{10,3},{11,18},{12,5},{13,... | collective-permute-start | bytes 122888 | tf_op jit(solution)/shard_map/ppermute | solution.py:241
  160.9 5.0 %collective-permute-start.9 = (bf16[16,384]{1,0:T(8,128)(2,1)S(1)}, bf16[16,384]{1,0:T(8,128)(2,1)S(1)}, u32[]{:S(2)}, u32[]{:S(2)}) collective-permute-start(bf16[16,384]{1,0:T(8,128)(2,1)S(1)} %get-tuple-element.34), channel_id=1, source_target_pairs={{1,8},{3,10},{5,12},{7,14},{8,1},{9,16},{10,3},{11,18},{12,5},{13,... | collective-permute-start | bytes 36872 | tf_op jit(solution)/shard_map/ppermute | solution.py:241
  167.7 5.3 %collective-permute-start.10 = (bf16[32,1536]{1,0:T(8,128)(2,1)S(1)}, bf16[32,1536]{1,0:T(8,128)(2,1)S(1)}, u32[]{:S(2)}, u32[]{:S(2)}) collective-permute-start(bf16[32,1536]{1,0:T(8,128)(2,1)S(1)} %get-tuple-element.38), channel_id=1, source_target_pairs={{0,2},{1,3},{2,0},{3,1},{4,6},{5,7},{6,4},{7,5},{8,10},{9,11},{10,... | collective-permute-start | bytes 294920 | tf_op jit(solution)/shard_map/ppermute | solution.py:241
  173.0 4.6 %collective-permute-start.11 = (bf16[32,1536]{1,0:T(8,128)(2,1)S(1)}, bf16[32,1536]{1,0:T(8,128)(2,1)S(1)}, u32[]{:S(2)}, u32[]{:S(2)}) collective-permute-start(bf16[32,1536]{1,0:T(8,128)(2,1)S(1)} %add_convert_fusion), channel_id=1, source_target_pairs={{0,1},{1,5},{2,3},{3,7},{4,0},{5,4},{6,2},{7,6},{8,9},{9,13},{10,1... | collective-permute-start | bytes 294920 | tf_op jit(solution)/shard_map/ppermute | solution.py:241
  173.1 4.6 %collective-permute-start.12 = (bf16[32,1536]{1,0:T(8,128)(2,1)S(1)}, bf16[32,1536]{1,0:T(8,128)(2,1)S(1)}, u32[]{:S(2)}, u32[]{:S(2)}) collective-permute-start(bf16[32,1536]{1,0:T(8,128)(2,1)S(1)} %add_convert_fusion), channel_id=1, source_target_pairs={{1,4},{3,6},{4,1},{6,3},{9,12},{11,14},{12,9},{14,11},{17,20},{19,... | collective-permute-start | bytes 294920 | tf_op jit(solution)/shard_map/ppermute | solution.py:241
Sparse Core Ops, SparseCore 0:
  11.6 63.8 all-gather.4
  78.3 58.2 all-gather.6

commit v4 on v3

--- a/solution.py
+++ b/solution.py
@@ -296,29 +296,45 @@
     return pl.ds(pl.multiple_of(c * CHUNK, 128), CHUNK)
 
 
-def pieces(mine, other, n, i):
-    first, second = mine[i], other[i]
-    return jnp.where(n == 0, first, second), jnp.where(n == 0, second, first)
+def arrived(z, y, x, n, same, other):
+    for j in range(3):
+        for core, (straight, beside, across, diagonal_a, diagonal_b) in enumerate((same, other)):
+            half = diagonal_a.shape[1]
+            for dy in range(2):
+                for dx in range(2):
+                    if dy and dx:
+                        first, second = diagonal_a[j], diagonal_b[j]
+                    else:
+                        whole = across if dy else beside if dx else straight
+                        first, second = whole[j, pl.ds(0, half), :], whole[j, pl.ds(half, half), :]
+                    yield j, z ^ (j + 1), y ^ dy, x ^ dx, n ^ core, first, second
+
+
+def times(value, factor, unit):
+    return pl.multiple_of(value * factor, unit)
 
 
 def forward_kernel(
-    noise, base, mine, other, gain, normed_out, resid_out, inv_out, hidden_out, conv_out, mix_out,
-    conv, mix, noisy, gelu_in, sems,
+    noise, base, *refs,
 ):
+    own_conv, own_mix = refs[:2]
+    same, other = refs[2:7], refs[7:12]
+    (
+        gain, normed_out, resid_out, inv_out, hidden_out, conv_out, mix_out,
+        conv, mix, noisy, gelu_in, sems,
+    ) = refs[12:]
     z, y, x, n = position()
 
-    def unpack(i, _):
-        source, b = i // 4, lax.rem(i, 4)
-        for core, piece in enumerate(pieces(mine, other, n, i)):
-            rows = pl.ds(pl.multiple_of(source * 384 + (b * 2 + core) * 48, 16), 48)
-            half = pl.ds(pl.multiple_of(source * 96 + core * 48, 16), 48)
-            columns = pl.ds(pl.multiple_of(b * 384, 128), 384)
-            for t in range(3):
-                conv[t, rows, :] = piece[48 * t : 48 * t + 48]
-            mix[half, columns] = piece[144:192]
-        return 0
-
-    lax.fori_loop(0, mine.shape[0], unpack, 0)
+    for t in range(3):
+        conv[t, pl.ds(times(z, 384, 128), 384), :] = own_conv[t]
+    mix[pl.ds(times(z, 96, 32), 96), :] = own_mix[...]
+    for _, sz, sy, sx, sn, first, second in arrived(z, y, x, n, same, other):
+        b = 2 * sy + sx
+        rows = pl.ds(pl.multiple_of(sz * 384 + (b * 2 + sn) * 48, 16), 48)
+        conv[0, rows, :] = first[:48]
+        conv[1, rows, :] = first[48:]
+        conv[2, rows, :] = second[:48]
+        mix[pl.ds(pl.multiple_of(sz * 96 + sn * 48, 16), 48), pl.ds(times(b, 384, 128), 384)] = second[48:]
     copies = [
         pltpu.make_async_copy(s, d, sems.at[i]) for i, (s, d) in enumerate(((conv, conv_out), (mix, mix_out)))
     ]
@@ -362,28 +378,36 @@
         copy.wait()
 
 
-def attention_kernel(
-    band, pairs, normed, cot, mine, other, d_q_out, d_kv_out, send, qkv_out, qkv, out, sems,
-):
+def attention_kernel(band, pairs, normed, cot, *refs):
+    own_qkv, own_out = refs[:2]
+    same, other = refs[2:7], refs[7:12]
+    d_q_out, d_kv_out, send, qkv_out, qkv, out, sems = refs[12:]
     z, y, x, n = position()
     length = lax.axis_size("sa") * 128
-    first = z * 128
+    first_bin = z * 128
     pair_flag = jnp.int32(0)
     for i in range(pairs.shape[0]):
         pair_flag = pair_flag | ((pairs[i, 0] == z) & (pairs[i, 1] == z)).astype(jnp.int32)
 
-    proj = jnp.zeros((192, 896), jnp.float32)
-    for source in range(4):
-        for b in range(4):
-            for core, piece in enumerate(pieces(mine, other, n, 4 * source + b)):
-                row = source * 384 + (b * 2 + core) * 48
-                out[pl.ds(source * 96 + core * 48, 48), pl.ds(b * 384, 384)] = piece[:48]
-                for k in range(2):
-                    qkv[pl.ds(row, 48), pl.ds(384 * k, 384)] = piece[48 + 48 * k : 96 + 48 * k]
-                for k in range(3):
-                    qkv[pl.ds(row + 16 * k, 16), pl.ds(768, 128)] = piece[144:160, 128 * k : 128 * k + 128]
-        rows = pl.ds(source * 384, 384)
-        proj = proj + nn(normed[:, rows], qkv[rows, :])
+    own_rows = pl.ds(times(z, 384, 128), 384)
+    qkv[own_rows, :] = own_qkv[...]
+    out[pl.ds(times(z, 96, 32), 96), :] = own_out[...]
+    proj = nn(normed[:, own_rows], own_qkv[...])
+    done = 0
+    for j, sz, sy, sx, sn, first, second in arrived(z, y, x, n, same, other):
+        b = 2 * sy + sx
+        row = sz * 384 + (b * 2 + sn) * 48
+        out[pl.ds(pl.multiple_of(sz * 96 + sn * 48, 16), 48), pl.ds(times(b, 384, 128), 384)] = first[:48]
+        qkv[pl.ds(pl.multiple_of(row, 16), 32), pl.ds(0, 384)] = first[48:]
+        qkv[pl.ds(pl.multiple_of(row + 32, 16), 16), pl.ds(0, 384)] = second[:16]
+        qkv[pl.ds(pl.multiple_of(row, 16), 48), pl.ds(384, 384)] = second[16:64]
+        for k in range(3):
+            third = pl.ds(pl.multiple_of(row + 16 * k, 16), 16)
+            qkv[third, pl.ds(768, 128)] = second[64:, 128 * k : 128 * k + 128]
+        done += 1
+        if done % 8 == 0:
+            rows = pl.ds(times(sz, 384, 128), 384)
+            proj = proj + nn(normed[:, rows], qkv[rows, :])
     proj = proj.astype(jnp.bfloat16)
     copy = pltpu.make_async_copy(qkv, qkv_out, sems.at[0])
     copy.start()
@@ -391,7 +415,7 @@
 
     row = lax.broadcasted_iota(jnp.int32, (128, 192), 0)
     column = lax.broadcasted_iota(jnp.int32, (128, 192), 1) - 32
-    inside = (column + first >= 0) & (column + first < length)
+    inside = (column + first_bin >= 0) & (column + first_bin < length)
     paired = (column >= 0) & (column < 128) & (pair_flag > 0)
     apart = jnp.abs(row - column)
     scale = KEY ** (-0.5)
@@ -528,8 +552,23 @@
         out_specs=tuple(vmem(2)),
         compiler_params=limit(8),
     )(convolution_weight, mix_w, qkv_w, out_w)
-    early = lax.all_gather(early, ("sa", "sb"), axis=0, tiled=False)
-    late = lax.all_gather(late, ("sa", "sb"), axis=0, tiled=False)
+    def along_z(step):
+        return routes(n_sa, lambda z, y, x, c: (z ^ step, y, x, c))
+
+    x_route = routes(n_sa, lambda z, y, x, c: (z, y, 1 - x, c))
+    y_route = routes(n_sa, lambda z, y, x, c: (z, 1 - y, x, c))
+    core_route = routes(n_sa, lambda z, y, x, c: (z, y, x, 1 - c))
+
+    def collected(piece):
+        half = piece.shape[0] // 2
+        straight = jnp.stack([permuted(piece, along_z(step)) for step in range(1, 4)])
+        beside, across = permuted(straight, x_route), permuted(straight, y_route)
+        diagonal_a = permuted(beside[:, :half], y_route)
+        diagonal_b = permuted(across[:, half:], x_route)
+        same = (straight, beside, across, diagonal_a, diagonal_b)
+        return same + tuple(permuted(part, core_route) for part in same)
+
+    early, late = collected(early), collected(late)
 
     def to_sample(shift):
         return routes(n_sa, lambda z, y, x, c: (z, c, (x + shift) % 2, y))
@@ -543,10 +582,9 @@
     both = jnp.stack([base, cot])
     across = permuted(both, routes(n_sa, lambda z, y, x, c: (z, 1 - y, x, 1 - c) if y != c else None))
     current = jnp.where(y == n, both, across)
-    beside = permuted(current, routes(n_sa, lambda z, y, x, c: (z, y, 1 - x, c)))
+    beside = permuted(current, x_route)
     halves = jnp.concatenate([jnp.where(even, current, beside), jnp.where(even, beside, current)], axis=1)
     edge_route = routes(n_sa, lambda z, y, x, c: (z - 1, y, x, 1) if c == 0 else (z + 1, y, x, 0))
-    core_route = routes(n_sa, lambda z, y, x, c: (z, y, x, 1 - c))
     mine = jnp.stack([noise_half, halves[0]])
     edge = permuted(jnp.where(n == 0, mine[:, :48], mine[:, 16:]), edge_route)
     wide = jnp.concatenate([jnp.where(n == 0, edge, mine[:, :48])] + [jnp.where(n == 0, mine, jnp.concatenate([mine[:, 48:], edge], axis=1))], axis=1)
@@ -559,14 +597,13 @@
     )
     gain = norm_gain.reshape(1, features)
 
-    early_other = permuted(early, core_route)
     normed, resid, inv_rms, hidden, conv, mix = pl.pallas_call(
         forward_kernel,
         out_shape=(
             shaped(192, features, dtype=bf16), shaped(128, features), shaped(128, 1), shaped(128, HID),
             shaped(3, features, HID, dtype=bf16), shaped(HID, features, dtype=bf16),
         ),
-        in_specs=vmem(5),
+        in_specs=vmem(15),
         out_specs=tuple(vmem(4) + hbm(2)),
         scratch_shapes=[
             pltpu.VMEM((3, features, HID), bf16), pltpu.VMEM((HID, features), bf16),
@@ -574,21 +611,20 @@
             pltpu.SemaphoreType.DMA((2,)),
         ],
         compiler_params=limit(28),
-    )(noise_rows, base_rows, early, early_other, gain)
-    late_other = permuted(late, core_route)
+    )(noise_rows, base_rows, convolution_weight, mix_w, *early, gain)
     d_q, d_kv, send, qkv = pl.pallas_call(
         attention_kernel,
         out_shape=(
             shaped(128, 256), shaped(128, 640), shaped(32, 640, dtype=bf16), shaped(features, 896, dtype=bf16)
         ),
-        in_specs=smem(2) + vmem(4),
+        in_specs=smem(2) + vmem(14),
         out_specs=tuple(vmem(3) + hbm(1)),
         scratch_shapes=[
             pltpu.VMEM((features, 896), bf16), pltpu.VMEM((HEADS * VAL, features), bf16),
             pltpu.SemaphoreType.DMA((1,)),
         ],
         compiler_params=limit(24),
-    )(band_width, pairs, normed, cot_rows, late, late_other)
+    )(band_width, pairs, normed, cot_rows, qkv_w, out_w, *late)
 
     received = permuted(send, edge_route)
     d_hidden, d_resid, send = pl.pallas_call(
@@ -612,7 +648,7 @@
         compiler_params=limit(16),
     )(d_hidden, received, d_resid, noise_rows, base_rows, conv)
 
-    received = permuted(send, routes(n_sa, lambda z, y, x, c: (z, y, 1 - x, c)))
+    received = permuted(send, x_route)
     partial = (keep + received.astype(f32)).astype(bf16)
     first_sum = permuted(
         partial, routes(n_sa, lambda z, y, x, c: (z, c, x, c) if y != c else (z, y, x, 1 - c))

time: 188 us -> 129 us (0.69)
  the two profiles are of different devices: /device:TPU:8 before, /device:TPU:1 now
where the time goes in v4:
time: 129 us; the launch traced here: 128 us
  starting transfers between devices  51.7 us (40%)
  waiting for transfers between devices  47.6 us (37%)
  Pallas kernels  17.2 us (13%)
  other arithmetic  6.44 us (5%)
  local copies, waits for them, and re-layouts  4.96 us (4%)
    ppermute x35, starting transfers between devices, permuted(): return lax.ppermute(value, ('sa', 'sb', 'noise'), pairs)  51.7 us
    ppermute x35, waiting for transfers between devices, permuted(): return lax.ppermute(value, ('sa', 'sb', 'noise'), pairs)  47.6 us
    pallas_call x1, Pallas kernels, stretch_shards(): pl.pallas_call(attention_kernel, out_shape=(shaped(128, 256), shaped(128,...  6.16 us
    pallas_call x1, Pallas kernels, stretch_shards(): pl.pallas_call(forward_kernel, out_shape=(shaped(192, features, dtype=bf1...  6.15 us
    pallas_call x1, Pallas kernels, stretch_shards(): pl.pallas_call(norm_kernel, out_shape=(shaped(128, HID, dtype=bf16), shap...  3.13 us
  transfers between devices with their start and end apart: 35, of which 12 were waited for; matrix products, arithmetic and copies ran while one was open for 5% of the time, Pallas kernels for 5%

profile of v4, /device:TPU:1, one launch (start us, length us, event | category | flops | bytes accessed | tf_op | source)
XLA Modules:
  0.0 128.4 jit_solution(14728164169587036476)
XLA Ops:
  0.0 1.0 select_bitcast_fusion.1
  1.0 4.5 %collective-permute-start = (bf16[32,1536]{1,0:T(8,128)(2,1)S(1)}, bf16[32,1536]{1,0:T(8,128)(2,1)S(1)}, u32[]{:S(2)}, u32[]{:S(2)}) collective-permute-start(bf16[32,1536]{1,0:T(8,128)(2,1)S(1)} %get-tuple-element.51), channel_id=1, source_target_pairs={{0,0},{1,4},{2,2},{3,6},{4,1},{5,5},{6,3},{7,7},{8,8},{9,12},{10,1... | collective-permute-start | bytes 294920 | tf_op jit(solution)/shard_map/ppermute | solution.py:241
  5.5 1.0 collective-permute-start.1
  6.6 1.0 pad_maximum_fusion.8
  7.5 3.6 %collective-permute-start.2 = (bf16[2,32,1536]{2,1,0:T(8,128)(2,1)S(1)}, bf16[2,32,1536]{2,1,0:T(8,128)(2,1)S(1)}, u32[]{:S(2)}, u32[]{:S(2)}) collective-permute-start(bf16[2,32,1536]{2,1,0:T(8,128)(2,1)S(1)} %pad_maximum_fusion.8), channel_id=1, source_target_pairs={{1,4},{3,6},{4,1},{6,3},{9,12},{11,14},{12,9},{14,11},{17,20},{19,... | collective-permute-start | bytes 589832 | tf_op jit(solution)/shard_map/ppermute | solution.py:241
  11.2 3.3 %collective-permute-done.2 = bf16[2,32,1536]{2,1,0:T(8,128)(2,1)S(1)} collective-permute-done((bf16[2,32,1536]{2,1,0:T(8,128)(2,1)S(1)}, bf16[2,32,1536]{2,1,0:T(8,128)(2,1)S(1)}, u32[]{:S(2)}, u32[]{:S(2)}) %collective-permute-start.2) | collective-permute-done | bytes 196640 | tf_op jit(solution)/shard_map/ppermute | solution.py:241
  14.5 1.0 broadcast_select_fusion.5
  15.5 0.6 collective-permute-start.3
  16.1 3.9 %collective-permute-done.3 = bf16[2,32,1536]{2,1,0:T(8,128)(2,1)S(1)} collective-permute-done((bf16[2,32,1536]{2,1,0:T(8,128)(2,1)S(1)}, bf16[2,32,1536]{2,1,0:T(8,128)(2,1)S(1)}, u32[]{:S(2)}, u32[]{:S(2)}) %collective-permute-start.3) | collective-permute-done | bytes 196640 | tf_op jit(solution)/shard_map/ppermute | solution.py:241
  20.2 1.9 %collective-permute-start.4 = (bf16[2,48,1536]{2,1,0:T(8,128)(2,1)S(1)}, bf16[2,48,1536]{2,1,0:T(8,128)(2,1)S(1)}, u32[]{:S(2)}, u32[]{:S(2)}) collective-permute-start(bf16[2,48,1536]{2,1,0:T(8,128)(2,1)S(1)} %fusion.6), channel_id=1, source_target_pairs={{1,8},{3,10},{5,12},{7,14},{8,1},{9,16},{10,3},{11,18},{12,5},{13,... | collective-permute-start | bytes 884744 | tf_op jit(solution)/shard_map/ppermute | solution.py:241
  22.2 6.1 %collective-permute-done.4 = bf16[2,48,1536]{2,1,0:T(8,128)(2,1)S(1)} collective-permute-done((bf16[2,48,1536]{2,1,0:T(8,128)(2,1)S(1)}, bf16[2,48,1536]{2,1,0:T(8,128)(2,1)S(1)}, u32[]{:S(2)}, u32[]{:S(2)}) %collective-permute-start.4) | collective-permute-done | bytes 294944 | tf_op jit(solution)/shard_map/ppermute | solution.py:241
  28.5 1.0 pad_maximum_fusion
  30.4 1.4 %collective-permute-start.6 = (bf16[192,384]{1,0:T(8,128)(2,1)S(1)}, bf16[192,384]{1,0:T(8,128)(2,1)S(1)}, u32[]{:S(2)}, u32[]{:S(2)}) collective-permute-start(bf16[192,384]{1,0:T(8,128)(2,1)S(1)} %get-tuple-element.22), channel_id=1, source_target_pairs={{0,8},{1,9},{2,10},{3,11},{4,12},{5,13},{6,14},{7,15},{8,0},{9,1},... | collective-permute-start | bytes 442376 | tf_op jit(solution)/shard_map/ppermute | solution.py:241
  31.8 1.1 collective-permute-start.7
  32.9 1.2 collective-permute-start.8
  34.4 4.6 %collective-permute-done.6 = bf16[192,384]{1,0:T(8,128)(2,1)S(1)} collective-permute-done((bf16[192,384]{1,0:T(8,128)(2,1)S(1)}, bf16[192,384]{1,0:T(8,128)(2,1)S(1)}, u32[]{:S(2)}, u32[]{:S(2)}) %collective-permute-start.6) | collective-permute-done | bytes 147488 | tf_op jit(solution)/shard_map/ppermute | solution.py:241
  39.1 7.7 %collective-permute-start.20 = (bf16[160,384]{1,0:T(8,128)(2,1)S(1)}, bf16[160,384]{1,0:T(8,128)(2,1)S(1)}, u32[]{:S(2)}, u32[]{:S(2)}) collective-permute-start(bf16[160,384]{1,0:T(8,128)(2,1)S(1)} %get-tuple-element.24), channel_id=1, source_target_pairs={{0,24},{1,25},{2,26},{3,27},{4,28},{5,29},{6,30},{7,31},{8,16},{9,... | collective-permute-start | bytes 368648 | tf_op jit(solution)/shard_map/ppermute | solution.py:241
  46.8 0.6 collective-permute-start.9
  47.5 1.1 collective-permute-start.10
  48.6 7.1 %collective-permute-done.19 = bf16[160,384]{1,0:T(8,128)(2,1)S(1)} collective-permute-done((bf16[160,384]{1,0:T(8,128)(2,1)S(1)}, bf16[160,384]{1,0:T(8,128)(2,1)S(1)}, u32[]{:S(2)}, u32[]{:S(2)}) %collective-permute-start.19) | collective-permute-done | bytes 122912 | tf_op jit(solution)/shard_map/ppermute | solution.py:241
  56.3 1.5 %collective-permute-start.22 = (bf16[3,160,384]{2,1,0:T(8,128)(2,1)S(1)}, bf16[3,160,384]{2,1,0:T(8,128)(2,1)}, u32[]{:S(2)}, u32[]{:S(2)}) collective-permute-start(bf16[3,160,384]{2,1,0:T(8,128)(2,1)S(1)} %pad_maximum_fusion.6.refs_2_), channel_id=1, source_target_pairs={{0,4},{1,5},{2,6},{3,7},{4,0},{5,1},{6,2},{7,3},{8,12},{9,13},{10,... | collective-permute-start | bytes 1105928 | tf_op jit(solution)/shard_map/ppermute | solution.py:241
  58.0 8.0 %collective-permute-done.21.refs_3_ = bf16[3,160,384]{2,1,0:T(8,128)(2,1)} collective-permute-done((bf16[3,160,384]{2,1,0:T(8,128)(2,1)S(1)}, bf16[3,160,384]{2,1,0:T(8,128)(2,1)}, u32[]{:S(2)}, u32[]{:S(2)}) %collective-permute-start.21) | collective-permute-done | bytes 368672 | tf_op jit(solution)/shard_map/ppermute | solution.py:241
  66.0 1.5 %collective-permute-start.13 = (bf16[3,192,384]{2,1,0:T(8,128)(2,1)S(1)}, bf16[3,192,384]{2,1,0:T(8,128)(2,1)S(1)}, u32[]{:S(2)}, u32[]{:S(2)}) collective-permute-start(bf16[3,192,384]{2,1,0:T(8,128)(2,1)S(1)} %pad_maximum_fusion.4.refs_2_), channel_id=1, source_target_pairs={{0,1},{1,0},{2,3},{3,2},{4,5},{5,4},{6,7},{7,6},{8,9},{9,8},{10,11... | collective-permute-start | bytes 1327112 | tf_op jit(solution)/shard_map/ppermute | solution.py:241
  67.5 0.9 slice.80
  68.5 1.5 %collective-permute-start.23 = (bf16[3,80,384]{2,1,0:T(8,128)(2,1)S(1)}, bf16[3,80,384]{2,1,0:T(8,128)(2,1)S(1)}, u32[]{:S(2)}, u32[]{:S(2)}) collective-permute-start(bf16[3,80,384]{2,1,0:T(8,128)(2,1)S(1)} %slice.80), channel_id=1, source_target_pairs={{0,4},{1,5},{2,6},{3,7},{4,0},{5,1},{6,2},{7,3},{8,12},{9,13},{10,... | collective-permute-start | bytes 552968 | tf_op jit(solution)/shard_map/ppermute | solution.py:241
  69.9 0.9 slice.81
  71.7 1.0 slice.78
  72.7 1.0 collective-permute-start.12
  73.7 1.1 slice.74
  75.1 1.2 collective-permute-start.14
  76.4 3.2 %collective-permute-done.11.refs_5_ = bf16[3,96,384]{2,1,0:T(8,128)(2,1)S(1)} collective-permute-done((bf16[3,96,384]{2,1,0:T(8,128)(2,1)S(1)}, bf16[3,96,384]{2,1,0:T(8,128)(2,1)S(1)}, u32[]{:S(2)}, u32[]{:S(2)}) %collective-permute-start.11) | collective-permute-done | bytes 221216 | tf_op jit(solution)/shard_map/ppermute | solution.py:241
  79.5 0.8 collective-permute-start.16
  80.3 1.3 %collective-permute-done.12.refs_6_ = bf16[3,96,384]{2,1,0:T(8,128)(2,1)S(1)} collective-permute-done((bf16[3,96,384]{2,1,0:T(8,128)(2,1)S(1)}, bf16[3,96,384]{2,1,0:T(8,128)(2,1)S(1)}, u32[]{:S(2)}, u32[]{:S(2)}) %collective-permute-start.12) | collective-permute-done | bytes 221216 | tf_op jit(solution)/shard_map/ppermute | solution.py:241
  81.6 1.1 collective-permute-start.17
  82.7 1.0 broadcast_select_fusion.4
  85.1 6.1 %shard_map.101 = (bf16[192,1536]{1,0:T(8,128)(2,1)S(1)}, f32[128,1536]{1,0:T(8,128)S(1)}, f32[128,1]{1,0:T(8,128)S(1)}, f32[128,384]{1,0:T(8,128)S(1)}, bf16[3,1...) custom-call(bf16[224,1536]{1,0:T(8,128)(2,1)S(1)} %get-tuple-element.40.noise, ...), custom_call_target="tpu_custom_call" | custom-call | tf_op jit(solution)/shard_map/pallas_call | solution.py:600
  91.3 6.2 %shard_map.102 = (f32[128,256]{1,0:T(8,128)S(1)}, f32[128,640]{1,0:T(8,128)S(1)}, bf16[32,640]{1,0:T(8,128)(2,1)S(1)}, bf16[1536,896]{1,0:T(8,128)(2,1)S(1)}) custom-call(s32[4]{0:T(128)S(1)} %copy-done.4, s32[16,2]{1,0:T(8,128)S(1)} %copy.11.pairs, bf16[192,1536]{1,0:T(8,128)(2,1)S(1)} %get-tuple-element.23.normed, ...), custom_call_target="tpu_custom_call" | custom-call | tf_op jit(solution)/shard_map/pallas_call | solution.py:615
  97.5 7.5 %collective-permute-start.30 = (bf16[32,640]{1,0:T(8,128)(2,1)S(1)}, bf16[32,640]{1,0:T(8,128)(2,1)S(1)}, u32[]{:S(2)}, u32[]{:S(2)}) collective-permute-start(bf16[32,640]{1,0:T(8,128)(2,1)S(1)} %get-tuple-element.27), channel_id=1, source_target_pairs={{1,8},{3,10},{5,12},{7,14},{8,1},{9,16},{10,3},{11,18},{12,5},{13,... | collective-permute-start | bytes 122888 | tf_op jit(solution)/shard_map/ppermute | solution.py:241
  105.0 1.7 %collective-permute-done.30.received = bf16[32,640]{1,0:T(8,128)(2,1)S(1)} collective-permute-done((bf16[32,640]{1,0:T(8,128)(2,1)S(1)}, bf16[32,640]{1,0:T(8,128)(2,1)S(1)}, u32[]{:S(2)}, u32[]{:S(2)}) %collective-permute-start.30) | collective-permute-done | bytes 40992 | tf_op jit(solution)/shard_map/ppermute | solution.py:241
  106.7 3.1 %shard_map.103 = (bf16[128,384]{1,0:T(8,128)(2,1)S(1)}, f32[64,1536]{1,0:T(8,128)S(1)}, bf16[16,384]{1,0:T(8,128)(2,1)S(1)}) custom-call(f32[128,256]{1,0:T(8,128)S(1)} %get-tuple-element.25.d_q, f32[128,640]{1,0:T(8,128)S(1)} %get-tuple-element.26.d_kv, bf16[32,640]{1,0:T(8,128)(2,1)S(1)} %collective-permute-done.30.received, ...), custom_call_target="tpu_custom_call" | custom-call | tf_op jit(solution)/shard_map/pallas_call | solution.py:630
  109.8 3.6 %collective-permute-start.31 = (bf16[16,384]{1,0:T(8,128)(2,1)S(1)}, bf16[16,384]{1,0:T(8,128)(2,1)S(1)}, u32[]{:S(2)}, u32[]{:S(2)}) collective-permute-start(bf16[16,384]{1,0:T(8,128)(2,1)S(1)} %get-tuple-element.34), channel_id=1, source_target_pairs={{1,8},{3,10},{5,12},{7,14},{8,1},{9,16},{10,3},{11,18},{12,5},{13,... | collective-permute-start | bytes 36872 | tf_op jit(solution)/shard_map/ppermute | solution.py:241
  113.5 1.4 %collective-permute-done.31.received = bf16[16,384]{1,0:T(8,128)(2,1)S(1)} collective-permute-done((bf16[16,384]{1,0:T(8,128)(2,1)S(1)}, bf16[16,384]{1,0:T(8,128)(2,1)S(1)}, u32[]{:S(2)}, u32[]{:S(2)}) %collective-permute-start.31) | collective-permute-done | bytes 12320 | tf_op jit(solution)/shard_map/ppermute | solution.py:241
  114.9 1.8 %shard_map.104 = (f32[32,1536]{1,0:T(8,128)S(1)}, bf16[32,1536]{1,0:T(8,128)(2,1)S(1)}) custom-call(bf16[128,384]{1,0:T(8,128)(2,1)S(1)} %get-tuple-element.33.d_hidden, bf16[16,384]{1,0:T(8,128)(2,1)S(1)} %collective-permute-done.31.received, f32[64,1536]{1,0:T(8,128)S(1)} %get-tuple-element.35.d_resid, bf16[224,1536]{1,0:T(8,128)(2,1)S(1)} %get-tuple-element.40.noise, ...), custom_call_target="tpu_custom_call" | custom-call | tf_op jit(solution)/shard_map/pallas_call | solution.py:642
  117.2 3.0 %collective-permute-done.32 = bf16[32,1536]{1,0:T(8,128)(2,1)S(1)} collective-permute-done((bf16[32,1536]{1,0:T(8,128)(2,1)S(1)}, bf16[32,1536]{1,0:T(8,128)(2,1)S(1)}, u32[]{:S(2)}, u32[]{:S(2)}) %collective-permute-start.32) | collective-permute-done | bytes 98336 | tf_op jit(solution)/shard_map/ppermute | solution.py:241
  120.2 1.6 %collective-permute-start.33 = (bf16[32,1536]{1,0:T(8,128)(2,1)S(1)}, bf16[32,1536]{1,0:T(8,128)(2,1)S(1)}, u32[]{:S(2)}, u32[]{:S(2)}) collective-permute-start(bf16[32,1536]{1,0:T(8,128)(2,1)S(1)} %add_convert_fusion), channel_id=1, source_target_pairs={{0,1},{1,5},{2,3},{3,7},{4,0},{5,4},{6,2},{7,6},{8,9},{9,13},{10,1... | collective-permute-start | bytes 294920 | tf_op jit(solution)/shard_map/ppermute | solution.py:241
  121.8 1.9 %collective-permute-start.34 = (bf16[32,1536]{1,0:T(8,128)(2,1)S(1)}, bf16[32,1536]{1,0:T(8,128)(2,1)S(1)}, u32[]{:S(2)}, u32[]{:S(2)}) collective-permute-start(bf16[32,1536]{1,0:T(8,128)(2,1)S(1)} %add_convert_fusion), channel_id=1, source_target_pairs={{1,4},{3,6},{4,1},{6,3},{9,12},{11,14},{12,9},{14,11},{17,20},{19,... | collective-permute-start | bytes 294920 | tf_op jit(solution)/shard_map/ppermute | solution.py:241
  123.7 4.0 %collective-permute-done.34 = bf16[32,1536]{1,0:T(8,128)(2,1)S(1)} collective-permute-done((bf16[32,1536]{1,0:T(8,128)(2,1)S(1)}, bf16[32,1536]{1,0:T(8,128)(2,1)S(1)}, u32[]{:S(2)}, u32[]{:S(2)}) %collective-permute-start.34) | collective-permute-done | bytes 98336 | tf_op jit(solution)/shard_map/ppermute | solution.py:241
  127.7 0.7 add_multiply_fusion
  (85 shorter events, 5.7 us)
Async XLA Ops:
  0.0 20.1 %copy-start.12 = (bf16[32,1536]{1,0:T(8,128)(2,1)S(1)}, bf16[32,1536]{1,0:T(8,128)(2,1)}, u32[]{:S(2)}) copy-start(bf16[32,1536]{1,0:T(8,128)(2,1)} %param.10) | copy-start | bytes 294916
  0.0 20.1 %copy-start.11 = (bf16[32,1536]{1,0:T(8,128)(2,1)S(1)}, bf16[32,1536]{1,0:T(8,128)(2,1)}, u32[]{:S(2)}) copy-start(bf16[32,1536]{1,0:T(8,128)(2,1)} %param.12) | copy-start | bytes 294916
  1.0 10.2 %collective-permute-start = (bf16[32,1536]{1,0:T(8,128)(2,1)S(1)}, bf16[32,1536]{1,0:T(8,128)(2,1)S(1)}, u32[]{:S(2)}, u32[]{:S(2)}) collective-permute-start(bf16[32,1536]{1,0:T(8,128)(2,1)S(1)} %get-tuple-element.51), channel_id=1, source_target_pairs={{0,0},{1,4},{2,2},{3,6},{4,1},{5,5},{6,3},{7,7},{8,8},{9,12},{10,1... | collective-permute-start | bytes 294920 | tf_op jit(solution)/shard_map/ppermute | solution.py:241
  5.5 5.6 %collective-permute-start.1 = (bf16[32,1536]{1,0:T(8,128)(2,1)S(1)}, bf16[32,1536]{1,0:T(8,128)(2,1)S(1)}, u32[]{:S(2)}, u32[]{:S(2)}) collective-permute-start(bf16[32,1536]{1,0:T(8,128)(2,1)S(1)} %get-tuple-element.52), channel_id=1, source_target_pairs={{0,2},{1,6},{2,0},{3,4},{4,3},{5,7},{6,1},{7,5},{8,10},{9,14},{10,... | collective-permute-start | bytes 294920 | tf_op jit(solution)/shard_map/ppermute | solution.py:241
  7.5 7.0 %collective-permute-start.2 = (bf16[2,32,1536]{2,1,0:T(8,128)(2,1)S(1)}, bf16[2,32,1536]{2,1,0:T(8,128)(2,1)S(1)}, u32[]{:S(2)}, u32[]{:S(2)}) collective-permute-start(bf16[2,32,1536]{2,1,0:T(8,128)(2,1)S(1)} %pad_maximum_fusion.8), channel_id=1, source_target_pairs={{1,4},{3,6},{4,1},{6,3},{9,12},{11,14},{12,9},{14,11},{17,20},{19,... | collective-permute-start | bytes 589832 | tf_op jit(solution)/shard_map/ppermute | solution.py:241
  15.5 4.6 %collective-permute-start.3 = (bf16[2,32,1536]{2,1,0:T(8,128)(2,1)S(1)}, bf16[2,32,1536]{2,1,0:T(8,128)(2,1)S(1)}, u32[]{:S(2)}, u32[]{:S(2)}) collective-permute-start(bf16[2,32,1536]{2,1,0:T(8,128)(2,1)S(1)} %broadcast_select_fusion.5), channel_id=1, source_target_pairs={{0,2},{1,3},{2,0},{3,1},{4,6},{5,7},{6,4},{7,5},{8,10},{9,11},{10,... | collective-permute-start | bytes 589832 | tf_op jit(solution)/shard_map/ppermute | solution.py:241
  20.2 8.4 %copy-start.9 = (bf16[64,1536]{1,0:T(8,128)(2,1)}, bf16[64,1536]{1,0:T(8,128)(2,1)S(1)}, u32[]{:S(2)}) copy-start(bf16[64,1536]{1,0:T(8,128)(2,1)S(1)} %get-tuple-element.46) | copy-start | bytes 589828
  20.2 8.0 %collective-permute-start.4 = (bf16[2,48,1536]{2,1,0:T(8,128)(2,1)S(1)}, bf16[2,48,1536]{2,1,0:T(8,128)(2,1)S(1)}, u32[]{:S(2)}, u32[]{:S(2)}) collective-permute-start(bf16[2,48,1536]{2,1,0:T(8,128)(2,1)S(1)} %fusion.6), channel_id=1, source_target_pairs={{1,8},{3,10},{5,12},{7,14},{8,1},{9,16},{10,3},{11,18},{12,5},{13,... | collective-permute-start | bytes 884744 | tf_op jit(solution)/shard_map/ppermute | solution.py:241
  28.4 1.6 %copy-start = (bf16[3,384,384]{2,1,0:T(8,128)(2,1)S(1)}, bf16[3,384,384]{2,1,0:T(8,128)(2,1)}, u32[]{:S(2)}) copy-start(bf16[3,384,384]{2,1,0:T(8,128)(2,1)} %refs_0_.2) | copy-start | bytes 2654212
  28.4 1.8 %copy-start.1 = (bf16[384,896]{1,0:T(8,128)(2,1)S(1)}, bf16[384,896]{1,0:T(8,128)(2,1)}, u32[]{:S(2)}) copy-start(bf16[384,896]{1,0:T(8,128)(2,1)} %refs_0_.3) | copy-start | bytes 2064388
  28.4 1.9 %copy-start.2 = (bf16[96,1536]{1,0:T(8,128)(2,1)S(1)}, bf16[96,1536]{1,0:T(8,128)(2,1)}, u32[]{:S(2)}) copy-start(bf16[96,1536]{1,0:T(8,128)(2,1)} %refs_1_.2) | copy-start | bytes 884740
  28.5 1.9 %copy-start.3 = (bf16[96,1536]{1,0:T(8,128)(2,1)S(1)}, bf16[96,1536]{1,0:T(8,128)(2,1)}, u32[]{:S(2)}) copy-start(bf16[96,1536]{1,0:T(8,128)(2,1)} %refs_1_.3) | copy-start | bytes 884740
  29.5 28.4 %copy-start.13 = (f32[1536]{0:T(1024)S(1)}, f32[1536]{0:T(1024)}, u32[]{:S(2)}) copy-start(f32[1536]{0:T(1024)} %param.15) | copy-start | bytes 18436
  29.5 28.4 %copy-start.14 = (s32[16,2]{0,1:T(2,128)S(1)}, s32[16,2]{0,1:T(2,128)}, u32[]{:S(2)}) copy-start(s32[16,2]{0,1:T(2,128)} %param.19) | copy-start | bytes 388
  29.5 43.1 %collective-permute-start.5 = (bf16[288,1536]{1,0:T(8,128)(2,1)}, bf16[288,1536]{1,0:T(8,128)(2,1)}, u32[]{:S(2)}, u32[]{:S(2)}) collective-permute-start(bf16[288,1536]{1,0:T(8,128)(2,1)} %pad_maximum_fusion), channel_id=1, source_target_pairs={{0,1},{1,0},{2,3},{3,2},{4,5},{5,4},{6,7},{7,6},{8,9},{9,8},{10,11... | collective-permute-start | bytes 2654216 | tf_op jit(solution)/shard_map/ppermute | solution.py:241
  30.4 8.6 %collective-permute-start.6 = (bf16[192,384]{1,0:T(8,128)(2,1)S(1)}, bf16[192,384]{1,0:T(8,128)(2,1)S(1)}, u32[]{:S(2)}, u32[]{:S(2)}) collective-permute-start(bf16[192,384]{1,0:T(8,128)(2,1)S(1)} %get-tuple-element.22), channel_id=1, source_target_pairs={{0,8},{1,9},{2,10},{3,11},{4,12},{5,13},{6,14},{7,15},{8,0},{9,1},... | collective-permute-start | bytes 442376 | tf_op jit(solution)/shard_map/ppermute | solution.py:241
  31.8 7.3 %collective-permute-start.7 = (bf16[192,384]{1,0:T(8,128)(2,1)S(1)}, bf16[192,384]{1,0:T(8,128)(2,1)S(1)}, u32[]{:S(2)}, u32[]{:S(2)}) collective-permute-start(bf16[192,384]{1,0:T(8,128)(2,1)S(1)} %get-tuple-element.22), channel_id=1, source_target_pairs={{0,16},{1,17},{2,18},{3,19},{4,20},{5,21},{6,22},{7,23},{8,24},{9,... | collective-permute-start | bytes 442376 | tf_op jit(solution)/shard_map/ppermute | solution.py:241
  32.9 13.9 %collective-permute-start.8 = (bf16[192,384]{1,0:T(8,128)(2,1)S(1)}, bf16[192,384]{1,0:T(8,128)(2,1)S(1)}, u32[]{:S(2)}, u32[]{:S(2)}) collective-permute-start(bf16[192,384]{1,0:T(8,128)(2,1)S(1)} %get-tuple-element.22), channel_id=1, source_target_pairs={{0,24},{1,25},{2,26},{3,27},{4,28},{5,29},{6,30},{7,31},{8,16},{9,... | collective-permute-start | bytes 442376 | tf_op jit(solution)/shard_map/ppermute | solution.py:241
  34.1 13.4 %collective-permute-start.18 = (bf16[160,384]{1,0:T(8,128)(2,1)S(1)}, bf16[160,384]{1,0:T(8,128)(2,1)S(1)}, u32[]{:S(2)}, u32[]{:S(2)}) collective-permute-start(bf16[160,384]{1,0:T(8,128)(2,1)S(1)} %get-tuple-element.24), channel_id=1, source_target_pairs={{0,8},{1,9},{2,10},{3,11},{4,12},{5,13},{6,14},{7,15},{8,0},{9,1},... | collective-permute-start | bytes 368648 | tf_op jit(solution)/shard_map/ppermute | solution.py:241
  39.1 16.6 %collective-permute-start.19 = (bf16[160,384]{1,0:T(8,128)(2,1)S(1)}, bf16[160,384]{1,0:T(8,128)(2,1)S(1)}, u32[]{:S(2)}, u32[]{:S(2)}) collective-permute-start(bf16[160,384]{1,0:T(8,128)(2,1)S(1)} %get-tuple-element.24), channel_id=1, source_target_pairs={{0,16},{1,17},{2,18},{3,19},{4,20},{5,21},{6,22},{7,23},{8,24},{9,... | collective-permute-start | bytes 368648 | tf_op jit(solution)/shard_map/ppermute | solution.py:241
  39.1 16.6 %collective-permute-start.20 = (bf16[160,384]{1,0:T(8,128)(2,1)S(1)}, bf16[160,384]{1,0:T(8,128)(2,1)S(1)}, u32[]{:S(2)}, u32[]{:S(2)}) collective-permute-start(bf16[160,384]{1,0:T(8,128)(2,1)S(1)} %get-tuple-element.24), channel_id=1, source_target_pairs={{0,24},{1,25},{2,26},{3,27},{4,28},{5,29},{6,30},{7,31},{8,16},{9,... | collective-permute-start | bytes 368648 | tf_op jit(solution)/shard_map/ppermute | solution.py:241
  46.8 24.0 %collective-permute-start.9 = (bf16[3,192,384]{2,1,0:T(8,128)(2,1)S(1)}, bf16[3,192,384]{2,1,0:T(8,128)(2,1)S(1)}, u32[]{:S(2)}, u32[]{:S(2)}) collective-permute-start(bf16[3,192,384]{2,1,0:T(8,128)(2,1)S(1)} %pad_maximum_fusion.4.refs_2_), channel_id=1, source_target_pairs={{0,2},{1,3},{2,0},{3,1},{4,6},{5,7},{6,4},{7,5},{8,10},{9,11},{10,... | collective-permute-start | bytes 1327112 | tf_op jit(solution)/shard_map/ppermute | solution.py:241
  47.5 23.7 %collective-permute-start.10 = (bf16[3,192,384]{2,1,0:T(8,128)(2,1)S(1)}, bf16[3,192,384]{2,1,0:T(8,128)(2,1)}, u32[]{:S(2)}, u32[]{:S(2)}) collective-permute-start(bf16[3,192,384]{2,1,0:T(8,128)(2,1)S(1)} %pad_maximum_fusion.4.refs_2_), channel_id=1, source_target_pairs={{0,4},{1,5},{2,6},{3,7},{4,0},{5,1},{6,2},{7,3},{8,12},{9,13},{10,... | collective-permute-start | bytes 1327112 | tf_op jit(solution)/shard_map/ppermute | solution.py:241
  55.7 10.3 %collective-permute-start.21 = (bf16[3,160,384]{2,1,0:T(8,128)(2,1)S(1)}, bf16[3,160,384]{2,1,0:T(8,128)(2,1)}, u32[]{:S(2)}, u32[]{:S(2)}) collective-permute-start(bf16[3,160,384]{2,1,0:T(8,128)(2,1)S(1)} %pad_maximum_fusion.6.refs_2_), channel_id=1, source_target_pairs={{0,2},{1,3},{2,0},{3,1},{4,6},{5,7},{6,4},{7,5},{8,10},{9,11},{10,... | collective-permute-start | bytes 1105928 | tf_op jit(solution)/shard_map/ppermute | solution.py:241
  56.3 12.1 %collective-permute-start.22 = (bf16[3,160,384]{2,1,0:T(8,128)(2,1)S(1)}, bf16[3,160,384]{2,1,0:T(8,128)(2,1)}, u32[]{:S(2)}, u32[]{:S(2)}) collective-permute-start(bf16[3,160,384]{2,1,0:T(8,128)(2,1)S(1)} %pad_maximum_fusion.6.refs_2_), channel_id=1, source_target_pairs={{0,4},{1,5},{2,6},{3,7},{4,0},{5,1},{6,2},{7,3},{8,12},{9,13},{10,... | collective-permute-start | bytes 1105928 | tf_op jit(solution)/shard_map/ppermute | solution.py:241
  66.0 9.1 %collective-permute-start.13 = (bf16[3,192,384]{2,1,0:T(8,128)(2,1)S(1)}, bf16[3,192,384]{2,1,0:T(8,128)(2,1)S(1)}, u32[]{:S(2)}, u32[]{:S(2)}) collective-permute-start(bf16[3,192,384]{2,1,0:T(8,128)(2,1)S(1)} %pad_maximum_fusion.4.refs_2_), channel_id=1, source_target_pairs={{0,1},{1,0},{2,3},{3,2},{4,5},{5,4},{6,7},{7,6},{8,9},{9,8},{10,11... | collective-permute-start | bytes 1327112 | tf_op jit(solution)/shard_map/ppermute | solution.py:241
  68.4 6.4 %copy-start.6 = (bf16[2,64,1536]{2,1,0:T(8,128)(2,1)S(1)}, bf16[2,64,1536]{2,1,0:T(8,128)(2,1)}, u32[]{:S(2)}) copy-start(bf16[2,64,1536]{2,1,0:T(8,128)(2,1)} %copy-done.5) | copy-start | bytes 1179652
  68.5 6.4 %copy-start.8 = (bf16[2,48,1536]{2,1,0:T(8,128)(2,1)S(1)}, bf16[2,48,1536]{2,1,0:T(8,128)(2,1)}, u32[]{:S(2)}) copy-start(bf16[2,48,1536]{2,1,0:T(8,128)(2,1)} %copy-done.7) | copy-start | bytes 884740
  68.5 7.8 %collective-permute-start.23 = (bf16[3,80,384]{2,1,0:T(8,128)(2,1)S(1)}, bf16[3,80,384]{2,1,0:T(8,128)(2,1)S(1)}, u32[]{:S(2)}, u32[]{:S(2)}) collective-permute-start(bf16[3,80,384]{2,1,0:T(8,128)(2,1)S(1)} %slice.80), channel_id=1, source_target_pairs={{0,4},{1,5},{2,6},{3,7},{4,0},{5,1},{6,2},{7,3},{8,12},{9,13},{10,... | collective-permute-start | bytes 552968 | tf_op jit(solution)/shard_map/ppermute | solution.py:241
  70.9 12.8 %collective-permute-start.24 = (bf16[3,80,384]{2,1,0:T(8,128)(2,1)S(1)}, bf16[3,80,384]{2,1,0:T(8,128)(2,1)S(1)}, u32[]{:S(2)}, u32[]{:S(2)}) collective-permute-start(bf16[3,80,384]{2,1,0:T(8,128)(2,1)S(1)} %slice.81), channel_id=1, source_target_pairs={{0,2},{1,3},{2,0},{3,1},{4,6},{5,7},{6,4},{7,5},{8,10},{9,11},{10,... | collective-permute-start | bytes 552968 | tf_op jit(solution)/shard_map/ppermute | solution.py:241
  71.2 8.3 %collective-permute-start.11 = (bf16[3,96,384]{2,1,0:T(8,128)(2,1)S(1)}, bf16[3,96,384]{2,1,0:T(8,128)(2,1)S(1)}, u32[]{:S(2)}, u32[]{:S(2)}) collective-permute-start(bf16[3,96,384]{2,1,0:T(8,128)(2,1)S(1)} %slice.77), channel_id=1, source_target_pairs={{0,4},{1,5},{2,6},{3,7},{4,0},{5,1},{6,2},{7,3},{8,12},{9,13},{10,... | collective-permute-start | bytes 663560 | tf_op jit(solution)/shard_map/ppermute | solution.py:241
  72.7 9.0 %collective-permute-start.12 = (bf16[3,96,384]{2,1,0:T(8,128)(2,1)S(1)}, bf16[3,96,384]{2,1,0:T(8,128)(2,1)S(1)}, u32[]{:S(2)}, u32[]{:S(2)}) collective-permute-start(bf16[3,96,384]{2,1,0:T(8,128)(2,1)S(1)} %slice.78), channel_id=1, source_target_pairs={{0,2},{1,3},{2,0},{3,1},{4,6},{5,7},{6,4},{7,5},{8,10},{9,11},{10,... | collective-permute-start | bytes 663560 | tf_op jit(solution)/shard_map/ppermute | solution.py:241
  74.8 7.9 %copy-start.10 = (bf16[64,1536]{1,0:T(8,128)(2,1)S(1)}, bf16[64,1536]{1,0:T(8,128)(2,1)}, u32[]{:S(2)}) copy-start(bf16[64,1536]{1,0:T(8,128)(2,1)} %copy-done.9) | copy-start | bytes 589828
  75.1 9.4 %collective-permute-start.14 = (bf16[3,192,384]{2,1,0:T(8,128)(2,1)S(1)}, bf16[3,192,384]{2,1,0:T(8,128)(2,1)S(1)}, u32[]{:S(2)}, u32[]{:S(2)}) collective-permute-start(bf16[3,192,384]{2,1,0:T(8,128)(2,1)S(1)} %collective-permute-done.9.refs_3_), channel_id=1, source_target_pairs={{0,1},{1,0},{2,3},{3,2},{4,5},{5,4},{6,7},{7,6},{8,9},{9,8},{10,11... | collective-permute-start | bytes 1327112 | tf_op jit(solution)/shard_map/ppermute | solution.py:241
  76.3 8.7 %collective-permute-start.15 = (bf16[3,192,384]{2,1,0:T(8,128)(2,1)}, bf16[3,192,384]{2,1,0:T(8,128)(2,1)S(1)}, u32[]{:S(2)}, u32[]{:S(2)}) collective-permute-start(bf16[3,192,384]{2,1,0:T(8,128)(2,1)} %collective-permute-done.10.refs_4_), channel_id=1, source_target_pairs={{0,1},{1,0},{2,3},{3,2},{4,5},{5,4},{6,7},{7,6},{8,9},{9,8},{10,11... | collective-permute-start | bytes 1327112 | tf_op jit(solution)/shard_map/ppermute | solution.py:241
  79.5 4.2 %collective-permute-start.16 = (bf16[3,96,384]{2,1,0:T(8,128)(2,1)S(1)}, bf16[3,96,384]{2,1,0:T(8,128)(2,1)S(1)}, u32[]{:S(2)}, u32[]{:S(2)}) collective-permute-start(bf16[3,96,384]{2,1,0:T(8,128)(2,1)S(1)} %collective-permute-done.11.refs_5_), channel_id=1, source_target_pairs={{0,1},{1,0},{2,3},{3,2},{4,5},{5,4},{6,7},{7,6},{8,9},{9,8},{10,11... | collective-permute-start | bytes 663560 | tf_op jit(solution)/shard_map/ppermute | solution.py:241
  81.6 2.7 %collective-permute-start.17 = (bf16[3,96,384]{2,1,0:T(8,128)(2,1)S(1)}, bf16[3,96,384]{2,1,0:T(8,128)(2,1)S(1)}, u32[]{:S(2)}, u32[]{:S(2)}) collective-permute-start(bf16[3,96,384]{2,1,0:T(8,128)(2,1)S(1)} %collective-permute-done.12.refs_6_), channel_id=1, source_target_pairs={{0,1},{1,0},{2,3},{3,2},{4,5},{5,4},{6,7},{7,6},{8,9},{9,8},{10,11... | collective-permute-start | bytes 663560 | tf_op jit(solution)/shard_map/ppermute | solution.py:241
  83.7 7.6 %collective-permute-start.25 = (bf16[3,160,384]{2,1,0:T(8,128)(2,1)S(1)}, bf16[3,160,384]{2,1,0:T(8,128)(2,1)S(1)}, u32[]{:S(2)}, u32[]{:S(2)}) collective-permute-start(bf16[3,160,384]{2,1,0:T(8,128)(2,1)S(1)} %pad_maximum_fusion.6.refs_2_), channel_id=1, source_target_pairs={{0,1},{1,0},{2,3},{3,2},{4,5},{5,4},{6,7},{7,6},{8,9},{9,8},{10,11... | collective-permute-start | bytes 1105928 | tf_op jit(solution)/shard_map/ppermute | solution.py:241
  83.8 7.5 %collective-permute-start.26 = (bf16[3,160,384]{2,1,0:T(8,128)(2,1)}, bf16[3,160,384]{2,1,0:T(8,128)(2,1)S(1)}, u32[]{:S(2)}, u32[]{:S(2)}) collective-permute-start(bf16[3,160,384]{2,1,0:T(8,128)(2,1)} %collective-permute-done.21.refs_3_), channel_id=1, source_target_pairs={{0,1},{1,0},{2,3},{3,2},{4,5},{5,4},{6,7},{7,6},{8,9},{9,8},{10,11... | collective-permute-start | bytes 1105928 | tf_op jit(solution)/shard_map/ppermute | solution.py:241
  84.3 7.0 %collective-permute-start.27 = (bf16[3,160,384]{2,1,0:T(8,128)(2,1)}, bf16[3,160,384]{2,1,0:T(8,128)(2,1)S(1)}, u32[]{:S(2)}, u32[]{:S(2)}) collective-permute-start(bf16[3,160,384]{2,1,0:T(8,128)(2,1)} %collective-permute-done.22.refs_4_), channel_id=1, source_target_pairs={{0,1},{1,0},{2,3},{3,2},{4,5},{5,4},{6,7},{7,6},{8,9},{9,8},{10,11... | collective-permute-start | bytes 1105928 | tf_op jit(solution)/shard_map/ppermute | solution.py:241
  84.5 6.8 %collective-permute-start.28 = (bf16[3,80,384]{2,1,0:T(8,128)(2,1)S(1)}, bf16[3,80,384]{2,1,0:T(8,128)(2,1)S(1)}, u32[]{:S(2)}, u32[]{:S(2)}) collective-permute-start(bf16[3,80,384]{2,1,0:T(8,128)(2,1)S(1)} %collective-permute-done.23.refs_5_), channel_id=1, source_target_pairs={{0,1},{1,0},{2,3},{3,2},{4,5},{5,4},{6,7},{7,6},{8,9},{9,8},{10,11... | collective-permute-start | bytes 552968 | tf_op jit(solution)/shard_map/ppermute | solution.py:241
  85.0 6.3 %collective-permute-start.29 = (bf16[3,80,384]{2,1,0:T(8,128)(2,1)S(1)}, bf16[3,80,384]{2,1,0:T(8,128)(2,1)S(1)}, u32[]{:S(2)}, u32[]{:S(2)}) collective-permute-start(bf16[3,80,384]{2,1,0:T(8,128)(2,1)S(1)} %collective-permute-done.24.refs_6_), channel_id=1, source_target_pairs={{0,1},{1,0},{2,3},{3,2},{4,5},{5,4},{6,7},{7,6},{8,9},{9,8},{10,11... | collective-permute-start | bytes 552968 | tf_op jit(solution)/shard_map/ppermute | solution.py:241
  85.1 6.2 %copy-start.4 = (s32[4]{0:T(128)S(1)}, s32[4]{0:T(128)}, u32[]{:S(2)}) copy-start(s32[4]{0:T(128)} %band.1) | copy-start | bytes 52
  97.5 9.2 %collective-permute-start.30 = (bf16[32,640]{1,0:T(8,128)(2,1)S(1)}, bf16[32,640]{1,0:T(8,128)(2,1)S(1)}, u32[]{:S(2)}, u32[]{:S(2)}) collective-permute-start(bf16[32,640]{1,0:T(8,128)(2,1)S(1)} %get-tuple-element.27), channel_id=1, source_target_pairs={{1,8},{3,10},{5,12},{7,14},{8,1},{9,16},{10,3},{11,18},{12,5},{13,... | collective-permute-start | bytes 122888 | tf_op jit(solution)/shard_map/ppermute | solution.py:241
  109.8 5.0 %collective-permute-start.31 = (bf16[16,384]{1,0:T(8,128)(2,1)S(1)}, bf16[16,384]{1,0:T(8,128)(2,1)S(1)}, u32[]{:S(2)}, u32[]{:S(2)}) collective-permute-start(bf16[16,384]{1,0:T(8,128)(2,1)S(1)} %get-tuple-element.34), channel_id=1, source_target_pairs={{1,8},{3,10},{5,12},{7,14},{8,1},{9,16},{10,3},{11,18},{12,5},{13,... | collective-permute-start | bytes 36872 | tf_op jit(solution)/shard_map/ppermute | solution.py:241
  116.6 3.5 %collective-permute-start.32 = (bf16[32,1536]{1,0:T(8,128)(2,1)S(1)}, bf16[32,1536]{1,0:T(8,128)(2,1)S(1)}, u32[]{:S(2)}, u32[]{:S(2)}) collective-permute-start(bf16[32,1536]{1,0:T(8,128)(2,1)S(1)} %get-tuple-element.38), channel_id=1, source_target_pairs={{0,2},{1,3},{2,0},{3,1},{4,6},{5,7},{6,4},{7,5},{8,10},{9,11},{10,... | collective-permute-start | bytes 294920 | tf_op jit(solution)/shard_map/ppermute | solution.py:241
  120.2 3.5 %collective-permute-start.33 = (bf16[32,1536]{1,0:T(8,128)(2,1)S(1)}, bf16[32,1536]{1,0:T(8,128)(2,1)S(1)}, u32[]{:S(2)}, u32[]{:S(2)}) collective-permute-start(bf16[32,1536]{1,0:T(8,128)(2,1)S(1)} %add_convert_fusion), channel_id=1, source_target_pairs={{0,1},{1,5},{2,3},{3,7},{4,0},{5,4},{6,2},{7,6},{8,9},{9,13},{10,1... | collective-permute-start | bytes 294920 | tf_op jit(solution)/shard_map/ppermute | solution.py:241
  121.8 5.9 %collective-permute-start.34 = (bf16[32,1536]{1,0:T(8,128)(2,1)S(1)}, bf16[32,1536]{1,0:T(8,128)(2,1)S(1)}, u32[]{:S(2)}, u32[]{:S(2)}) collective-permute-start(bf16[32,1536]{1,0:T(8,128)(2,1)S(1)} %add_convert_fusion), channel_id=1, source_target_pairs={{1,4},{3,6},{4,1},{6,3},{9,12},{11,14},{12,9},{14,11},{17,20},{19,... | collective-permute-start | bytes 294920 | tf_op jit(solution)/shard_map/ppermute | solution.py:241
  (2 other events, 2.3 us)

commit v5 on v4

--- a/solution.py
+++ b/solution.py
@@ -259,6 +259,10 @@
     return lax.axis_index("sa"), b // 2, lax.rem(b, 2), lax.axis_index("noise")
 
 
+def half_index():
+    return lax.rem(lax.axis_index("noise") + lax.axis_index("sa"), 2)
+
+
 def pack_kernel(conv, mix, qkv, out, early, late):
     z, y, x, n = position()
     b = 2 * y + x
@@ -315,7 +319,7 @@
 
 
 def forward_kernel(
-    noise, base, *refs,
+    blocks_even, blocks_odd, edge, other_even, other_odd, other_edge, *refs,
 ):
     own_conv, own_mix = refs[:2]
     same, other = refs[2:7], refs[7:12]
@@ -341,10 +345,17 @@
     for copy in copies:
         copy.start()
 
+    m = half_index()
+    for half, (even, odd, outer) in (
+        (m, (blocks_even, blocks_odd, edge)), (1 - m, (other_even, other_odd, other_edge))
+    ):
+        noisy[pl.ds(times(half, 176, 16), 48), :] = outer[...].astype(jnp.float32)
+        for shift, block in enumerate((even, odd)):
+            row = 48 + 64 * half + 32 * lax.rem(x + shift, 2)
+            noisy[pl.ds(pl.multiple_of(row, 16), 32), :] = block[...].astype(jnp.float32)
+
     def activate(c, _):
-        values = base[:, chunk(c)].astype(jnp.float32) + noise[:, chunk(c)].astype(jnp.float32)
-        noisy[:, chunk(c)] = values
-        gelu_in[:, chunk(c)] = gelu_tanh(values).astype(jnp.bfloat16)
+        gelu_in[:, chunk(c)] = gelu_tanh(noisy[:, chunk(c)]).astype(jnp.bfloat16)
         return 0
 
     lax.fori_loop(0, 4, activate, 0)
@@ -378,10 +389,10 @@
         copy.wait()
 
 
-def attention_kernel(band, pairs, normed, cot, *refs):
+def attention_kernel(band, pairs, normed, cot_block, cot_beside, other_block, other_beside, *refs):
     own_qkv, own_out = refs[:2]
     same, other = refs[2:7], refs[7:12]
-    d_q_out, d_kv_out, send, qkv_out, qkv, out, sems = refs[12:]
+    d_q_out, d_kv_out, send, qkv_out, cot_out, qkv, out, sems = refs[12:]
     z, y, x, n = position()
     length = lax.axis_size("sa") * 128
     first_bin = z * 128
@@ -411,7 +422,12 @@
     proj = proj.astype(jnp.bfloat16)
     copy = pltpu.make_async_copy(qkv, qkv_out, sems.at[0])
     copy.start()
-    d_att = nt(cot[...], out[...]).astype(jnp.bfloat16)
+    m = half_index()
+    for half, (block, beside) in ((m, (cot_block, cot_beside)), (1 - m, (other_block, other_beside))):
+        for shift, rows in enumerate((block, beside)):
+            row = 64 * half + 32 * lax.rem(x + shift, 2)
+            cot_out[pl.ds(pl.multiple_of(row, 32), 32), :] = rows[...]
+    d_att = nt(cot_out[...], out[...]).astype(jnp.bfloat16)
 
     row = lax.broadcasted_iota(jnp.int32, (128, 192), 0)
     column = lax.broadcasted_iota(jnp.int32, (128, 192), 1) - 32
@@ -440,7 +456,7 @@
     d_q_out[...] = jnp.concatenate(d_queries, axis=1)
     d_kv = jnp.concatenate(d_keys + d_values, axis=1)
     d_kv_out[...] = d_kv[32:160]
-    send[...] = jnp.where(n == 0, d_kv[:32], d_kv[160:]).astype(jnp.bfloat16)
+    send[...] = jnp.where(m == 0, d_kv[:32], d_kv[160:]).astype(jnp.bfloat16)
     copy.wait()
 
 
@@ -448,7 +464,7 @@
     d_q, d_kv, received, resid, inv_rms_ref, hidden, cot, gain, mix, qkv,
     d_hidden_out, d_resid_out, send, total_kv, gained, d_resid_all,
 ):
-    z, y, x, n = position()
+    n = half_index()
     total_kv[...] = d_kv[...]
     edge = pl.ds(pl.multiple_of(n * 96, 32), 32)
     total_kv[edge, :] = total_kv[edge, :] + received[...].astype(jnp.float32)
@@ -486,8 +502,8 @@
         send[...] = d_hidden[112:]
 
 
-def taps_kernel(d_hidden, received, d_resid, noise, base, conv, keep, send, extended_ref, grads):
-    z, y, x, n = position()
+def taps_kernel(d_hidden, received, d_resid, blocks_even, blocks_odd, conv, keep, send, extended_ref, noisy, grads):
+    x, n = lax.rem(lax.axis_index("sb"), 2), half_index()
 
     @pl.when(n == 0)
     def _():
@@ -499,14 +515,14 @@
         extended_ref[pl.ds(0, 80), :] = d_hidden[pl.ds(48, 80), :]
         extended_ref[pl.ds(80, 16), :] = received[...]
 
-    rows = pl.ds(pl.multiple_of(48 + 64 * n, 16), 64)
+    for shift, block in enumerate((blocks_even, blocks_odd)):
+        noisy[pl.ds(times(lax.rem(x + shift, 2), 32, 32), 32), :] = block[...].astype(jnp.float32)
 
     def taps(c, _):
-        noisy = base[rows, chunk(c)].astype(jnp.float32) + noise[rows, chunk(c)].astype(jnp.float32)
         total = nt(extended_ref[pl.ds(32, 64), :], conv[0, chunk(c), :])
         total = total + nt(extended_ref[pl.ds(16, 64), :], conv[1, chunk(c), :])
         total = total + nt(extended_ref[pl.ds(0, 64), :], conv[2, chunk(c), :])
-        grads[:, chunk(c)] = d_resid[:, chunk(c)] + total * gelu_slope(noisy)
+        grads[:, chunk(c)] = d_resid[:, chunk(c)] + total * gelu_slope(noisy[:, chunk(c)])
         return 0
 
     lax.fori_loop(0, 4, taps, 0)
@@ -541,7 +557,8 @@
     base, noise, cot, convolution_weight, mix_w, norm_gain, qkv_w, out_w, band_width, pairs
 ):
     n_sa = lax.axis_size("sa")
-    z, b, n = (lax.axis_index("sa"), lax.axis_index("sb"), lax.axis_index("noise"))
+    b = lax.axis_index("sb")
+    m = half_index()
     y, x = (b >> 1, b & 1)
     features = base.shape[1]
 
@@ -559,42 +576,46 @@
     y_route = routes(n_sa, lambda z, y, x, c: (z, 1 - y, x, c))
     core_route = routes(n_sa, lambda z, y, x, c: (z, y, x, 1 - c))
 
-    def collected(piece):
+    def collected(piece, nearest):
         half = piece.shape[0] // 2
-        straight = jnp.stack([permuted(piece, along_z(step)) for step in range(1, 4)])
+        straight = jnp.stack([nearest] + [permuted(piece, along_z(step)) for step in range(2, 4)])
         beside, across = permuted(straight, x_route), permuted(straight, y_route)
         diagonal_a = permuted(beside[:, :half], y_route)
         diagonal_b = permuted(across[:, half:], x_route)
         same = (straight, beside, across, diagonal_a, diagonal_b)
-        return same + tuple(permuted(part, core_route) for part in same)
-
-    early, late = collected(early), collected(late)
+        return same, tuple(permuted(part, core_route) for part in same[:3])
+
+    nearest = permuted(early, along_z(1))
+    early, early_other = collected(early, nearest)
+    early += early_other + tuple(permuted(part, core_route) for part in early[3:])
+    late, _ = lax.optimization_barrier((late, early[0]))
+    late, late_other = collected(late, permuted(late, along_z(1)))
+    noise, base, _ = lax.optimization_barrier((noise, base, early[0]))
+    cot, _ = lax.optimization_barrier((cot, late[0]))
 
     def to_sample(shift):
-        return routes(n_sa, lambda z, y, x, c: (z, c, (x + shift) % 2, y))
-
-    got = [
-        permuted(jnp.where(x == shift, noise[0], noise[1]), to_sample(shift))
-        for shift in range(2)
+        return routes(n_sa, lambda z, y, x, c: (z, c, (x + shift) % 2, y ^ (z & 1)))
+
+    noisy = (base.astype(f32)[None] + noise.astype(f32)).astype(bf16)
+    even = x == 0
+    blocks = [
+        permuted(jnp.where(x == shift, noisy[0], noisy[1]), to_sample(shift)) for shift in range(2)
     ]
-    even = x == 0
-    noise_half = jnp.concatenate([jnp.where(even, got[0], got[1]), jnp.where(even, got[1], got[0])], axis=0)
-    both = jnp.stack([base, cot])
-    across = permuted(both, routes(n_sa, lambda z, y, x, c: (z, 1 - y, x, 1 - c) if y != c else None))
-    current = jnp.where(y == n, both, across)
-    beside = permuted(current, x_route)
-    halves = jnp.concatenate([jnp.where(even, current, beside), jnp.where(even, beside, current)], axis=1)
-    edge_route = routes(n_sa, lambda z, y, x, c: (z - 1, y, x, 1) if c == 0 else (z + 1, y, x, 0))
-    mine = jnp.stack([noise_half, halves[0]])
-    edge = permuted(jnp.where(n == 0, mine[:, :48], mine[:, 16:]), edge_route)
-    wide = jnp.concatenate([jnp.where(n == 0, edge, mine[:, :48])] + [jnp.where(n == 0, mine, jnp.concatenate([mine[:, 48:], edge], axis=1))], axis=1)
-    swap = permuted(jnp.concatenate([wide.reshape(224, features), halves[1]], axis=0), core_route)
-    wide_other = swap[:224].reshape(2, 112, features)
-    whole = jnp.concatenate([jnp.where(n == 0, wide, wide_other), jnp.where(n == 0, wide_other, wide)], axis=1)
-    noise_rows, base_rows = whole[0], whole[1]
-    cot_rows = jnp.concatenate(
-        [jnp.where(n == 0, halves[1], swap[224:]), jnp.where(n == 0, swap[224:], halves[1])], axis=0
-    )
+    edge_route = routes(
+        n_sa, lambda z, y, x, c: (z - 1, y, x, c) if c ^ (z & 1) == 0 else (z + 1, y, x, c)
+    )
+    low, high = jnp.where(even, blocks[0], blocks[1]), jnp.where(even, blocks[1], blocks[0])
+    outer = jnp.concatenate(
+        [jnp.where(m == 0, low[:16], low[16:]), jnp.where(m == 0, low[16:], high[:16]), jnp.where(m == 0, high[:16], high[16:])]
+    )
+    mine = (blocks[0], blocks[1], permuted(outer, edge_route))
+    noisy_rows = mine + tuple(permuted(part, core_route) for part in mine)
+    across = permuted(
+        cot, routes(n_sa, lambda z, y, x, c: (z, 1 - y, x, c) if y == c ^ (z & 1) else None)
+    )
+    cot_block = jnp.where(y == m, cot, across)
+    cot_rows = (cot_block, permuted(cot_block, x_route))
+    cot_rows = cot_rows + tuple(permuted(part, core_route) for part in cot_rows)
     gain = norm_gain.reshape(1, features)
 
     normed, resid, inv_rms, hidden, conv, mix = pl.pallas_call(
@@ -603,7 +624,7 @@
             shaped(192, features, dtype=bf16), shaped(128, features), shaped(128, 1), shaped(128, HID),
             shaped(3, features, HID, dtype=bf16), shaped(HID, features, dtype=bf16),
         ),
-        in_specs=vmem(15),
+        in_specs=vmem(19),
         out_specs=tuple(vmem(4) + hbm(2)),
         scratch_shapes=[
             pltpu.VMEM((3, features, HID), bf16), pltpu.VMEM((HID, features), bf16),
@@ -611,20 +632,23 @@
             pltpu.SemaphoreType.DMA((2,)),
         ],
         compiler_params=limit(28),
-    )(noise_rows, base_rows, convolution_weight, mix_w, *early, gain)
-    d_q, d_kv, send, qkv = pl.pallas_call(
+    )(*noisy_rows, convolution_weight, mix_w, *early, gain)
+    *diagonals, normed = lax.optimization_barrier((*late[3:], normed))
+    late += late_other + tuple(permuted(part, core_route) for part in diagonals)
+    d_q, d_kv, send, qkv, cot_all = pl.pallas_call(
         attention_kernel,
         out_shape=(
-            shaped(128, 256), shaped(128, 640), shaped(32, 640, dtype=bf16), shaped(features, 896, dtype=bf16)
+            shaped(128, 256), shaped(128, 640), shaped(32, 640, dtype=bf16), shaped(features, 896, dtype=bf16),
+            shaped(128, features, dtype=bf16),
         ),
-        in_specs=smem(2) + vmem(14),
-        out_specs=tuple(vmem(3) + hbm(1)),
+        in_specs=smem(2) + vmem(17),
+        out_specs=tuple(vmem(3) + hbm(1) + vmem(1)),
         scratch_shapes=[
             pltpu.VMEM((features, 896), bf16), pltpu.VMEM((HEADS * VAL, features), bf16),
             pltpu.SemaphoreType.DMA((1,)),
         ],
         compiler_params=limit(24),
-    )(band_width, pairs, normed, cot_rows, qkv_w, out_w, *late)
+    )(band_width, pairs, normed, *cot_rows, qkv_w, out_w, *late)
 
     received = permuted(send, edge_route)
     d_hidden, d_resid, send = pl.pallas_call(
@@ -636,7 +660,7 @@
             pltpu.VMEM((128, 640), f32), pltpu.VMEM((128, features), f32), pltpu.VMEM((128, features), f32),
         ],
         compiler_params=limit(16),
-    )(d_q, d_kv, received, resid, inv_rms, hidden, cot_rows, gain, mix, qkv)
+    )(d_q, d_kv, received, resid, inv_rms, hidden, cot_all, gain, mix, qkv)
 
     received = permuted(send, edge_route)
     keep, send = pl.pallas_call(
@@ -644,17 +668,19 @@
         out_shape=(shaped(32, features), shaped(32, features, dtype=bf16)),
         in_specs=vmem(6),
         out_specs=tuple(vmem(2)),
-        scratch_shapes=[pltpu.VMEM((96, HID), bf16), pltpu.VMEM((64, features), f32)],
+        scratch_shapes=[
+            pltpu.VMEM((96, HID), bf16), pltpu.VMEM((64, features), f32), pltpu.VMEM((64, features), f32),
+        ],
         compiler_params=limit(16),
-    )(d_hidden, received, d_resid, noise_rows, base_rows, conv)
+    )(d_hidden, received, d_resid, *blocks, conv)
 
     received = permuted(send, x_route)
     partial = (keep + received.astype(f32)).astype(bf16)
     first_sum = permuted(
-        partial, routes(n_sa, lambda z, y, x, c: (z, c, x, c) if y != c else (z, y, x, 1 - c))
-    )
-    second_sum = permuted(partial, routes(n_sa, lambda z, y, x, c: (z, c, x, 1 - c) if y != c else None))
-    other = jnp.where(y == n, partial, second_sum)
+        partial, routes(n_sa, lambda z, y, x, c: (z, 1 - y, x, c) if y != c ^ (z & 1) else (z, y, x, 1 - c))
+    )
+    second_sum = permuted(partial, routes(n_sa, lambda z, y, x, c: (z, 1 - y, x, 1 - c) if y != c ^ (z & 1) else None))
+    other = jnp.where(y == m, partial, second_sum)
     return (first_sum.astype(f32) + other.astype(f32)) * 0.25
 
 

time: 129 us -> 147 us (1.14)
  the two profiles are of different devices: /device:TPU:1 before, /device:TPU:8 now
where the time goes in v5:
time: 147 us; the launch traced here: 146 us
  waiting for transfers between devices  68.5 us (47%)
  starting transfers between devices  30.8 us (21%)
  local copies, waits for them, and re-layouts  27.2 us (19%)
  Pallas kernels  17 us (12%)
  other arithmetic  1.73 us (1%)
    ppermute x39, waiting for transfers between devices, permuted(): return lax.ppermute(value, ('sa', 'sb', 'noise'), pairs)  68.5 us
    ppermute x39, starting transfers between devices, permuted(): return lax.ppermute(value, ('sa', 'sb', 'noise'), pairs)  30.8 us
    unnamed x91, local copies, waits for them, and re-layouts  25.2 us
    pallas_call x1, Pallas kernels, stretch_shards(): pl.pallas_call(attention_kernel, out_shape=(shaped(128, 256), shaped(128,...  7 us
    pallas_call x1, Pallas kernels, stretch_shards(): pl.pallas_call(forward_kernel, out_shape=(shaped(192, features, dtype=bf1...  5.09 us
    pallas_call x1, Pallas kernels, stretch_shards(): pl.pallas_call(norm_kernel, out_shape=(shaped(128, HID, dtype=bf16), shap...  3.13 us
  transfers between devices with their start and end apart: 39, of which 19 were waited for; matrix products, arithmetic and copies ran while one was open for 2% of the time, Pallas kernels for 3%

profile of v5, /device:TPU:8, one launch (start us, length us, event | category | flops | bytes accessed | tf_op | source)
XLA Modules:
  0.0 145.6 jit_solution(17969131192325223303)
XLA Ops:
  0.0 1.2 copy-done
  1.2 1.1 copy-done.2
  2.3 1.0 copy-done.6
  3.2 1.0 copy-done.8
  4.3 3.0 %collective-permute-start.1 = (bf16[192,384]{1,0:T(8,128)(2,1)S(1)}, bf16[192,384]{1,0:T(8,128)(2,1)S(1)}, u32[]{:S(2)}, u32[]{:S(2)}) collective-permute-start(bf16[192,384]{1,0:T(8,128)(2,1)S(1)} %get-tuple-element.31), channel_id=1, source_target_pairs={{0,16},{1,17},{2,18},{3,19},{4,20},{5,21},{6,22},{7,23},{8,24},{9,... | collective-permute-start | bytes 442376 | tf_op jit(solution)/shard_map/ppermute | solution.py:241
  7.8 2.9 %collective-permute-done = bf16[192,384]{1,0:T(8,128)(2,1)S(1)} collective-permute-done((bf16[192,384]{1,0:T(8,128)(2,1)S(1)}, bf16[192,384]{1,0:T(8,128)(2,1)S(1)}, u32[]{:S(2)}, u32[]{:S(2)}) %collective-permute-start) | collective-permute-done | bytes 147488 | tf_op jit(solution)/shard_map/ppermute | solution.py:241
  10.7 7.0 %collective-permute-done.1 = bf16[192,384]{1,0:T(8,128)(2,1)S(1)} collective-permute-done((bf16[192,384]{1,0:T(8,128)(2,1)S(1)}, bf16[192,384]{1,0:T(8,128)(2,1)S(1)}, u32[]{:S(2)}, u32[]{:S(2)}) %collective-permute-start.1) | collective-permute-done | bytes 147488 | tf_op jit(solution)/shard_map/ppermute | solution.py:241
  17.8 2.8 %collective-permute-done.2 = bf16[192,384]{1,0:T(8,128)(2,1)S(1)} collective-permute-done((bf16[192,384]{1,0:T(8,128)(2,1)S(1)}, bf16[192,384]{1,0:T(8,128)(2,1)S(1)}, u32[]{:S(2)}, u32[]{:S(2)}) %collective-permute-start.2) | collective-permute-done | bytes 147488 | tf_op jit(solution)/shard_map/ppermute | solution.py:241
  20.8 1.9 %collective-permute-start.10 = (bf16[32,1536]{1,0:T(8,128)(2,1)S(1)}, bf16[32,1536]{1,0:T(8,128)(2,1)S(1)}, u32[]{:S(2)}, u32[]{:S(2)}) collective-permute-start(bf16[32,1536]{1,0:T(8,128)(2,1)S(1)} %get-tuple-element.58), channel_id=1, source_target_pairs={{0,0},{1,4},{2,2},{3,6},{4,1},{5,5},{6,3},{7,7},{8,9},{9,13},{10,1... | collective-permute-start | bytes 294920 | tf_op jit(solution)/shard_map/ppermute | solution.py:241
  22.7 1.1 collective-permute-start.11
  23.8 2.3 %collective-permute-start.4 = (bf16[160,384]{1,0:T(8,128)(2,1)S(1)}, bf16[160,384]{1,0:T(8,128)(2,1)S(1)}, u32[]{:S(2)}, u32[]{:S(2)}) collective-permute-start(bf16[160,384]{1,0:T(8,128)(2,1)S(1)} %get-tuple-element.32), channel_id=1, source_target_pairs={{0,16},{1,17},{2,18},{3,19},{4,20},{5,21},{6,22},{7,23},{8,24},{9,... | collective-permute-start | bytes 368648 | tf_op jit(solution)/shard_map/ppermute | solution.py:241
  26.0 1.2 collective-permute-start.5
  27.3 2.0 %collective-permute-done.11.blocks_odd = bf16[32,1536]{1,0:T(8,128)(2,1)S(1)} collective-permute-done((bf16[32,1536]{1,0:T(8,128)(2,1)S(1)}, bf16[32,1536]{1,0:T(8,128)(2,1)S(1)}, u32[]{:S(2)}, u32[]{:S(2)}) %collective-permute-start.11) | collective-permute-done | bytes 98336 | tf_op jit(solution)/shard_map/ppermute | solution.py:241
  29.4 1.9 %collective-permute-start.12 = (bf16[48,1536]{1,0:T(8,128)(2,1)S(1)}, bf16[48,1536]{1,0:T(8,128)(2,1)S(1)}, u32[]{:S(2)}, u32[]{:S(2)}) collective-permute-start(bf16[48,1536]{1,0:T(8,128)(2,1)S(1)} %pad_maximum_fusion.2), channel_id=1, source_target_pairs={{1,9},{3,11},{5,13},{7,15},{8,16},{9,1},{10,18},{11,3},{12,20},{13... | collective-permute-start | bytes 442376 | tf_op jit(solution)/shard_map/ppermute | solution.py:241
  31.9 7.3 %collective-permute-done.5 = bf16[160,384]{1,0:T(8,128)(2,1)S(1)} collective-permute-done((bf16[160,384]{1,0:T(8,128)(2,1)S(1)}, bf16[160,384]{1,0:T(8,128)(2,1)S(1)}, u32[]{:S(2)}, u32[]{:S(2)}) %collective-permute-start.5) | collective-permute-done | bytes 122912 | tf_op jit(solution)/shard_map/ppermute | solution.py:241
  40.0 1.3 collective-permute-start.25
  41.9 2.6 %collective-permute-start.17 = (bf16[3,192,384]{2,1,0:T(8,128)(2,1)S(1)}, bf16[3,192,384]{2,1,0:T(8,128)(2,1)S(1)}, u32[]{:S(2)}, u32[]{:S(2)}) collective-permute-start(bf16[3,192,384]{2,1,0:T(8,128)(2,1)S(1)} %pad_maximum_fusion.refs_2_), channel_id=1, source_target_pairs={{0,4},{1,5},{2,6},{3,7},{4,0},{5,1},{6,2},{7,3},{8,12},{9,13},{10,... | collective-permute-start | bytes 1327112 | tf_op jit(solution)/shard_map/ppermute | solution.py:241
  44.6 2.6 %collective-permute-done.25 = bf16[32,1536]{1,0:T(8,128)(2,1)S(1)} collective-permute-done((bf16[32,1536]{1,0:T(8,128)(2,1)S(1)}, bf16[32,1536]{1,0:T(8,128)(2,1)S(1)}, u32[]{:S(2)}, u32[]{:S(2)}) %collective-permute-start.25) | collective-permute-done | bytes 98336 | tf_op jit(solution)/shard_map/ppermute | solution.py:241
  47.3 6.4 %collective-permute-done.16.refs_3_ = bf16[3,192,384]{2,1,0:T(8,128)(2,1)S(1)} collective-permute-done((bf16[3,192,384]{2,1,0:T(8,128)(2,1)S(1)}, bf16[3,192,384]{2,1,0:T(8,128)(2,1)S(1)}, u32[]{:S(2)}, u32[]{:S(2)}) %collective-permute-start.16) | collective-permute-done | bytes 442400 | tf_op jit(solution)/shard_map/ppermute | solution.py:241
  54.5 2.2 %collective-permute-done.17.refs_4_ = bf16[3,192,384]{2,1,0:T(8,128)(2,1)S(1)} collective-permute-done((bf16[3,192,384]{2,1,0:T(8,128)(2,1)S(1)}, bf16[3,192,384]{2,1,0:T(8,128)(2,1)S(1)}, u32[]{:S(2)}, u32[]{:S(2)}) %collective-permute-start.17) | collective-permute-done | bytes 442400 | tf_op jit(solution)/shard_map/ppermute | solution.py:241
  56.7 7.0 %collective-permute-done.26.cot_beside = bf16[32,1536]{1,0:T(8,128)(2,1)S(1)} collective-permute-done((bf16[32,1536]{1,0:T(8,128)(2,1)S(1)}, bf16[32,1536]{1,0:T(8,128)(2,1)S(1)}, u32[]{:S(2)}, u32[]{:S(2)}) %collective-permute-start.26) | collective-permute-done | bytes 98336 | tf_op jit(solution)/shard_map/ppermute | solution.py:241
  63.8 0.9 collective-permute-start.18
  65.2 0.9 slice.44
  66.2 1.3 collective-permute-start.7
  68.0 4.0 %collective-permute-done.18.refs_5_ = bf16[3,96,384]{2,1,0:T(8,128)(2,1)S(1)} collective-permute-done((bf16[3,96,384]{2,1,0:T(8,128)(2,1)S(1)}, bf16[3,96,384]{2,1,0:T(8,128)(2,1)S(1)}, u32[]{:S(2)}, u32[]{:S(2)}) %collective-permute-start.18) | collective-permute-done | bytes 221216 | tf_op jit(solution)/shard_map/ppermute | solution.py:241
  72.5 0.9 slice.45
  73.5 2.1 %collective-permute-done.7.refs_5_ = bf16[3,80,384]{2,1,0:T(8,128)(2,1)} collective-permute-done((bf16[3,80,384]{2,1,0:T(8,128)(2,1)S(1)}, bf16[3,80,384]{2,1,0:T(8,128)(2,1)}, u32[]{:S(2)}, u32[]{:S(2)}) %collective-permute-start.7) | collective-permute-done | bytes 184352 | tf_op jit(solution)/shard_map/ppermute | solution.py:241
  76.3 5.6 %collective-permute-done.9.refs_6_ = bf16[3,80,384]{2,1,0:T(8,128)(2,1)} collective-permute-done((bf16[3,80,384]{2,1,0:T(8,128)(2,1)S(1)}, bf16[3,80,384]{2,1,0:T(8,128)(2,1)}, u32[]{:S(2)}, u32[]{:S(2)}) %collective-permute-start.9) | collective-permute-done | bytes 184352 | tf_op jit(solution)/shard_map/ppermute | solution.py:241
  83.1 1.2 copy-done.1
  84.2 1.0 copy-done.5
  85.2 1.0 copy-done.7
  88.0 0.9 copy-done.27
  90.7 5.1 %shard_map.101 = (bf16[192,1536]{1,0:T(8,128)(2,1)S(1)}, f32[128,1536]{1,0:T(8,128)S(1)}, f32[128,1]{1,0:T(8,128)S(1)}, f32[128,384]{1,0:T(8,128)S(1)}, bf16[3,1...) custom-call(bf16[32,1536]{1,0:T(8,128)(2,1)S(1)} %copy-done.13, bf16[32,1536]{1,0:T(8,128)(2,1)S(1)} %copy-done.16, ...), custom_call_target="tpu_custom_call" | custom-call | tf_op jit(solution)/shard_map/pallas_call | solution.py:621
  95.8 1.0 copy-done.10
  102.3 0.9 collective-permute-done.33.refs_11_
  103.3 1.1 copy-done.3
  104.4 1.0 copy-done.9
  105.3 1.1 copy-done.21
  110.6 7.0 %shard_map.102 = (f32[128,256]{1,0:T(8,128)S(1)}, f32[128,640]{1,0:T(8,128)S(1)}, bf16[32,640]{1,0:T(8,128)(2,1)S(1)}, bf16[1536,896]{1,0:T(8,128)(2,1)S(1)}, bf16[128,1536]{1,0:T(8,128)(2,1)S(1)}) custom-call(s32[4]{0:T(128)S(1)} %copy-done.40, s32[16,2]{1,0:T(8,128)S(1)} %copy.11.pairs, bf16[192,1536]{1,0:T(8,128)(2,1)S(1)} %copy-done.21, ...), custom_call_target="tpu_custom_call" | custom-call | tf_op jit(solution)/shard_map/pallas_call | solution.py:638
  117.6 2.0 %collective-permute-start.34 = (bf16[32,640]{1,0:T(8,128)(2,1)S(1)}, bf16[32,640]{1,0:T(8,128)(2,1)S(1)}, u32[]{:S(2)}, u32[]{:S(2)}) collective-permute-start(bf16[32,640]{1,0:T(8,128)(2,1)S(1)} %get-tuple-element.42), channel_id=1, source_target_pairs={{1,9},{3,11},{5,13},{7,15},{8,16},{9,1},{10,18},{11,3},{12,20},{13... | collective-permute-start | bytes 122888 | tf_op jit(solution)/shard_map/ppermute | solution.py:241
  119.6 3.9 %collective-permute-done.34.received = bf16[32,640]{1,0:T(8,128)(2,1)S(1)} collective-permute-done((bf16[32,640]{1,0:T(8,128)(2,1)S(1)}, bf16[32,640]{1,0:T(8,128)(2,1)S(1)}, u32[]{:S(2)}, u32[]{:S(2)}) %collective-permute-start.34) | collective-permute-done | bytes 40992 | tf_op jit(solution)/shard_map/ppermute | solution.py:241
  123.6 3.1 %shard_map.103 = (bf16[128,384]{1,0:T(8,128)(2,1)S(1)}, f32[64,1536]{1,0:T(8,128)S(1)}, bf16[16,384]{1,0:T(8,128)(2,1)S(1)}) custom-call(f32[128,256]{1,0:T(8,128)S(1)} %get-tuple-element.40.d_q, f32[128,640]{1,0:T(8,128)S(1)} %get-tuple-element.41.d_kv, bf16[32,640]{1,0:T(8,128)(2,1)S(1)} %collective-permute-done.34.received, f32[128,1536]{1,0:T(8,128)S(1)} %copy-done.19, ...), custom_call_target="tpu_custom_call" | custom-call | tf_op jit(solution)/shard_map/pallas_call | solution.py:654
  126.7 2.0 %collective-permute-start.35 = (bf16[16,384]{1,0:T(8,128)(2,1)S(1)}, bf16[16,384]{1,0:T(8,128)(2,1)S(1)}, u32[]{:S(2)}, u32[]{:S(2)}) collective-permute-start(bf16[16,384]{1,0:T(8,128)(2,1)S(1)} %get-tuple-element.50), channel_id=1, source_target_pairs={{1,9},{3,11},{5,13},{7,15},{8,16},{9,1},{10,18},{11,3},{12,20},{13... | collective-permute-start | bytes 36872 | tf_op jit(solution)/shard_map/ppermute | solution.py:241
  128.7 3.6 %collective-permute-done.35.received = bf16[16,384]{1,0:T(8,128)(2,1)S(1)} collective-permute-done((bf16[16,384]{1,0:T(8,128)(2,1)S(1)}, bf16[16,384]{1,0:T(8,128)(2,1)S(1)}, u32[]{:S(2)}, u32[]{:S(2)}) %collective-permute-start.35) | collective-permute-done | bytes 12320 | tf_op jit(solution)/shard_map/ppermute | solution.py:241
  132.3 1.8 %shard_map.104 = (f32[32,1536]{1,0:T(8,128)S(1)}, bf16[32,1536]{1,0:T(8,128)(2,1)S(1)}) custom-call(bf16[128,384]{1,0:T(8,128)(2,1)S(1)} %get-tuple-element.49.d_hidden, bf16[16,384]{1,0:T(8,128)(2,1)S(1)} %collective-permute-done.35.received, f32[64,1536]{1,0:T(8,128)S(1)} %get-tuple-element.51.d_resid, bf16[32,1536]{1,0:T(8,128)(2,1)S(1)} %copy-done.14, ...), custom_call_target="tpu_custom_call" | custom-call | tf_op jit(solution)/shard_map/pallas_call | solution.py:666
  134.9 3.9 %collective-permute-done.36 = bf16[32,1536]{1,0:T(8,128)(2,1)S(1)} collective-permute-done((bf16[32,1536]{1,0:T(8,128)(2,1)S(1)}, bf16[32,1536]{1,0:T(8,128)(2,1)S(1)}, u32[]{:S(2)}, u32[]{:S(2)}) %collective-permute-start.36) | collective-permute-done | bytes 98336 | tf_op jit(solution)/shard_map/ppermute | solution.py:241
  138.9 1.9 %collective-permute-start.38 = (bf16[32,1536]{1,0:T(8,128)(2,1)S(1)}, bf16[32,1536]{1,0:T(8,128)(2,1)S(1)}, u32[]{:S(2)}, u32[]{:S(2)}) collective-permute-start(bf16[32,1536]{1,0:T(8,128)(2,1)S(1)} %add_convert_fusion.1), channel_id=1, source_target_pairs={{1,4},{3,6},{4,1},{6,3},{8,13},{10,15},{13,8},{15,10},{17,20},{19,... | collective-permute-start | bytes 294920 | tf_op jit(solution)/shard_map/ppermute | solution.py:241
  141.1 3.7 %collective-permute-done.38 = bf16[32,1536]{1,0:T(8,128)(2,1)S(1)} collective-permute-done((bf16[32,1536]{1,0:T(8,128)(2,1)S(1)}, bf16[32,1536]{1,0:T(8,128)(2,1)S(1)}, u32[]{:S(2)}, u32[]{:S(2)}) %collective-permute-start.38) | collective-permute-done | bytes 98336 | tf_op jit(solution)/shard_map/ppermute | solution.py:241
  (142 shorter events, 22.4 us)
Async XLA Ops:
  4.2 35.8 %copy-start.43 = (bf16[32,1536]{1,0:T(8,128)(2,1)S(1)}, bf16[32,1536]{1,0:T(8,128)(2,1)}, u32[]{:S(2)}) copy-start(bf16[32,1536]{1,0:T(8,128)(2,1)} %param.12) | copy-start | bytes 294916
  4.2 6.5 %collective-permute-start = (bf16[192,384]{1,0:T(8,128)(2,1)S(1)}, bf16[192,384]{1,0:T(8,128)(2,1)S(1)}, u32[]{:S(2)}, u32[]{:S(2)}) collective-permute-start(bf16[192,384]{1,0:T(8,128)(2,1)S(1)} %get-tuple-element.31), channel_id=1, source_target_pairs={{0,8},{1,9},{2,10},{3,11},{4,12},{5,13},{6,14},{7,15},{8,0},{9,1},... | collective-permute-start | bytes 442376 | tf_op jit(solution)/shard_map/ppermute | solution.py:241
  4.3 13.4 %collective-permute-start.1 = (bf16[192,384]{1,0:T(8,128)(2,1)S(1)}, bf16[192,384]{1,0:T(8,128)(2,1)S(1)}, u32[]{:S(2)}, u32[]{:S(2)}) collective-permute-start(bf16[192,384]{1,0:T(8,128)(2,1)S(1)} %get-tuple-element.31), channel_id=1, source_target_pairs={{0,16},{1,17},{2,18},{3,19},{4,20},{5,21},{6,22},{7,23},{8,24},{9,... | collective-permute-start | bytes 442376 | tf_op jit(solution)/shard_map/ppermute | solution.py:241
  7.3 13.3 %collective-permute-start.2 = (bf16[192,384]{1,0:T(8,128)(2,1)S(1)}, bf16[192,384]{1,0:T(8,128)(2,1)S(1)}, u32[]{:S(2)}, u32[]{:S(2)}) collective-permute-start(bf16[192,384]{1,0:T(8,128)(2,1)S(1)} %get-tuple-element.31), channel_id=1, source_target_pairs={{0,24},{1,25},{2,26},{3,27},{4,28},{5,29},{6,30},{7,31},{8,16},{9,... | collective-permute-start | bytes 442376 | tf_op jit(solution)/shard_map/ppermute | solution.py:241
  20.6 62.4 %copy-start.44 = (f32[1536]{0:T(1024)S(1)}, f32[1536]{0:T(1024)}, u32[]{:S(2)}) copy-start(f32[1536]{0:T(1024)} %param.15) | copy-start | bytes 18436
  20.7 62.3 %copy-start.4 = (bf16[3,192,384]{2,1,0:T(8,128)(2,1)}, bf16[3,192,384]{2,1,0:T(8,128)(2,1)S(1)}, u32[]{:S(2)}) copy-start(bf16[3,192,384]{2,1,0:T(8,128)(2,1)S(1)} %pad_maximum_fusion.refs_2_) | copy-start | bytes 1327108
  20.8 6.5 %collective-permute-start.10 = (bf16[32,1536]{1,0:T(8,128)(2,1)S(1)}, bf16[32,1536]{1,0:T(8,128)(2,1)S(1)}, u32[]{:S(2)}, u32[]{:S(2)}) collective-permute-start(bf16[32,1536]{1,0:T(8,128)(2,1)S(1)} %get-tuple-element.58), channel_id=1, source_target_pairs={{0,0},{1,4},{2,2},{3,6},{4,1},{5,5},{6,3},{7,7},{8,9},{9,13},{10,1... | collective-permute-start | bytes 294920 | tf_op jit(solution)/shard_map/ppermute | solution.py:241
  22.7 6.6 %collective-permute-start.11 = (bf16[32,1536]{1,0:T(8,128)(2,1)S(1)}, bf16[32,1536]{1,0:T(8,128)(2,1)S(1)}, u32[]{:S(2)}, u32[]{:S(2)}) collective-permute-start(bf16[32,1536]{1,0:T(8,128)(2,1)S(1)} %get-tuple-element.57), channel_id=1, source_target_pairs={{0,2},{1,6},{2,0},{3,4},{4,3},{5,7},{6,1},{7,5},{8,11},{9,15},{10,... | collective-permute-start | bytes 294920 | tf_op jit(solution)/shard_map/ppermute | solution.py:241
  23.8 7.6 %collective-permute-start.3 = (bf16[160,384]{1,0:T(8,128)(2,1)S(1)}, bf16[160,384]{1,0:T(8,128)(2,1)S(1)}, u32[]{:S(2)}, u32[]{:S(2)}) collective-permute-start(bf16[160,384]{1,0:T(8,128)(2,1)S(1)} %get-tuple-element.32), channel_id=1, source_target_pairs={{0,8},{1,9},{2,10},{3,11},{4,12},{5,13},{6,14},{7,15},{8,0},{9,1},... | collective-permute-start | bytes 368648 | tf_op jit(solution)/shard_map/ppermute | solution.py:241
  23.8 8.1 %collective-permute-start.4 = (bf16[160,384]{1,0:T(8,128)(2,1)S(1)}, bf16[160,384]{1,0:T(8,128)(2,1)S(1)}, u32[]{:S(2)}, u32[]{:S(2)}) collective-permute-start(bf16[160,384]{1,0:T(8,128)(2,1)S(1)} %get-tuple-element.32), channel_id=1, source_target_pairs={{0,16},{1,17},{2,18},{3,19},{4,20},{5,21},{6,22},{7,23},{8,24},{9,... | collective-permute-start | bytes 368648 | tf_op jit(solution)/shard_map/ppermute | solution.py:241
  26.0 13.1 %collective-permute-start.5 = (bf16[160,384]{1,0:T(8,128)(2,1)S(1)}, bf16[160,384]{1,0:T(8,128)(2,1)S(1)}, u32[]{:S(2)}, u32[]{:S(2)}) collective-permute-start(bf16[160,384]{1,0:T(8,128)(2,1)S(1)} %get-tuple-element.32), channel_id=1, source_target_pairs={{0,24},{1,25},{2,26},{3,27},{4,28},{5,29},{6,30},{7,31},{8,16},{9,... | collective-permute-start | bytes 368648 | tf_op jit(solution)/shard_map/ppermute | solution.py:241
  27.3 55.7 %copy-start.12 = (bf16[32,1536]{1,0:T(8,128)(2,1)}, bf16[32,1536]{1,0:T(8,128)(2,1)S(1)}, u32[]{:S(2)}) copy-start(bf16[32,1536]{1,0:T(8,128)(2,1)S(1)} %collective-permute-done.10.blocks_even) | copy-start | bytes 294916
  29.3 53.7 %copy-start.15 = (bf16[32,1536]{1,0:T(8,128)(2,1)}, bf16[32,1536]{1,0:T(8,128)(2,1)S(1)}, u32[]{:S(2)}) copy-start(bf16[32,1536]{1,0:T(8,128)(2,1)S(1)} %collective-permute-done.11.blocks_odd) | copy-start | bytes 294916
  29.4 17.8 %collective-permute-start.12 = (bf16[48,1536]{1,0:T(8,128)(2,1)S(1)}, bf16[48,1536]{1,0:T(8,128)(2,1)S(1)}, u32[]{:S(2)}, u32[]{:S(2)}) collective-permute-start(bf16[48,1536]{1,0:T(8,128)(2,1)S(1)} %pad_maximum_fusion.2), channel_id=1, source_target_pairs={{1,9},{3,11},{5,13},{7,15},{8,16},{9,1},{10,18},{11,3},{12,20},{13... | collective-permute-start | bytes 442376 | tf_op jit(solution)/shard_map/ppermute | solution.py:241
  31.3 10.6 %collective-permute-start.13 = (bf16[32,1536]{1,0:T(8,128)(2,1)S(1)}, bf16[32,1536]{1,0:T(8,128)(2,1)S(1)}, u32[]{:S(2)}, u32[]{:S(2)}) collective-permute-start(bf16[32,1536]{1,0:T(8,128)(2,1)S(1)} %collective-permute-done.10.blocks_even), channel_id=1, source_target_pairs={{0,1},{1,0},{2,3},{3,2},{4,5},{5,4},{6,7},{7,6},{8,9},{9,8},{10,11... | collective-permute-start | bytes 294920 | tf_op jit(solution)/shard_map/ppermute | solution.py:241
  31.4 13.2 %collective-permute-start.14 = (bf16[32,1536]{1,0:T(8,128)(2,1)S(1)}, bf16[32,1536]{1,0:T(8,128)(2,1)S(1)}, u32[]{:S(2)}, u32[]{:S(2)}) collective-permute-start(bf16[32,1536]{1,0:T(8,128)(2,1)S(1)} %collective-permute-done.11.blocks_odd), channel_id=1, source_target_pairs={{0,1},{1,0},{2,3},{3,2},{4,5},{5,4},{6,7},{7,6},{8,9},{9,8},{10,11... | collective-permute-start | bytes 294920 | tf_op jit(solution)/shard_map/ppermute | solution.py:241
  40.0 7.2 %collective-permute-start.25 = (bf16[32,1536]{1,0:T(8,128)(2,1)S(1)}, bf16[32,1536]{1,0:T(8,128)(2,1)S(1)}, u32[]{:S(2)}, u32[]{:S(2)}) collective-permute-start(bf16[32,1536]{1,0:T(8,128)(2,1)S(1)} %copy-done.43), channel_id=1, source_target_pairs={{0,4},{2,6},{5,1},{7,3},{9,13},{11,15},{12,8},{14,10},{16,20},{18,... | collective-permute-start | bytes 294920 | tf_op jit(solution)/shard_map/ppermute | solution.py:241
  41.3 12.5 %collective-permute-start.16 = (bf16[3,192,384]{2,1,0:T(8,128)(2,1)S(1)}, bf16[3,192,384]{2,1,0:T(8,128)(2,1)S(1)}, u32[]{:S(2)}, u32[]{:S(2)}) collective-permute-start(bf16[3,192,384]{2,1,0:T(8,128)(2,1)S(1)} %pad_maximum_fusion.refs_2_), channel_id=1, source_target_pairs={{0,2},{1,3},{2,0},{3,1},{4,6},{5,7},{6,4},{7,5},{8,10},{9,11},{10,... | collective-permute-start | bytes 1327112 | tf_op jit(solution)/shard_map/ppermute | solution.py:241
  41.9 41.1 %copy-start.28 = (bf16[32,1536]{1,0:T(8,128)(2,1)}, bf16[32,1536]{1,0:T(8,128)(2,1)S(1)}, u32[]{:S(2)}) copy-start(bf16[32,1536]{1,0:T(8,128)(2,1)S(1)} %collective-permute-done.13.other_even) | copy-start | bytes 294916
  41.9 14.7 %collective-permute-start.17 = (bf16[3,192,384]{2,1,0:T(8,128)(2,1)S(1)}, bf16[3,192,384]{2,1,0:T(8,128)(2,1)S(1)}, u32[]{:S(2)}, u32[]{:S(2)}) collective-permute-start(bf16[3,192,384]{2,1,0:T(8,128)(2,1)S(1)} %pad_maximum_fusion.refs_2_), channel_id=1, source_target_pairs={{0,4},{1,5},{2,6},{3,7},{4,0},{5,1},{6,2},{7,3},{8,12},{9,13},{10,... | collective-permute-start | bytes 1327112 | tf_op jit(solution)/shard_map/ppermute | solution.py:241
  44.6 38.4 %copy-start.30 = (bf16[32,1536]{1,0:T(8,128)(2,1)}, bf16[32,1536]{1,0:T(8,128)(2,1)S(1)}, u32[]{:S(2)}) copy-start(bf16[32,1536]{1,0:T(8,128)(2,1)S(1)} %collective-permute-done.14.other_odd) | copy-start | bytes 294916
  44.6 22.9 %collective-permute-start.20 = (bf16[3,192,384]{2,1,0:T(8,128)(2,1)S(1)}, bf16[3,192,384]{2,1,0:T(8,128)(2,1)S(1)}, u32[]{:S(2)}, u32[]{:S(2)}) collective-permute-start(bf16[3,192,384]{2,1,0:T(8,128)(2,1)S(1)} %pad_maximum_fusion.refs_2_), channel_id=1, source_target_pairs={{0,1},{1,0},{2,3},{3,2},{4,5},{5,4},{6,7},{7,6},{8,9},{9,8},{10,11... | collective-permute-start | bytes 1327112 | tf_op jit(solution)/shard_map/ppermute | solution.py:241
  47.2 17.5 %collective-permute-start.6 = (bf16[3,160,384]{2,1,0:T(8,128)(2,1)}, bf16[3,160,384]{2,1,0:T(8,128)(2,1)}, u32[]{:S(2)}, u32[]{:S(2)}) collective-permute-start(bf16[3,160,384]{2,1,0:T(8,128)(2,1)} %pad_maximum_fusion.1.refs_2_), channel_id=1, source_target_pairs={{0,2},{1,3},{2,0},{3,1},{4,6},{5,7},{6,4},{7,5},{8,10},{9,11},{10,... | collective-permute-start | bytes 1105928 | tf_op jit(solution)/shard_map/ppermute | solution.py:241
  47.2 35.8 %copy-start.26 = (bf16[48,1536]{1,0:T(8,128)(2,1)}, bf16[48,1536]{1,0:T(8,128)(2,1)S(1)}, u32[]{:S(2)}) copy-start(bf16[48,1536]{1,0:T(8,128)(2,1)S(1)} %collective-permute-done.12.edge) | copy-start | bytes 442372
  47.2 20.3 %collective-permute-start.8 = (bf16[3,160,384]{2,1,0:T(8,128)(2,1)}, bf16[3,160,384]{2,1,0:T(8,128)(2,1)}, u32[]{:S(2)}, u32[]{:S(2)}) collective-permute-start(bf16[3,160,384]{2,1,0:T(8,128)(2,1)} %pad_maximum_fusion.1.refs_2_), channel_id=1, source_target_pairs={{0,4},{1,5},{2,6},{3,7},{4,0},{5,1},{6,2},{7,3},{8,12},{9,13},{10,... | collective-permute-start | bytes 1105928 | tf_op jit(solution)/shard_map/ppermute | solution.py:241
  47.3 48.5 %copy-start.22 = (bf16[32,1536]{1,0:T(8,128)(2,1)}, bf16[32,1536]{1,0:T(8,128)(2,1)S(1)}, u32[]{:S(2)}) copy-start(bf16[32,1536]{1,0:T(8,128)(2,1)S(1)} %broadcast_select_fusion.cot_block) | copy-start | bytes 294916
  53.8 10.0 %collective-permute-start.26 = (bf16[32,1536]{1,0:T(8,128)(2,1)S(1)}, bf16[32,1536]{1,0:T(8,128)(2,1)S(1)}, u32[]{:S(2)}, u32[]{:S(2)}) collective-permute-start(bf16[32,1536]{1,0:T(8,128)(2,1)S(1)} %broadcast_select_fusion.cot_block), channel_id=1, source_target_pairs={{0,2},{1,3},{2,0},{3,1},{4,6},{5,7},{6,4},{7,5},{8,10},{9,11},{10,... | collective-permute-start | bytes 294920 | tf_op jit(solution)/shard_map/ppermute | solution.py:241
  56.7 9.5 %collective-permute-start.15 = (bf16[48,1536]{1,0:T(8,128)(2,1)S(1)}, bf16[48,1536]{1,0:T(8,128)(2,1)S(1)}, u32[]{:S(2)}, u32[]{:S(2)}) collective-permute-start(bf16[48,1536]{1,0:T(8,128)(2,1)S(1)} %collective-permute-done.12.edge), channel_id=1, source_target_pairs={{0,1},{1,0},{2,3},{3,2},{4,5},{5,4},{6,7},{7,6},{8,9},{9,8},{10,11... | collective-permute-start | bytes 442376 | tf_op jit(solution)/shard_map/ppermute | solution.py:241
  63.8 8.2 %collective-permute-start.18 = (bf16[3,96,384]{2,1,0:T(8,128)(2,1)S(1)}, bf16[3,96,384]{2,1,0:T(8,128)(2,1)S(1)}, u32[]{:S(2)}, u32[]{:S(2)}) collective-permute-start(bf16[3,96,384]{2,1,0:T(8,128)(2,1)S(1)} %slice.52), channel_id=1, source_target_pairs={{0,4},{1,5},{2,6},{3,7},{4,0},{5,1},{6,2},{7,3},{8,12},{9,13},{10,... | collective-permute-start | bytes 663560 | tf_op jit(solution)/shard_map/ppermute | solution.py:241
  64.7 7.3 %collective-permute-start.19 = (bf16[3,96,384]{2,1,0:T(8,128)(2,1)S(1)}, bf16[3,96,384]{2,1,0:T(8,128)(2,1)S(1)}, u32[]{:S(2)}, u32[]{:S(2)}) collective-permute-start(bf16[3,96,384]{2,1,0:T(8,128)(2,1)S(1)} %slice.53), channel_id=1, source_target_pairs={{0,2},{1,3},{2,0},{3,1},{4,6},{5,7},{6,4},{7,5},{8,10},{9,11},{10,... | collective-permute-start | bytes 663560 | tf_op jit(solution)/shard_map/ppermute | solution.py:241
  66.2 9.4 %collective-permute-start.7 = (bf16[3,80,384]{2,1,0:T(8,128)(2,1)S(1)}, bf16[3,80,384]{2,1,0:T(8,128)(2,1)}, u32[]{:S(2)}, u32[]{:S(2)}) collective-permute-start(bf16[3,80,384]{2,1,0:T(8,128)(2,1)S(1)} %slice.44), channel_id=1, source_target_pairs={{0,4},{1,5},{2,6},{3,7},{4,0},{5,1},{6,2},{7,3},{8,12},{9,13},{10,... | collective-permute-start | bytes 552968 | tf_op jit(solution)/shard_map/ppermute | solution.py:241
  67.5 15.0 %collective-permute-start.21 = (bf16[3,192,384]{2,1,0:T(8,128)(2,1)S(1)}, bf16[3,192,384]{2,1,0:T(8,128)(2,1)S(1)}, u32[]{:S(2)}, u32[]{:S(2)}) collective-permute-start(bf16[3,192,384]{2,1,0:T(8,128)(2,1)S(1)} %collective-permute-done.16.refs_3_), channel_id=1, source_target_pairs={{0,1},{1,0},{2,3},{3,2},{4,5},{5,4},{6,7},{7,6},{8,9},{9,8},{10,11... | collective-permute-start | bytes 1327112 | tf_op jit(solution)/shard_map/ppermute | solution.py:241
  67.5 15.4 %collective-permute-start.22 = (bf16[3,192,384]{2,1,0:T(8,128)(2,1)S(1)}, bf16[3,192,384]{2,1,0:T(8,128)(2,1)S(1)}, u32[]{:S(2)}, u32[]{:S(2)}) collective-permute-start(bf16[3,192,384]{2,1,0:T(8,128)(2,1)S(1)} %collective-permute-done.17.refs_4_), channel_id=1, source_target_pairs={{0,1},{1,0},{2,3},{3,2},{4,5},{5,4},{6,7},{7,6},{8,9},{9,8},{10,11... | collective-permute-start | bytes 1327112 | tf_op jit(solution)/shard_map/ppermute | solution.py:241
  72.0 9.9 %collective-permute-start.23 = (bf16[3,96,384]{2,1,0:T(8,128)(2,1)S(1)}, bf16[3,96,384]{2,1,0:T(8,128)(2,1)S(1)}, u32[]{:S(2)}, u32[]{:S(2)}) collective-permute-start(bf16[3,96,384]{2,1,0:T(8,128)(2,1)S(1)} %collective-permute-done.18.refs_5_), channel_id=1, source_target_pairs={{0,1},{1,0},{2,3},{3,2},{4,5},{5,4},{6,7},{7,6},{8,9},{9,8},{10,11... | collective-permute-start | bytes 663560 | tf_op jit(solution)/shard_map/ppermute | solution.py:241
  72.0 10.4 %collective-permute-start.24 = (bf16[3,96,384]{2,1,0:T(8,128)(2,1)S(1)}, bf16[3,96,384]{2,1,0:T(8,128)(2,1)S(1)}, u32[]{:S(2)}, u32[]{:S(2)}) collective-permute-start(bf16[3,96,384]{2,1,0:T(8,128)(2,1)S(1)} %collective-permute-done.19.refs_6_), channel_id=1, source_target_pairs={{0,1},{1,0},{2,3},{3,2},{4,5},{5,4},{6,7},{7,6},{8,9},{9,8},{10,11... | collective-permute-start | bytes 663560 | tf_op jit(solution)/shard_map/ppermute | solution.py:241
  75.6 6.3 %collective-permute-start.9 = (bf16[3,80,384]{2,1,0:T(8,128)(2,1)S(1)}, bf16[3,80,384]{2,1,0:T(8,128)(2,1)}, u32[]{:S(2)}, u32[]{:S(2)}) collective-permute-start(bf16[3,80,384]{2,1,0:T(8,128)(2,1)S(1)} %slice.45), channel_id=1, source_target_pairs={{0,2},{1,3},{2,0},{3,1},{4,6},{5,7},{6,4},{7,5},{8,10},{9,11},{10,... | collective-permute-start | bytes 552968 | tf_op jit(solution)/shard_map/ppermute | solution.py:241
  81.9 20.4 %collective-permute-start.29 = (bf16[3,160,384]{2,1,0:T(8,128)(2,1)}, bf16[3,160,384]{2,1,0:T(8,128)(2,1)}, u32[]{:S(2)}, u32[]{:S(2)}) collective-permute-start(bf16[3,160,384]{2,1,0:T(8,128)(2,1)} %pad_maximum_fusion.1.refs_2_), channel_id=1, source_target_pairs={{0,1},{1,0},{2,3},{3,2},{4,5},{5,4},{6,7},{7,6},{8,9},{9,8},{10,11... | collective-permute-start | bytes 1105928 | tf_op jit(solution)/shard_map/ppermute | solution.py:241
  81.9 20.4 %collective-permute-start.30 = (bf16[3,160,384]{2,1,0:T(8,128)(2,1)}, bf16[3,160,384]{2,1,0:T(8,128)(2,1)}, u32[]{:S(2)}, u32[]{:S(2)}) collective-permute-start(bf16[3,160,384]{2,1,0:T(8,128)(2,1)} %collective-permute-done.6.refs_3_), channel_id=1, source_target_pairs={{0,1},{1,0},{2,3},{3,2},{4,5},{5,4},{6,7},{7,6},{8,9},{9,8},{10,11... | collective-permute-start | bytes 1105928 | tf_op jit(solution)/shard_map/ppermute | solution.py:241
  82.4 19.9 %collective-permute-start.31 = (bf16[3,160,384]{2,1,0:T(8,128)(2,1)}, bf16[3,160,384]{2,1,0:T(8,128)(2,1)}, u32[]{:S(2)}, u32[]{:S(2)}) collective-permute-start(bf16[3,160,384]{2,1,0:T(8,128)(2,1)} %collective-permute-done.8.refs_4_), channel_id=1, source_target_pairs={{0,1},{1,0},{2,3},{3,2},{4,5},{5,4},{6,7},{7,6},{8,9},{9,8},{10,11... | collective-permute-start | bytes 1105928 | tf_op jit(solution)/shard_map/ppermute | solution.py:241
  82.5 17.3 %collective-permute-start.27 = (bf16[32,1536]{1,0:T(8,128)(2,1)S(1)}, bf16[32,1536]{1,0:T(8,128)(2,1)S(1)}, u32[]{:S(2)}, u32[]{:S(2)}) collective-permute-start(bf16[32,1536]{1,0:T(8,128)(2,1)S(1)} %broadcast_select_fusion.cot_block), channel_id=1, source_target_pairs={{0,1},{1,0},{2,3},{3,2},{4,5},{5,4},{6,7},{7,6},{8,9},{9,8},{10,11... | collective-permute-start | bytes 294920 | tf_op jit(solution)/shard_map/ppermute | solution.py:241
  82.9 17.9 %collective-permute-start.28 = (bf16[32,1536]{1,0:T(8,128)(2,1)S(1)}, bf16[32,1536]{1,0:T(8,128)(2,1)S(1)}, u32[]{:S(2)}, u32[]{:S(2)}) collective-permute-start(bf16[32,1536]{1,0:T(8,128)(2,1)S(1)} %collective-permute-done.26.cot_beside), channel_id=1, source_target_pairs={{0,1},{1,0},{2,3},{3,2},{4,5},{5,4},{6,7},{7,6},{8,9},{9,8},{10,11... | collective-permute-start | bytes 294920 | tf_op jit(solution)/shard_map/ppermute | solution.py:241
  100.4 1.9 %collective-permute-start.32 = (bf16[3,80,384]{2,1,0:T(8,128)(2,1)}, bf16[3,80,384]{2,1,0:T(8,128)(2,1)}, u32[]{:S(2)}, u32[]{:S(2)}) collective-permute-start(bf16[3,80,384]{2,1,0:T(8,128)(2,1)} %collective-permute-done.7.refs_5_), channel_id=1, source_target_pairs={{0,1},{1,0},{2,3},{3,2},{4,5},{5,4},{6,7},{7,6},{8,9},{9,8},{10,11... | collective-permute-start | bytes 552968 | tf_op jit(solution)/shard_map/ppermute | solution.py:241
  101.5 1.8 %collective-permute-start.33 = (bf16[3,80,384]{2,1,0:T(8,128)(2,1)}, bf16[3,80,384]{2,1,0:T(8,128)(2,1)}, u32[]{:S(2)}, u32[]{:S(2)}) collective-permute-start(bf16[3,80,384]{2,1,0:T(8,128)(2,1)} %collective-permute-done.9.refs_6_), channel_id=1, source_target_pairs={{0,1},{1,0},{2,3},{3,2},{4,5},{5,4},{6,7},{7,6},{8,9},{9,8},{10,11... | collective-permute-start | bytes 552968 | tf_op jit(solution)/shard_map/ppermute | solution.py:241
  117.6 5.9 %collective-permute-start.34 = (bf16[32,640]{1,0:T(8,128)(2,1)S(1)}, bf16[32,640]{1,0:T(8,128)(2,1)S(1)}, u32[]{:S(2)}, u32[]{:S(2)}) collective-permute-start(bf16[32,640]{1,0:T(8,128)(2,1)S(1)} %get-tuple-element.42), channel_id=1, source_target_pairs={{1,9},{3,11},{5,13},{7,15},{8,16},{9,1},{10,18},{11,3},{12,20},{13... | collective-permute-start | bytes 122888 | tf_op jit(solution)/shard_map/ppermute | solution.py:241
  126.7 5.6 %collective-permute-start.35 = (bf16[16,384]{1,0:T(8,128)(2,1)S(1)}, bf16[16,384]{1,0:T(8,128)(2,1)S(1)}, u32[]{:S(2)}, u32[]{:S(2)}) collective-permute-start(bf16[16,384]{1,0:T(8,128)(2,1)S(1)} %get-tuple-element.50), channel_id=1, source_target_pairs={{1,9},{3,11},{5,13},{7,15},{8,16},{9,1},{10,18},{11,3},{12,20},{13... | collective-permute-start | bytes 36872 | tf_op jit(solution)/shard_map/ppermute | solution.py:241
  134.1 4.7 %collective-permute-start.36 = (bf16[32,1536]{1,0:T(8,128)(2,1)S(1)}, bf16[32,1536]{1,0:T(8,128)(2,1)S(1)}, u32[]{:S(2)}, u32[]{:S(2)}) collective-permute-start(bf16[32,1536]{1,0:T(8,128)(2,1)S(1)} %get-tuple-element.54), channel_id=1, source_target_pairs={{0,2},{1,3},{2,0},{3,1},{4,6},{5,7},{6,4},{7,5},{8,10},{9,11},{10,... | collective-permute-start | bytes 294920 | tf_op jit(solution)/shard_map/ppermute | solution.py:241
  138.8 2.3 %collective-permute-start.37 = (bf16[32,1536]{1,0:T(8,128)(2,1)S(1)}, bf16[32,1536]{1,0:T(8,128)(2,1)S(1)}, u32[]{:S(2)}, u32[]{:S(2)}) collective-permute-start(bf16[32,1536]{1,0:T(8,128)(2,1)S(1)} %add_convert_fusion.1), channel_id=1, source_target_pairs={{0,1},{1,5},{2,3},{3,7},{4,0},{5,4},{6,2},{7,6},{8,12},{9,8},{10,1... | collective-permute-start | bytes 294920 | tf_op jit(solution)/shard_map/ppermute | solution.py:241
  138.9 5.9 %collective-permute-start.38 = (bf16[32,1536]{1,0:T(8,128)(2,1)S(1)}, bf16[32,1536]{1,0:T(8,128)(2,1)S(1)}, u32[]{:S(2)}, u32[]{:S(2)}) collective-permute-start(bf16[32,1536]{1,0:T(8,128)(2,1)S(1)} %add_convert_fusion.1), channel_id=1, source_target_pairs={{1,4},{3,6},{4,1},{6,3},{8,13},{10,15},{13,8},{15,10},{17,20},{19,... | collective-permute-start | bytes 294920 | tf_op jit(solution)/shard_map/ppermute | solution.py:241
  (36 other events, 158.6 us)

commit v6 on v5

--- a/solution.py
+++ b/solution.py
@@ -576,31 +576,34 @@
     y_route = routes(n_sa, lambda z, y, x, c: (z, 1 - y, x, c))
     core_route = routes(n_sa, lambda z, y, x, c: (z, y, x, 1 - c))
 
-    def collected(piece, nearest):
-        half = piece.shape[0] // 2
-        straight = jnp.stack([nearest] + [permuted(piece, along_z(step)) for step in range(2, 4)])
-        beside, across = permuted(straight, x_route), permuted(straight, y_route)
-        diagonal_a = permuted(beside[:, :half], y_route)
-        diagonal_b = permuted(across[:, half:], x_route)
-        same = (straight, beside, across, diagonal_a, diagonal_b)
-        return same, tuple(permuted(part, core_route) for part in same[:3])
-
-    nearest = permuted(early, along_z(1))
-    early, early_other = collected(early, nearest)
-    early += early_other + tuple(permuted(part, core_route) for part in early[3:])
-    late, _ = lax.optimization_barrier((late, early[0]))
-    late, late_other = collected(late, permuted(late, along_z(1)))
-    noise, base, _ = lax.optimization_barrier((noise, base, early[0]))
-    cot, _ = lax.optimization_barrier((cot, late[0]))
+    def over_z(piece):
+        return [permuted(piece, along_z(step)) for step in range(1, 4)]
+
+    def diagonals(beside, across):
+        half = beside.shape[1] // 2
+        return permuted(beside[:, :half], y_route), permuted(across[:, half:], x_route)
+
+    def swapped(parts):
+        return tuple(permuted(part, core_route) for part in parts)
+
+    def after(values, *earlier):
+        count = len(values)
+        return lax.optimization_barrier((*values, *earlier))[:count]
 
     def to_sample(shift):
         return routes(n_sa, lambda z, y, x, c: (z, c, (x + shift) % 2, y ^ (z & 1)))
 
     noisy = (base.astype(f32)[None] + noise.astype(f32)).astype(bf16)
     even = x == 0
+    straight, late, noisy, cot = after((jnp.stack(over_z(early)), late, noisy, cot))
+    beside, across = permuted(straight, x_route), permuted(straight, y_route)
+    late_straight = jnp.stack(over_z(late))
     blocks = [
         permuted(jnp.where(x == shift, noisy[0], noisy[1]), to_sample(shift)) for shift in range(2)
     ]
+    across_cot = permuted(
+        cot, routes(n_sa, lambda z, y, x, c: (z, 1 - y, x, c) if y == c ^ (z & 1) else None)
+    )
     edge_route = routes(
         n_sa, lambda z, y, x, c: (z - 1, y, x, c) if c ^ (z & 1) == 0 else (z + 1, y, x, c)
     )
@@ -608,14 +611,23 @@
     outer = jnp.concatenate(
         [jnp.where(m == 0, low[:16], low[16:]), jnp.where(m == 0, low[16:], high[:16]), jnp.where(m == 0, high[:16], high[16:])]
     )
-    mine = (blocks[0], blocks[1], permuted(outer, edge_route))
-    noisy_rows = mine + tuple(permuted(part, core_route) for part in mine)
-    across = permuted(
-        cot, routes(n_sa, lambda z, y, x, c: (z, 1 - y, x, c) if y == c ^ (z & 1) else None)
-    )
-    cot_block = jnp.where(y == m, cot, across)
+    cot_block = jnp.where(y == m, cot, across_cot)
+    straight, beside, across, late_straight, outer, cot_block = after(
+        (straight, beside, across, late_straight, outer, cot_block)
+    )
+    early = (straight, beside, across) + diagonals(beside, across)
+    late_beside, late_across = permuted(late_straight, x_route), permuted(late_straight, y_route)
     cot_rows = (cot_block, permuted(cot_block, x_route))
-    cot_rows = cot_rows + tuple(permuted(part, core_route) for part in cot_rows)
+    mine = (*blocks, permuted(outer, edge_route))
+    early_other = swapped(early[:3])
+    early, early_other, late, cot_rows, mine = (
+        lambda v: (v[:5], v[5:8], v[8:11], v[11:13], v[13:])
+    )(after((*early, *early_other, late_straight, late_beside, late_across, *cot_rows, *mine)))
+    late = tuple(late) + diagonals(late[1], late[2])
+    early = tuple(early) + tuple(early_other) + swapped(early[3:])
+    cot_rows = tuple(cot_rows) + swapped(cot_rows)
+    late_other = swapped(late[:3])
+    noisy_rows = tuple(mine) + swapped(mine)
     gain = norm_gain.reshape(1, features)
 
     normed, resid, inv_rms, hidden, conv, mix = pl.pallas_call(
@@ -631,10 +643,9 @@
             pltpu.VMEM((224, features), f32), pltpu.VMEM((224, features), bf16),
             pltpu.SemaphoreType.DMA((2,)),
         ],
-        compiler_params=limit(28),
+        compiler_params=limit(18),
     )(*noisy_rows, convolution_weight, mix_w, *early, gain)
-    *diagonals, normed = lax.optimization_barrier((*late[3:], normed))
-    late += late_other + tuple(permuted(part, core_route) for part in diagonals)
+    late += late_other + swapped(late[3:])
     d_q, d_kv, send, qkv, cot_all = pl.pallas_call(
         attention_kernel,
         out_shape=(
@@ -647,7 +658,7 @@
             pltpu.VMEM((features, 896), bf16), pltpu.VMEM((HEADS * VAL, features), bf16),
             pltpu.SemaphoreType.DMA((1,)),
         ],
-        compiler_params=limit(24),
+        compiler_params=limit(14),
     )(band_width, pairs, normed, *cot_rows, qkv_w, out_w, *late)
 
     received = permuted(send, edge_route)
@@ -659,7 +670,7 @@
         scratch_shapes=[
             pltpu.VMEM((128, 640), f32), pltpu.VMEM((128, features), f32), pltpu.VMEM((128, features), f32),
         ],
-        compiler_params=limit(16),
+        compiler_params=limit(12),
     )(d_q, d_kv, received, resid, inv_rms, hidden, cot_all, gain, mix, qkv)
 
     received = permuted(send, edge_route)
@@ -671,7 +682,7 @@
         scratch_shapes=[
             pltpu.VMEM((96, HID), bf16), pltpu.VMEM((64, features), f32), pltpu.VMEM((64, features), f32),
         ],
-        compiler_params=limit(16),
+        compiler_params=limit(6),
     )(d_hidden, received, d_resid, *blocks, conv)
 
     received = permuted(send, x_route)

time: 147 us -> 140 us (0.952)
  waiting for transfers between devices: 68.5 us -> 51.8 us
  starting transfers between devices: 30.8 us -> 37 us
  other arithmetic: 1.73 us -> 3.81 us
  Pallas kernels: 17 us -> 18.6 us
    ppermute x39, waiting for transfers between devices: 68.5 us -> 51.8 us  [permuted(): return lax.ppermute(value, ('sa', 'sb', 'noise'), pairs)]
    ppermute x39, starting transfers between devices: 30.8 us -> 37 us  [permuted(): return lax.ppermute(value, ('sa', 'sb', 'noise'), pairs)]
    convert_element_type x2, other arithmetic: 0.06 us -> 1.97 us  [stretch_shards(): noisy = (base.astype(f32)[None] + noise.astype(f32)).astype(bf16)]
    unnamed x91 -> x89, local copies, waits for them, and re-layouts: 25.2 us -> 25.3 us
  transfers between devices with their start and end apart: 39 -> 39, of which waited for: 19 -> 17; matrix products, arithmetic and copies ran while one was open for 2% -> 4% of each run, Pallas kernels for 3% -> 4%
where the time goes in v6:
time: 140 us; the launch traced here: 139 us
  waiting for transfers between devices  51.8 us (37%)
  starting transfers between devices  37 us (26%)
  local copies, waits for them, and re-layouts  27.3 us (20%)
  Pallas kernels  18.6 us (13%)
  other arithmetic  3.81 us (3%)
    ppermute x39, waiting for transfers between devices, permuted(): return lax.ppermute(value, ('sa', 'sb', 'noise'), pairs)  51.8 us
    ppermute x39, starting transfers between devices, permuted(): return lax.ppermute(value, ('sa', 'sb', 'noise'), pairs)  37 us
    unnamed x89, local copies, waits for them, and re-layouts  25.3 us
    pallas_call x1, Pallas kernels, stretch_shards(): pl.pallas_call(attention_kernel, out_shape=(shaped(128, 256), shaped(128,...  6.76 us
    pallas_call x1, Pallas kernels, stretch_shards(): pl.pallas_call(forward_kernel, out_shape=(shaped(192, features, dtype=bf1...  6.04 us
    pallas_call x1, Pallas kernels, stretch_shards(): pl.pallas_call(norm_kernel, out_shape=(shaped(128, HID, dtype=bf16), shap...  3.13 us
  transfers between devices with their start and end apart: 39, of which 17 were waited for; matrix products, arithmetic and copies ran while one was open for 4% of the time, Pallas kernels for 4%

profile of v6, /device:TPU:8, one launch (start us, length us, event | category | flops | bytes accessed | tf_op | source)
XLA Modules:
  0.0 138.9 jit_solution(4310315794104749251)
XLA Ops:
  0.0 1.2 copy-done
  1.2 1.1 copy-done.2
  2.3 1.0 copy-done.4
  3.2 1.0 copy-done.6
  4.3 3.0 %collective-permute-start.1 = (bf16[192,384]{1,0:T(8,128)(2,1)S(1)}, bf16[192,384]{1,0:T(8,128)(2,1)S(1)}, u32[]{:S(2)}, u32[]{:S(2)}) collective-permute-start(bf16[192,384]{1,0:T(8,128)(2,1)S(1)} %get-tuple-element.49), channel_id=1, source_target_pairs={{0,16},{1,17},{2,18},{3,19},{4,20},{5,21},{6,22},{7,23},{8,24},{9,... | collective-permute-start | bytes 442376 | tf_op jit(solution)/shard_map/ppermute | solution.py:241
  8.7 1.1 add_convert_fusion
  10.7 7.0 %collective-permute-done.1 = bf16[192,384]{1,0:T(8,128)(2,1)S(1)} collective-permute-done((bf16[192,384]{1,0:T(8,128)(2,1)S(1)}, bf16[192,384]{1,0:T(8,128)(2,1)S(1)}, u32[]{:S(2)}, u32[]{:S(2)}) %collective-permute-start.1) | collective-permute-done | bytes 147488 | tf_op jit(solution)/shard_map/ppermute | solution.py:241
  17.7 2.8 %collective-permute-done.2 = bf16[192,384]{1,0:T(8,128)(2,1)S(1)} collective-permute-done((bf16[192,384]{1,0:T(8,128)(2,1)S(1)}, bf16[192,384]{1,0:T(8,128)(2,1)S(1)}, u32[]{:S(2)}, u32[]{:S(2)}) %collective-permute-start.2) | collective-permute-done | bytes 147488 | tf_op jit(solution)/shard_map/ppermute | solution.py:241
  20.7 1.9 %collective-permute-start.8 = (bf16[32,1536]{1,0:T(8,128)(2,1)S(1)}, bf16[32,1536]{1,0:T(8,128)(2,1)S(1)}, u32[]{:S(2)}, u32[]{:S(2)}) collective-permute-start(bf16[32,1536]{1,0:T(8,128)(2,1)S(1)} %get-tuple-element.95), channel_id=1, source_target_pairs={{0,0},{1,4},{2,2},{3,6},{4,1},{5,5},{6,3},{7,7},{8,9},{9,13},{10,1... | collective-permute-start | bytes 294920 | tf_op jit(solution)/shard_map/ppermute | solution.py:241
  22.6 1.1 collective-permute-start.9
  23.7 2.3 %collective-permute-start.6 = (bf16[160,384]{1,0:T(8,128)(2,1)S(1)}, bf16[160,384]{1,0:T(8,128)(2,1)S(1)}, u32[]{:S(2)}, u32[]{:S(2)}) collective-permute-start(bf16[160,384]{1,0:T(8,128)(2,1)S(1)} %get-tuple-element.52), channel_id=1, source_target_pairs={{0,16},{1,17},{2,18},{3,19},{4,20},{5,21},{6,22},{7,23},{8,24},{9,... | collective-permute-start | bytes 368648 | tf_op jit(solution)/shard_map/ppermute | solution.py:241
  25.9 1.2 collective-permute-start.7
  27.2 1.3 collective-permute-start.10
  29.3 1.5 %collective-permute-start.3 = (bf16[3,192,384]{2,1,0:T(8,128)(2,1)S(1)}, bf16[3,192,384]{2,1,0:T(8,128)(2,1)S(1)}, u32[]{:S(2)}, u32[]{:S(2)}) collective-permute-start(bf16[3,192,384]{2,1,0:T(8,128)(2,1)S(1)} %pad_maximum_fusion.refs_2_), channel_id=1, source_target_pairs={{0,2},{1,3},{2,0},{3,1},{4,6},{5,7},{6,4},{7,5},{8,10},{9,11},{10,... | collective-permute-start | bytes 1327112 | tf_op jit(solution)/shard_map/ppermute | solution.py:241
  31.7 2.0 %collective-permute-done.10 = bf16[32,1536]{1,0:T(8,128)(2,1)S(1)} collective-permute-done((bf16[32,1536]{1,0:T(8,128)(2,1)S(1)}, bf16[32,1536]{1,0:T(8,128)(2,1)S(1)}, u32[]{:S(2)}, u32[]{:S(2)}) %collective-permute-start.10) | collective-permute-done | bytes 98336 | tf_op jit(solution)/shard_map/ppermute | solution.py:241
  33.9 5.2 %collective-permute-done.7 = bf16[160,384]{1,0:T(8,128)(2,1)S(1)} collective-permute-done((bf16[160,384]{1,0:T(8,128)(2,1)S(1)}, bf16[160,384]{1,0:T(8,128)(2,1)S(1)}, u32[]{:S(2)}, u32[]{:S(2)}) %collective-permute-start.7) | collective-permute-done | bytes 122912 | tf_op jit(solution)/shard_map/ppermute | solution.py:241
  39.1 3.0 %collective-permute-done.3.refs_3_ = bf16[3,192,384]{2,1,0:T(8,128)(2,1)S(1)} collective-permute-done((bf16[3,192,384]{2,1,0:T(8,128)(2,1)S(1)}, bf16[3,192,384]{2,1,0:T(8,128)(2,1)S(1)}, u32[]{:S(2)}, u32[]{:S(2)}) %collective-permute-start.3) | collective-permute-done | bytes 442400 | tf_op jit(solution)/shard_map/ppermute | solution.py:241
  42.1 2.8 %collective-permute-done.4.refs_4_ = bf16[3,192,384]{2,1,0:T(8,128)(2,1)S(1)} collective-permute-done((bf16[3,192,384]{2,1,0:T(8,128)(2,1)S(1)}, bf16[3,192,384]{2,1,0:T(8,128)(2,1)S(1)}, u32[]{:S(2)}, u32[]{:S(2)}) %collective-permute-start.4) | collective-permute-done | bytes 442400 | tf_op jit(solution)/shard_map/ppermute | solution.py:241
  44.9 1.8 %collective-permute-start.11 = (bf16[3,96,384]{2,1,0:T(8,128)(2,1)S(1)}, bf16[3,96,384]{2,1,0:T(8,128)(2,1)S(1)}, u32[]{:S(2)}, u32[]{:S(2)}) collective-permute-start(bf16[3,96,384]{2,1,0:T(8,128)(2,1)S(1)} %slice.40), channel_id=1, source_target_pairs={{0,4},{1,5},{2,6},{3,7},{4,0},{5,1},{6,2},{7,3},{8,12},{9,13},{10,... | collective-permute-start | bytes 663560 | tf_op jit(solution)/shard_map/ppermute | solution.py:241
  47.4 3.2 %collective-permute-start.19 = (bf16[48,1536]{1,0:T(8,128)(2,1)S(1)}, bf16[48,1536]{1,0:T(8,128)(2,1)S(1)}, u32[]{:S(2)}, u32[]{:S(2)}) collective-permute-start(bf16[48,1536]{1,0:T(8,128)(2,1)S(1)} %pad_maximum_fusion.2), channel_id=1, source_target_pairs={{1,9},{3,11},{5,13},{7,15},{8,16},{9,1},{10,18},{11,3},{12,20},{13... | collective-permute-start | bytes 442376 | tf_op jit(solution)/shard_map/ppermute | solution.py:241
  50.6 1.9 %collective-permute-start.18 = (bf16[32,1536]{1,0:T(8,128)(2,1)S(1)}, bf16[32,1536]{1,0:T(8,128)(2,1)S(1)}, u32[]{:S(2)}, u32[]{:S(2)}) collective-permute-start(bf16[32,1536]{1,0:T(8,128)(2,1)S(1)} %broadcast_select_fusion.cot_block), channel_id=1, source_target_pairs={{0,2},{1,3},{2,0},{3,1},{4,6},{5,7},{6,4},{7,5},{8,10},{9,11},{10,... | collective-permute-start | bytes 294920 | tf_op jit(solution)/shard_map/ppermute | solution.py:241
  52.5 3.5 %collective-permute-done.18.cot_beside = bf16[32,1536]{1,0:T(8,128)(2,1)S(1)} collective-permute-done((bf16[32,1536]{1,0:T(8,128)(2,1)S(1)}, bf16[32,1536]{1,0:T(8,128)(2,1)S(1)}, u32[]{:S(2)}, u32[]{:S(2)}) %collective-permute-start.18) | collective-permute-done | bytes 98336 | tf_op jit(solution)/shard_map/ppermute | solution.py:241
  56.5 1.1 collective-permute-start.16
  57.6 0.9 collective-permute-start.17
  58.5 8.6 %collective-permute-done.16.refs_3_ = bf16[3,160,384]{2,1,0:T(8,128)(2,1)} collective-permute-done((bf16[3,160,384]{2,1,0:T(8,128)(2,1)S(1)}, bf16[3,160,384]{2,1,0:T(8,128)(2,1)}, u32[]{:S(2)}, u32[]{:S(2)}) %collective-permute-start.16) | collective-permute-done | bytes 368672 | tf_op jit(solution)/shard_map/ppermute | solution.py:241
  70.8 0.9 slice.42
  71.8 1.0 collective-permute-start.27
  72.8 1.0 slice.43
  84.5 1.0 copy-done.9
  85.5 1.0 copy-done.11
  86.5 1.0 copy-done.13
  87.5 1.0 copy-done.15
  88.5 0.9 copy-done.19
  89.5 0.9 copy-done.21
  90.4 0.9 copy-done.23
  95.9 6.0 %shard_map.101 = (bf16[192,1536]{1,0:T(8,128)(2,1)S(1)}, f32[128,1536]{1,0:T(8,128)S(1)}, f32[128,1]{1,0:T(8,128)S(1)}, f32[128,384]{1,0:T(8,128)S(1)}, bf16[3,1...) custom-call(bf16[32,1536]{1,0:T(8,128)(2,1)S(1)} %collective-permute-done.8.blocks_even, ...), custom_call_target="tpu_custom_call" | custom-call | tf_op jit(solution)/shard_map/pallas_call | solution.py:633
  102.1 6.8 %shard_map.102 = (f32[128,256]{1,0:T(8,128)S(1)}, f32[128,640]{1,0:T(8,128)S(1)}, bf16[32,640]{1,0:T(8,128)(2,1)S(1)}, bf16[1536,896]{1,0:T(8,128)(2,1)S(1)}, bf16[128,1536]{1,0:T(8,128)(2,1)S(1)}) custom-call(s32[4]{0:T(128)S(1)} %copy-done.40, s32[16,2]{1,0:T(8,128)S(1)} %copy.11.pairs, bf16[192,1536]{1,0:T(8,128)(2,1)S(1)} %get-tuple-element.72.normed, ...), custom_call_target="tpu_custom_call" | custom-call | tf_op jit(solution)/shard_map/pallas_call | solution.py:649
  108.8 2.3 %collective-permute-start.34 = (bf16[32,640]{1,0:T(8,128)(2,1)S(1)}, bf16[32,640]{1,0:T(8,128)(2,1)S(1)}, u32[]{:S(2)}, u32[]{:S(2)}) collective-permute-start(bf16[32,640]{1,0:T(8,128)(2,1)S(1)} %get-tuple-element.80), channel_id=1, source_target_pairs={{1,9},{3,11},{5,13},{7,15},{8,16},{9,1},{10,18},{11,3},{12,20},{13... | collective-permute-start | bytes 122888 | tf_op jit(solution)/shard_map/ppermute | solution.py:241
  111.1 3.6 %collective-permute-done.34.received = bf16[32,640]{1,0:T(8,128)(2,1)S(1)} collective-permute-done((bf16[32,640]{1,0:T(8,128)(2,1)S(1)}, bf16[32,640]{1,0:T(8,128)(2,1)S(1)}, u32[]{:S(2)}, u32[]{:S(2)}) %collective-permute-start.34) | collective-permute-done | bytes 40992 | tf_op jit(solution)/shard_map/ppermute | solution.py:241
  114.7 3.1 %shard_map.103 = (bf16[128,384]{1,0:T(8,128)(2,1)S(1)}, f32[64,1536]{1,0:T(8,128)S(1)}, bf16[16,384]{1,0:T(8,128)(2,1)S(1)}) custom-call(f32[128,256]{1,0:T(8,128)S(1)} %get-tuple-element.78.d_q, f32[128,640]{1,0:T(8,128)S(1)} %get-tuple-element.79.d_kv, bf16[32,640]{1,0:T(8,128)(2,1)S(1)} %collective-permute-done.34.received, ...), custom_call_target="tpu_custom_call" | custom-call | tf_op jit(solution)/shard_map/pallas_call | solution.py:665
  117.9 2.3 %collective-permute-start.35 = (bf16[16,384]{1,0:T(8,128)(2,1)S(1)}, bf16[16,384]{1,0:T(8,128)(2,1)S(1)}, u32[]{:S(2)}, u32[]{:S(2)}) collective-permute-start(bf16[16,384]{1,0:T(8,128)(2,1)S(1)} %get-tuple-element.88), channel_id=1, source_target_pairs={{1,9},{3,11},{5,13},{7,15},{8,16},{9,1},{10,18},{11,3},{12,20},{13... | collective-permute-start | bytes 36872 | tf_op jit(solution)/shard_map/ppermute | solution.py:241
  120.1 3.3 %collective-permute-done.35.received = bf16[16,384]{1,0:T(8,128)(2,1)S(1)} collective-permute-done((bf16[16,384]{1,0:T(8,128)(2,1)S(1)}, bf16[16,384]{1,0:T(8,128)(2,1)S(1)}, u32[]{:S(2)}, u32[]{:S(2)}) %collective-permute-start.35) | collective-permute-done | bytes 12320 | tf_op jit(solution)/shard_map/ppermute | solution.py:241
  123.4 2.7 %shard_map.104 = (f32[32,1536]{1,0:T(8,128)S(1)}, bf16[32,1536]{1,0:T(8,128)(2,1)S(1)}) custom-call(bf16[128,384]{1,0:T(8,128)(2,1)S(1)} %get-tuple-element.87.d_hidden, bf16[16,384]{1,0:T(8,128)(2,1)S(1)} %collective-permute-done.35.received, f32[64,1536]{1,0:T(8,128)S(1)} %get-tuple-element.89.d_resid, ...), custom_call_target="tpu_custom_call" | custom-call | tf_op jit(solution)/shard_map/pallas_call | solution.py:677
  126.1 1.4 %collective-permute-start.36 = (bf16[32,1536]{1,0:T(8,128)(2,1)S(1)}, bf16[32,1536]{1,0:T(8,128)(2,1)S(1)}, u32[]{:S(2)}, u32[]{:S(2)}) collective-permute-start(bf16[32,1536]{1,0:T(8,128)(2,1)S(1)} %get-tuple-element.92), channel_id=1, source_target_pairs={{0,2},{1,3},{2,0},{3,1},{4,6},{5,7},{6,4},{7,5},{8,10},{9,11},{10,... | collective-permute-start | bytes 294920 | tf_op jit(solution)/shard_map/ppermute | solution.py:241
  127.6 3.2 %collective-permute-done.36 = bf16[32,1536]{1,0:T(8,128)(2,1)S(1)} collective-permute-done((bf16[32,1536]{1,0:T(8,128)(2,1)S(1)}, bf16[32,1536]{1,0:T(8,128)(2,1)S(1)}, u32[]{:S(2)}, u32[]{:S(2)}) %collective-permute-start.36) | collective-permute-done | bytes 98336 | tf_op jit(solution)/shard_map/ppermute | solution.py:241
  130.9 1.4 %collective-permute-start.37 = (bf16[32,1536]{1,0:T(8,128)(2,1)S(1)}, bf16[32,1536]{1,0:T(8,128)(2,1)S(1)}, u32[]{:S(2)}, u32[]{:S(2)}) collective-permute-start(bf16[32,1536]{1,0:T(8,128)(2,1)S(1)} %add_convert_fusion.1), channel_id=1, source_target_pairs={{0,1},{1,5},{2,3},{3,7},{4,0},{5,4},{6,2},{7,6},{8,12},{9,8},{10,1... | collective-permute-start | bytes 294920 | tf_op jit(solution)/shard_map/ppermute | solution.py:241
  132.3 1.9 %collective-permute-start.38 = (bf16[32,1536]{1,0:T(8,128)(2,1)S(1)}, bf16[32,1536]{1,0:T(8,128)(2,1)S(1)}, u32[]{:S(2)}, u32[]{:S(2)}) collective-permute-start(bf16[32,1536]{1,0:T(8,128)(2,1)S(1)} %add_convert_fusion.1), channel_id=1, source_target_pairs={{1,4},{3,6},{4,1},{6,3},{8,13},{10,15},{13,8},{15,10},{17,20},{19,... | collective-permute-start | bytes 294920 | tf_op jit(solution)/shard_map/ppermute | solution.py:241
  134.5 3.7 %collective-permute-done.38 = bf16[32,1536]{1,0:T(8,128)(2,1)S(1)} collective-permute-done((bf16[32,1536]{1,0:T(8,128)(2,1)S(1)}, bf16[32,1536]{1,0:T(8,128)(2,1)S(1)}, u32[]{:S(2)}, u32[]{:S(2)}) %collective-permute-start.38) | collective-permute-done | bytes 98336 | tf_op jit(solution)/shard_map/ppermute | solution.py:241
  (140 shorter events, 25.5 us)
Async XLA Ops:
  4.2 6.5 %collective-permute-start = (bf16[192,384]{1,0:T(8,128)(2,1)S(1)}, bf16[192,384]{1,0:T(8,128)(2,1)S(1)}, u32[]{:S(2)}, u32[]{:S(2)}) collective-permute-start(bf16[192,384]{1,0:T(8,128)(2,1)S(1)} %get-tuple-element.49), channel_id=1, source_target_pairs={{0,8},{1,9},{2,10},{3,11},{4,12},{5,13},{6,14},{7,15},{8,0},{9,1},... | collective-permute-start | bytes 442376 | tf_op jit(solution)/shard_map/ppermute | solution.py:241
  4.3 13.4 %collective-permute-start.1 = (bf16[192,384]{1,0:T(8,128)(2,1)S(1)}, bf16[192,384]{1,0:T(8,128)(2,1)S(1)}, u32[]{:S(2)}, u32[]{:S(2)}) collective-permute-start(bf16[192,384]{1,0:T(8,128)(2,1)S(1)} %get-tuple-element.49), channel_id=1, source_target_pairs={{0,16},{1,17},{2,18},{3,19},{4,20},{5,21},{6,22},{7,23},{8,24},{9,... | collective-permute-start | bytes 442376 | tf_op jit(solution)/shard_map/ppermute | solution.py:241
  7.3 13.3 %collective-permute-start.2 = (bf16[192,384]{1,0:T(8,128)(2,1)S(1)}, bf16[192,384]{1,0:T(8,128)(2,1)S(1)}, u32[]{:S(2)}, u32[]{:S(2)}) collective-permute-start(bf16[192,384]{1,0:T(8,128)(2,1)S(1)} %get-tuple-element.49), channel_id=1, source_target_pairs={{0,24},{1,25},{2,26},{3,27},{4,28},{5,29},{6,30},{7,31},{8,16},{9,... | collective-permute-start | bytes 442376 | tf_op jit(solution)/shard_map/ppermute | solution.py:241
  8.7 75.7 %copy-start.42 = (f32[1536]{0:T(1024)S(1)}, f32[1536]{0:T(1024)}, u32[]{:S(2)}) copy-start(f32[1536]{0:T(1024)} %param.15) | copy-start | bytes 18436
  8.7 75.7 %copy-start.43 = (s32[16,2]{0,1:T(2,128)S(1)}, s32[16,2]{0,1:T(2,128)}, u32[]{:S(2)}) copy-start(s32[16,2]{0,1:T(2,128)} %param.19) | copy-start | bytes 388
  8.7 75.7 %copy-start.1 = (bf16[3,384,384]{2,1,0:T(8,128)(2,1)S(1)}, bf16[3,384,384]{2,1,0:T(8,128)(2,1)}, u32[]{:S(2)}) copy-start(bf16[3,384,384]{2,1,0:T(8,128)(2,1)} %refs_0_.2) | copy-start | bytes 2654212
  8.7 75.7 %copy-start.5 = (bf16[96,1536]{1,0:T(8,128)(2,1)S(1)}, bf16[96,1536]{1,0:T(8,128)(2,1)}, u32[]{:S(2)}) copy-start(bf16[96,1536]{1,0:T(8,128)(2,1)} %refs_1_.2) | copy-start | bytes 884740
  20.7 6.5 %collective-permute-start.8 = (bf16[32,1536]{1,0:T(8,128)(2,1)S(1)}, bf16[32,1536]{1,0:T(8,128)(2,1)S(1)}, u32[]{:S(2)}, u32[]{:S(2)}) collective-permute-start(bf16[32,1536]{1,0:T(8,128)(2,1)S(1)} %get-tuple-element.95), channel_id=1, source_target_pairs={{0,0},{1,4},{2,2},{3,6},{4,1},{5,5},{6,3},{7,7},{8,9},{9,13},{10,1... | collective-permute-start | bytes 294920 | tf_op jit(solution)/shard_map/ppermute | solution.py:241
  22.6 6.7 %collective-permute-start.9 = (bf16[32,1536]{1,0:T(8,128)(2,1)S(1)}, bf16[32,1536]{1,0:T(8,128)(2,1)}, u32[]{:S(2)}, u32[]{:S(2)}) collective-permute-start(bf16[32,1536]{1,0:T(8,128)(2,1)S(1)} %get-tuple-element.96), channel_id=1, source_target_pairs={{0,2},{1,6},{2,0},{3,4},{4,3},{5,7},{6,1},{7,5},{8,11},{9,15},{10,... | collective-permute-start | bytes 294920 | tf_op jit(solution)/shard_map/ppermute | solution.py:241
  23.7 10.2 %collective-permute-start.5 = (bf16[160,384]{1,0:T(8,128)(2,1)S(1)}, bf16[160,384]{1,0:T(8,128)(2,1)S(1)}, u32[]{:S(2)}, u32[]{:S(2)}) collective-permute-start(bf16[160,384]{1,0:T(8,128)(2,1)S(1)} %get-tuple-element.52), channel_id=1, source_target_pairs={{0,8},{1,9},{2,10},{3,11},{4,12},{5,13},{6,14},{7,15},{8,0},{9,1},... | collective-permute-start | bytes 368648 | tf_op jit(solution)/shard_map/ppermute | solution.py:241
  23.7 10.2 %collective-permute-start.6 = (bf16[160,384]{1,0:T(8,128)(2,1)S(1)}, bf16[160,384]{1,0:T(8,128)(2,1)S(1)}, u32[]{:S(2)}, u32[]{:S(2)}) collective-permute-start(bf16[160,384]{1,0:T(8,128)(2,1)S(1)} %get-tuple-element.52), channel_id=1, source_target_pairs={{0,16},{1,17},{2,18},{3,19},{4,20},{5,21},{6,22},{7,23},{8,24},{9,... | collective-permute-start | bytes 368648 | tf_op jit(solution)/shard_map/ppermute | solution.py:241
  25.9 13.1 %collective-permute-start.7 = (bf16[160,384]{1,0:T(8,128)(2,1)S(1)}, bf16[160,384]{1,0:T(8,128)(2,1)S(1)}, u32[]{:S(2)}, u32[]{:S(2)}) collective-permute-start(bf16[160,384]{1,0:T(8,128)(2,1)S(1)} %get-tuple-element.52), channel_id=1, source_target_pairs={{0,24},{1,25},{2,26},{3,27},{4,28},{5,29},{6,30},{7,31},{8,16},{9,... | collective-permute-start | bytes 368648 | tf_op jit(solution)/shard_map/ppermute | solution.py:241
  27.2 6.5 %collective-permute-start.10 = (bf16[32,1536]{1,0:T(8,128)(2,1)S(1)}, bf16[32,1536]{1,0:T(8,128)(2,1)S(1)}, u32[]{:S(2)}, u32[]{:S(2)}) collective-permute-start(bf16[32,1536]{1,0:T(8,128)(2,1)S(1)} %copy-done.41), channel_id=1, source_target_pairs={{0,4},{2,6},{5,1},{7,3},{9,13},{11,15},{12,8},{14,10},{16,20},{18,... | collective-permute-start | bytes 294920 | tf_op jit(solution)/shard_map/ppermute | solution.py:241
  29.3 12.8 %collective-permute-start.3 = (bf16[3,192,384]{2,1,0:T(8,128)(2,1)S(1)}, bf16[3,192,384]{2,1,0:T(8,128)(2,1)S(1)}, u32[]{:S(2)}, u32[]{:S(2)}) collective-permute-start(bf16[3,192,384]{2,1,0:T(8,128)(2,1)S(1)} %pad_maximum_fusion.refs_2_), channel_id=1, source_target_pairs={{0,2},{1,3},{2,0},{3,1},{4,6},{5,7},{6,4},{7,5},{8,10},{9,11},{10,... | collective-permute-start | bytes 1327112 | tf_op jit(solution)/shard_map/ppermute | solution.py:241
  33.8 11.2 %collective-permute-start.4 = (bf16[3,192,384]{2,1,0:T(8,128)(2,1)S(1)}, bf16[3,192,384]{2,1,0:T(8,128)(2,1)S(1)}, u32[]{:S(2)}, u32[]{:S(2)}) collective-permute-start(bf16[3,192,384]{2,1,0:T(8,128)(2,1)S(1)} %pad_maximum_fusion.refs_2_), channel_id=1, source_target_pairs={{0,4},{1,5},{2,6},{3,7},{4,0},{5,1},{6,2},{7,3},{8,12},{9,13},{10,... | collective-permute-start | bytes 1327112 | tf_op jit(solution)/shard_map/ppermute | solution.py:241
  33.8 48.1 %copy-start.16 = (bf16[32,1536]{1,0:T(8,128)(2,1)}, bf16[32,1536]{1,0:T(8,128)(2,1)S(1)}, u32[]{:S(2)}) copy-start(bf16[32,1536]{1,0:T(8,128)(2,1)S(1)} %broadcast_select_fusion.cot_block) | copy-start | bytes 294916
  44.9 27.9 %copy-start.8 = (bf16[3,192,384]{2,1,0:T(8,128)(2,1)}, bf16[3,192,384]{2,1,0:T(8,128)(2,1)S(1)}, u32[]{:S(2)}) copy-start(bf16[3,192,384]{2,1,0:T(8,128)(2,1)S(1)} %collective-permute-done.4.refs_4_) | copy-start | bytes 1327108
  44.9 11.5 %collective-permute-start.11 = (bf16[3,96,384]{2,1,0:T(8,128)(2,1)S(1)}, bf16[3,96,384]{2,1,0:T(8,128)(2,1)S(1)}, u32[]{:S(2)}, u32[]{:S(2)}) collective-permute-start(bf16[3,96,384]{2,1,0:T(8,128)(2,1)S(1)} %slice.40), channel_id=1, source_target_pairs={{0,4},{1,5},{2,6},{3,7},{4,0},{5,1},{6,2},{7,3},{8,12},{9,13},{10,... | collective-permute-start | bytes 663560 | tf_op jit(solution)/shard_map/ppermute | solution.py:241
  46.8 10.8 %collective-permute-start.12 = (bf16[3,96,384]{2,1,0:T(8,128)(2,1)S(1)}, bf16[3,96,384]{2,1,0:T(8,128)(2,1)S(1)}, u32[]{:S(2)}, u32[]{:S(2)}) collective-permute-start(bf16[3,96,384]{2,1,0:T(8,128)(2,1)S(1)} %slice.41), channel_id=1, source_target_pairs={{0,2},{1,3},{2,0},{3,1},{4,6},{5,7},{6,4},{7,5},{8,10},{9,11},{10,... | collective-permute-start | bytes 663560 | tf_op jit(solution)/shard_map/ppermute | solution.py:241
  47.4 8.6 %collective-permute-start.19 = (bf16[48,1536]{1,0:T(8,128)(2,1)S(1)}, bf16[48,1536]{1,0:T(8,128)(2,1)S(1)}, u32[]{:S(2)}, u32[]{:S(2)}) collective-permute-start(bf16[48,1536]{1,0:T(8,128)(2,1)S(1)} %pad_maximum_fusion.2), channel_id=1, source_target_pairs={{1,9},{3,11},{5,13},{7,15},{8,16},{9,1},{10,18},{11,3},{12,20},{13... | collective-permute-start | bytes 442376 | tf_op jit(solution)/shard_map/ppermute | solution.py:241
  50.6 5.4 %collective-permute-start.18 = (bf16[32,1536]{1,0:T(8,128)(2,1)S(1)}, bf16[32,1536]{1,0:T(8,128)(2,1)S(1)}, u32[]{:S(2)}, u32[]{:S(2)}) collective-permute-start(bf16[32,1536]{1,0:T(8,128)(2,1)S(1)} %broadcast_select_fusion.cot_block), channel_id=1, source_target_pairs={{0,2},{1,3},{2,0},{3,1},{4,6},{5,7},{6,4},{7,5},{8,10},{9,11},{10,... | collective-permute-start | bytes 294920 | tf_op jit(solution)/shard_map/ppermute | solution.py:241
  52.5 16.3 %collective-permute-start.14 = (bf16[3,192,384]{2,1,0:T(8,128)(2,1)S(1)}, bf16[3,192,384]{2,1,0:T(8,128)(2,1)S(1)}, u32[]{:S(2)}, u32[]{:S(2)}) collective-permute-start(bf16[3,192,384]{2,1,0:T(8,128)(2,1)S(1)} %collective-permute-done.3.refs_3_), channel_id=1, source_target_pairs={{0,1},{1,0},{2,3},{3,2},{4,5},{5,4},{6,7},{7,6},{8,9},{9,8},{10,11... | collective-permute-start | bytes 1327112 | tf_op jit(solution)/shard_map/ppermute | solution.py:241
  56.0 12.0 %collective-permute-start.13 = (bf16[3,192,384]{2,1,0:T(8,128)(2,1)S(1)}, bf16[3,192,384]{2,1,0:T(8,128)(2,1)S(1)}, u32[]{:S(2)}, u32[]{:S(2)}) collective-permute-start(bf16[3,192,384]{2,1,0:T(8,128)(2,1)S(1)} %pad_maximum_fusion.refs_2_), channel_id=1, source_target_pairs={{0,1},{1,0},{2,3},{3,2},{4,5},{5,4},{6,7},{7,6},{8,9},{9,8},{10,11... | collective-permute-start | bytes 1327112 | tf_op jit(solution)/shard_map/ppermute | solution.py:241
  56.0 13.6 %collective-permute-start.15 = (bf16[3,192,384]{2,1,0:T(8,128)(2,1)S(1)}, bf16[3,192,384]{2,1,0:T(8,128)(2,1)S(1)}, u32[]{:S(2)}, u32[]{:S(2)}) collective-permute-start(bf16[3,192,384]{2,1,0:T(8,128)(2,1)S(1)} %collective-permute-done.4.refs_4_), channel_id=1, source_target_pairs={{0,1},{1,0},{2,3},{3,2},{4,5},{5,4},{6,7},{7,6},{8,9},{9,8},{10,11... | collective-permute-start | bytes 1327112 | tf_op jit(solution)/shard_map/ppermute | solution.py:241
  56.5 10.7 %collective-permute-start.16 = (bf16[3,160,384]{2,1,0:T(8,128)(2,1)S(1)}, bf16[3,160,384]{2,1,0:T(8,128)(2,1)}, u32[]{:S(2)}, u32[]{:S(2)}) collective-permute-start(bf16[3,160,384]{2,1,0:T(8,128)(2,1)S(1)} %pad_maximum_fusion.1.refs_2_), channel_id=1, source_target_pairs={{0,2},{1,3},{2,0},{3,1},{4,6},{5,7},{6,4},{7,5},{8,10},{9,11},{10,... | collective-permute-start | bytes 1105928 | tf_op jit(solution)/shard_map/ppermute | solution.py:241
  57.6 10.4 %collective-permute-start.17 = (bf16[3,160,384]{2,1,0:T(8,128)(2,1)S(1)}, bf16[3,160,384]{2,1,0:T(8,128)(2,1)}, u32[]{:S(2)}, u32[]{:S(2)}) collective-permute-start(bf16[3,160,384]{2,1,0:T(8,128)(2,1)S(1)} %pad_maximum_fusion.1.refs_2_), channel_id=1, source_target_pairs={{0,4},{1,5},{2,6},{3,7},{4,0},{5,1},{6,2},{7,3},{8,12},{9,13},{10,... | collective-permute-start | bytes 1105928 | tf_op jit(solution)/shard_map/ppermute | solution.py:241
  70.3 4.8 %collective-permute-start.20 = (bf16[32,1536]{1,0:T(8,128)(2,1)S(1)}, bf16[32,1536]{1,0:T(8,128)(2,1)S(1)}, u32[]{:S(2)}, u32[]{:S(2)}) collective-permute-start(bf16[32,1536]{1,0:T(8,128)(2,1)S(1)} %collective-permute-done.8.blocks_even), channel_id=1, source_target_pairs={{0,1},{1,0},{2,3},{3,2},{4,5},{5,4},{6,7},{7,6},{8,9},{9,8},{10,11... | collective-permute-start | bytes 294920 | tf_op jit(solution)/shard_map/ppermute | solution.py:241
  70.3 6.0 %collective-permute-start.21 = (bf16[32,1536]{1,0:T(8,128)(2,1)}, bf16[32,1536]{1,0:T(8,128)(2,1)S(1)}, u32[]{:S(2)}, u32[]{:S(2)}) collective-permute-start(bf16[32,1536]{1,0:T(8,128)(2,1)} %collective-permute-done.9.blocks_odd), channel_id=1, source_target_pairs={{0,1},{1,0},{2,3},{3,2},{4,5},{5,4},{6,7},{7,6},{8,9},{9,8},{10,11... | collective-permute-start | bytes 294920 | tf_op jit(solution)/shard_map/ppermute | solution.py:241
  71.8 10.1 %collective-permute-start.27 = (bf16[3,80,384]{2,1,0:T(8,128)(2,1)S(1)}, bf16[3,80,384]{2,1,0:T(8,128)(2,1)}, u32[]{:S(2)}, u32[]{:S(2)}) collective-permute-start(bf16[3,80,384]{2,1,0:T(8,128)(2,1)S(1)} %slice.42), channel_id=1, source_target_pairs={{0,4},{1,5},{2,6},{3,7},{4,0},{5,1},{6,2},{7,3},{8,12},{9,13},{10,... | collective-permute-start | bytes 552968 | tf_op jit(solution)/shard_map/ppermute | solution.py:241
  72.8 29.2 %copy-start.40 = (s32[4]{0:T(128)S(1)}, s32[4]{0:T(128)}, u32[]{:S(2)}) copy-start(s32[4]{0:T(128)} %band.1) | copy-start | bytes 52
  73.7 28.3 %copy-start.3 = (bf16[384,896]{1,0:T(8,128)(2,1)S(1)}, bf16[384,896]{1,0:T(8,128)(2,1)}, u32[]{:S(2)}) copy-start(bf16[384,896]{1,0:T(8,128)(2,1)} %refs_0_.3) | copy-start | bytes 2064388
  73.7 28.3 %copy-start.7 = (bf16[96,1536]{1,0:T(8,128)(2,1)S(1)}, bf16[96,1536]{1,0:T(8,128)(2,1)}, u32[]{:S(2)}) copy-start(bf16[96,1536]{1,0:T(8,128)(2,1)} %refs_1_.3) | copy-start | bytes 884740
  73.8 8.2 %collective-permute-start.28 = (bf16[3,80,384]{2,1,0:T(8,128)(2,1)S(1)}, bf16[3,80,384]{2,1,0:T(8,128)(2,1)}, u32[]{:S(2)}, u32[]{:S(2)}) collective-permute-start(bf16[3,80,384]{2,1,0:T(8,128)(2,1)S(1)} %slice.43), channel_id=1, source_target_pairs={{0,2},{1,3},{2,0},{3,1},{4,6},{5,7},{6,4},{7,5},{8,10},{9,11},{10,... | collective-permute-start | bytes 552968 | tf_op jit(solution)/shard_map/ppermute | solution.py:241
  74.5 6.3 %collective-permute-start.22 = (bf16[48,1536]{1,0:T(8,128)(2,1)S(1)}, bf16[48,1536]{1,0:T(8,128)(2,1)S(1)}, u32[]{:S(2)}, u32[]{:S(2)}) collective-permute-start(bf16[48,1536]{1,0:T(8,128)(2,1)S(1)} %collective-permute-done.19.edge), channel_id=1, source_target_pairs={{0,1},{1,0},{2,3},{3,2},{4,5},{5,4},{6,7},{7,6},{8,9},{9,8},{10,11... | collective-permute-start | bytes 442376 | tf_op jit(solution)/shard_map/ppermute | solution.py:241
  75.8 1.8 %collective-permute-start.25 = (bf16[32,1536]{1,0:T(8,128)(2,1)S(1)}, bf16[32,1536]{1,0:T(8,128)(2,1)S(1)}, u32[]{:S(2)}, u32[]{:S(2)}) collective-permute-start(bf16[32,1536]{1,0:T(8,128)(2,1)S(1)} %broadcast_select_fusion.cot_block), channel_id=1, source_target_pairs={{0,1},{1,0},{2,3},{3,2},{4,5},{5,4},{6,7},{7,6},{8,9},{9,8},{10,11... | collective-permute-start | bytes 294920 | tf_op jit(solution)/shard_map/ppermute | solution.py:241
  76.9 2.5 %collective-permute-start.26 = (bf16[32,1536]{1,0:T(8,128)(2,1)S(1)}, bf16[32,1536]{1,0:T(8,128)(2,1)S(1)}, u32[]{:S(2)}, u32[]{:S(2)}) collective-permute-start(bf16[32,1536]{1,0:T(8,128)(2,1)S(1)} %collective-permute-done.18.cot_beside), channel_id=1, source_target_pairs={{0,1},{1,0},{2,3},{3,2},{4,5},{5,4},{6,7},{7,6},{8,9},{9,8},{10,11... | collective-permute-start | bytes 294920 | tf_op jit(solution)/shard_map/ppermute | solution.py:241
  78.2 4.2 %collective-permute-start.23 = (bf16[3,96,384]{2,1,0:T(8,128)(2,1)S(1)}, bf16[3,96,384]{2,1,0:T(8,128)(2,1)S(1)}, u32[]{:S(2)}, u32[]{:S(2)}) collective-permute-start(bf16[3,96,384]{2,1,0:T(8,128)(2,1)S(1)} %collective-permute-done.11.refs_5_), channel_id=1, source_target_pairs={{0,1},{1,0},{2,3},{3,2},{4,5},{5,4},{6,7},{7,6},{8,9},{9,8},{10,11... | collective-permute-start | bytes 663560 | tf_op jit(solution)/shard_map/ppermute | solution.py:241
  80.0 3.2 %collective-permute-start.24 = (bf16[3,96,384]{2,1,0:T(8,128)(2,1)S(1)}, bf16[3,96,384]{2,1,0:T(8,128)(2,1)S(1)}, u32[]{:S(2)}, u32[]{:S(2)}) collective-permute-start(bf16[3,96,384]{2,1,0:T(8,128)(2,1)S(1)} %collective-permute-done.12.refs_6_), channel_id=1, source_target_pairs={{0,1},{1,0},{2,3},{3,2},{4,5},{5,4},{6,7},{7,6},{8,9},{9,8},{10,11... | collective-permute-start | bytes 663560 | tf_op jit(solution)/shard_map/ppermute | solution.py:241
  81.4 20.6 %collective-permute-start.30 = (bf16[3,160,384]{2,1,0:T(8,128)(2,1)}, bf16[3,160,384]{2,1,0:T(8,128)(2,1)}, u32[]{:S(2)}, u32[]{:S(2)}) collective-permute-start(bf16[3,160,384]{2,1,0:T(8,128)(2,1)} %collective-permute-done.16.refs_3_), channel_id=1, source_target_pairs={{0,1},{1,0},{2,3},{3,2},{4,5},{5,4},{6,7},{7,6},{8,9},{9,8},{10,11... | collective-permute-start | bytes 1105928 | tf_op jit(solution)/shard_map/ppermute | solution.py:241
  81.9 20.0 %collective-permute-start.29 = (bf16[3,160,384]{2,1,0:T(8,128)(2,1)S(1)}, bf16[3,160,384]{2,1,0:T(8,128)(2,1)}, u32[]{:S(2)}, u32[]{:S(2)}) collective-permute-start(bf16[3,160,384]{2,1,0:T(8,128)(2,1)S(1)} %pad_maximum_fusion.1.refs_2_), channel_id=1, source_target_pairs={{0,1},{1,0},{2,3},{3,2},{4,5},{5,4},{6,7},{7,6},{8,9},{9,8},{10,11... | collective-permute-start | bytes 1105928 | tf_op jit(solution)/shard_map/ppermute | solution.py:241
  82.0 20.0 %collective-permute-start.31 = (bf16[3,160,384]{2,1,0:T(8,128)(2,1)}, bf16[3,160,384]{2,1,0:T(8,128)(2,1)}, u32[]{:S(2)}, u32[]{:S(2)}) collective-permute-start(bf16[3,160,384]{2,1,0:T(8,128)(2,1)} %collective-permute-done.17.refs_4_), channel_id=1, source_target_pairs={{0,1},{1,0},{2,3},{3,2},{4,5},{5,4},{6,7},{7,6},{8,9},{9,8},{10,11... | collective-permute-start | bytes 1105928 | tf_op jit(solution)/shard_map/ppermute | solution.py:241
  83.1 18.8 %collective-permute-start.32 = (bf16[3,80,384]{2,1,0:T(8,128)(2,1)}, bf16[3,80,384]{2,1,0:T(8,128)(2,1)}, u32[]{:S(2)}, u32[]{:S(2)}) collective-permute-start(bf16[3,80,384]{2,1,0:T(8,128)(2,1)} %collective-permute-done.27.refs_5_), channel_id=1, source_target_pairs={{0,1},{1,0},{2,3},{3,2},{4,5},{5,4},{6,7},{7,6},{8,9},{9,8},{10,11... | collective-permute-start | bytes 552968 | tf_op jit(solution)/shard_map/ppermute | solution.py:241
  83.9 18.0 %collective-permute-start.33 = (bf16[3,80,384]{2,1,0:T(8,128)(2,1)}, bf16[3,80,384]{2,1,0:T(8,128)(2,1)}, u32[]{:S(2)}, u32[]{:S(2)}) collective-permute-start(bf16[3,80,384]{2,1,0:T(8,128)(2,1)} %collective-permute-done.28.refs_6_), channel_id=1, source_target_pairs={{0,1},{1,0},{2,3},{3,2},{4,5},{5,4},{6,7},{7,6},{8,9},{9,8},{10,11... | collective-permute-start | bytes 552968 | tf_op jit(solution)/shard_map/ppermute | solution.py:241
  108.8 5.9 %collective-permute-start.34 = (bf16[32,640]{1,0:T(8,128)(2,1)S(1)}, bf16[32,640]{1,0:T(8,128)(2,1)S(1)}, u32[]{:S(2)}, u32[]{:S(2)}) collective-permute-start(bf16[32,640]{1,0:T(8,128)(2,1)S(1)} %get-tuple-element.80), channel_id=1, source_target_pairs={{1,9},{3,11},{5,13},{7,15},{8,16},{9,1},{10,18},{11,3},{12,20},{13... | collective-permute-start | bytes 122888 | tf_op jit(solution)/shard_map/ppermute | solution.py:241
  117.9 5.6 %collective-permute-start.35 = (bf16[16,384]{1,0:T(8,128)(2,1)S(1)}, bf16[16,384]{1,0:T(8,128)(2,1)S(1)}, u32[]{:S(2)}, u32[]{:S(2)}) collective-permute-start(bf16[16,384]{1,0:T(8,128)(2,1)S(1)} %get-tuple-element.88), channel_id=1, source_target_pairs={{1,9},{3,11},{5,13},{7,15},{8,16},{9,1},{10,18},{11,3},{12,20},{13... | collective-permute-start | bytes 36872 | tf_op jit(solution)/shard_map/ppermute | solution.py:241
  126.1 4.7 %collective-permute-start.36 = (bf16[32,1536]{1,0:T(8,128)(2,1)S(1)}, bf16[32,1536]{1,0:T(8,128)(2,1)S(1)}, u32[]{:S(2)}, u32[]{:S(2)}) collective-permute-start(bf16[32,1536]{1,0:T(8,128)(2,1)S(1)} %get-tuple-element.92), channel_id=1, source_target_pairs={{0,2},{1,3},{2,0},{3,1},{4,6},{5,7},{6,4},{7,5},{8,10},{9,11},{10,... | collective-permute-start | bytes 294920 | tf_op jit(solution)/shard_map/ppermute | solution.py:241
  130.9 3.6 %collective-permute-start.37 = (bf16[32,1536]{1,0:T(8,128)(2,1)S(1)}, bf16[32,1536]{1,0:T(8,128)(2,1)S(1)}, u32[]{:S(2)}, u32[]{:S(2)}) collective-permute-start(bf16[32,1536]{1,0:T(8,128)(2,1)S(1)} %add_convert_fusion.1), channel_id=1, source_target_pairs={{0,1},{1,5},{2,3},{3,7},{4,0},{5,4},{6,2},{7,6},{8,12},{9,8},{10,1... | collective-permute-start | bytes 294920 | tf_op jit(solution)/shard_map/ppermute | solution.py:241
  132.3 5.9 %collective-permute-start.38 = (bf16[32,1536]{1,0:T(8,128)(2,1)S(1)}, bf16[32,1536]{1,0:T(8,128)(2,1)S(1)}, u32[]{:S(2)}, u32[]{:S(2)}) collective-permute-start(bf16[32,1536]{1,0:T(8,128)(2,1)S(1)} %add_convert_fusion.1), channel_id=1, source_target_pairs={{1,4},{3,6},{4,1},{6,3},{8,13},{10,15},{13,8},{15,10},{17,20},{19,... | collective-permute-start | bytes 294920 | tf_op jit(solution)/shard_map/ppermute | solution.py:241
  (35 other events, 72.9 us)

commit v7 on v6

--- a/solution.py
+++ b/solution.py
@@ -389,17 +389,13 @@
         copy.wait()
 
 
-def attention_kernel(band, pairs, normed, cot_block, cot_beside, other_block, other_beside, *refs):
+def attention_kernel(band, flag, normed, cot_block, cot_beside, other_block, other_beside, *refs):
     own_qkv, own_out = refs[:2]
     same, other = refs[2:7], refs[7:12]
     d_q_out, d_kv_out, send, qkv_out, cot_out, qkv, out, sems = refs[12:]
     z, y, x, n = position()
     length = lax.axis_size("sa") * 128
     first_bin = z * 128
-    pair_flag = jnp.int32(0)
-    for i in range(pairs.shape[0]):
-        pair_flag = pair_flag | ((pairs[i, 0] == z) & (pairs[i, 1] == z)).astype(jnp.int32)
-
     own_rows = pl.ds(times(z, 384, 128), 384)
     qkv[own_rows, :] = own_qkv[...]
     out[pl.ds(times(z, 96, 32), 96), :] = own_out[...]
@@ -432,7 +428,7 @@
     row = lax.broadcasted_iota(jnp.int32, (128, 192), 0)
     column = lax.broadcasted_iota(jnp.int32, (128, 192), 1) - 32
     inside = (column + first_bin >= 0) & (column + first_bin < length)
-    paired = (column >= 0) & (column < 128) & (pair_flag > 0)
+    paired = (column >= 0) & (column < 128) & (flag[0] > 0)
     apart = jnp.abs(row - column)
     scale = KEY ** (-0.5)
     d_queries, d_keys, d_values = [], [], []
@@ -595,39 +591,43 @@
 
     noisy = (base.astype(f32)[None] + noise.astype(f32)).astype(bf16)
     even = x == 0
-    straight, late, noisy, cot = after((jnp.stack(over_z(early)), late, noisy, cot))
-    beside, across = permuted(straight, x_route), permuted(straight, y_route)
-    late_straight = jnp.stack(over_z(late))
+    edge_route = routes(
+        n_sa, lambda z, y, x, c: (z - 1, y, x, c) if c ^ (z & 1) == 0 else (z + 1, y, x, c)
+    )
+    z = lax.axis_index("sa")
+    flag = jnp.any((pairs[:, 0] == z) & (pairs[:, 1] == z)).astype(jnp.int32).reshape(1)
+    straight = over_z(early)
+    noisy, cot = after((noisy, cot), *straight[:1])
     blocks = [
         permuted(jnp.where(x == shift, noisy[0], noisy[1]), to_sample(shift)) for shift in range(2)
     ]
     across_cot = permuted(
         cot, routes(n_sa, lambda z, y, x, c: (z, 1 - y, x, c) if y == c ^ (z & 1) else None)
     )
-    edge_route = routes(
-        n_sa, lambda z, y, x, c: (z - 1, y, x, c) if c ^ (z & 1) == 0 else (z + 1, y, x, c)
-    )
     low, high = jnp.where(even, blocks[0], blocks[1]), jnp.where(even, blocks[1], blocks[0])
     outer = jnp.concatenate(
         [jnp.where(m == 0, low[:16], low[16:]), jnp.where(m == 0, low[16:], high[:16]), jnp.where(m == 0, high[:16], high[16:])]
     )
     cot_block = jnp.where(y == m, cot, across_cot)
-    straight, beside, across, late_straight, outer, cot_block = after(
-        (straight, beside, across, late_straight, outer, cot_block)
+    straight = jnp.stack(straight)
+    straight, late, flag, outer, cot_block = after((straight, late, flag, outer, cot_block))
+    beside, across = permuted(straight, x_route), permuted(straight, y_route)
+    late_straight = jnp.stack(over_z(late))
+    edge = permuted(outer, edge_route)
+    straight, beside, across, late_straight, edge, cot_block, *blocks = after(
+        (straight, beside, across, late_straight, edge, cot_block, *blocks)
     )
     early = (straight, beside, across) + diagonals(beside, across)
     late_beside, late_across = permuted(late_straight, x_route), permuted(late_straight, y_route)
+    early, late, cot_block, mine = (
+        lambda v: (v[:5], v[5:8], v[8], v[9:])
+    )(after((*early, late_straight, late_beside, late_across, cot_block, *blocks, edge)))
+    late = tuple(late) + diagonals(late[1], late[2])
+    noisy_rows = tuple(mine) + swapped(mine)
+    early = tuple(early) + swapped(early)
     cot_rows = (cot_block, permuted(cot_block, x_route))
-    mine = (*blocks, permuted(outer, edge_route))
-    early_other = swapped(early[:3])
-    early, early_other, late, cot_rows, mine = (
-        lambda v: (v[:5], v[5:8], v[8:11], v[11:13], v[13:])
-    )(after((*early, *early_other, late_straight, late_beside, late_across, *cot_rows, *mine)))
-    late = tuple(late) + diagonals(late[1], late[2])
-    early = tuple(early) + tuple(early_other) + swapped(early[3:])
-    cot_rows = tuple(cot_rows) + swapped(cot_rows)
+    cot_rows = cot_rows + swapped(cot_rows)
     late_other = swapped(late[:3])
-    noisy_rows = tuple(mine) + swapped(mine)
     gain = norm_gain.reshape(1, features)
 
     normed, resid, inv_rms, hidden, conv, mix = pl.pallas_call(
@@ -659,7 +659,7 @@
             pltpu.SemaphoreType.DMA((1,)),
         ],
         compiler_params=limit(14),
-    )(band_width, pairs, normed, *cot_rows, qkv_w, out_w, *late)
+    )(band_width, flag, normed, *cot_rows, qkv_w, out_w, *late)
 
     received = permuted(send, edge_route)
     d_hidden, d_resid, send = pl.pallas_call(

time: 140 us -> 106 us (0.76)
  local copies, waits for them, and re-layouts: 27.3 us -> 4.32 us
  waiting for transfers between devices: 51.8 us -> 44.8 us
  Pallas kernels: 18.6 us -> 15.6 us
    unnamed x89 -> x24, local copies, waits for them, and re-layouts: 25.3 us -> 4.23 us
    ppermute x39, waiting for transfers between devices: 51.8 us -> 44.8 us  [permuted(): return lax.ppermute(value, ('sa', 'sb', 'noise'), pairs)]
  transfers between devices with their start and end apart: 39 -> 39, of which waited for: 17 -> 18; matrix products, arithmetic and copies ran while one was open for 4% -> 3% of each run, Pallas kernels for 4% -> 5%
where the time goes in v7:
time: 106 us
  waiting for transfers between devices  44.8 us (42%)
  starting transfers between devices  36.4 us (34%)
  Pallas kernels  15.6 us (15%)
  local copies, waits for them, and re-layouts  4.32 us (4%)
  other arithmetic  3.55 us (3%)
    ppermute x39, waiting for transfers between devices, permuted(): return lax.ppermute(value, ('sa', 'sb', 'noise'), pairs)  44.8 us
    ppermute x39, starting transfers between devices, permuted(): return lax.ppermute(value, ('sa', 'sb', 'noise'), pairs)  36.4 us
    pallas_call x1, Pallas kernels, stretch_shards(): pl.pallas_call(attention_kernel, out_shape=(shaped(128, 256), shaped(128,...  5.59 us
    pallas_call x1, Pallas kernels, stretch_shards(): pl.pallas_call(forward_kernel, out_shape=(shaped(192, features, dtype=bf1...  5.1 us
    unnamed x24, local copies, waits for them, and re-layouts  4.23 us
    pallas_call x1, Pallas kernels, stretch_shards(): pl.pallas_call(norm_kernel, out_shape=(shaped(128, HID, dtype=bf16), shap...  3.12 us
  transfers between devices with their start and end apart: 39, of which 18 were waited for; matrix products, arithmetic and copies ran while one was open for 3% of the time, Pallas kernels for 5%

profile of v7, /device:TPU:8, one launch (start us, length us, event | category | flops | bytes accessed | tf_op | source)
XLA Modules:
  0.0 105.8 jit_solution(14711818112527688444)
XLA Ops:
  0.0 1.2 %copy-done = bf16[3,384,384]{2,1,0:T(8,128)(2,1)S(1)} copy-done((bf16[3,384,384]{2,1,0:T(8,128)(2,1)S(1)}, bf16[3,384,384]{2,1,0:T(8,128)(2,1)}, u32[]{:S(2)}) %copy-start) | copy-done | bytes 884760
  1.2 1.1 %copy-done.2 = bf16[384,896]{1,0:T(8,128)(2,1)S(1)} copy-done((bf16[384,896]{1,0:T(8,128)(2,1)S(1)}, bf16[384,896]{1,0:T(8,128)(2,1)}, u32[]{:S(2)}) %copy-start.2) | copy-done | bytes 688152
  2.3 1.0 copy-done.4
  3.2 1.0 copy-done.6
  4.3 3.0 %collective-permute-start.1 = (bf16[192,384]{1,0:T(8,128)(2,1)S(1)}, bf16[192,384]{1,0:T(8,128)(2,1)S(1)}, u32[]{:S(2)}, u32[]{:S(2)}) collective-permute-start(bf16[192,384]{1,0:T(8,128)(2,1)S(1)} %get-tuple-element.50), channel_id=1, source_target_pairs={{0,16},{1,17},{2,18},{3,19},{4,20},{5,21},{6,22},{7,23},{8,24},{9,... | collective-permute-start | bytes 442376 | tf_op jit(solution)/shard_map/ppermute | solution.py:241
  7.8 0.9 convert_element_type.22
  8.7 1.1 %add_convert_fusion = bf16[2,32,1536]{2,1,0:T(8,128)(2,1)S(1)} fusion(bf16[2,32,1536]{2,1,0:T(8,128)(2,1)} %param.11, f32[32,1536]{1,0:T(8,128)S(1)} %convert_element_type.22), kind=kLoop, calls=%fused_computation.1 | loop fusion | flops 294912 | bytes 589824 | tf_op jit(solution)/shard_map/convert_element_type | solution.py:592
  9.8 0.6 and_reduce_fusion
  11.1 1.9 %collective-permute-start.3 = (bf16[32,1536]{1,0:T(8,128)(2,1)S(1)}, bf16[32,1536]{1,0:T(8,128)(2,1)S(1)}, u32[]{:S(2)}, u32[]{:S(2)}) collective-permute-start(bf16[32,1536]{1,0:T(8,128)(2,1)S(1)} %get-tuple-element.97), channel_id=1, source_target_pairs={{0,0},{1,4},{2,2},{3,6},{4,1},{5,5},{6,3},{7,7},{8,9},{9,13},{10,1... | collective-permute-start | bytes 294920 | tf_op jit(solution)/shard_map/ppermute | solution.py:241
  13.1 1.4 %collective-permute-start.4 = (bf16[32,1536]{1,0:T(8,128)(2,1)S(1)}, bf16[32,1536]{1,0:T(8,128)(2,1)S(1)}, u32[]{:S(2)}, u32[]{:S(2)}) collective-permute-start(bf16[32,1536]{1,0:T(8,128)(2,1)S(1)} %get-tuple-element.98), channel_id=1, source_target_pairs={{0,2},{1,6},{2,0},{3,4},{4,3},{5,7},{6,1},{7,5},{8,11},{9,15},{10,... | collective-permute-start | bytes 294920 | tf_op jit(solution)/shard_map/ppermute | solution.py:241
  14.4 1.3 %collective-permute-start.5 = (bf16[32,1536]{1,0:T(8,128)(2,1)S(1)}, bf16[32,1536]{1,0:T(8,128)(2,1)S(1)}, u32[]{:S(2)}, u32[]{:S(2)}) collective-permute-start(bf16[32,1536]{1,0:T(8,128)(2,1)S(1)} %copy-done.9), channel_id=1, source_target_pairs={{0,4},{2,6},{5,1},{7,3},{9,13},{11,15},{12,8},{14,10},{16,20},{18,... | collective-permute-start | bytes 294920 | tf_op jit(solution)/shard_map/ppermute | solution.py:241
  15.7 2.0 %collective-permute-done.1 = bf16[192,384]{1,0:T(8,128)(2,1)S(1)} collective-permute-done((bf16[192,384]{1,0:T(8,128)(2,1)S(1)}, bf16[192,384]{1,0:T(8,128)(2,1)S(1)}, u32[]{:S(2)}, u32[]{:S(2)}) %collective-permute-start.1) | collective-permute-done | bytes 147488 | tf_op jit(solution)/shard_map/ppermute | solution.py:241
  17.8 2.8 %collective-permute-done.2 = bf16[192,384]{1,0:T(8,128)(2,1)S(1)} collective-permute-done((bf16[192,384]{1,0:T(8,128)(2,1)S(1)}, bf16[192,384]{1,0:T(8,128)(2,1)S(1)}, u32[]{:S(2)}, u32[]{:S(2)}) %collective-permute-start.2) | collective-permute-done | bytes 147488 | tf_op jit(solution)/shard_map/ppermute | solution.py:241
  21.0 1.4 %collective-permute-start.6 = (bf16[3,192,384]{2,1,0:T(8,128)(2,1)S(1)}, bf16[3,192,384]{2,1,0:T(8,128)(2,1)S(1)}, u32[]{:S(2)}, u32[]{:S(2)}) collective-permute-start(bf16[3,192,384]{2,1,0:T(8,128)(2,1)S(1)} %pad_maximum_fusion.refs_2_), channel_id=1, source_target_pairs={{0,2},{1,3},{2,0},{3,1},{4,6},{5,7},{6,4},{7,5},{8,10},{9,11},{10,... | collective-permute-start | bytes 1327112 | tf_op jit(solution)/shard_map/ppermute | solution.py:241
  22.3 1.5 %collective-permute-start.7 = (bf16[3,192,384]{2,1,0:T(8,128)(2,1)S(1)}, bf16[3,192,384]{2,1,0:T(8,128)(2,1)S(1)}, u32[]{:S(2)}, u32[]{:S(2)}) collective-permute-start(bf16[3,192,384]{2,1,0:T(8,128)(2,1)S(1)} %pad_maximum_fusion.refs_2_), channel_id=1, source_target_pairs={{0,4},{1,5},{2,6},{3,7},{4,0},{5,1},{6,2},{7,3},{8,12},{9,13},{10,... | collective-permute-start | bytes 1327112 | tf_op jit(solution)/shard_map/ppermute | solution.py:241
  23.9 1.9 %collective-permute-start.8 = (bf16[160,384]{1,0:T(8,128)(2,1)S(1)}, bf16[160,384]{1,0:T(8,128)(2,1)S(1)}, u32[]{:S(2)}, u32[]{:S(2)}) collective-permute-start(bf16[160,384]{1,0:T(8,128)(2,1)S(1)} %get-tuple-element.56), channel_id=1, source_target_pairs={{0,8},{1,9},{2,10},{3,11},{4,12},{5,13},{6,14},{7,15},{8,0},{9,1},... | collective-permute-start | bytes 368648 | tf_op jit(solution)/shard_map/ppermute | solution.py:241
  25.8 1.7 %collective-permute-start.9 = (bf16[160,384]{1,0:T(8,128)(2,1)S(1)}, bf16[160,384]{1,0:T(8,128)(2,1)S(1)}, u32[]{:S(2)}, u32[]{:S(2)}) collective-permute-start(bf16[160,384]{1,0:T(8,128)(2,1)S(1)} %get-tuple-element.56), channel_id=1, source_target_pairs={{0,16},{1,17},{2,18},{3,19},{4,20},{5,21},{6,22},{7,23},{8,24},{9,... | collective-permute-start | bytes 368648 | tf_op jit(solution)/shard_map/ppermute | solution.py:241
  27.5 2.1 %collective-permute-done.8 = bf16[160,384]{1,0:T(8,128)(2,1)S(1)} collective-permute-done((bf16[160,384]{1,0:T(8,128)(2,1)S(1)}, bf16[160,384]{1,0:T(8,128)(2,1)S(1)}, u32[]{:S(2)}, u32[]{:S(2)}) %collective-permute-start.8) | collective-permute-done | bytes 122912 | tf_op jit(solution)/shard_map/ppermute | solution.py:241
  29.6 3.8 %collective-permute-start.11 = (bf16[48,1536]{1,0:T(8,128)(2,1)S(1)}, bf16[48,1536]{1,0:T(8,128)(2,1)S(1)}, u32[]{:S(2)}, u32[]{:S(2)}) collective-permute-start(bf16[48,1536]{1,0:T(8,128)(2,1)S(1)} %pad_maximum_fusion.2), channel_id=1, source_target_pairs={{1,9},{3,11},{5,13},{7,15},{8,16},{9,1},{10,18},{11,3},{12,20},{13... | collective-permute-start | bytes 442376 | tf_op jit(solution)/shard_map/ppermute | solution.py:241
  33.4 1.6 %collective-permute-done.9 = bf16[160,384]{1,0:T(8,128)(2,1)S(1)} collective-permute-done((bf16[160,384]{1,0:T(8,128)(2,1)S(1)}, bf16[160,384]{1,0:T(8,128)(2,1)S(1)}, u32[]{:S(2)}, u32[]{:S(2)}) %collective-permute-start.9) | collective-permute-done | bytes 122912 | tf_op jit(solution)/shard_map/ppermute | solution.py:241
  35.0 2.3 %collective-permute-done.10 = bf16[160,384]{1,0:T(8,128)(2,1)S(1)} collective-permute-done((bf16[160,384]{1,0:T(8,128)(2,1)S(1)}, bf16[160,384]{1,0:T(8,128)(2,1)S(1)}, u32[]{:S(2)}, u32[]{:S(2)}) %collective-permute-start.10) | collective-permute-done | bytes 122912 | tf_op jit(solution)/shard_map/ppermute | solution.py:241
  37.4 1.5 %collective-permute-done.11.edge = bf16[48,1536]{1,0:T(8,128)(2,1)S(1)} collective-permute-done((bf16[48,1536]{1,0:T(8,128)(2,1)S(1)}, bf16[48,1536]{1,0:T(8,128)(2,1)S(1)}, u32[]{:S(2)}, u32[]{:S(2)}) %collective-permute-start.11) | collective-permute-done | bytes 147488 | tf_op jit(solution)/shard_map/ppermute | solution.py:241
  38.9 1.5 %collective-permute-start.14 = (bf16[3,160,384]{2,1,0:T(8,128)(2,1)S(1)}, bf16[3,160,384]{2,1,0:T(8,128)(2,1)S(1)}, u32[]{:S(2)}, u32[]{:S(2)}) collective-permute-start(bf16[3,160,384]{2,1,0:T(8,128)(2,1)S(1)} %pad_maximum_fusion.1.refs_2_), channel_id=1, source_target_pairs={{0,2},{1,3},{2,0},{3,1},{4,6},{5,7},{6,4},{7,5},{8,10},{9,11},{10,... | collective-permute-start | bytes 1105928 | tf_op jit(solution)/shard_map/ppermute | solution.py:241
  40.7 1.8 %collective-permute-start.12 = (bf16[3,96,384]{2,1,0:T(8,128)(2,1)S(1)}, bf16[3,96,384]{2,1,0:T(8,128)(2,1)S(1)}, u32[]{:S(2)}, u32[]{:S(2)}) collective-permute-start(bf16[3,96,384]{2,1,0:T(8,128)(2,1)S(1)} %slice.48), channel_id=1, source_target_pairs={{0,4},{1,5},{2,6},{3,7},{4,0},{5,1},{6,2},{7,3},{8,12},{9,13},{10,... | collective-permute-start | bytes 663560 | tf_op jit(solution)/shard_map/ppermute | solution.py:241
  42.5 0.6 collective-permute-start.13
  43.2 9.7 %collective-permute-done.12.refs_5_ = bf16[3,96,384]{2,1,0:T(8,128)(2,1)S(1)} collective-permute-done((bf16[3,96,384]{2,1,0:T(8,128)(2,1)S(1)}, bf16[3,96,384]{2,1,0:T(8,128)(2,1)S(1)}, u32[]{:S(2)}, u32[]{:S(2)}) %collective-permute-start.12) | collective-permute-done | bytes 221216 | tf_op jit(solution)/shard_map/ppermute | solution.py:241
  53.4 0.6 collective-permute-start.24
  54.4 0.5 collective-permute-start.25
  55.0 3.2 %collective-permute-done.24.cot_beside = bf16[32,1536]{1,0:T(8,128)(2,1)S(1)} collective-permute-done((bf16[32,1536]{1,0:T(8,128)(2,1)S(1)}, bf16[32,1536]{1,0:T(8,128)(2,1)S(1)}, u32[]{:S(2)}, u32[]{:S(2)}) %collective-permute-start.24) | collective-permute-done | bytes 98336 | tf_op jit(solution)/shard_map/ppermute | solution.py:241
  58.2 0.6 collective-permute-start.28
  58.8 0.5 collective-permute-start.20
  59.3 1.1 %collective-permute-done.27.refs_5_ = bf16[3,80,384]{2,1,0:T(8,128)(2,1)S(1)} collective-permute-done((bf16[3,80,384]{2,1,0:T(8,128)(2,1)S(1)}, bf16[3,80,384]{2,1,0:T(8,128)(2,1)S(1)}, u32[]{:S(2)}, u32[]{:S(2)}) %collective-permute-start.27) | collective-permute-done | bytes 184352 | tf_op jit(solution)/shard_map/ppermute | solution.py:241
  60.4 3.6 %collective-permute-done.28.refs_6_ = bf16[3,80,384]{2,1,0:T(8,128)(2,1)S(1)} collective-permute-done((bf16[3,80,384]{2,1,0:T(8,128)(2,1)S(1)}, bf16[3,80,384]{2,1,0:T(8,128)(2,1)S(1)}, u32[]{:S(2)}, u32[]{:S(2)}) %collective-permute-start.28) | collective-permute-done | bytes 184352 | tf_op jit(solution)/shard_map/ppermute | solution.py:241
  64.0 0.5 collective-permute-start.23
  64.5 1.0 collective-permute-done.22.refs_10_
  66.8 5.1 %shard_map.101 = (bf16[192,1536]{1,0:T(8,128)(2,1)S(1)}, f32[128,1536]{1,0:T(8,128)S(1)}, f32[128,1]{1,0:T(8,128)S(1)}, f32[128,384]{1,0:T(8,128)S(1)}, bf16[3,1...) custom-call(bf16[32,1536]{1,0:T(8,128)(2,1)S(1)} %collective-permute-done.3.blocks_even, ...), custom_call_target="tpu_custom_call" | custom-call | tf_op jit(solution)/shard_map/pallas_call | solution.py:633
  72.0 5.6 %shard_map.102 = (f32[128,256]{1,0:T(8,128)S(1)}, f32[128,640]{1,0:T(8,128)S(1)}, bf16[32,640]{1,0:T(8,128)(2,1)S(1)}, bf16[1536,896]{1,0:T(8,128)(2,1)S(1)}, bf16[128,1536]{1,0:T(8,128)(2,1)S(1)}) custom-call(s32[4]{0:T(128)S(1)} %copy-done.8, s32[1]{0:T(128)} %bitcast.3.flag, bf16[192,1536]{1,0:T(8,128)(2,1)S(1)} %get-tuple-element.75.normed, ...), custom_call_target="tpu_custom_call" | custom-call | tf_op jit(solution)/shard_map/pallas_call | solution.py:649
  77.6 3.1 %collective-permute-start.34 = (bf16[32,640]{1,0:T(8,128)(2,1)S(1)}, bf16[32,640]{1,0:T(8,128)(2,1)S(1)}, u32[]{:S(2)}, u32[]{:S(2)}) collective-permute-start(bf16[32,640]{1,0:T(8,128)(2,1)S(1)} %get-tuple-element.82), channel_id=1, source_target_pairs={{1,9},{3,11},{5,13},{7,15},{8,16},{9,1},{10,18},{11,3},{12,20},{13... | collective-permute-start | bytes 122888 | tf_op jit(solution)/shard_map/ppermute | solution.py:241
  80.7 2.8 %collective-permute-done.34.received = bf16[32,640]{1,0:T(8,128)(2,1)S(1)} collective-permute-done((bf16[32,640]{1,0:T(8,128)(2,1)S(1)}, bf16[32,640]{1,0:T(8,128)(2,1)S(1)}, u32[]{:S(2)}, u32[]{:S(2)}) %collective-permute-start.34) | collective-permute-done | bytes 40992 | tf_op jit(solution)/shard_map/ppermute | solution.py:241
  83.5 3.1 %shard_map.103 = (bf16[128,384]{1,0:T(8,128)(2,1)S(1)}, f32[64,1536]{1,0:T(8,128)S(1)}, bf16[16,384]{1,0:T(8,128)(2,1)S(1)}) custom-call(f32[128,256]{1,0:T(8,128)S(1)} %get-tuple-element.80.d_q, f32[128,640]{1,0:T(8,128)S(1)} %get-tuple-element.81.d_kv, bf16[32,640]{1,0:T(8,128)(2,1)S(1)} %collective-permute-done.34.received, ...), custom_call_target="tpu_custom_call" | custom-call | tf_op jit(solution)/shard_map/pallas_call | solution.py:665
  86.7 3.1 %collective-permute-start.35 = (bf16[16,384]{1,0:T(8,128)(2,1)S(1)}, bf16[16,384]{1,0:T(8,128)(2,1)S(1)}, u32[]{:S(2)}, u32[]{:S(2)}) collective-permute-start(bf16[16,384]{1,0:T(8,128)(2,1)S(1)} %get-tuple-element.90), channel_id=1, source_target_pairs={{1,9},{3,11},{5,13},{7,15},{8,16},{9,1},{10,18},{11,3},{12,20},{13... | collective-permute-start | bytes 36872 | tf_op jit(solution)/shard_map/ppermute | solution.py:241
  89.7 2.5 %collective-permute-done.35.received = bf16[16,384]{1,0:T(8,128)(2,1)S(1)} collective-permute-done((bf16[16,384]{1,0:T(8,128)(2,1)S(1)}, bf16[16,384]{1,0:T(8,128)(2,1)S(1)}, u32[]{:S(2)}, u32[]{:S(2)}) %collective-permute-start.35) | collective-permute-done | bytes 12320 | tf_op jit(solution)/shard_map/ppermute | solution.py:241
  92.2 1.8 %shard_map.104 = (f32[32,1536]{1,0:T(8,128)S(1)}, bf16[32,1536]{1,0:T(8,128)(2,1)S(1)}) custom-call(bf16[128,384]{1,0:T(8,128)(2,1)S(1)} %get-tuple-element.89.d_hidden, bf16[16,384]{1,0:T(8,128)(2,1)S(1)} %collective-permute-done.35.received, f32[64,1536]{1,0:T(8,128)S(1)} %get-tuple-element.91.d_resid, ...), custom_call_target="tpu_custom_call" | custom-call | tf_op jit(solution)/shard_map/pallas_call | solution.py:677
  94.0 0.6 collective-permute-start.36
  94.7 4.1 %collective-permute-done.36 = bf16[32,1536]{1,0:T(8,128)(2,1)S(1)} collective-permute-done((bf16[32,1536]{1,0:T(8,128)(2,1)S(1)}, bf16[32,1536]{1,0:T(8,128)(2,1)S(1)}, u32[]{:S(2)}, u32[]{:S(2)}) %collective-permute-start.36) | collective-permute-done | bytes 98336 | tf_op jit(solution)/shard_map/ppermute | solution.py:241
  99.1 1.9 %collective-permute-start.38 = (bf16[32,1536]{1,0:T(8,128)(2,1)S(1)}, bf16[32,1536]{1,0:T(8,128)(2,1)S(1)}, u32[]{:S(2)}, u32[]{:S(2)}) collective-permute-start(bf16[32,1536]{1,0:T(8,128)(2,1)S(1)} %add_convert_fusion.1), channel_id=1, source_target_pairs={{1,4},{3,6},{4,1},{6,3},{8,13},{10,15},{13,8},{15,10},{17,20},{19,... | collective-permute-start | bytes 294920 | tf_op jit(solution)/shard_map/ppermute | solution.py:241
  101.3 3.7 %collective-permute-done.38 = bf16[32,1536]{1,0:T(8,128)(2,1)S(1)} collective-permute-done((bf16[32,1536]{1,0:T(8,128)(2,1)S(1)}, bf16[32,1536]{1,0:T(8,128)(2,1)S(1)}, u32[]{:S(2)}, u32[]{:S(2)}) %collective-permute-start.38) | collective-permute-done | bytes 98336 | tf_op jit(solution)/shard_map/ppermute | solution.py:241
  105.1 0.7 add_multiply_fusion
  (76 shorter events, 4.5 us)
Async XLA Ops:
  0.0 1.2 %copy-start = (bf16[3,384,384]{2,1,0:T(8,128)(2,1)S(1)}, bf16[3,384,384]{2,1,0:T(8,128)(2,1)}, u32[]{:S(2)}) copy-start(bf16[3,384,384]{2,1,0:T(8,128)(2,1)} %refs_0_.2) | copy-start | bytes 2654212
  4.2 5.6 %copy-start.11 = (s32[16,2]{0,1:T(2,128)S(1)}, s32[16,2]{0,1:T(2,128)}, u32[]{:S(2)}) copy-start(s32[16,2]{0,1:T(2,128)} %param.19) | copy-start | bytes 388
  4.2 10.3 %copy-start.9 = (bf16[32,1536]{1,0:T(8,128)(2,1)S(1)}, bf16[32,1536]{1,0:T(8,128)(2,1)}, u32[]{:S(2)}) copy-start(bf16[32,1536]{1,0:T(8,128)(2,1)} %param.12) | copy-start | bytes 294916
  4.2 6.9 %collective-permute-start = (bf16[192,384]{1,0:T(8,128)(2,1)S(1)}, bf16[192,384]{1,0:T(8,128)(2,1)S(1)}, u32[]{:S(2)}, u32[]{:S(2)}) collective-permute-start(bf16[192,384]{1,0:T(8,128)(2,1)S(1)} %get-tuple-element.50), channel_id=1, source_target_pairs={{0,8},{1,9},{2,10},{3,11},{4,12},{5,13},{6,14},{7,15},{8,0},{9,1},... | collective-permute-start | bytes 442376 | tf_op jit(solution)/shard_map/ppermute | solution.py:241
  4.3 13.4 %collective-permute-start.1 = (bf16[192,384]{1,0:T(8,128)(2,1)S(1)}, bf16[192,384]{1,0:T(8,128)(2,1)S(1)}, u32[]{:S(2)}, u32[]{:S(2)}) collective-permute-start(bf16[192,384]{1,0:T(8,128)(2,1)S(1)} %get-tuple-element.50), channel_id=1, source_target_pairs={{0,16},{1,17},{2,18},{3,19},{4,20},{5,21},{6,22},{7,23},{8,24},{9,... | collective-permute-start | bytes 442376 | tf_op jit(solution)/shard_map/ppermute | solution.py:241
  7.3 13.3 %collective-permute-start.2 = (bf16[192,384]{1,0:T(8,128)(2,1)S(1)}, bf16[192,384]{1,0:T(8,128)(2,1)S(1)}, u32[]{:S(2)}, u32[]{:S(2)}) collective-permute-start(bf16[192,384]{1,0:T(8,128)(2,1)S(1)} %get-tuple-element.50), channel_id=1, source_target_pairs={{0,24},{1,25},{2,26},{3,27},{4,28},{5,29},{6,30},{7,31},{8,16},{9,... | collective-permute-start | bytes 442376 | tf_op jit(solution)/shard_map/ppermute | solution.py:241
  8.7 58.1 %copy-start.10 = (f32[1536]{0:T(1024)S(1)}, f32[1536]{0:T(1024)}, u32[]{:S(2)}) copy-start(f32[1536]{0:T(1024)} %param.15) | copy-start | bytes 18436
  8.7 58.1 %copy-start.1 = (bf16[3,384,384]{2,1,0:T(8,128)(2,1)S(1)}, bf16[3,384,384]{2,1,0:T(8,128)(2,1)}, u32[]{:S(2)}) copy-start(bf16[3,384,384]{2,1,0:T(8,128)(2,1)} %refs_0_.2) | copy-start | bytes 2654212
  8.7 58.1 %copy-start.5 = (bf16[96,1536]{1,0:T(8,128)(2,1)S(1)}, bf16[96,1536]{1,0:T(8,128)(2,1)}, u32[]{:S(2)}) copy-start(bf16[96,1536]{1,0:T(8,128)(2,1)} %refs_1_.2) | copy-start | bytes 884740
  11.1 9.5 %collective-permute-start.3 = (bf16[32,1536]{1,0:T(8,128)(2,1)S(1)}, bf16[32,1536]{1,0:T(8,128)(2,1)S(1)}, u32[]{:S(2)}, u32[]{:S(2)}) collective-permute-start(bf16[32,1536]{1,0:T(8,128)(2,1)S(1)} %get-tuple-element.97), channel_id=1, source_target_pairs={{0,0},{1,4},{2,2},{3,6},{4,1},{5,5},{6,3},{7,7},{8,9},{9,13},{10,1... | collective-permute-start | bytes 294920 | tf_op jit(solution)/shard_map/ppermute | solution.py:241
  13.1 7.6 %collective-permute-start.4 = (bf16[32,1536]{1,0:T(8,128)(2,1)S(1)}, bf16[32,1536]{1,0:T(8,128)(2,1)S(1)}, u32[]{:S(2)}, u32[]{:S(2)}) collective-permute-start(bf16[32,1536]{1,0:T(8,128)(2,1)S(1)} %get-tuple-element.98), channel_id=1, source_target_pairs={{0,2},{1,6},{2,0},{3,4},{4,3},{5,7},{6,1},{7,5},{8,11},{9,15},{10,... | collective-permute-start | bytes 294920 | tf_op jit(solution)/shard_map/ppermute | solution.py:241
  14.4 6.5 %collective-permute-start.5 = (bf16[32,1536]{1,0:T(8,128)(2,1)S(1)}, bf16[32,1536]{1,0:T(8,128)(2,1)S(1)}, u32[]{:S(2)}, u32[]{:S(2)}) collective-permute-start(bf16[32,1536]{1,0:T(8,128)(2,1)S(1)} %copy-done.9), channel_id=1, source_target_pairs={{0,4},{2,6},{5,1},{7,3},{9,13},{11,15},{12,8},{14,10},{16,20},{18,... | collective-permute-start | bytes 294920 | tf_op jit(solution)/shard_map/ppermute | solution.py:241
  21.0 18.0 %collective-permute-start.6 = (bf16[3,192,384]{2,1,0:T(8,128)(2,1)S(1)}, bf16[3,192,384]{2,1,0:T(8,128)(2,1)S(1)}, u32[]{:S(2)}, u32[]{:S(2)}) collective-permute-start(bf16[3,192,384]{2,1,0:T(8,128)(2,1)S(1)} %pad_maximum_fusion.refs_2_), channel_id=1, source_target_pairs={{0,2},{1,3},{2,0},{3,1},{4,6},{5,7},{6,4},{7,5},{8,10},{9,11},{10,... | collective-permute-start | bytes 1327112 | tf_op jit(solution)/shard_map/ppermute | solution.py:241
  22.3 16.6 %collective-permute-start.7 = (bf16[3,192,384]{2,1,0:T(8,128)(2,1)S(1)}, bf16[3,192,384]{2,1,0:T(8,128)(2,1)S(1)}, u32[]{:S(2)}, u32[]{:S(2)}) collective-permute-start(bf16[3,192,384]{2,1,0:T(8,128)(2,1)S(1)} %pad_maximum_fusion.refs_2_), channel_id=1, source_target_pairs={{0,4},{1,5},{2,6},{3,7},{4,0},{5,1},{6,2},{7,3},{8,12},{9,13},{10,... | collective-permute-start | bytes 1327112 | tf_op jit(solution)/shard_map/ppermute | solution.py:241
  23.9 5.7 %collective-permute-start.8 = (bf16[160,384]{1,0:T(8,128)(2,1)S(1)}, bf16[160,384]{1,0:T(8,128)(2,1)S(1)}, u32[]{:S(2)}, u32[]{:S(2)}) collective-permute-start(bf16[160,384]{1,0:T(8,128)(2,1)S(1)} %get-tuple-element.56), channel_id=1, source_target_pairs={{0,8},{1,9},{2,10},{3,11},{4,12},{5,13},{6,14},{7,15},{8,0},{9,1},... | collective-permute-start | bytes 368648 | tf_op jit(solution)/shard_map/ppermute | solution.py:241
  25.8 9.2 %collective-permute-start.9 = (bf16[160,384]{1,0:T(8,128)(2,1)S(1)}, bf16[160,384]{1,0:T(8,128)(2,1)S(1)}, u32[]{:S(2)}, u32[]{:S(2)}) collective-permute-start(bf16[160,384]{1,0:T(8,128)(2,1)S(1)} %get-tuple-element.56), channel_id=1, source_target_pairs={{0,16},{1,17},{2,18},{3,19},{4,20},{5,21},{6,22},{7,23},{8,24},{9,... | collective-permute-start | bytes 368648 | tf_op jit(solution)/shard_map/ppermute | solution.py:241
  27.5 9.9 %collective-permute-start.10 = (bf16[160,384]{1,0:T(8,128)(2,1)S(1)}, bf16[160,384]{1,0:T(8,128)(2,1)S(1)}, u32[]{:S(2)}, u32[]{:S(2)}) collective-permute-start(bf16[160,384]{1,0:T(8,128)(2,1)S(1)} %get-tuple-element.56), channel_id=1, source_target_pairs={{0,24},{1,25},{2,26},{3,27},{4,28},{5,29},{6,30},{7,31},{8,16},{9,... | collective-permute-start | bytes 368648 | tf_op jit(solution)/shard_map/ppermute | solution.py:241
  29.6 9.3 %collective-permute-start.11 = (bf16[48,1536]{1,0:T(8,128)(2,1)S(1)}, bf16[48,1536]{1,0:T(8,128)(2,1)S(1)}, u32[]{:S(2)}, u32[]{:S(2)}) collective-permute-start(bf16[48,1536]{1,0:T(8,128)(2,1)S(1)} %pad_maximum_fusion.2), channel_id=1, source_target_pairs={{1,9},{3,11},{5,13},{7,15},{8,16},{9,1},{10,18},{11,3},{12,20},{13... | collective-permute-start | bytes 442376 | tf_op jit(solution)/shard_map/ppermute | solution.py:241
  38.9 13.9 %collective-permute-start.14 = (bf16[3,160,384]{2,1,0:T(8,128)(2,1)S(1)}, bf16[3,160,384]{2,1,0:T(8,128)(2,1)S(1)}, u32[]{:S(2)}, u32[]{:S(2)}) collective-permute-start(bf16[3,160,384]{2,1,0:T(8,128)(2,1)S(1)} %pad_maximum_fusion.1.refs_2_), channel_id=1, source_target_pairs={{0,2},{1,3},{2,0},{3,1},{4,6},{5,7},{6,4},{7,5},{8,10},{9,11},{10,... | collective-permute-start | bytes 1105928 | tf_op jit(solution)/shard_map/ppermute | solution.py:241
  40.4 12.4 %collective-permute-start.15 = (bf16[3,160,384]{2,1,0:T(8,128)(2,1)S(1)}, bf16[3,160,384]{2,1,0:T(8,128)(2,1)S(1)}, u32[]{:S(2)}, u32[]{:S(2)}) collective-permute-start(bf16[3,160,384]{2,1,0:T(8,128)(2,1)S(1)} %pad_maximum_fusion.1.refs_2_), channel_id=1, source_target_pairs={{0,4},{1,5},{2,6},{3,7},{4,0},{5,1},{6,2},{7,3},{8,12},{9,13},{10,... | collective-permute-start | bytes 1105928 | tf_op jit(solution)/shard_map/ppermute | solution.py:241
  40.7 12.1 %collective-permute-start.12 = (bf16[3,96,384]{2,1,0:T(8,128)(2,1)S(1)}, bf16[3,96,384]{2,1,0:T(8,128)(2,1)S(1)}, u32[]{:S(2)}, u32[]{:S(2)}) collective-permute-start(bf16[3,96,384]{2,1,0:T(8,128)(2,1)S(1)} %slice.48), channel_id=1, source_target_pairs={{0,4},{1,5},{2,6},{3,7},{4,0},{5,1},{6,2},{7,3},{8,12},{9,13},{10,... | collective-permute-start | bytes 663560 | tf_op jit(solution)/shard_map/ppermute | solution.py:241
  42.5 10.3 %collective-permute-start.13 = (bf16[3,96,384]{2,1,0:T(8,128)(2,1)S(1)}, bf16[3,96,384]{2,1,0:T(8,128)(2,1)S(1)}, u32[]{:S(2)}, u32[]{:S(2)}) collective-permute-start(bf16[3,96,384]{2,1,0:T(8,128)(2,1)S(1)} %slice.49), channel_id=1, source_target_pairs={{0,2},{1,3},{2,0},{3,1},{4,6},{5,7},{6,4},{7,5},{8,10},{9,11},{10,... | collective-permute-start | bytes 663560 | tf_op jit(solution)/shard_map/ppermute | solution.py:241
  52.8 1.5 %collective-permute-start.16 = (bf16[32,1536]{1,0:T(8,128)(2,1)S(1)}, bf16[32,1536]{1,0:T(8,128)(2,1)S(1)}, u32[]{:S(2)}, u32[]{:S(2)}) collective-permute-start(bf16[32,1536]{1,0:T(8,128)(2,1)S(1)} %collective-permute-done.3.blocks_even), channel_id=1, source_target_pairs={{0,1},{1,0},{2,3},{3,2},{4,5},{5,4},{6,7},{7,6},{8,9},{9,8},{10,11... | collective-permute-start | bytes 294920 | tf_op jit(solution)/shard_map/ppermute | solution.py:241
  52.9 2.0 %collective-permute-start.17 = (bf16[32,1536]{1,0:T(8,128)(2,1)S(1)}, bf16[32,1536]{1,0:T(8,128)(2,1)S(1)}, u32[]{:S(2)}, u32[]{:S(2)}) collective-permute-start(bf16[32,1536]{1,0:T(8,128)(2,1)S(1)} %collective-permute-done.4.blocks_odd), channel_id=1, source_target_pairs={{0,1},{1,0},{2,3},{3,2},{4,5},{5,4},{6,7},{7,6},{8,9},{9,8},{10,11... | collective-permute-start | bytes 294920 | tf_op jit(solution)/shard_map/ppermute | solution.py:241
  53.4 4.8 %collective-permute-start.24 = (bf16[32,1536]{1,0:T(8,128)(2,1)S(1)}, bf16[32,1536]{1,0:T(8,128)(2,1)S(1)}, u32[]{:S(2)}, u32[]{:S(2)}) collective-permute-start(bf16[32,1536]{1,0:T(8,128)(2,1)S(1)} %broadcast_select_fusion.cot_block), channel_id=1, source_target_pairs={{0,2},{1,3},{2,0},{3,1},{4,6},{5,7},{6,4},{7,5},{8,10},{9,11},{10,... | collective-permute-start | bytes 294920 | tf_op jit(solution)/shard_map/ppermute | solution.py:241
  54.0 6.4 %collective-permute-start.27 = (bf16[3,80,384]{2,1,0:T(8,128)(2,1)S(1)}, bf16[3,80,384]{2,1,0:T(8,128)(2,1)S(1)}, u32[]{:S(2)}, u32[]{:S(2)}) collective-permute-start(bf16[3,80,384]{2,1,0:T(8,128)(2,1)S(1)} %slice.50), channel_id=1, source_target_pairs={{0,4},{1,5},{2,6},{3,7},{4,0},{5,1},{6,2},{7,3},{8,12},{9,13},{10,... | collective-permute-start | bytes 552968 | tf_op jit(solution)/shard_map/ppermute | solution.py:241
  54.3 11.6 %collective-permute-start.19 = (bf16[3,192,384]{2,1,0:T(8,128)(2,1)S(1)}, bf16[3,192,384]{2,1,0:T(8,128)(2,1)S(1)}, u32[]{:S(2)}, u32[]{:S(2)}) collective-permute-start(bf16[3,192,384]{2,1,0:T(8,128)(2,1)S(1)} %pad_maximum_fusion.refs_2_), channel_id=1, source_target_pairs={{0,1},{1,0},{2,3},{3,2},{4,5},{5,4},{6,7},{7,6},{8,9},{9,8},{10,11... | collective-permute-start | bytes 1327112 | tf_op jit(solution)/shard_map/ppermute | solution.py:241
  54.4 4.4 %collective-permute-start.25 = (bf16[32,1536]{1,0:T(8,128)(2,1)S(1)}, bf16[32,1536]{1,0:T(8,128)(2,1)S(1)}, u32[]{:S(2)}, u32[]{:S(2)}) collective-permute-start(bf16[32,1536]{1,0:T(8,128)(2,1)S(1)} %broadcast_select_fusion.cot_block), channel_id=1, source_target_pairs={{0,1},{1,0},{2,3},{3,2},{4,5},{5,4},{6,7},{7,6},{8,9},{9,8},{10,11... | collective-permute-start | bytes 294920 | tf_op jit(solution)/shard_map/ppermute | solution.py:241
  54.9 17.1 %copy-start.3 = (bf16[384,896]{1,0:T(8,128)(2,1)S(1)}, bf16[384,896]{1,0:T(8,128)(2,1)}, u32[]{:S(2)}) copy-start(bf16[384,896]{1,0:T(8,128)(2,1)} %refs_0_.3) | copy-start | bytes 2064388
  54.9 17.1 %copy-start.7 = (bf16[96,1536]{1,0:T(8,128)(2,1)S(1)}, bf16[96,1536]{1,0:T(8,128)(2,1)}, u32[]{:S(2)}) copy-start(bf16[96,1536]{1,0:T(8,128)(2,1)} %refs_1_.3) | copy-start | bytes 884740
  54.9 17.1 %copy-start.8 = (s32[4]{0:T(128)S(1)}, s32[4]{0:T(128)}, u32[]{:S(2)}) copy-start(s32[4]{0:T(128)} %band.1) | copy-start | bytes 52
  54.9 3.8 %collective-permute-start.18 = (bf16[48,1536]{1,0:T(8,128)(2,1)S(1)}, bf16[48,1536]{1,0:T(8,128)(2,1)S(1)}, u32[]{:S(2)}, u32[]{:S(2)}) collective-permute-start(bf16[48,1536]{1,0:T(8,128)(2,1)S(1)} %collective-permute-done.11.edge), channel_id=1, source_target_pairs={{0,1},{1,0},{2,3},{3,2},{4,5},{5,4},{6,7},{7,6},{8,9},{9,8},{10,11... | collective-permute-start | bytes 442376 | tf_op jit(solution)/shard_map/ppermute | solution.py:241
  58.2 5.8 %collective-permute-start.28 = (bf16[3,80,384]{2,1,0:T(8,128)(2,1)S(1)}, bf16[3,80,384]{2,1,0:T(8,128)(2,1)S(1)}, u32[]{:S(2)}, u32[]{:S(2)}) collective-permute-start(bf16[3,80,384]{2,1,0:T(8,128)(2,1)S(1)} %slice.51), channel_id=1, source_target_pairs={{0,2},{1,3},{2,0},{3,1},{4,6},{5,7},{6,4},{7,5},{8,10},{9,11},{10,... | collective-permute-start | bytes 552968 | tf_op jit(solution)/shard_map/ppermute | solution.py:241
  58.8 5.2 %collective-permute-start.26 = (bf16[32,1536]{1,0:T(8,128)(2,1)S(1)}, bf16[32,1536]{1,0:T(8,128)(2,1)S(1)}, u32[]{:S(2)}, u32[]{:S(2)}) collective-permute-start(bf16[32,1536]{1,0:T(8,128)(2,1)S(1)} %collective-permute-done.24.cot_beside), channel_id=1, source_target_pairs={{0,1},{1,0},{2,3},{3,2},{4,5},{5,4},{6,7},{7,6},{8,9},{9,8},{10,11... | collective-permute-start | bytes 294920 | tf_op jit(solution)/shard_map/ppermute | solution.py:241
  58.8 7.5 %collective-permute-start.20 = (bf16[3,192,384]{2,1,0:T(8,128)(2,1)S(1)}, bf16[3,192,384]{2,1,0:T(8,128)(2,1)S(1)}, u32[]{:S(2)}, u32[]{:S(2)}) collective-permute-start(bf16[3,192,384]{2,1,0:T(8,128)(2,1)S(1)} %collective-permute-done.6.refs_3_), channel_id=1, source_target_pairs={{0,1},{1,0},{2,3},{3,2},{4,5},{5,4},{6,7},{7,6},{8,9},{9,8},{10,11... | collective-permute-start | bytes 1327112 | tf_op jit(solution)/shard_map/ppermute | solution.py:241
  60.4 6.1 %collective-permute-start.21 = (bf16[3,192,384]{2,1,0:T(8,128)(2,1)S(1)}, bf16[3,192,384]{2,1,0:T(8,128)(2,1)S(1)}, u32[]{:S(2)}, u32[]{:S(2)}) collective-permute-start(bf16[3,192,384]{2,1,0:T(8,128)(2,1)S(1)} %collective-permute-done.7.refs_4_), channel_id=1, source_target_pairs={{0,1},{1,0},{2,3},{3,2},{4,5},{5,4},{6,7},{7,6},{8,9},{9,8},{10,11... | collective-permute-start | bytes 1327112 | tf_op jit(solution)/shard_map/ppermute | solution.py:241
  64.0 1.5 %collective-permute-start.22 = (bf16[3,96,384]{2,1,0:T(8,128)(2,1)S(1)}, bf16[3,96,384]{2,1,0:T(8,128)(2,1)S(1)}, u32[]{:S(2)}, u32[]{:S(2)}) collective-permute-start(bf16[3,96,384]{2,1,0:T(8,128)(2,1)S(1)} %collective-permute-done.12.refs_5_), channel_id=1, source_target_pairs={{0,1},{1,0},{2,3},{3,2},{4,5},{5,4},{6,7},{7,6},{8,9},{9,8},{10,11... | collective-permute-start | bytes 663560 | tf_op jit(solution)/shard_map/ppermute | solution.py:241
  64.0 1.8 %collective-permute-start.23 = (bf16[3,96,384]{2,1,0:T(8,128)(2,1)S(1)}, bf16[3,96,384]{2,1,0:T(8,128)(2,1)S(1)}, u32[]{:S(2)}, u32[]{:S(2)}) collective-permute-start(bf16[3,96,384]{2,1,0:T(8,128)(2,1)S(1)} %collective-permute-done.13.refs_6_), channel_id=1, source_target_pairs={{0,1},{1,0},{2,3},{3,2},{4,5},{5,4},{6,7},{7,6},{8,9},{9,8},{10,11... | collective-permute-start | bytes 663560 | tf_op jit(solution)/shard_map/ppermute | solution.py:241
  65.5 6.5 %collective-permute-start.30 = (bf16[3,160,384]{2,1,0:T(8,128)(2,1)S(1)}, bf16[3,160,384]{2,1,0:T(8,128)(2,1)S(1)}, u32[]{:S(2)}, u32[]{:S(2)}) collective-permute-start(bf16[3,160,384]{2,1,0:T(8,128)(2,1)S(1)} %collective-permute-done.14.refs_3_), channel_id=1, source_target_pairs={{0,1},{1,0},{2,3},{3,2},{4,5},{5,4},{6,7},{7,6},{8,9},{9,8},{10,11... | collective-permute-start | bytes 1105928 | tf_op jit(solution)/shard_map/ppermute | solution.py:241
  65.8 6.2 %collective-permute-start.29 = (bf16[3,160,384]{2,1,0:T(8,128)(2,1)S(1)}, bf16[3,160,384]{2,1,0:T(8,128)(2,1)S(1)}, u32[]{:S(2)}, u32[]{:S(2)}) collective-permute-start(bf16[3,160,384]{2,1,0:T(8,128)(2,1)S(1)} %pad_maximum_fusion.1.refs_2_), channel_id=1, source_target_pairs={{0,1},{1,0},{2,3},{3,2},{4,5},{5,4},{6,7},{7,6},{8,9},{9,8},{10,11... | collective-permute-start | bytes 1105928 | tf_op jit(solution)/shard_map/ppermute | solution.py:241
  66.0 6.0 %collective-permute-start.31 = (bf16[3,160,384]{2,1,0:T(8,128)(2,1)S(1)}, bf16[3,160,384]{2,1,0:T(8,128)(2,1)S(1)}, u32[]{:S(2)}, u32[]{:S(2)}) collective-permute-start(bf16[3,160,384]{2,1,0:T(8,128)(2,1)S(1)} %collective-permute-done.15.refs_4_), channel_id=1, source_target_pairs={{0,1},{1,0},{2,3},{3,2},{4,5},{5,4},{6,7},{7,6},{8,9},{9,8},{10,11... | collective-permute-start | bytes 1105928 | tf_op jit(solution)/shard_map/ppermute | solution.py:241
  66.3 5.7 %collective-permute-start.32 = (bf16[3,80,384]{2,1,0:T(8,128)(2,1)S(1)}, bf16[3,80,384]{2,1,0:T(8,128)(2,1)S(1)}, u32[]{:S(2)}, u32[]{:S(2)}) collective-permute-start(bf16[3,80,384]{2,1,0:T(8,128)(2,1)S(1)} %collective-permute-done.27.refs_5_), channel_id=1, source_target_pairs={{0,1},{1,0},{2,3},{3,2},{4,5},{5,4},{6,7},{7,6},{8,9},{9,8},{10,11... | collective-permute-start | bytes 552968 | tf_op jit(solution)/shard_map/ppermute | solution.py:241
  66.5 5.5 %collective-permute-start.33 = (bf16[3,80,384]{2,1,0:T(8,128)(2,1)S(1)}, bf16[3,80,384]{2,1,0:T(8,128)(2,1)S(1)}, u32[]{:S(2)}, u32[]{:S(2)}) collective-permute-start(bf16[3,80,384]{2,1,0:T(8,128)(2,1)S(1)} %collective-permute-done.28.refs_6_), channel_id=1, source_target_pairs={{0,1},{1,0},{2,3},{3,2},{4,5},{5,4},{6,7},{7,6},{8,9},{9,8},{10,11... | collective-permute-start | bytes 552968 | tf_op jit(solution)/shard_map/ppermute | solution.py:241
  77.6 5.9 %collective-permute-start.34 = (bf16[32,640]{1,0:T(8,128)(2,1)S(1)}, bf16[32,640]{1,0:T(8,128)(2,1)S(1)}, u32[]{:S(2)}, u32[]{:S(2)}) collective-permute-start(bf16[32,640]{1,0:T(8,128)(2,1)S(1)} %get-tuple-element.82), channel_id=1, source_target_pairs={{1,9},{3,11},{5,13},{7,15},{8,16},{9,1},{10,18},{11,3},{12,20},{13... | collective-permute-start | bytes 122888 | tf_op jit(solution)/shard_map/ppermute | solution.py:241
  86.7 5.6 %collective-permute-start.35 = (bf16[16,384]{1,0:T(8,128)(2,1)S(1)}, bf16[16,384]{1,0:T(8,128)(2,1)S(1)}, u32[]{:S(2)}, u32[]{:S(2)}) collective-permute-start(bf16[16,384]{1,0:T(8,128)(2,1)S(1)} %get-tuple-element.90), channel_id=1, source_target_pairs={{1,9},{3,11},{5,13},{7,15},{8,16},{9,1},{10,18},{11,3},{12,20},{13... | collective-permute-start | bytes 36872 | tf_op jit(solution)/shard_map/ppermute | solution.py:241
  94.0 4.7 %collective-permute-start.36 = (bf16[32,1536]{1,0:T(8,128)(2,1)S(1)}, bf16[32,1536]{1,0:T(8,128)(2,1)S(1)}, u32[]{:S(2)}, u32[]{:S(2)}) collective-permute-start(bf16[32,1536]{1,0:T(8,128)(2,1)S(1)} %get-tuple-element.94), channel_id=1, source_target_pairs={{0,2},{1,3},{2,0},{3,1},{4,6},{5,7},{6,4},{7,5},{8,10},{9,11},{10,... | collective-permute-start | bytes 294920 | tf_op jit(solution)/shard_map/ppermute | solution.py:241
  98.8 2.6 %collective-permute-start.37 = (bf16[32,1536]{1,0:T(8,128)(2,1)S(1)}, bf16[32,1536]{1,0:T(8,128)(2,1)S(1)}, u32[]{:S(2)}, u32[]{:S(2)}) collective-permute-start(bf16[32,1536]{1,0:T(8,128)(2,1)S(1)} %add_convert_fusion.1), channel_id=1, source_target_pairs={{0,1},{1,5},{2,3},{3,7},{4,0},{5,4},{6,2},{7,6},{8,12},{9,8},{10,1... | collective-permute-start | bytes 294920 | tf_op jit(solution)/shard_map/ppermute | solution.py:241
  99.1 5.9 %collective-permute-start.38 = (bf16[32,1536]{1,0:T(8,128)(2,1)S(1)}, bf16[32,1536]{1,0:T(8,128)(2,1)S(1)}, u32[]{:S(2)}, u32[]{:S(2)}) collective-permute-start(bf16[32,1536]{1,0:T(8,128)(2,1)S(1)} %add_convert_fusion.1), channel_id=1, source_target_pairs={{1,4},{3,6},{4,1},{6,3},{8,13},{10,15},{13,8},{15,10},{17,20},{19,... | collective-permute-start | bytes 294920 | tf_op jit(solution)/shard_map/ppermute | solution.py:241
  (3 other events, 3.0 us)

commit v8 on v7

--- a/solution.py
+++ b/solution.py
@@ -263,22 +263,28 @@
     return lax.rem(lax.axis_index("noise") + lax.axis_index("sa"), 2)
 
 
-def pack_kernel(conv, mix, qkv, out, early, late):
+def pack_kernel(conv, mix, qkv, out, early, late, taps, rows_qkv, sems):
     z, y, x, n = position()
     b = 2 * y + x
     part = b * 2 + n
     rows = pl.ds(pl.multiple_of(part * 48, 16), 48)
     half = pl.ds(pl.multiple_of(n * 48, 16), 48)
     columns = pl.ds(pl.multiple_of(b * 384, 128), 384)
+    pairs = (
+        (conv.at[:, rows, :], taps), (mix.at[half, columns], early.at[pl.ds(144, 48), :]),
+        (qkv.at[rows, :], rows_qkv), (out.at[half, columns], late.at[pl.ds(0, 48), :]),
+    )
+    copies = [pltpu.make_async_copy(source, target, sems.at[i]) for i, (source, target) in enumerate(pairs)]
+    for copy in copies:
+        copy.start()
+    for copy in copies:
+        copy.wait()
     for t in range(3):
-        early[pl.ds(48 * t, 48), :] = conv[t, rows, :]
-    early[pl.ds(144, 48), :] = mix[half, columns]
-    late[pl.ds(0, 48), :] = out[half, columns]
+        early[pl.ds(48 * t, 48), :] = taps[t]
     for k in range(2):
-        late[pl.ds(48 + 48 * k, 48), :] = qkv[rows, pl.ds(384 * k, 384)]
+        late[pl.ds(48 + 48 * k, 48), :] = rows_qkv[:, pl.ds(384 * k, 384)]
     for k in range(3):
-        third = pl.ds(pl.multiple_of(part * 48 + 16 * k, 16), 16)
-        late[pl.ds(144, 16), pl.ds(128 * k, 128)] = qkv[third, pl.ds(768, 128)]
+        late[pl.ds(144, 16), pl.ds(128 * k, 128)] = rows_qkv[pl.ds(16 * k, 16), pl.ds(768, 128)]
 
 
 def nt(a, b):
@@ -561,9 +567,12 @@
     early, late = pl.pallas_call(
         pack_kernel,
         out_shape=(shaped(192, CHUNK, dtype=bf16), shaped(160, CHUNK, dtype=bf16)),
-        in_specs=vmem(4),
+        in_specs=hbm(4),
         out_specs=tuple(vmem(2)),
-        compiler_params=limit(8),
+        scratch_shapes=[
+            pltpu.VMEM((3, 48, HID), bf16), pltpu.VMEM((48, 896), bf16), pltpu.SemaphoreType.DMA((4,))
+        ],
+        compiler_params=limit(4),
     )(convolution_weight, mix_w, qkv_w, out_w)
     def along_z(step):
         return routes(n_sa, lambda z, y, x, c: (z ^ step, y, x, c))
@@ -613,20 +622,21 @@
     straight, late, flag, outer, cot_block = after((straight, late, flag, outer, cot_block))
     beside, across = permuted(straight, x_route), permuted(straight, y_route)
     late_straight = jnp.stack(over_z(late))
-    edge = permuted(outer, edge_route)
-    straight, beside, across, late_straight, edge, cot_block, *blocks = after(
-        (straight, beside, across, late_straight, edge, cot_block, *blocks)
+    straight_other = permuted(straight, core_route)
+    straight, beside, across, late_straight, outer, cot_block, straight_other, *blocks = after(
+        (straight, beside, across, late_straight, outer, cot_block, straight_other, *blocks)
     )
     early = (straight, beside, across) + diagonals(beside, across)
     late_beside, late_across = permuted(late_straight, x_route), permuted(late_straight, y_route)
-    early, late, cot_block, mine = (
-        lambda v: (v[:5], v[5:8], v[8], v[9:])
-    )(after((*early, late_straight, late_beside, late_across, cot_block, *blocks, edge)))
+    cot_rows = (cot_block, permuted(cot_block, x_route))
+    mine = (*blocks, permuted(outer, edge_route))
+    early, late, cot_rows, mine = (
+        lambda v: (v[:5], v[5:8], v[8:10], v[10:])
+    )(after((*early, late_straight, late_beside, late_across, *cot_rows, *mine)))
     late = tuple(late) + diagonals(late[1], late[2])
     noisy_rows = tuple(mine) + swapped(mine)
-    early = tuple(early) + swapped(early)
-    cot_rows = (cot_block, permuted(cot_block, x_route))
-    cot_rows = cot_rows + swapped(cot_rows)
+    early = tuple(early) + (straight_other,) + swapped(early[1:])
+    cot_rows = tuple(cot_rows) + swapped(cot_rows)
     late_other = swapped(late[:3])
     gain = norm_gain.reshape(1, features)
 
@@ -687,12 +697,10 @@
 
     received = permuted(send, x_route)
     partial = (keep + received.astype(f32)).astype(bf16)
-    first_sum = permuted(
-        partial, routes(n_sa, lambda z, y, x, c: (z, 1 - y, x, c) if y != c ^ (z & 1) else (z, y, x, 1 - c))
-    )
-    second_sum = permuted(partial, routes(n_sa, lambda z, y, x, c: (z, 1 - y, x, 1 - c) if y != c ^ (z & 1) else None))
-    other = jnp.where(y == m, partial, second_sum)
-    return (first_sum.astype(f32) + other.astype(f32)) * 0.25
+    received = permuted(partial, y_route)
+    total = (partial.astype(f32) + received.astype(f32)) * 0.25
+    swapped_total = permuted(total, core_route)
+    return jnp.where(y == m, total, swapped_total)
 
 
 def solution(mesh):

time: 106 us -> 114 us (1.075)
  starting transfers between devices: 36.4 us -> 40.8 us
  waiting for transfers between devices: 44.8 us -> 47.1 us
    ppermute x39, starting transfers between devices: 36.4 us -> 40.8 us  [permuted(): return lax.ppermute(value, ('sa', 'sb', 'noise'), pairs)]
    ppermute x39, waiting for transfers between devices: 44.8 us -> 47.1 us  [permuted(): return lax.ppermute(value, ('sa', 'sb', 'noise'), pairs)]
where the time goes in v8:
time: 114 us; the launch traced here: 113 us
  waiting for transfers between devices  47.1 us (41%)
  starting transfers between devices  40.8 us (36%)
  Pallas kernels  15.8 us (14%)
  local copies, waits for them, and re-layouts  4.32 us (4%)
  other arithmetic  3.58 us (3%)
    ppermute x39, waiting for transfers between devices, permuted(): return lax.ppermute(value, ('sa', 'sb', 'noise'), pairs)  47.1 us
    ppermute x39, starting transfers between devices, permuted(): return lax.ppermute(value, ('sa', 'sb', 'noise'), pairs)  40.8 us
    pallas_call x1, Pallas kernels, stretch_shards(): pl.pallas_call(attention_kernel, out_shape=(shaped(128, 256), shaped(128,...  5.59 us
    pallas_call x1, Pallas kernels, stretch_shards(): pl.pallas_call(forward_kernel, out_shape=(shaped(192, features, dtype=bf1...  5.1 us
    unnamed x24, local copies, waits for them, and re-layouts  4.23 us
    pallas_call x1, Pallas kernels, stretch_shards(): pl.pallas_call(norm_kernel, out_shape=(shaped(128, HID, dtype=bf16), shap...  3.12 us
  transfers between devices with their start and end apart: 39, of which 18 were waited for; matrix products, arithmetic and copies ran while one was open for 3% of the time, Pallas kernels for 5%

profile of v8, /device:TPU:8, one launch (start us, length us, event | category | flops | bytes accessed | tf_op | source)
XLA Modules:
  0.0 112.8 jit_solution(10247436029450671285)
XLA Ops:
  0.0 1.2 %copy-done = bf16[3,384,384]{2,1,0:T(8,128)(2,1)S(1)} copy-done((bf16[3,384,384]{2,1,0:T(8,128)(2,1)S(1)}, bf16[3,384,384]{2,1,0:T(8,128)(2,1)}, u32[]{:S(2)}) %copy-start) | copy-done | bytes 884760
  1.2 1.1 copy-done.2
  2.3 1.0 copy-done.4
  3.2 1.0 copy-done.6
  4.5 3.0 %collective-permute-start.1 = (bf16[192,384]{1,0:T(8,128)(2,1)S(1)}, bf16[192,384]{1,0:T(8,128)(2,1)S(1)}, u32[]{:S(2)}, u32[]{:S(2)}) collective-permute-start(bf16[192,384]{1,0:T(8,128)(2,1)S(1)} %get-tuple-element.52), channel_id=1, source_target_pairs={{0,16},{1,17},{2,18},{3,19},{4,20},{5,21},{6,22},{7,23},{8,24},{9,... | collective-permute-start | bytes 442376 | tf_op jit(solution)/shard_map/ppermute | solution.py:241
  7.5 0.5 collective-permute-start.2
  8.0 0.9 convert_element_type.22
  8.9 1.1 add_convert_fusion
  10.0 0.6 and_reduce_fusion
  11.3 1.9 %collective-permute-start.3 = (bf16[32,1536]{1,0:T(8,128)(2,1)S(1)}, bf16[32,1536]{1,0:T(8,128)(2,1)S(1)}, u32[]{:S(2)}, u32[]{:S(2)}) collective-permute-start(bf16[32,1536]{1,0:T(8,128)(2,1)S(1)} %get-tuple-element.101), channel_id=1, source_target_pairs={{0,0},{1,4},{2,2},{3,6},{4,1},{5,5},{6,3},{7,7},{8,9},{9,13},{10,1... | collective-permute-start | bytes 294920 | tf_op jit(solution)/shard_map/ppermute | solution.py:241
  13.3 1.4 %collective-permute-start.4 = (bf16[32,1536]{1,0:T(8,128)(2,1)S(1)}, bf16[32,1536]{1,0:T(8,128)(2,1)S(1)}, u32[]{:S(2)}, u32[]{:S(2)}) collective-permute-start(bf16[32,1536]{1,0:T(8,128)(2,1)S(1)} %get-tuple-element.102), channel_id=1, source_target_pairs={{0,2},{1,6},{2,0},{3,4},{4,3},{5,7},{6,1},{7,5},{8,11},{9,15},{10,... | collective-permute-start | bytes 294920 | tf_op jit(solution)/shard_map/ppermute | solution.py:241
  14.7 1.3 %collective-permute-start.5 = (bf16[32,1536]{1,0:T(8,128)(2,1)S(1)}, bf16[32,1536]{1,0:T(8,128)(2,1)S(1)}, u32[]{:S(2)}, u32[]{:S(2)}) collective-permute-start(bf16[32,1536]{1,0:T(8,128)(2,1)S(1)} %copy-done.9), channel_id=1, source_target_pairs={{0,4},{2,6},{5,1},{7,3},{9,13},{11,15},{12,8},{14,10},{16,20},{18,... | collective-permute-start | bytes 294920 | tf_op jit(solution)/shard_map/ppermute | solution.py:241
  15.9 2.0 %collective-permute-done.1 = bf16[192,384]{1,0:T(8,128)(2,1)S(1)} collective-permute-done((bf16[192,384]{1,0:T(8,128)(2,1)S(1)}, bf16[192,384]{1,0:T(8,128)(2,1)S(1)}, u32[]{:S(2)}, u32[]{:S(2)}) %collective-permute-start.1) | collective-permute-done | bytes 147488 | tf_op jit(solution)/shard_map/ppermute | solution.py:241
  18.0 2.8 %collective-permute-done.2 = bf16[192,384]{1,0:T(8,128)(2,1)S(1)} collective-permute-done((bf16[192,384]{1,0:T(8,128)(2,1)S(1)}, bf16[192,384]{1,0:T(8,128)(2,1)S(1)}, u32[]{:S(2)}, u32[]{:S(2)}) %collective-permute-start.2) | collective-permute-done | bytes 147488 | tf_op jit(solution)/shard_map/ppermute | solution.py:241
  21.2 1.4 %collective-permute-start.6 = (bf16[3,192,384]{2,1,0:T(8,128)(2,1)S(1)}, bf16[3,192,384]{2,1,0:T(8,128)(2,1)S(1)}, u32[]{:S(2)}, u32[]{:S(2)}) collective-permute-start(bf16[3,192,384]{2,1,0:T(8,128)(2,1)S(1)} %pad_maximum_fusion.refs_2_), channel_id=1, source_target_pairs={{0,2},{1,3},{2,0},{3,1},{4,6},{5,7},{6,4},{7,5},{8,10},{9,11},{10,... | collective-permute-start | bytes 1327112 | tf_op jit(solution)/shard_map/ppermute | solution.py:241
  22.6 1.5 %collective-permute-start.7 = (bf16[3,192,384]{2,1,0:T(8,128)(2,1)S(1)}, bf16[3,192,384]{2,1,0:T(8,128)(2,1)S(1)}, u32[]{:S(2)}, u32[]{:S(2)}) collective-permute-start(bf16[3,192,384]{2,1,0:T(8,128)(2,1)S(1)} %pad_maximum_fusion.refs_2_), channel_id=1, source_target_pairs={{0,4},{1,5},{2,6},{3,7},{4,0},{5,1},{6,2},{7,3},{8,12},{9,13},{10,... | collective-permute-start | bytes 1327112 | tf_op jit(solution)/shard_map/ppermute | solution.py:241
  24.1 1.9 %collective-permute-start.8 = (bf16[160,384]{1,0:T(8,128)(2,1)S(1)}, bf16[160,384]{1,0:T(8,128)(2,1)S(1)}, u32[]{:S(2)}, u32[]{:S(2)}) collective-permute-start(bf16[160,384]{1,0:T(8,128)(2,1)S(1)} %get-tuple-element.58), channel_id=1, source_target_pairs={{0,8},{1,9},{2,10},{3,11},{4,12},{5,13},{6,14},{7,15},{8,0},{9,1},... | collective-permute-start | bytes 368648 | tf_op jit(solution)/shard_map/ppermute | solution.py:241
  26.1 1.7 %collective-permute-start.9 = (bf16[160,384]{1,0:T(8,128)(2,1)S(1)}, bf16[160,384]{1,0:T(8,128)(2,1)S(1)}, u32[]{:S(2)}, u32[]{:S(2)}) collective-permute-start(bf16[160,384]{1,0:T(8,128)(2,1)S(1)} %get-tuple-element.58), channel_id=1, source_target_pairs={{0,16},{1,17},{2,18},{3,19},{4,20},{5,21},{6,22},{7,23},{8,24},{9,... | collective-permute-start | bytes 368648 | tf_op jit(solution)/shard_map/ppermute | solution.py:241
  27.7 3.6 %collective-permute-done.8 = bf16[160,384]{1,0:T(8,128)(2,1)S(1)} collective-permute-done((bf16[160,384]{1,0:T(8,128)(2,1)S(1)}, bf16[160,384]{1,0:T(8,128)(2,1)S(1)}, u32[]{:S(2)}, u32[]{:S(2)}) %collective-permute-start.8) | collective-permute-done | bytes 122912 | tf_op jit(solution)/shard_map/ppermute | solution.py:241
  31.3 1.2 %collective-permute-start.10 = (bf16[160,384]{1,0:T(8,128)(2,1)S(1)}, bf16[160,384]{1,0:T(8,128)(2,1)S(1)}, u32[]{:S(2)}, u32[]{:S(2)}) collective-permute-start(bf16[160,384]{1,0:T(8,128)(2,1)S(1)} %get-tuple-element.58), channel_id=1, source_target_pairs={{0,24},{1,25},{2,26},{3,27},{4,28},{5,29},{6,30},{7,31},{8,16},{9,... | collective-permute-start | bytes 368648 | tf_op jit(solution)/shard_map/ppermute | solution.py:241
  32.5 3.5 %collective-permute-done.9 = bf16[160,384]{1,0:T(8,128)(2,1)S(1)} collective-permute-done((bf16[160,384]{1,0:T(8,128)(2,1)S(1)}, bf16[160,384]{1,0:T(8,128)(2,1)S(1)}, u32[]{:S(2)}, u32[]{:S(2)}) %collective-permute-start.9) | collective-permute-done | bytes 122912 | tf_op jit(solution)/shard_map/ppermute | solution.py:241
  36.0 2.0 %collective-permute-done.10 = bf16[160,384]{1,0:T(8,128)(2,1)S(1)} collective-permute-done((bf16[160,384]{1,0:T(8,128)(2,1)S(1)}, bf16[160,384]{1,0:T(8,128)(2,1)S(1)}, u32[]{:S(2)}, u32[]{:S(2)}) %collective-permute-start.10) | collective-permute-done | bytes 122912 | tf_op jit(solution)/shard_map/ppermute | solution.py:241
  38.1 1.6 %collective-permute-start.14 = (bf16[3,160,384]{2,1,0:T(8,128)(2,1)S(1)}, bf16[3,160,384]{2,1,0:T(8,128)(2,1)S(1)}, u32[]{:S(2)}, u32[]{:S(2)}) collective-permute-start(bf16[3,160,384]{2,1,0:T(8,128)(2,1)S(1)} %pad_maximum_fusion.1.refs_2_), channel_id=1, source_target_pairs={{0,2},{1,3},{2,0},{3,1},{4,6},{5,7},{6,4},{7,5},{8,10},{9,11},{10,... | collective-permute-start | bytes 1105928 | tf_op jit(solution)/shard_map/ppermute | solution.py:241
  39.9 1.6 %collective-permute-start.16 = (bf16[32,1536]{1,0:T(8,128)(2,1)S(1)}, bf16[32,1536]{1,0:T(8,128)(2,1)S(1)}, u32[]{:S(2)}, u32[]{:S(2)}) collective-permute-start(bf16[32,1536]{1,0:T(8,128)(2,1)S(1)} %broadcast_select_fusion.3.cot_block), channel_id=1, source_target_pairs={{0,2},{1,3},{2,0},{3,1},{4,6},{5,7},{6,4},{7,5},{8,10},{9,11},{10,... | collective-permute-start | bytes 294920 | tf_op jit(solution)/shard_map/ppermute | solution.py:241
  41.5 0.8 collective-permute-start.12
  42.3 1.6 %collective-permute-start.13 = (bf16[3,96,384]{2,1,0:T(8,128)(2,1)S(1)}, bf16[3,96,384]{2,1,0:T(8,128)(2,1)S(1)}, u32[]{:S(2)}, u32[]{:S(2)}) collective-permute-start(bf16[3,96,384]{2,1,0:T(8,128)(2,1)S(1)} %slice.49), channel_id=1, source_target_pairs={{0,2},{1,3},{2,0},{3,1},{4,6},{5,7},{6,4},{7,5},{8,10},{9,11},{10,... | collective-permute-start | bytes 663560 | tf_op jit(solution)/shard_map/ppermute | solution.py:241
  43.9 7.9 %collective-permute-done.16.cot_beside = bf16[32,1536]{1,0:T(8,128)(2,1)S(1)} collective-permute-done((bf16[32,1536]{1,0:T(8,128)(2,1)S(1)}, bf16[32,1536]{1,0:T(8,128)(2,1)S(1)}, u32[]{:S(2)}, u32[]{:S(2)}) %collective-permute-start.16) | collective-permute-done | bytes 98336 | tf_op jit(solution)/shard_map/ppermute | solution.py:241
  51.8 4.4 %collective-permute-start.17 = (bf16[48,1536]{1,0:T(8,128)(2,1)S(1)}, bf16[48,1536]{1,0:T(8,128)(2,1)S(1)}, u32[]{:S(2)}, u32[]{:S(2)}) collective-permute-start(bf16[48,1536]{1,0:T(8,128)(2,1)S(1)} %pad_maximum_fusion.2), channel_id=1, source_target_pairs={{1,9},{3,11},{5,13},{7,15},{8,16},{9,1},{10,18},{11,3},{12,20},{13... | collective-permute-start | bytes 442376 | tf_op jit(solution)/shard_map/ppermute | solution.py:241
  56.2 3.1 %collective-permute-done.17.edge = bf16[48,1536]{1,0:T(8,128)(2,1)S(1)} collective-permute-done((bf16[48,1536]{1,0:T(8,128)(2,1)S(1)}, bf16[48,1536]{1,0:T(8,128)(2,1)S(1)}, u32[]{:S(2)}, u32[]{:S(2)}) %collective-permute-start.17) | collective-permute-done | bytes 147488 | tf_op jit(solution)/shard_map/ppermute | solution.py:241
  60.8 0.5 collective-permute-done.19.other_odd
  62.5 4.0 %collective-permute-done.27.refs_5_ = bf16[3,80,384]{2,1,0:T(8,128)(2,1)S(1)} collective-permute-done((bf16[3,80,384]{2,1,0:T(8,128)(2,1)S(1)}, bf16[3,80,384]{2,1,0:T(8,128)(2,1)S(1)}, u32[]{:S(2)}, u32[]{:S(2)}) %collective-permute-start.27) | collective-permute-done | bytes 184352 | tf_op jit(solution)/shard_map/ppermute | solution.py:241
  66.5 1.5 %collective-permute-start.28 = (bf16[3,80,384]{2,1,0:T(8,128)(2,1)S(1)}, bf16[3,80,384]{2,1,0:T(8,128)(2,1)S(1)}, u32[]{:S(2)}, u32[]{:S(2)}) collective-permute-start(bf16[3,80,384]{2,1,0:T(8,128)(2,1)S(1)} %slice.51), channel_id=1, source_target_pairs={{0,2},{1,3},{2,0},{3,1},{4,6},{5,7},{6,4},{7,5},{8,10},{9,11},{10,... | collective-permute-start | bytes 552968 | tf_op jit(solution)/shard_map/ppermute | solution.py:241
  68.0 4.8 %collective-permute-done.28.refs_6_ = bf16[3,80,384]{2,1,0:T(8,128)(2,1)S(1)} collective-permute-done((bf16[3,80,384]{2,1,0:T(8,128)(2,1)S(1)}, bf16[3,80,384]{2,1,0:T(8,128)(2,1)S(1)}, u32[]{:S(2)}, u32[]{:S(2)}) %collective-permute-start.28) | collective-permute-done | bytes 184352 | tf_op jit(solution)/shard_map/ppermute | solution.py:241
  72.8 0.5 collective-permute-start.29
  73.4 0.4 collective-permute-start.32
  73.9 5.1 %shard_map.101 = (bf16[192,1536]{1,0:T(8,128)(2,1)S(1)}, f32[128,1536]{1,0:T(8,128)S(1)}, f32[128,1]{1,0:T(8,128)S(1)}, f32[128,384]{1,0:T(8,128)S(1)}, bf16[3,1...) custom-call(bf16[32,1536]{1,0:T(8,128)(2,1)S(1)} %collective-permute-done.3.blocks_even, ...), custom_call_target="tpu_custom_call" | custom-call | tf_op jit(solution)/shard_map/pallas_call | solution.py:643
  79.1 5.6 %shard_map.102 = (f32[128,256]{1,0:T(8,128)S(1)}, f32[128,640]{1,0:T(8,128)S(1)}, bf16[32,640]{1,0:T(8,128)(2,1)S(1)}, bf16[1536,896]{1,0:T(8,128)(2,1)S(1)}, bf16[128,1536]{1,0:T(8,128)(2,1)S(1)}) custom-call(s32[4]{0:T(128)S(1)} %copy-done.8, s32[1]{0:T(128)} %bitcast.3.flag, bf16[192,1536]{1,0:T(8,128)(2,1)S(1)} %get-tuple-element.78.normed, ...), custom_call_target="tpu_custom_call" | custom-call | tf_op jit(solution)/shard_map/pallas_call | solution.py:659
  84.7 3.9 %collective-permute-start.34 = (bf16[32,640]{1,0:T(8,128)(2,1)S(1)}, bf16[32,640]{1,0:T(8,128)(2,1)S(1)}, u32[]{:S(2)}, u32[]{:S(2)}) collective-permute-start(bf16[32,640]{1,0:T(8,128)(2,1)S(1)} %get-tuple-element.86), channel_id=1, source_target_pairs={{1,9},{3,11},{5,13},{7,15},{8,16},{9,1},{10,18},{11,3},{12,20},{13... | collective-permute-start | bytes 122888 | tf_op jit(solution)/shard_map/ppermute | solution.py:241
  88.6 2.0 %collective-permute-done.34.received = bf16[32,640]{1,0:T(8,128)(2,1)S(1)} collective-permute-done((bf16[32,640]{1,0:T(8,128)(2,1)S(1)}, bf16[32,640]{1,0:T(8,128)(2,1)S(1)}, u32[]{:S(2)}, u32[]{:S(2)}) %collective-permute-start.34) | collective-permute-done | bytes 40992 | tf_op jit(solution)/shard_map/ppermute | solution.py:241
  90.6 3.1 %shard_map.103 = (bf16[128,384]{1,0:T(8,128)(2,1)S(1)}, f32[64,1536]{1,0:T(8,128)S(1)}, bf16[16,384]{1,0:T(8,128)(2,1)S(1)}) custom-call(f32[128,256]{1,0:T(8,128)S(1)} %get-tuple-element.84.d_q, f32[128,640]{1,0:T(8,128)S(1)} %get-tuple-element.85.d_kv, bf16[32,640]{1,0:T(8,128)(2,1)S(1)} %collective-permute-done.34.received, ...), custom_call_target="tpu_custom_call" | custom-call | tf_op jit(solution)/shard_map/pallas_call | solution.py:675
  93.7 3.9 %collective-permute-start.35 = (bf16[16,384]{1,0:T(8,128)(2,1)S(1)}, bf16[16,384]{1,0:T(8,128)(2,1)S(1)}, u32[]{:S(2)}, u32[]{:S(2)}) collective-permute-start(bf16[16,384]{1,0:T(8,128)(2,1)S(1)} %get-tuple-element.94), channel_id=1, source_target_pairs={{1,9},{3,11},{5,13},{7,15},{8,16},{9,1},{10,18},{11,3},{12,20},{13... | collective-permute-start | bytes 36872 | tf_op jit(solution)/shard_map/ppermute | solution.py:241
  97.7 1.7 %collective-permute-done.35.received = bf16[16,384]{1,0:T(8,128)(2,1)S(1)} collective-permute-done((bf16[16,384]{1,0:T(8,128)(2,1)S(1)}, bf16[16,384]{1,0:T(8,128)(2,1)S(1)}, u32[]{:S(2)}, u32[]{:S(2)}) %collective-permute-start.35) | collective-permute-done | bytes 12320 | tf_op jit(solution)/shard_map/ppermute | solution.py:241
  99.3 1.8 %shard_map.104 = (f32[32,1536]{1,0:T(8,128)S(1)}, bf16[32,1536]{1,0:T(8,128)(2,1)S(1)}) custom-call(bf16[128,384]{1,0:T(8,128)(2,1)S(1)} %get-tuple-element.93.d_hidden, bf16[16,384]{1,0:T(8,128)(2,1)S(1)} %collective-permute-done.35.received, f32[64,1536]{1,0:T(8,128)S(1)} %get-tuple-element.95.d_resid, ...), custom_call_target="tpu_custom_call" | custom-call | tf_op jit(solution)/shard_map/pallas_call | solution.py:687
  101.1 1.6 %collective-permute-start.36 = (bf16[32,1536]{1,0:T(8,128)(2,1)S(1)}, bf16[32,1536]{1,0:T(8,128)(2,1)S(1)}, u32[]{:S(2)}, u32[]{:S(2)}) collective-permute-start(bf16[32,1536]{1,0:T(8,128)(2,1)S(1)} %get-tuple-element.98), channel_id=1, source_target_pairs={{0,2},{1,3},{2,0},{3,1},{4,6},{5,7},{6,4},{7,5},{8,10},{9,11},{10,... | collective-permute-start | bytes 294920 | tf_op jit(solution)/shard_map/ppermute | solution.py:241
  102.7 3.1 %collective-permute-done.36 = bf16[32,1536]{1,0:T(8,128)(2,1)S(1)} collective-permute-done((bf16[32,1536]{1,0:T(8,128)(2,1)S(1)}, bf16[32,1536]{1,0:T(8,128)(2,1)S(1)}, u32[]{:S(2)}, u32[]{:S(2)}) %collective-permute-start.36) | collective-permute-done | bytes 98336 | tf_op jit(solution)/shard_map/ppermute | solution.py:241
  106.2 4.3 %collective-permute-done.37 = bf16[32,1536]{1,0:T(8,128)(2,1)S(1)} collective-permute-done((bf16[32,1536]{1,0:T(8,128)(2,1)S(1)}, bf16[32,1536]{1,0:T(8,128)(2,1)S(1)}, u32[]{:S(2)}, u32[]{:S(2)}) %collective-permute-start.37) | collective-permute-done | bytes 98336 | tf_op jit(solution)/shard_map/ppermute | solution.py:241
  110.6 1.4 %collective-permute-done.38 = f32[32,1536]{1,0:T(8,128)S(1)} collective-permute-done((f32[32,1536]{1,0:T(8,128)S(1)}, f32[32,1536]{1,0:T(8,128)S(1)}, u32[]{:S(2)}, u32[]{:S(2)}) %collective-permute-start.38) | collective-permute-done | bytes 196640 | tf_op jit(solution)/shard_map/ppermute | solution.py:241
  112.0 0.7 broadcast_select_fusion.2
  (77 shorter events, 4.5 us)
Async XLA Ops:
  0.0 1.2 %copy-start = (bf16[3,384,384]{2,1,0:T(8,128)(2,1)S(1)}, bf16[3,384,384]{2,1,0:T(8,128)(2,1)}, u32[]{:S(2)}) copy-start(bf16[3,384,384]{2,1,0:T(8,128)(2,1)} %refs_0_.2) | copy-start | bytes 2654212
  4.2 5.8 %copy-start.11 = (s32[16,2]{0,1:T(2,128)S(1)}, s32[16,2]{0,1:T(2,128)}, u32[]{:S(2)}) copy-start(s32[16,2]{0,1:T(2,128)} %param.19) | copy-start | bytes 388
  4.2 10.5 %copy-start.9 = (bf16[32,1536]{1,0:T(8,128)(2,1)S(1)}, bf16[32,1536]{1,0:T(8,128)(2,1)}, u32[]{:S(2)}) copy-start(bf16[32,1536]{1,0:T(8,128)(2,1)} %param.12) | copy-start | bytes 294916
  4.4 6.9 %collective-permute-start = (bf16[192,384]{1,0:T(8,128)(2,1)S(1)}, bf16[192,384]{1,0:T(8,128)(2,1)S(1)}, u32[]{:S(2)}, u32[]{:S(2)}) collective-permute-start(bf16[192,384]{1,0:T(8,128)(2,1)S(1)} %get-tuple-element.52), channel_id=1, source_target_pairs={{0,8},{1,9},{2,10},{3,11},{4,12},{5,13},{6,14},{7,15},{8,0},{9,1},... | collective-permute-start | bytes 442376 | tf_op jit(solution)/shard_map/ppermute | solution.py:241
  4.5 13.4 %collective-permute-start.1 = (bf16[192,384]{1,0:T(8,128)(2,1)S(1)}, bf16[192,384]{1,0:T(8,128)(2,1)S(1)}, u32[]{:S(2)}, u32[]{:S(2)}) collective-permute-start(bf16[192,384]{1,0:T(8,128)(2,1)S(1)} %get-tuple-element.52), channel_id=1, source_target_pairs={{0,16},{1,17},{2,18},{3,19},{4,20},{5,21},{6,22},{7,23},{8,24},{9,... | collective-permute-start | bytes 442376 | tf_op jit(solution)/shard_map/ppermute | solution.py:241
  7.5 13.3 %collective-permute-start.2 = (bf16[192,384]{1,0:T(8,128)(2,1)S(1)}, bf16[192,384]{1,0:T(8,128)(2,1)S(1)}, u32[]{:S(2)}, u32[]{:S(2)}) collective-permute-start(bf16[192,384]{1,0:T(8,128)(2,1)S(1)} %get-tuple-element.52), channel_id=1, source_target_pairs={{0,24},{1,25},{2,26},{3,27},{4,28},{5,29},{6,30},{7,31},{8,16},{9,... | collective-permute-start | bytes 442376 | tf_op jit(solution)/shard_map/ppermute | solution.py:241
  8.9 65.0 %copy-start.10 = (f32[1536]{0:T(1024)S(1)}, f32[1536]{0:T(1024)}, u32[]{:S(2)}) copy-start(f32[1536]{0:T(1024)} %param.15) | copy-start | bytes 18436
  8.9 65.0 %copy-start.1 = (bf16[3,384,384]{2,1,0:T(8,128)(2,1)S(1)}, bf16[3,384,384]{2,1,0:T(8,128)(2,1)}, u32[]{:S(2)}) copy-start(bf16[3,384,384]{2,1,0:T(8,128)(2,1)} %refs_0_.2) | copy-start | bytes 2654212
  8.9 65.0 %copy-start.5 = (bf16[96,1536]{1,0:T(8,128)(2,1)S(1)}, bf16[96,1536]{1,0:T(8,128)(2,1)}, u32[]{:S(2)}) copy-start(bf16[96,1536]{1,0:T(8,128)(2,1)} %refs_1_.2) | copy-start | bytes 884740
  11.3 9.5 %collective-permute-start.3 = (bf16[32,1536]{1,0:T(8,128)(2,1)S(1)}, bf16[32,1536]{1,0:T(8,128)(2,1)S(1)}, u32[]{:S(2)}, u32[]{:S(2)}) collective-permute-start(bf16[32,1536]{1,0:T(8,128)(2,1)S(1)} %get-tuple-element.101), channel_id=1, source_target_pairs={{0,0},{1,4},{2,2},{3,6},{4,1},{5,5},{6,3},{7,7},{8,9},{9,13},{10,1... | collective-permute-start | bytes 294920 | tf_op jit(solution)/shard_map/ppermute | solution.py:241
  13.3 7.6 %collective-permute-start.4 = (bf16[32,1536]{1,0:T(8,128)(2,1)S(1)}, bf16[32,1536]{1,0:T(8,128)(2,1)S(1)}, u32[]{:S(2)}, u32[]{:S(2)}) collective-permute-start(bf16[32,1536]{1,0:T(8,128)(2,1)S(1)} %get-tuple-element.102), channel_id=1, source_target_pairs={{0,2},{1,6},{2,0},{3,4},{4,3},{5,7},{6,1},{7,5},{8,11},{9,15},{10,... | collective-permute-start | bytes 294920 | tf_op jit(solution)/shard_map/ppermute | solution.py:241
  14.7 6.5 %collective-permute-start.5 = (bf16[32,1536]{1,0:T(8,128)(2,1)S(1)}, bf16[32,1536]{1,0:T(8,128)(2,1)S(1)}, u32[]{:S(2)}, u32[]{:S(2)}) collective-permute-start(bf16[32,1536]{1,0:T(8,128)(2,1)S(1)} %copy-done.9), channel_id=1, source_target_pairs={{0,4},{2,6},{5,1},{7,3},{9,13},{11,15},{12,8},{14,10},{16,20},{18,... | collective-permute-start | bytes 294920 | tf_op jit(solution)/shard_map/ppermute | solution.py:241
  21.2 16.9 %collective-permute-start.11 = (bf16[3,192,384]{2,1,0:T(8,128)(2,1)S(1)}, bf16[3,192,384]{2,1,0:T(8,128)(2,1)S(1)}, u32[]{:S(2)}, u32[]{:S(2)}) collective-permute-start(bf16[3,192,384]{2,1,0:T(8,128)(2,1)S(1)} %pad_maximum_fusion.refs_2_), channel_id=1, source_target_pairs={{0,1},{1,0},{2,3},{3,2},{4,5},{5,4},{6,7},{7,6},{8,9},{9,8},{10,11... | collective-permute-start | bytes 1327112 | tf_op jit(solution)/shard_map/ppermute | solution.py:241
  21.2 16.8 %collective-permute-start.6 = (bf16[3,192,384]{2,1,0:T(8,128)(2,1)S(1)}, bf16[3,192,384]{2,1,0:T(8,128)(2,1)S(1)}, u32[]{:S(2)}, u32[]{:S(2)}) collective-permute-start(bf16[3,192,384]{2,1,0:T(8,128)(2,1)S(1)} %pad_maximum_fusion.refs_2_), channel_id=1, source_target_pairs={{0,2},{1,3},{2,0},{3,1},{4,6},{5,7},{6,4},{7,5},{8,10},{9,11},{10,... | collective-permute-start | bytes 1327112 | tf_op jit(solution)/shard_map/ppermute | solution.py:241
  22.6 15.5 %collective-permute-start.7 = (bf16[3,192,384]{2,1,0:T(8,128)(2,1)S(1)}, bf16[3,192,384]{2,1,0:T(8,128)(2,1)S(1)}, u32[]{:S(2)}, u32[]{:S(2)}) collective-permute-start(bf16[3,192,384]{2,1,0:T(8,128)(2,1)S(1)} %pad_maximum_fusion.refs_2_), channel_id=1, source_target_pairs={{0,4},{1,5},{2,6},{3,7},{4,0},{5,1},{6,2},{7,3},{8,12},{9,13},{10,... | collective-permute-start | bytes 1327112 | tf_op jit(solution)/shard_map/ppermute | solution.py:241
  24.1 7.2 %collective-permute-start.8 = (bf16[160,384]{1,0:T(8,128)(2,1)S(1)}, bf16[160,384]{1,0:T(8,128)(2,1)S(1)}, u32[]{:S(2)}, u32[]{:S(2)}) collective-permute-start(bf16[160,384]{1,0:T(8,128)(2,1)S(1)} %get-tuple-element.58), channel_id=1, source_target_pairs={{0,8},{1,9},{2,10},{3,11},{4,12},{5,13},{6,14},{7,15},{8,0},{9,1},... | collective-permute-start | bytes 368648 | tf_op jit(solution)/shard_map/ppermute | solution.py:241
  26.1 9.9 %collective-permute-start.9 = (bf16[160,384]{1,0:T(8,128)(2,1)S(1)}, bf16[160,384]{1,0:T(8,128)(2,1)S(1)}, u32[]{:S(2)}, u32[]{:S(2)}) collective-permute-start(bf16[160,384]{1,0:T(8,128)(2,1)S(1)} %get-tuple-element.58), channel_id=1, source_target_pairs={{0,16},{1,17},{2,18},{3,19},{4,20},{5,21},{6,22},{7,23},{8,24},{9,... | collective-permute-start | bytes 368648 | tf_op jit(solution)/shard_map/ppermute | solution.py:241
  31.3 6.7 %collective-permute-start.10 = (bf16[160,384]{1,0:T(8,128)(2,1)S(1)}, bf16[160,384]{1,0:T(8,128)(2,1)S(1)}, u32[]{:S(2)}, u32[]{:S(2)}) collective-permute-start(bf16[160,384]{1,0:T(8,128)(2,1)S(1)} %get-tuple-element.58), channel_id=1, source_target_pairs={{0,24},{1,25},{2,26},{3,27},{4,28},{5,29},{6,30},{7,31},{8,16},{9,... | collective-permute-start | bytes 368648 | tf_op jit(solution)/shard_map/ppermute | solution.py:241
  38.1 21.2 %collective-permute-start.14 = (bf16[3,160,384]{2,1,0:T(8,128)(2,1)S(1)}, bf16[3,160,384]{2,1,0:T(8,128)(2,1)S(1)}, u32[]{:S(2)}, u32[]{:S(2)}) collective-permute-start(bf16[3,160,384]{2,1,0:T(8,128)(2,1)S(1)} %pad_maximum_fusion.1.refs_2_), channel_id=1, source_target_pairs={{0,2},{1,3},{2,0},{3,1},{4,6},{5,7},{6,4},{7,5},{8,10},{9,11},{10,... | collective-permute-start | bytes 1105928 | tf_op jit(solution)/shard_map/ppermute | solution.py:241
  39.6 19.6 %collective-permute-start.15 = (bf16[3,160,384]{2,1,0:T(8,128)(2,1)S(1)}, bf16[3,160,384]{2,1,0:T(8,128)(2,1)S(1)}, u32[]{:S(2)}, u32[]{:S(2)}) collective-permute-start(bf16[3,160,384]{2,1,0:T(8,128)(2,1)S(1)} %pad_maximum_fusion.1.refs_2_), channel_id=1, source_target_pairs={{0,4},{1,5},{2,6},{3,7},{4,0},{5,1},{6,2},{7,3},{8,12},{9,13},{10,... | collective-permute-start | bytes 1105928 | tf_op jit(solution)/shard_map/ppermute | solution.py:241
  39.9 11.9 %collective-permute-start.16 = (bf16[32,1536]{1,0:T(8,128)(2,1)S(1)}, bf16[32,1536]{1,0:T(8,128)(2,1)S(1)}, u32[]{:S(2)}, u32[]{:S(2)}) collective-permute-start(bf16[32,1536]{1,0:T(8,128)(2,1)S(1)} %broadcast_select_fusion.3.cot_block), channel_id=1, source_target_pairs={{0,2},{1,3},{2,0},{3,1},{4,6},{5,7},{6,4},{7,5},{8,10},{9,11},{10,... | collective-permute-start | bytes 294920 | tf_op jit(solution)/shard_map/ppermute | solution.py:241
  41.5 17.7 %collective-permute-start.12 = (bf16[3,96,384]{2,1,0:T(8,128)(2,1)S(1)}, bf16[3,96,384]{2,1,0:T(8,128)(2,1)S(1)}, u32[]{:S(2)}, u32[]{:S(2)}) collective-permute-start(bf16[3,96,384]{2,1,0:T(8,128)(2,1)S(1)} %slice.48), channel_id=1, source_target_pairs={{0,4},{1,5},{2,6},{3,7},{4,0},{5,1},{6,2},{7,3},{8,12},{9,13},{10,... | collective-permute-start | bytes 663560 | tf_op jit(solution)/shard_map/ppermute | solution.py:241
  42.3 17.0 %collective-permute-start.13 = (bf16[3,96,384]{2,1,0:T(8,128)(2,1)S(1)}, bf16[3,96,384]{2,1,0:T(8,128)(2,1)S(1)}, u32[]{:S(2)}, u32[]{:S(2)}) collective-permute-start(bf16[3,96,384]{2,1,0:T(8,128)(2,1)S(1)} %slice.49), channel_id=1, source_target_pairs={{0,2},{1,3},{2,0},{3,1},{4,6},{5,7},{6,4},{7,5},{8,10},{9,11},{10,... | collective-permute-start | bytes 663560 | tf_op jit(solution)/shard_map/ppermute | solution.py:241
  51.8 7.5 %collective-permute-start.17 = (bf16[48,1536]{1,0:T(8,128)(2,1)S(1)}, bf16[48,1536]{1,0:T(8,128)(2,1)S(1)}, u32[]{:S(2)}, u32[]{:S(2)}) collective-permute-start(bf16[48,1536]{1,0:T(8,128)(2,1)S(1)} %pad_maximum_fusion.2), channel_id=1, source_target_pairs={{1,9},{3,11},{5,13},{7,15},{8,16},{9,1},{10,18},{11,3},{12,20},{13... | collective-permute-start | bytes 442376 | tf_op jit(solution)/shard_map/ppermute | solution.py:241
  59.3 1.4 %collective-permute-start.18 = (bf16[32,1536]{1,0:T(8,128)(2,1)S(1)}, bf16[32,1536]{1,0:T(8,128)(2,1)S(1)}, u32[]{:S(2)}, u32[]{:S(2)}) collective-permute-start(bf16[32,1536]{1,0:T(8,128)(2,1)S(1)} %collective-permute-done.3.blocks_even), channel_id=1, source_target_pairs={{0,1},{1,0},{2,3},{3,2},{4,5},{5,4},{6,7},{7,6},{8,9},{9,8},{10,11... | collective-permute-start | bytes 294920 | tf_op jit(solution)/shard_map/ppermute | solution.py:241
  59.4 7.1 %collective-permute-start.27 = (bf16[3,80,384]{2,1,0:T(8,128)(2,1)S(1)}, bf16[3,80,384]{2,1,0:T(8,128)(2,1)S(1)}, u32[]{:S(2)}, u32[]{:S(2)}) collective-permute-start(bf16[3,80,384]{2,1,0:T(8,128)(2,1)S(1)} %slice.50), channel_id=1, source_target_pairs={{0,4},{1,5},{2,6},{3,7},{4,0},{5,1},{6,2},{7,3},{8,12},{9,13},{10,... | collective-permute-start | bytes 552968 | tf_op jit(solution)/shard_map/ppermute | solution.py:241
  59.8 2.3 %collective-permute-start.20 = (bf16[48,1536]{1,0:T(8,128)(2,1)S(1)}, bf16[48,1536]{1,0:T(8,128)(2,1)S(1)}, u32[]{:S(2)}, u32[]{:S(2)}) collective-permute-start(bf16[48,1536]{1,0:T(8,128)(2,1)S(1)} %collective-permute-done.17.edge), channel_id=1, source_target_pairs={{0,1},{1,0},{2,3},{3,2},{4,5},{5,4},{6,7},{7,6},{8,9},{9,8},{10,11... | collective-permute-start | bytes 442376 | tf_op jit(solution)/shard_map/ppermute | solution.py:241
  60.0 1.3 %collective-permute-start.19 = (bf16[32,1536]{1,0:T(8,128)(2,1)S(1)}, bf16[32,1536]{1,0:T(8,128)(2,1)S(1)}, u32[]{:S(2)}, u32[]{:S(2)}) collective-permute-start(bf16[32,1536]{1,0:T(8,128)(2,1)S(1)} %collective-permute-done.4.blocks_odd), channel_id=1, source_target_pairs={{0,1},{1,0},{2,3},{3,2},{4,5},{5,4},{6,7},{7,6},{8,9},{9,8},{10,11... | collective-permute-start | bytes 294920 | tf_op jit(solution)/shard_map/ppermute | solution.py:241
  60.3 1.3 %collective-permute-start.25 = (bf16[32,1536]{1,0:T(8,128)(2,1)S(1)}, bf16[32,1536]{1,0:T(8,128)(2,1)S(1)}, u32[]{:S(2)}, u32[]{:S(2)}) collective-permute-start(bf16[32,1536]{1,0:T(8,128)(2,1)S(1)} %broadcast_select_fusion.3.cot_block), channel_id=1, source_target_pairs={{0,1},{1,0},{2,3},{3,2},{4,5},{5,4},{6,7},{7,6},{8,9},{9,8},{10,11... | collective-permute-start | bytes 294920 | tf_op jit(solution)/shard_map/ppermute | solution.py:241
  60.7 1.3 %collective-permute-start.26 = (bf16[32,1536]{1,0:T(8,128)(2,1)S(1)}, bf16[32,1536]{1,0:T(8,128)(2,1)S(1)}, u32[]{:S(2)}, u32[]{:S(2)}) collective-permute-start(bf16[32,1536]{1,0:T(8,128)(2,1)S(1)} %collective-permute-done.16.cot_beside), channel_id=1, source_target_pairs={{0,1},{1,0},{2,3},{3,2},{4,5},{5,4},{6,7},{7,6},{8,9},{9,8},{10,11... | collective-permute-start | bytes 294920 | tf_op jit(solution)/shard_map/ppermute | solution.py:241
  61.3 12.0 %collective-permute-start.21 = (bf16[3,192,384]{2,1,0:T(8,128)(2,1)S(1)}, bf16[3,192,384]{2,1,0:T(8,128)(2,1)S(1)}, u32[]{:S(2)}, u32[]{:S(2)}) collective-permute-start(bf16[3,192,384]{2,1,0:T(8,128)(2,1)S(1)} %collective-permute-done.6.refs_3_), channel_id=1, source_target_pairs={{0,1},{1,0},{2,3},{3,2},{4,5},{5,4},{6,7},{7,6},{8,9},{9,8},{10,11... | collective-permute-start | bytes 1327112 | tf_op jit(solution)/shard_map/ppermute | solution.py:241
  61.6 12.2 %collective-permute-start.22 = (bf16[3,192,384]{2,1,0:T(8,128)(2,1)S(1)}, bf16[3,192,384]{2,1,0:T(8,128)(2,1)S(1)}, u32[]{:S(2)}, u32[]{:S(2)}) collective-permute-start(bf16[3,192,384]{2,1,0:T(8,128)(2,1)S(1)} %collective-permute-done.7.refs_4_), channel_id=1, source_target_pairs={{0,1},{1,0},{2,3},{3,2},{4,5},{5,4},{6,7},{7,6},{8,9},{9,8},{10,11... | collective-permute-start | bytes 1327112 | tf_op jit(solution)/shard_map/ppermute | solution.py:241
  62.0 10.8 %collective-permute-start.23 = (bf16[3,96,384]{2,1,0:T(8,128)(2,1)S(1)}, bf16[3,96,384]{2,1,0:T(8,128)(2,1)S(1)}, u32[]{:S(2)}, u32[]{:S(2)}) collective-permute-start(bf16[3,96,384]{2,1,0:T(8,128)(2,1)S(1)} %collective-permute-done.12.refs_5_), channel_id=1, source_target_pairs={{0,1},{1,0},{2,3},{3,2},{4,5},{5,4},{6,7},{7,6},{8,9},{9,8},{10,11... | collective-permute-start | bytes 663560 | tf_op jit(solution)/shard_map/ppermute | solution.py:241
  62.1 11.1 %collective-permute-start.24 = (bf16[3,96,384]{2,1,0:T(8,128)(2,1)S(1)}, bf16[3,96,384]{2,1,0:T(8,128)(2,1)S(1)}, u32[]{:S(2)}, u32[]{:S(2)}) collective-permute-start(bf16[3,96,384]{2,1,0:T(8,128)(2,1)S(1)} %collective-permute-done.13.refs_6_), channel_id=1, source_target_pairs={{0,1},{1,0},{2,3},{3,2},{4,5},{5,4},{6,7},{7,6},{8,9},{9,8},{10,11... | collective-permute-start | bytes 663560 | tf_op jit(solution)/shard_map/ppermute | solution.py:241
  62.5 16.6 %copy-start.3 = (bf16[384,896]{1,0:T(8,128)(2,1)S(1)}, bf16[384,896]{1,0:T(8,128)(2,1)}, u32[]{:S(2)}) copy-start(bf16[384,896]{1,0:T(8,128)(2,1)} %refs_0_.3) | copy-start | bytes 2064388
  62.5 16.6 %copy-start.7 = (bf16[96,1536]{1,0:T(8,128)(2,1)S(1)}, bf16[96,1536]{1,0:T(8,128)(2,1)}, u32[]{:S(2)}) copy-start(bf16[96,1536]{1,0:T(8,128)(2,1)} %refs_1_.3) | copy-start | bytes 884740
  62.5 16.6 %copy-start.8 = (s32[4]{0:T(128)S(1)}, s32[4]{0:T(128)}, u32[]{:S(2)}) copy-start(s32[4]{0:T(128)} %band.1) | copy-start | bytes 52
  66.5 6.3 %collective-permute-start.28 = (bf16[3,80,384]{2,1,0:T(8,128)(2,1)S(1)}, bf16[3,80,384]{2,1,0:T(8,128)(2,1)S(1)}, u32[]{:S(2)}, u32[]{:S(2)}) collective-permute-start(bf16[3,80,384]{2,1,0:T(8,128)(2,1)S(1)} %slice.51), channel_id=1, source_target_pairs={{0,2},{1,3},{2,0},{3,1},{4,6},{5,7},{6,4},{7,5},{8,10},{9,11},{10,... | collective-permute-start | bytes 552968 | tf_op jit(solution)/shard_map/ppermute | solution.py:241
  72.8 6.3 %collective-permute-start.30 = (bf16[3,160,384]{2,1,0:T(8,128)(2,1)S(1)}, bf16[3,160,384]{2,1,0:T(8,128)(2,1)S(1)}, u32[]{:S(2)}, u32[]{:S(2)}) collective-permute-start(bf16[3,160,384]{2,1,0:T(8,128)(2,1)S(1)} %collective-permute-done.14.refs_3_), channel_id=1, source_target_pairs={{0,1},{1,0},{2,3},{3,2},{4,5},{5,4},{6,7},{7,6},{8,9},{9,8},{10,11... | collective-permute-start | bytes 1105928 | tf_op jit(solution)/shard_map/ppermute | solution.py:241
  72.8 6.3 %collective-permute-start.29 = (bf16[3,160,384]{2,1,0:T(8,128)(2,1)S(1)}, bf16[3,160,384]{2,1,0:T(8,128)(2,1)S(1)}, u32[]{:S(2)}, u32[]{:S(2)}) collective-permute-start(bf16[3,160,384]{2,1,0:T(8,128)(2,1)S(1)} %pad_maximum_fusion.1.refs_2_), channel_id=1, source_target_pairs={{0,1},{1,0},{2,3},{3,2},{4,5},{5,4},{6,7},{7,6},{8,9},{9,8},{10,11... | collective-permute-start | bytes 1105928 | tf_op jit(solution)/shard_map/ppermute | solution.py:241
  73.3 5.8 %collective-permute-start.31 = (bf16[3,160,384]{2,1,0:T(8,128)(2,1)S(1)}, bf16[3,160,384]{2,1,0:T(8,128)(2,1)S(1)}, u32[]{:S(2)}, u32[]{:S(2)}) collective-permute-start(bf16[3,160,384]{2,1,0:T(8,128)(2,1)S(1)} %collective-permute-done.15.refs_4_), channel_id=1, source_target_pairs={{0,1},{1,0},{2,3},{3,2},{4,5},{5,4},{6,7},{7,6},{8,9},{9,8},{10,11... | collective-permute-start | bytes 1105928 | tf_op jit(solution)/shard_map/ppermute | solution.py:241
  73.4 5.7 %collective-permute-start.32 = (bf16[3,80,384]{2,1,0:T(8,128)(2,1)S(1)}, bf16[3,80,384]{2,1,0:T(8,128)(2,1)S(1)}, u32[]{:S(2)}, u32[]{:S(2)}) collective-permute-start(bf16[3,80,384]{2,1,0:T(8,128)(2,1)S(1)} %collective-permute-done.27.refs_5_), channel_id=1, source_target_pairs={{0,1},{1,0},{2,3},{3,2},{4,5},{5,4},{6,7},{7,6},{8,9},{9,8},{10,11... | collective-permute-start | bytes 552968 | tf_op jit(solution)/shard_map/ppermute | solution.py:241
  73.8 5.2 %collective-permute-start.33 = (bf16[3,80,384]{2,1,0:T(8,128)(2,1)S(1)}, bf16[3,80,384]{2,1,0:T(8,128)(2,1)S(1)}, u32[]{:S(2)}, u32[]{:S(2)}) collective-permute-start(bf16[3,80,384]{2,1,0:T(8,128)(2,1)S(1)} %collective-permute-done.28.refs_6_), channel_id=1, source_target_pairs={{0,1},{1,0},{2,3},{3,2},{4,5},{5,4},{6,7},{7,6},{8,9},{9,8},{10,11... | collective-permute-start | bytes 552968 | tf_op jit(solution)/shard_map/ppermute | solution.py:241
  84.7 5.9 %collective-permute-start.34 = (bf16[32,640]{1,0:T(8,128)(2,1)S(1)}, bf16[32,640]{1,0:T(8,128)(2,1)S(1)}, u32[]{:S(2)}, u32[]{:S(2)}) collective-permute-start(bf16[32,640]{1,0:T(8,128)(2,1)S(1)} %get-tuple-element.86), channel_id=1, source_target_pairs={{1,9},{3,11},{5,13},{7,15},{8,16},{9,1},{10,18},{11,3},{12,20},{13... | collective-permute-start | bytes 122888 | tf_op jit(solution)/shard_map/ppermute | solution.py:241
  93.7 5.6 %collective-permute-start.35 = (bf16[16,384]{1,0:T(8,128)(2,1)S(1)}, bf16[16,384]{1,0:T(8,128)(2,1)S(1)}, u32[]{:S(2)}, u32[]{:S(2)}) collective-permute-start(bf16[16,384]{1,0:T(8,128)(2,1)S(1)} %get-tuple-element.94), channel_id=1, source_target_pairs={{1,9},{3,11},{5,13},{7,15},{8,16},{9,1},{10,18},{11,3},{12,20},{13... | collective-permute-start | bytes 36872 | tf_op jit(solution)/shard_map/ppermute | solution.py:241
  101.1 4.7 %collective-permute-start.36 = (bf16[32,1536]{1,0:T(8,128)(2,1)S(1)}, bf16[32,1536]{1,0:T(8,128)(2,1)S(1)}, u32[]{:S(2)}, u32[]{:S(2)}) collective-permute-start(bf16[32,1536]{1,0:T(8,128)(2,1)S(1)} %get-tuple-element.98), channel_id=1, source_target_pairs={{0,2},{1,3},{2,0},{3,1},{4,6},{5,7},{6,4},{7,5},{8,10},{9,11},{10,... | collective-permute-start | bytes 294920 | tf_op jit(solution)/shard_map/ppermute | solution.py:241
  105.8 4.7 %collective-permute-start.37 = (bf16[32,1536]{1,0:T(8,128)(2,1)S(1)}, bf16[32,1536]{1,0:T(8,128)(2,1)S(1)}, u32[]{:S(2)}, u32[]{:S(2)}) collective-permute-start(bf16[32,1536]{1,0:T(8,128)(2,1)S(1)} %add_convert_fusion.1), channel_id=1, source_target_pairs={{0,4},{1,5},{2,6},{3,7},{4,0},{5,1},{6,2},{7,3},{8,12},{9,13},{10,... | collective-permute-start | bytes 294920 | tf_op jit(solution)/shard_map/ppermute | solution.py:241
  110.5 1.5 %collective-permute-start.38 = (f32[32,1536]{1,0:T(8,128)S(1)}, f32[32,1536]{1,0:T(8,128)S(1)}, u32[]{:S(2)}, u32[]{:S(2)}) collective-permute-start(f32[32,1536]{1,0:T(8,128)S(1)} %add_multiply_fusion), channel_id=1, source_target_pairs={{0,1},{1,0},{2,3},{3,2},{4,5},{5,4},{6,7},{7,6},{8,9},{9,8},{10,11... | collective-permute-start | bytes 589832 | tf_op jit(solution)/shard_map/ppermute | solution.py:241
  (3 other events, 3.0 us)

commit v9 on v8

--- a/solution.py
+++ b/solution.py
@@ -567,12 +567,12 @@
     early, late = pl.pallas_call(
         pack_kernel,
         out_shape=(shaped(192, CHUNK, dtype=bf16), shaped(160, CHUNK, dtype=bf16)),
-        in_specs=hbm(4),
+        in_specs=[pl.BlockSpec(memory_space=pltpu.HBM)] * 4,
         out_specs=tuple(vmem(2)),
         scratch_shapes=[
             pltpu.VMEM((3, 48, HID), bf16), pltpu.VMEM((48, 896), bf16), pltpu.SemaphoreType.DMA((4,))
         ],
-        compiler_params=limit(4),
+        compiler_params=limit(60),
     )(convolution_weight, mix_w, qkv_w, out_w)
     def along_z(step):
         return routes(n_sa, lambda z, y, x, c: (z ^ step, y, x, c))
@@ -622,20 +622,19 @@
     straight, late, flag, outer, cot_block = after((straight, late, flag, outer, cot_block))
     beside, across = permuted(straight, x_route), permuted(straight, y_route)
     late_straight = jnp.stack(over_z(late))
-    straight_other = permuted(straight, core_route)
-    straight, beside, across, late_straight, outer, cot_block, straight_other, *blocks = after(
-        (straight, beside, across, late_straight, outer, cot_block, straight_other, *blocks)
+    edge = permuted(outer, edge_route)
+    straight, beside, across, late_straight, edge, cot_block, *blocks = after(
+        (straight, beside, across, late_straight, edge, cot_block, *blocks)
     )
     early = (straight, beside, across) + diagonals(beside, across)
     late_beside, late_across = permuted(late_straight, x_route), permuted(late_straight, y_route)
     cot_rows = (cot_block, permuted(cot_block, x_route))
-    mine = (*blocks, permuted(outer, edge_route))
     early, late, cot_rows, mine = (
         lambda v: (v[:5], v[5:8], v[8:10], v[10:])
-    )(after((*early, late_straight, late_beside, late_across, *cot_rows, *mine)))
+    )(after((*early, late_straight, late_beside, late_across, *cot_rows, *blocks, edge)))
     late = tuple(late) + diagonals(late[1], late[2])
     noisy_rows = tuple(mine) + swapped(mine)
-    early = tuple(early) + (straight_other,) + swapped(early[1:])
+    early = tuple(early) + swapped(early)
     cot_rows = tuple(cot_rows) + swapped(cot_rows)
     late_other = swapped(late[:3])
     gain = norm_gain.reshape(1, features)
@@ -697,10 +696,12 @@
 
     received = permuted(send, x_route)
     partial = (keep + received.astype(f32)).astype(bf16)
-    received = permuted(partial, y_route)
-    total = (partial.astype(f32) + received.astype(f32)) * 0.25
-    swapped_total = permuted(total, core_route)
-    return jnp.where(y == m, total, swapped_total)
+    first_sum = permuted(
+        partial, routes(n_sa, lambda z, y, x, c: (z, 1 - y, x, c) if y != c ^ (z & 1) else (z, y, x, 1 - c))
+    )
+    second_sum = permuted(partial, routes(n_sa, lambda z, y, x, c: (z, 1 - y, x, 1 - c) if y != c ^ (z & 1) else None))
+    other = jnp.where(y == m, partial, second_sum)
+    return (first_sum.astype(f32) + other.astype(f32)) * 0.25
 
 
 def solution(mesh):

time: 114 us -> 103 us (0.904); the launches traced: 113 us -> 103 us
  waiting for transfers between devices: 47.1 us -> 38.8 us
  local copies, waits for them, and re-layouts: 4.32 us -> 0.14 us
  Pallas kernels: 15.8 us -> 17.4 us
  starting transfers between devices: 40.8 us -> 42 us
    ppermute x39, waiting for transfers between devices: 47.1 us -> 38.8 us  [permuted(): return lax.ppermute(value, ('sa', 'sb', 'noise'), pairs)]
    unnamed x24 -> x18, local copies, waits for them, and re-layouts: 4.23 us -> 0.05 us
    pallas_call x1, Pallas kernels: 0.23 us -> 1.76 us  [stretch_shards(): pl.pallas_call(pack_kernel, out_shape=(shaped(192, CHUNK, dtype=bf16), sh...]
    ppermute x39, starting transfers between devices: 40.8 us -> 42 us  [permuted(): return lax.ppermute(value, ('sa', 'sb', 'noise'), pairs)]
where the time goes in v9:
time: 103 us
  starting transfers between devices  42 us (41%)
  waiting for transfers between devices  38.8 us (38%)
  Pallas kernels  17.4 us (17%)
  other arithmetic  3.63 us (4%)
  between operations  1.09 us (1%)
    ppermute x39, starting transfers between devices, permuted(): return lax.ppermute(value, ('sa', 'sb', 'noise'), pairs)  42 us
    ppermute x39, waiting for transfers between devices, permuted(): return lax.ppermute(value, ('sa', 'sb', 'noise'), pairs)  38.8 us
    pallas_call x1, Pallas kernels, stretch_shards(): pl.pallas_call(attention_kernel, out_shape=(shaped(128, 256), shaped(128,...  5.59 us
    pallas_call x1, Pallas kernels, stretch_shards(): pl.pallas_call(forward_kernel, out_shape=(shaped(192, features, dtype=bf1...  5.1 us
    pallas_call x1, Pallas kernels, stretch_shards(): pl.pallas_call(norm_kernel, out_shape=(shaped(128, HID, dtype=bf16), shap...  3.12 us
  transfers between devices with their start and end apart: 39, of which 18 were waited for; matrix products, arithmetic and copies ran while one was open for 3% of the time, Pallas kernels for 5%

profile of v9, /device:TPU:8, one launch (start us, length us, event | category | flops | bytes accessed | tf_op | source)
XLA Modules:
  0.0 103.0 jit_solution(1719422112846716046)
XLA Ops:
  0.0 1.8 %shard_map.100 = (bf16[192,384]{1,0:T(8,128)(2,1)}, bf16[160,384]{1,0:T(8,128)(2,1)}) custom-call(bf16[3,384,384]{2,1,0:T(8,128)(2,1)} %refs_0_.2, bf16[96,1536]{1,0:T(8,128)(2,1)} %refs_1_.2, bf16[384,896]{1,0:T(8,128)(2,1)} %refs_0_.3, bf16[96,1536]{1,0:T(8,128)(2,1)} %refs_1_.3), custom_call_target="tpu_custom_call" | custom-call | tf_op jit(solution)/shard_map/pallas_call | solution.py:567
  1.9 3.0 %collective-permute-start.1 = (bf16[192,384]{1,0:T(8,128)(2,1)}, bf16[192,384]{1,0:T(8,128)(2,1)S(1)}, u32[]{:S(2)}, u32[]{:S(2)}) collective-permute-start(bf16[192,384]{1,0:T(8,128)(2,1)} %get-tuple-element.51), channel_id=1, source_target_pairs={{0,16},{1,17},{2,18},{3,19},{4,20},{5,21},{6,22},{7,23},{8,24},{9,... | collective-permute-start | bytes 442376 | tf_op jit(solution)/shard_map/ppermute | solution.py:241
  4.9 0.5 collective-permute-start.2
  5.3 0.9 convert_element_type.22
  6.3 1.1 %add_convert_fusion = bf16[2,32,1536]{2,1,0:T(8,128)(2,1)S(1)} fusion(bf16[2,32,1536]{2,1,0:T(8,128)(2,1)} %param.11, f32[32,1536]{1,0:T(8,128)S(1)} %convert_element_type.22), kind=kLoop, calls=%fused_computation.1 | loop fusion | flops 294912 | bytes 589824 | tf_op jit(solution)/shard_map/convert_element_type | solution.py:601
  7.4 0.7 and_reduce_fusion
  8.8 1.9 %collective-permute-start.3 = (bf16[32,1536]{1,0:T(8,128)(2,1)S(1)}, bf16[32,1536]{1,0:T(8,128)(2,1)S(1)}, u32[]{:S(2)}, u32[]{:S(2)}) collective-permute-start(bf16[32,1536]{1,0:T(8,128)(2,1)S(1)} %get-tuple-element.99), channel_id=1, source_target_pairs={{0,0},{1,4},{2,2},{3,6},{4,1},{5,5},{6,3},{7,7},{8,9},{9,13},{10,1... | collective-permute-start | bytes 294920 | tf_op jit(solution)/shard_map/ppermute | solution.py:241
  10.7 1.4 %collective-permute-start.4 = (bf16[32,1536]{1,0:T(8,128)(2,1)S(1)}, bf16[32,1536]{1,0:T(8,128)(2,1)S(1)}, u32[]{:S(2)}, u32[]{:S(2)}) collective-permute-start(bf16[32,1536]{1,0:T(8,128)(2,1)S(1)} %get-tuple-element.100), channel_id=1, source_target_pairs={{0,2},{1,6},{2,0},{3,4},{4,3},{5,7},{6,1},{7,5},{8,11},{9,15},{10,... | collective-permute-start | bytes 294920 | tf_op jit(solution)/shard_map/ppermute | solution.py:241
  12.1 1.3 %collective-permute-start.5 = (bf16[32,1536]{1,0:T(8,128)(2,1)S(1)}, bf16[32,1536]{1,0:T(8,128)(2,1)S(1)}, u32[]{:S(2)}, u32[]{:S(2)}) collective-permute-start(bf16[32,1536]{1,0:T(8,128)(2,1)S(1)} %copy-done.5), channel_id=1, source_target_pairs={{0,4},{2,6},{5,1},{7,3},{9,13},{11,15},{12,8},{14,10},{16,20},{18,... | collective-permute-start | bytes 294920 | tf_op jit(solution)/shard_map/ppermute | solution.py:241
  13.4 2.2 %collective-permute-done.1 = bf16[192,384]{1,0:T(8,128)(2,1)S(1)} collective-permute-done((bf16[192,384]{1,0:T(8,128)(2,1)}, bf16[192,384]{1,0:T(8,128)(2,1)S(1)}, u32[]{:S(2)}, u32[]{:S(2)}) %collective-permute-start.1) | collective-permute-done | bytes 147488 | tf_op jit(solution)/shard_map/ppermute | solution.py:241
  15.6 2.8 %collective-permute-done.2 = bf16[192,384]{1,0:T(8,128)(2,1)S(1)} collective-permute-done((bf16[192,384]{1,0:T(8,128)(2,1)}, bf16[192,384]{1,0:T(8,128)(2,1)S(1)}, u32[]{:S(2)}, u32[]{:S(2)}) %collective-permute-start.2) | collective-permute-done | bytes 147488 | tf_op jit(solution)/shard_map/ppermute | solution.py:241
  18.6 1.5 %collective-permute-start.6 = (bf16[3,192,384]{2,1,0:T(8,128)(2,1)S(1)}, bf16[3,192,384]{2,1,0:T(8,128)(2,1)S(1)}, u32[]{:S(2)}, u32[]{:S(2)}) collective-permute-start(bf16[3,192,384]{2,1,0:T(8,128)(2,1)S(1)} %pad_maximum_fusion.refs_2_), channel_id=1, source_target_pairs={{0,2},{1,3},{2,0},{3,1},{4,6},{5,7},{6,4},{7,5},{8,10},{9,11},{10,... | collective-permute-start | bytes 1327112 | tf_op jit(solution)/shard_map/ppermute | solution.py:241
  20.1 1.5 %collective-permute-start.7 = (bf16[3,192,384]{2,1,0:T(8,128)(2,1)S(1)}, bf16[3,192,384]{2,1,0:T(8,128)(2,1)S(1)}, u32[]{:S(2)}, u32[]{:S(2)}) collective-permute-start(bf16[3,192,384]{2,1,0:T(8,128)(2,1)S(1)} %pad_maximum_fusion.refs_2_), channel_id=1, source_target_pairs={{0,4},{1,5},{2,6},{3,7},{4,0},{5,1},{6,2},{7,3},{8,12},{9,13},{10,... | collective-permute-start | bytes 1327112 | tf_op jit(solution)/shard_map/ppermute | solution.py:241
  21.6 1.8 %collective-permute-start.8 = (bf16[160,384]{1,0:T(8,128)(2,1)S(1)}, bf16[160,384]{1,0:T(8,128)(2,1)S(1)}, u32[]{:S(2)}, u32[]{:S(2)}) collective-permute-start(bf16[160,384]{1,0:T(8,128)(2,1)S(1)} %copy-done.8), channel_id=1, source_target_pairs={{0,8},{1,9},{2,10},{3,11},{4,12},{5,13},{6,14},{7,15},{8,0},{9,1},... | collective-permute-start | bytes 368648 | tf_op jit(solution)/shard_map/ppermute | solution.py:241
  23.5 1.7 %collective-permute-start.9 = (bf16[160,384]{1,0:T(8,128)(2,1)S(1)}, bf16[160,384]{1,0:T(8,128)(2,1)S(1)}, u32[]{:S(2)}, u32[]{:S(2)}) collective-permute-start(bf16[160,384]{1,0:T(8,128)(2,1)S(1)} %copy-done.8), channel_id=1, source_target_pairs={{0,16},{1,17},{2,18},{3,19},{4,20},{5,21},{6,22},{7,23},{8,24},{9,... | collective-permute-start | bytes 368648 | tf_op jit(solution)/shard_map/ppermute | solution.py:241
  25.1 2.4 %collective-permute-done.8 = bf16[160,384]{1,0:T(8,128)(2,1)S(1)} collective-permute-done((bf16[160,384]{1,0:T(8,128)(2,1)S(1)}, bf16[160,384]{1,0:T(8,128)(2,1)S(1)}, u32[]{:S(2)}, u32[]{:S(2)}) %collective-permute-start.8) | collective-permute-done | bytes 122912 | tf_op jit(solution)/shard_map/ppermute | solution.py:241
  27.5 3.6 %collective-permute-start.11 = (bf16[48,1536]{1,0:T(8,128)(2,1)S(1)}, bf16[48,1536]{1,0:T(8,128)(2,1)S(1)}, u32[]{:S(2)}, u32[]{:S(2)}) collective-permute-start(bf16[48,1536]{1,0:T(8,128)(2,1)S(1)} %pad_maximum_fusion.2), channel_id=1, source_target_pairs={{1,9},{3,11},{5,13},{7,15},{8,16},{9,1},{10,18},{11,3},{12,20},{13... | collective-permute-start | bytes 442376 | tf_op jit(solution)/shard_map/ppermute | solution.py:241
  31.1 1.6 %collective-permute-done.9 = bf16[160,384]{1,0:T(8,128)(2,1)S(1)} collective-permute-done((bf16[160,384]{1,0:T(8,128)(2,1)S(1)}, bf16[160,384]{1,0:T(8,128)(2,1)S(1)}, u32[]{:S(2)}, u32[]{:S(2)}) %collective-permute-start.9) | collective-permute-done | bytes 122912 | tf_op jit(solution)/shard_map/ppermute | solution.py:241
  32.7 2.3 %collective-permute-done.10 = bf16[160,384]{1,0:T(8,128)(2,1)S(1)} collective-permute-done((bf16[160,384]{1,0:T(8,128)(2,1)S(1)}, bf16[160,384]{1,0:T(8,128)(2,1)S(1)}, u32[]{:S(2)}, u32[]{:S(2)}) %collective-permute-start.10) | collective-permute-done | bytes 122912 | tf_op jit(solution)/shard_map/ppermute | solution.py:241
  35.1 1.5 %collective-permute-done.11.edge = bf16[48,1536]{1,0:T(8,128)(2,1)S(1)} collective-permute-done((bf16[48,1536]{1,0:T(8,128)(2,1)S(1)}, bf16[48,1536]{1,0:T(8,128)(2,1)S(1)}, u32[]{:S(2)}, u32[]{:S(2)}) %collective-permute-start.11) | collective-permute-done | bytes 147488 | tf_op jit(solution)/shard_map/ppermute | solution.py:241
  36.6 1.5 %collective-permute-start.14 = (bf16[3,160,384]{2,1,0:T(8,128)(2,1)S(1)}, bf16[3,160,384]{2,1,0:T(8,128)(2,1)S(1)}, u32[]{:S(2)}, u32[]{:S(2)}) collective-permute-start(bf16[3,160,384]{2,1,0:T(8,128)(2,1)S(1)} %pad_maximum_fusion.1.refs_2_), channel_id=1, source_target_pairs={{0,2},{1,3},{2,0},{3,1},{4,6},{5,7},{6,4},{7,5},{8,10},{9,11},{10,... | collective-permute-start | bytes 1105928 | tf_op jit(solution)/shard_map/ppermute | solution.py:241
  38.4 1.8 %collective-permute-start.12 = (bf16[3,96,384]{2,1,0:T(8,128)(2,1)S(1)}, bf16[3,96,384]{2,1,0:T(8,128)(2,1)S(1)}, u32[]{:S(2)}, u32[]{:S(2)}) collective-permute-start(bf16[3,96,384]{2,1,0:T(8,128)(2,1)S(1)} %slice.48), channel_id=1, source_target_pairs={{0,4},{1,5},{2,6},{3,7},{4,0},{5,1},{6,2},{7,3},{8,12},{9,13},{10,... | collective-permute-start | bytes 663560 | tf_op jit(solution)/shard_map/ppermute | solution.py:241
  40.2 0.6 collective-permute-start.13
  40.8 1.5 %collective-permute-start.16 = (bf16[32,1536]{1,0:T(8,128)(2,1)S(1)}, bf16[32,1536]{1,0:T(8,128)(2,1)S(1)}, u32[]{:S(2)}, u32[]{:S(2)}) collective-permute-start(bf16[32,1536]{1,0:T(8,128)(2,1)S(1)} %broadcast_select_fusion.cot_block), channel_id=1, source_target_pairs={{0,2},{1,3},{2,0},{3,1},{4,6},{5,7},{6,4},{7,5},{8,10},{9,11},{10,... | collective-permute-start | bytes 294920 | tf_op jit(solution)/shard_map/ppermute | solution.py:241
  42.3 9.1 %collective-permute-done.16.cot_beside = bf16[32,1536]{1,0:T(8,128)(2,1)S(1)} collective-permute-done((bf16[32,1536]{1,0:T(8,128)(2,1)S(1)}, bf16[32,1536]{1,0:T(8,128)(2,1)S(1)}, u32[]{:S(2)}, u32[]{:S(2)}) %collective-permute-start.16) | collective-permute-done | bytes 98336 | tf_op jit(solution)/shard_map/ppermute | solution.py:241
  51.5 0.5 collective-permute-start.18
  52.1 0.4 collective-permute-start.20
  53.0 1.6 %collective-permute-start.28 = (bf16[3,80,384]{2,1,0:T(8,128)(2,1)S(1)}, bf16[3,80,384]{2,1,0:T(8,128)(2,1)S(1)}, u32[]{:S(2)}, u32[]{:S(2)}) collective-permute-start(bf16[3,80,384]{2,1,0:T(8,128)(2,1)S(1)} %slice.51), channel_id=1, source_target_pairs={{0,2},{1,3},{2,0},{3,1},{4,6},{5,7},{6,4},{7,5},{8,10},{9,11},{10,... | collective-permute-start | bytes 552968 | tf_op jit(solution)/shard_map/ppermute | solution.py:241
  54.8 1.1 %collective-permute-done.26.other_beside = bf16[32,1536]{1,0:T(8,128)(2,1)S(1)} collective-permute-done((bf16[32,1536]{1,0:T(8,128)(2,1)S(1)}, bf16[32,1536]{1,0:T(8,128)(2,1)S(1)}, u32[]{:S(2)}, u32[]{:S(2)}) %collective-permute-start.26) | collective-permute-done | bytes 98336 | tf_op jit(solution)/shard_map/ppermute | solution.py:241
  56.4 2.8 %collective-permute-done.27.refs_5_ = bf16[3,80,384]{2,1,0:T(8,128)(2,1)S(1)} collective-permute-done((bf16[3,80,384]{2,1,0:T(8,128)(2,1)S(1)}, bf16[3,80,384]{2,1,0:T(8,128)(2,1)S(1)}, u32[]{:S(2)}, u32[]{:S(2)}) %collective-permute-start.27) | collective-permute-done | bytes 184352 | tf_op jit(solution)/shard_map/ppermute | solution.py:241
  59.3 0.7 collective-permute-done.28.refs_6_
  59.9 0.8 collective-permute-done.23.refs_10_
  60.9 0.5 collective-permute-done.24.refs_11_
  61.5 0.4 collective-permute-start.31
  62.5 5.1 %shard_map.101 = (bf16[192,1536]{1,0:T(8,128)(2,1)S(1)}, f32[128,1536]{1,0:T(8,128)S(1)}, f32[128,1]{1,0:T(8,128)S(1)}, f32[128,384]{1,0:T(8,128)S(1)}, bf16[3,1...) custom-call(bf16[32,1536]{1,0:T(8,128)(2,1)S(1)} %collective-permute-done.3.blocks_even, ...), custom_call_target="tpu_custom_call" | custom-call | tf_op jit(solution)/shard_map/pallas_call | solution.py:642
  67.6 5.6 %shard_map.102 = (f32[128,256]{1,0:T(8,128)S(1)}, f32[128,640]{1,0:T(8,128)S(1)}, bf16[32,640]{1,0:T(8,128)(2,1)S(1)}, bf16[1536,896]{1,0:T(8,128)(2,1)S(1)}, bf16[128,1536]{1,0:T(8,128)(2,1)S(1)}) custom-call(s32[4]{0:T(128)S(1)} %copy-done.4, s32[1]{0:T(128)} %bitcast.3.flag, bf16[192,1536]{1,0:T(8,128)(2,1)S(1)} %get-tuple-element.76.normed, ...), custom_call_target="tpu_custom_call" | custom-call | tf_op jit(solution)/shard_map/pallas_call | solution.py:658
  73.2 4.1 %collective-permute-start.34 = (bf16[32,640]{1,0:T(8,128)(2,1)S(1)}, bf16[32,640]{1,0:T(8,128)(2,1)S(1)}, u32[]{:S(2)}, u32[]{:S(2)}) collective-permute-start(bf16[32,640]{1,0:T(8,128)(2,1)S(1)} %get-tuple-element.84), channel_id=1, source_target_pairs={{1,9},{3,11},{5,13},{7,15},{8,16},{9,1},{10,18},{11,3},{12,20},{13... | collective-permute-start | bytes 122888 | tf_op jit(solution)/shard_map/ppermute | solution.py:241
  77.4 2.0 %collective-permute-done.34.received = bf16[32,640]{1,0:T(8,128)(2,1)S(1)} collective-permute-done((bf16[32,640]{1,0:T(8,128)(2,1)S(1)}, bf16[32,640]{1,0:T(8,128)(2,1)S(1)}, u32[]{:S(2)}, u32[]{:S(2)}) %collective-permute-start.34) | collective-permute-done | bytes 40992 | tf_op jit(solution)/shard_map/ppermute | solution.py:241
  79.4 3.1 %shard_map.103 = (bf16[128,384]{1,0:T(8,128)(2,1)S(1)}, f32[64,1536]{1,0:T(8,128)S(1)}, bf16[16,384]{1,0:T(8,128)(2,1)S(1)}) custom-call(f32[128,256]{1,0:T(8,128)S(1)} %get-tuple-element.82.d_q, f32[128,640]{1,0:T(8,128)S(1)} %get-tuple-element.83.d_kv, bf16[32,640]{1,0:T(8,128)(2,1)S(1)} %collective-permute-done.34.received, ...), custom_call_target="tpu_custom_call" | custom-call | tf_op jit(solution)/shard_map/pallas_call | solution.py:674
  82.5 3.9 %collective-permute-start.35 = (bf16[16,384]{1,0:T(8,128)(2,1)S(1)}, bf16[16,384]{1,0:T(8,128)(2,1)S(1)}, u32[]{:S(2)}, u32[]{:S(2)}) collective-permute-start(bf16[16,384]{1,0:T(8,128)(2,1)S(1)} %get-tuple-element.92), channel_id=1, source_target_pairs={{1,9},{3,11},{5,13},{7,15},{8,16},{9,1},{10,18},{11,3},{12,20},{13... | collective-permute-start | bytes 36872 | tf_op jit(solution)/shard_map/ppermute | solution.py:241
  86.4 1.7 %collective-permute-done.35.received = bf16[16,384]{1,0:T(8,128)(2,1)S(1)} collective-permute-done((bf16[16,384]{1,0:T(8,128)(2,1)S(1)}, bf16[16,384]{1,0:T(8,128)(2,1)S(1)}, u32[]{:S(2)}, u32[]{:S(2)}) %collective-permute-start.35) | collective-permute-done | bytes 12320 | tf_op jit(solution)/shard_map/ppermute | solution.py:241
  88.1 1.8 %shard_map.104 = (f32[32,1536]{1,0:T(8,128)S(1)}, bf16[32,1536]{1,0:T(8,128)(2,1)S(1)}) custom-call(bf16[128,384]{1,0:T(8,128)(2,1)S(1)} %get-tuple-element.91.d_hidden, bf16[16,384]{1,0:T(8,128)(2,1)S(1)} %collective-permute-done.35.received, f32[64,1536]{1,0:T(8,128)S(1)} %get-tuple-element.93.d_resid, ...), custom_call_target="tpu_custom_call" | custom-call | tf_op jit(solution)/shard_map/pallas_call | solution.py:686
  89.9 1.5 %collective-permute-start.36 = (bf16[32,1536]{1,0:T(8,128)(2,1)S(1)}, bf16[32,1536]{1,0:T(8,128)(2,1)S(1)}, u32[]{:S(2)}, u32[]{:S(2)}) collective-permute-start(bf16[32,1536]{1,0:T(8,128)(2,1)S(1)} %get-tuple-element.96), channel_id=1, source_target_pairs={{0,2},{1,3},{2,0},{3,1},{4,6},{5,7},{6,4},{7,5},{8,10},{9,11},{10,... | collective-permute-start | bytes 294920 | tf_op jit(solution)/shard_map/ppermute | solution.py:241
  91.4 3.2 %collective-permute-done.36 = bf16[32,1536]{1,0:T(8,128)(2,1)S(1)} collective-permute-done((bf16[32,1536]{1,0:T(8,128)(2,1)S(1)}, bf16[32,1536]{1,0:T(8,128)(2,1)S(1)}, u32[]{:S(2)}, u32[]{:S(2)}) %collective-permute-start.36) | collective-permute-done | bytes 98336 | tf_op jit(solution)/shard_map/ppermute | solution.py:241
  94.6 1.8 %collective-permute-start.37 = (bf16[32,1536]{1,0:T(8,128)(2,1)S(1)}, bf16[32,1536]{1,0:T(8,128)(2,1)S(1)}, u32[]{:S(2)}, u32[]{:S(2)}) collective-permute-start(bf16[32,1536]{1,0:T(8,128)(2,1)S(1)} %add_convert_fusion.1), channel_id=1, source_target_pairs={{0,1},{1,5},{2,3},{3,7},{4,0},{5,4},{6,2},{7,6},{8,12},{9,8},{10,1... | collective-permute-start | bytes 294920 | tf_op jit(solution)/shard_map/ppermute | solution.py:241
  96.4 1.9 %collective-permute-start.38 = (bf16[32,1536]{1,0:T(8,128)(2,1)S(1)}, bf16[32,1536]{1,0:T(8,128)(2,1)S(1)}, u32[]{:S(2)}, u32[]{:S(2)}) collective-permute-start(bf16[32,1536]{1,0:T(8,128)(2,1)S(1)} %add_convert_fusion.1), channel_id=1, source_target_pairs={{1,4},{3,6},{4,1},{6,3},{8,13},{10,15},{13,8},{15,10},{17,20},{19,... | collective-permute-start | bytes 294920 | tf_op jit(solution)/shard_map/ppermute | solution.py:241
  98.6 3.7 %collective-permute-done.38 = bf16[32,1536]{1,0:T(8,128)(2,1)S(1)} collective-permute-done((bf16[32,1536]{1,0:T(8,128)(2,1)S(1)}, bf16[32,1536]{1,0:T(8,128)(2,1)S(1)}, u32[]{:S(2)}, u32[]{:S(2)}) %collective-permute-start.38) | collective-permute-done | bytes 98336 | tf_op jit(solution)/shard_map/ppermute | solution.py:241
  102.3 0.7 add_multiply_fusion
  (70 shorter events, 3.1 us)
Async XLA Ops:
  0.0 7.4 %copy-start.7 = (s32[16,2]{0,1:T(2,128)S(1)}, s32[16,2]{0,1:T(2,128)}, u32[]{:S(2)}) copy-start(s32[16,2]{0,1:T(2,128)} %param.19) | copy-start | bytes 388
  0.0 12.1 %copy-start.5 = (bf16[32,1536]{1,0:T(8,128)(2,1)S(1)}, bf16[32,1536]{1,0:T(8,128)(2,1)}, u32[]{:S(2)}) copy-start(bf16[32,1536]{1,0:T(8,128)(2,1)} %param.12) | copy-start | bytes 294916
  1.8 19.9 %copy-start.8 = (bf16[160,384]{1,0:T(8,128)(2,1)S(1)}, bf16[160,384]{1,0:T(8,128)(2,1)}, u32[]{:S(2)}) copy-start(bf16[160,384]{1,0:T(8,128)(2,1)} %get-tuple-element.57) | copy-start | bytes 368644
  1.8 7.0 %collective-permute-start = (bf16[192,384]{1,0:T(8,128)(2,1)}, bf16[192,384]{1,0:T(8,128)(2,1)S(1)}, u32[]{:S(2)}, u32[]{:S(2)}) collective-permute-start(bf16[192,384]{1,0:T(8,128)(2,1)} %get-tuple-element.51), channel_id=1, source_target_pairs={{0,8},{1,9},{2,10},{3,11},{4,12},{5,13},{6,14},{7,15},{8,0},{9,1},... | collective-permute-start | bytes 442376 | tf_op jit(solution)/shard_map/ppermute | solution.py:241
  1.9 13.8 %collective-permute-start.1 = (bf16[192,384]{1,0:T(8,128)(2,1)}, bf16[192,384]{1,0:T(8,128)(2,1)S(1)}, u32[]{:S(2)}, u32[]{:S(2)}) collective-permute-start(bf16[192,384]{1,0:T(8,128)(2,1)} %get-tuple-element.51), channel_id=1, source_target_pairs={{0,16},{1,17},{2,18},{3,19},{4,20},{5,21},{6,22},{7,23},{8,24},{9,... | collective-permute-start | bytes 442376 | tf_op jit(solution)/shard_map/ppermute | solution.py:241
  4.9 13.5 %collective-permute-start.2 = (bf16[192,384]{1,0:T(8,128)(2,1)}, bf16[192,384]{1,0:T(8,128)(2,1)S(1)}, u32[]{:S(2)}, u32[]{:S(2)}) collective-permute-start(bf16[192,384]{1,0:T(8,128)(2,1)} %get-tuple-element.51), channel_id=1, source_target_pairs={{0,24},{1,25},{2,26},{3,27},{4,28},{5,29},{6,30},{7,31},{8,16},{9,... | collective-permute-start | bytes 442376 | tf_op jit(solution)/shard_map/ppermute | solution.py:241
  6.2 56.2 %copy-start.6 = (f32[1536]{0:T(1024)S(1)}, f32[1536]{0:T(1024)}, u32[]{:S(2)}) copy-start(f32[1536]{0:T(1024)} %param.15) | copy-start | bytes 18436
  6.3 56.2 %copy-start = (bf16[3,384,384]{2,1,0:T(8,128)(2,1)S(1)}, bf16[3,384,384]{2,1,0:T(8,128)(2,1)}, u32[]{:S(2)}) copy-start(bf16[3,384,384]{2,1,0:T(8,128)(2,1)} %refs_0_.2) | copy-start | bytes 2654212
  6.3 56.2 %copy-start.2 = (bf16[96,1536]{1,0:T(8,128)(2,1)S(1)}, bf16[96,1536]{1,0:T(8,128)(2,1)}, u32[]{:S(2)}) copy-start(bf16[96,1536]{1,0:T(8,128)(2,1)} %refs_1_.2) | copy-start | bytes 884740
  8.8 9.6 %collective-permute-start.3 = (bf16[32,1536]{1,0:T(8,128)(2,1)S(1)}, bf16[32,1536]{1,0:T(8,128)(2,1)S(1)}, u32[]{:S(2)}, u32[]{:S(2)}) collective-permute-start(bf16[32,1536]{1,0:T(8,128)(2,1)S(1)} %get-tuple-element.99), channel_id=1, source_target_pairs={{0,0},{1,4},{2,2},{3,6},{4,1},{5,5},{6,3},{7,7},{8,9},{9,13},{10,1... | collective-permute-start | bytes 294920 | tf_op jit(solution)/shard_map/ppermute | solution.py:241
  10.7 7.7 %collective-permute-start.4 = (bf16[32,1536]{1,0:T(8,128)(2,1)S(1)}, bf16[32,1536]{1,0:T(8,128)(2,1)S(1)}, u32[]{:S(2)}, u32[]{:S(2)}) collective-permute-start(bf16[32,1536]{1,0:T(8,128)(2,1)S(1)} %get-tuple-element.100), channel_id=1, source_target_pairs={{0,2},{1,6},{2,0},{3,4},{4,3},{5,7},{6,1},{7,5},{8,11},{9,15},{10,... | collective-permute-start | bytes 294920 | tf_op jit(solution)/shard_map/ppermute | solution.py:241
  12.1 6.5 %collective-permute-start.5 = (bf16[32,1536]{1,0:T(8,128)(2,1)S(1)}, bf16[32,1536]{1,0:T(8,128)(2,1)S(1)}, u32[]{:S(2)}, u32[]{:S(2)}) collective-permute-start(bf16[32,1536]{1,0:T(8,128)(2,1)S(1)} %copy-done.5), channel_id=1, source_target_pairs={{0,4},{2,6},{5,1},{7,3},{9,13},{11,15},{12,8},{14,10},{16,20},{18,... | collective-permute-start | bytes 294920 | tf_op jit(solution)/shard_map/ppermute | solution.py:241
  18.6 18.0 %collective-permute-start.6 = (bf16[3,192,384]{2,1,0:T(8,128)(2,1)S(1)}, bf16[3,192,384]{2,1,0:T(8,128)(2,1)S(1)}, u32[]{:S(2)}, u32[]{:S(2)}) collective-permute-start(bf16[3,192,384]{2,1,0:T(8,128)(2,1)S(1)} %pad_maximum_fusion.refs_2_), channel_id=1, source_target_pairs={{0,2},{1,3},{2,0},{3,1},{4,6},{5,7},{6,4},{7,5},{8,10},{9,11},{10,... | collective-permute-start | bytes 1327112 | tf_op jit(solution)/shard_map/ppermute | solution.py:241
  20.1 16.5 %collective-permute-start.7 = (bf16[3,192,384]{2,1,0:T(8,128)(2,1)S(1)}, bf16[3,192,384]{2,1,0:T(8,128)(2,1)S(1)}, u32[]{:S(2)}, u32[]{:S(2)}) collective-permute-start(bf16[3,192,384]{2,1,0:T(8,128)(2,1)S(1)} %pad_maximum_fusion.refs_2_), channel_id=1, source_target_pairs={{0,4},{1,5},{2,6},{3,7},{4,0},{5,1},{6,2},{7,3},{8,12},{9,13},{10,... | collective-permute-start | bytes 1327112 | tf_op jit(solution)/shard_map/ppermute | solution.py:241
  21.6 5.9 %collective-permute-start.8 = (bf16[160,384]{1,0:T(8,128)(2,1)S(1)}, bf16[160,384]{1,0:T(8,128)(2,1)S(1)}, u32[]{:S(2)}, u32[]{:S(2)}) collective-permute-start(bf16[160,384]{1,0:T(8,128)(2,1)S(1)} %copy-done.8), channel_id=1, source_target_pairs={{0,8},{1,9},{2,10},{3,11},{4,12},{5,13},{6,14},{7,15},{8,0},{9,1},... | collective-permute-start | bytes 368648 | tf_op jit(solution)/shard_map/ppermute | solution.py:241
  23.5 9.2 %collective-permute-start.9 = (bf16[160,384]{1,0:T(8,128)(2,1)S(1)}, bf16[160,384]{1,0:T(8,128)(2,1)S(1)}, u32[]{:S(2)}, u32[]{:S(2)}) collective-permute-start(bf16[160,384]{1,0:T(8,128)(2,1)S(1)} %copy-done.8), channel_id=1, source_target_pairs={{0,16},{1,17},{2,18},{3,19},{4,20},{5,21},{6,22},{7,23},{8,24},{9,... | collective-permute-start | bytes 368648 | tf_op jit(solution)/shard_map/ppermute | solution.py:241
  25.1 9.9 %collective-permute-start.10 = (bf16[160,384]{1,0:T(8,128)(2,1)S(1)}, bf16[160,384]{1,0:T(8,128)(2,1)S(1)}, u32[]{:S(2)}, u32[]{:S(2)}) collective-permute-start(bf16[160,384]{1,0:T(8,128)(2,1)S(1)} %copy-done.8), channel_id=1, source_target_pairs={{0,24},{1,25},{2,26},{3,27},{4,28},{5,29},{6,30},{7,31},{8,16},{9,... | collective-permute-start | bytes 368648 | tf_op jit(solution)/shard_map/ppermute | solution.py:241
  27.5 9.1 %collective-permute-start.11 = (bf16[48,1536]{1,0:T(8,128)(2,1)S(1)}, bf16[48,1536]{1,0:T(8,128)(2,1)S(1)}, u32[]{:S(2)}, u32[]{:S(2)}) collective-permute-start(bf16[48,1536]{1,0:T(8,128)(2,1)S(1)} %pad_maximum_fusion.2), channel_id=1, source_target_pairs={{1,9},{3,11},{5,13},{7,15},{8,16},{9,1},{10,18},{11,3},{12,20},{13... | collective-permute-start | bytes 442376 | tf_op jit(solution)/shard_map/ppermute | solution.py:241
  36.6 14.8 %collective-permute-start.14 = (bf16[3,160,384]{2,1,0:T(8,128)(2,1)S(1)}, bf16[3,160,384]{2,1,0:T(8,128)(2,1)S(1)}, u32[]{:S(2)}, u32[]{:S(2)}) collective-permute-start(bf16[3,160,384]{2,1,0:T(8,128)(2,1)S(1)} %pad_maximum_fusion.1.refs_2_), channel_id=1, source_target_pairs={{0,2},{1,3},{2,0},{3,1},{4,6},{5,7},{6,4},{7,5},{8,10},{9,11},{10,... | collective-permute-start | bytes 1105928 | tf_op jit(solution)/shard_map/ppermute | solution.py:241
  38.1 13.4 %collective-permute-start.15 = (bf16[3,160,384]{2,1,0:T(8,128)(2,1)S(1)}, bf16[3,160,384]{2,1,0:T(8,128)(2,1)S(1)}, u32[]{:S(2)}, u32[]{:S(2)}) collective-permute-start(bf16[3,160,384]{2,1,0:T(8,128)(2,1)S(1)} %pad_maximum_fusion.1.refs_2_), channel_id=1, source_target_pairs={{0,4},{1,5},{2,6},{3,7},{4,0},{5,1},{6,2},{7,3},{8,12},{9,13},{10,... | collective-permute-start | bytes 1105928 | tf_op jit(solution)/shard_map/ppermute | solution.py:241
  38.4 13.0 %collective-permute-start.12 = (bf16[3,96,384]{2,1,0:T(8,128)(2,1)S(1)}, bf16[3,96,384]{2,1,0:T(8,128)(2,1)S(1)}, u32[]{:S(2)}, u32[]{:S(2)}) collective-permute-start(bf16[3,96,384]{2,1,0:T(8,128)(2,1)S(1)} %slice.48), channel_id=1, source_target_pairs={{0,4},{1,5},{2,6},{3,7},{4,0},{5,1},{6,2},{7,3},{8,12},{9,13},{10,... | collective-permute-start | bytes 663560 | tf_op jit(solution)/shard_map/ppermute | solution.py:241
  40.2 11.2 %collective-permute-start.13 = (bf16[3,96,384]{2,1,0:T(8,128)(2,1)S(1)}, bf16[3,96,384]{2,1,0:T(8,128)(2,1)S(1)}, u32[]{:S(2)}, u32[]{:S(2)}) collective-permute-start(bf16[3,96,384]{2,1,0:T(8,128)(2,1)S(1)} %slice.49), channel_id=1, source_target_pairs={{0,2},{1,3},{2,0},{3,1},{4,6},{5,7},{6,4},{7,5},{8,10},{9,11},{10,... | collective-permute-start | bytes 663560 | tf_op jit(solution)/shard_map/ppermute | solution.py:241
  40.8 10.6 %collective-permute-start.16 = (bf16[32,1536]{1,0:T(8,128)(2,1)S(1)}, bf16[32,1536]{1,0:T(8,128)(2,1)S(1)}, u32[]{:S(2)}, u32[]{:S(2)}) collective-permute-start(bf16[32,1536]{1,0:T(8,128)(2,1)S(1)} %broadcast_select_fusion.cot_block), channel_id=1, source_target_pairs={{0,2},{1,3},{2,0},{3,1},{4,6},{5,7},{6,4},{7,5},{8,10},{9,11},{10,... | collective-permute-start | bytes 294920 | tf_op jit(solution)/shard_map/ppermute | solution.py:241
  51.5 1.4 %collective-permute-start.17 = (bf16[32,1536]{1,0:T(8,128)(2,1)S(1)}, bf16[32,1536]{1,0:T(8,128)(2,1)S(1)}, u32[]{:S(2)}, u32[]{:S(2)}) collective-permute-start(bf16[32,1536]{1,0:T(8,128)(2,1)S(1)} %collective-permute-done.3.blocks_even), channel_id=1, source_target_pairs={{0,1},{1,0},{2,3},{3,2},{4,5},{5,4},{6,7},{7,6},{8,9},{9,8},{10,11... | collective-permute-start | bytes 294920 | tf_op jit(solution)/shard_map/ppermute | solution.py:241
  51.5 1.4 %collective-permute-start.18 = (bf16[32,1536]{1,0:T(8,128)(2,1)S(1)}, bf16[32,1536]{1,0:T(8,128)(2,1)S(1)}, u32[]{:S(2)}, u32[]{:S(2)}) collective-permute-start(bf16[32,1536]{1,0:T(8,128)(2,1)S(1)} %collective-permute-done.4.blocks_odd), channel_id=1, source_target_pairs={{0,1},{1,0},{2,3},{3,2},{4,5},{5,4},{6,7},{7,6},{8,9},{9,8},{10,11... | collective-permute-start | bytes 294920 | tf_op jit(solution)/shard_map/ppermute | solution.py:241
  52.0 2.6 %collective-permute-start.25 = (bf16[32,1536]{1,0:T(8,128)(2,1)S(1)}, bf16[32,1536]{1,0:T(8,128)(2,1)S(1)}, u32[]{:S(2)}, u32[]{:S(2)}) collective-permute-start(bf16[32,1536]{1,0:T(8,128)(2,1)S(1)} %broadcast_select_fusion.cot_block), channel_id=1, source_target_pairs={{0,1},{1,0},{2,3},{3,2},{4,5},{5,4},{6,7},{7,6},{8,9},{9,8},{10,11... | collective-permute-start | bytes 294920 | tf_op jit(solution)/shard_map/ppermute | solution.py:241
  52.1 9.4 %collective-permute-start.20 = (bf16[3,192,384]{2,1,0:T(8,128)(2,1)S(1)}, bf16[3,192,384]{2,1,0:T(8,128)(2,1)S(1)}, u32[]{:S(2)}, u32[]{:S(2)}) collective-permute-start(bf16[3,192,384]{2,1,0:T(8,128)(2,1)S(1)} %pad_maximum_fusion.refs_2_), channel_id=1, source_target_pairs={{0,1},{1,0},{2,3},{3,2},{4,5},{5,4},{6,7},{7,6},{8,9},{9,8},{10,11... | collective-permute-start | bytes 1327112 | tf_op jit(solution)/shard_map/ppermute | solution.py:241
  52.6 6.7 %collective-permute-start.27 = (bf16[3,80,384]{2,1,0:T(8,128)(2,1)S(1)}, bf16[3,80,384]{2,1,0:T(8,128)(2,1)S(1)}, u32[]{:S(2)}, u32[]{:S(2)}) collective-permute-start(bf16[3,80,384]{2,1,0:T(8,128)(2,1)S(1)} %slice.50), channel_id=1, source_target_pairs={{0,4},{1,5},{2,6},{3,7},{4,0},{5,1},{6,2},{7,3},{8,12},{9,13},{10,... | collective-permute-start | bytes 552968 | tf_op jit(solution)/shard_map/ppermute | solution.py:241
  52.7 14.9 %copy-start.1 = (bf16[384,896]{1,0:T(8,128)(2,1)S(1)}, bf16[384,896]{1,0:T(8,128)(2,1)}, u32[]{:S(2)}) copy-start(bf16[384,896]{1,0:T(8,128)(2,1)} %refs_0_.3) | copy-start | bytes 2064388
  52.8 14.9 %copy-start.3 = (bf16[96,1536]{1,0:T(8,128)(2,1)S(1)}, bf16[96,1536]{1,0:T(8,128)(2,1)}, u32[]{:S(2)}) copy-start(bf16[96,1536]{1,0:T(8,128)(2,1)} %refs_1_.3) | copy-start | bytes 884740
  52.8 14.9 %copy-start.4 = (s32[4]{0:T(128)S(1)}, s32[4]{0:T(128)}, u32[]{:S(2)}) copy-start(s32[4]{0:T(128)} %band.1) | copy-start | bytes 52
  52.8 3.3 %collective-permute-start.19 = (bf16[48,1536]{1,0:T(8,128)(2,1)S(1)}, bf16[48,1536]{1,0:T(8,128)(2,1)S(1)}, u32[]{:S(2)}, u32[]{:S(2)}) collective-permute-start(bf16[48,1536]{1,0:T(8,128)(2,1)S(1)} %collective-permute-done.11.edge), channel_id=1, source_target_pairs={{0,1},{1,0},{2,3},{3,2},{4,5},{5,4},{6,7},{7,6},{8,9},{9,8},{10,11... | collective-permute-start | bytes 442376 | tf_op jit(solution)/shard_map/ppermute | solution.py:241
  53.0 6.9 %collective-permute-start.28 = (bf16[3,80,384]{2,1,0:T(8,128)(2,1)S(1)}, bf16[3,80,384]{2,1,0:T(8,128)(2,1)S(1)}, u32[]{:S(2)}, u32[]{:S(2)}) collective-permute-start(bf16[3,80,384]{2,1,0:T(8,128)(2,1)S(1)} %slice.51), channel_id=1, source_target_pairs={{0,2},{1,3},{2,0},{3,1},{4,6},{5,7},{6,4},{7,5},{8,10},{9,11},{10,... | collective-permute-start | bytes 552968 | tf_op jit(solution)/shard_map/ppermute | solution.py:241
  54.6 1.3 %collective-permute-start.26 = (bf16[32,1536]{1,0:T(8,128)(2,1)S(1)}, bf16[32,1536]{1,0:T(8,128)(2,1)S(1)}, u32[]{:S(2)}, u32[]{:S(2)}) collective-permute-start(bf16[32,1536]{1,0:T(8,128)(2,1)S(1)} %collective-permute-done.16.cot_beside), channel_id=1, source_target_pairs={{0,1},{1,0},{2,3},{3,2},{4,5},{5,4},{6,7},{7,6},{8,9},{9,8},{10,11... | collective-permute-start | bytes 294920 | tf_op jit(solution)/shard_map/ppermute | solution.py:241
  55.9 6.0 %collective-permute-start.21 = (bf16[3,192,384]{2,1,0:T(8,128)(2,1)S(1)}, bf16[3,192,384]{2,1,0:T(8,128)(2,1)S(1)}, u32[]{:S(2)}, u32[]{:S(2)}) collective-permute-start(bf16[3,192,384]{2,1,0:T(8,128)(2,1)S(1)} %collective-permute-done.6.refs_3_), channel_id=1, source_target_pairs={{0,1},{1,0},{2,3},{3,2},{4,5},{5,4},{6,7},{7,6},{8,9},{9,8},{10,11... | collective-permute-start | bytes 1327112 | tf_op jit(solution)/shard_map/ppermute | solution.py:241
  56.1 6.0 %collective-permute-start.22 = (bf16[3,192,384]{2,1,0:T(8,128)(2,1)S(1)}, bf16[3,192,384]{2,1,0:T(8,128)(2,1)S(1)}, u32[]{:S(2)}, u32[]{:S(2)}) collective-permute-start(bf16[3,192,384]{2,1,0:T(8,128)(2,1)S(1)} %collective-permute-done.7.refs_4_), channel_id=1, source_target_pairs={{0,1},{1,0},{2,3},{3,2},{4,5},{5,4},{6,7},{7,6},{8,9},{9,8},{10,11... | collective-permute-start | bytes 1327112 | tf_op jit(solution)/shard_map/ppermute | solution.py:241
  59.2 1.5 %collective-permute-start.23 = (bf16[3,96,384]{2,1,0:T(8,128)(2,1)S(1)}, bf16[3,96,384]{2,1,0:T(8,128)(2,1)S(1)}, u32[]{:S(2)}, u32[]{:S(2)}) collective-permute-start(bf16[3,96,384]{2,1,0:T(8,128)(2,1)S(1)} %collective-permute-done.12.refs_5_), channel_id=1, source_target_pairs={{0,1},{1,0},{2,3},{3,2},{4,5},{5,4},{6,7},{7,6},{8,9},{9,8},{10,11... | collective-permute-start | bytes 663560 | tf_op jit(solution)/shard_map/ppermute | solution.py:241
  59.9 1.5 %collective-permute-start.24 = (bf16[3,96,384]{2,1,0:T(8,128)(2,1)S(1)}, bf16[3,96,384]{2,1,0:T(8,128)(2,1)S(1)}, u32[]{:S(2)}, u32[]{:S(2)}) collective-permute-start(bf16[3,96,384]{2,1,0:T(8,128)(2,1)S(1)} %collective-permute-done.13.refs_6_), channel_id=1, source_target_pairs={{0,1},{1,0},{2,3},{3,2},{4,5},{5,4},{6,7},{7,6},{8,9},{9,8},{10,11... | collective-permute-start | bytes 663560 | tf_op jit(solution)/shard_map/ppermute | solution.py:241
  60.7 6.9 %collective-permute-start.30 = (bf16[3,160,384]{2,1,0:T(8,128)(2,1)S(1)}, bf16[3,160,384]{2,1,0:T(8,128)(2,1)S(1)}, u32[]{:S(2)}, u32[]{:S(2)}) collective-permute-start(bf16[3,160,384]{2,1,0:T(8,128)(2,1)S(1)} %collective-permute-done.14.refs_3_), channel_id=1, source_target_pairs={{0,1},{1,0},{2,3},{3,2},{4,5},{5,4},{6,7},{7,6},{8,9},{9,8},{10,11... | collective-permute-start | bytes 1105928 | tf_op jit(solution)/shard_map/ppermute | solution.py:241
  61.4 6.2 %collective-permute-start.29 = (bf16[3,160,384]{2,1,0:T(8,128)(2,1)S(1)}, bf16[3,160,384]{2,1,0:T(8,128)(2,1)S(1)}, u32[]{:S(2)}, u32[]{:S(2)}) collective-permute-start(bf16[3,160,384]{2,1,0:T(8,128)(2,1)S(1)} %pad_maximum_fusion.1.refs_2_), channel_id=1, source_target_pairs={{0,1},{1,0},{2,3},{3,2},{4,5},{5,4},{6,7},{7,6},{8,9},{9,8},{10,11... | collective-permute-start | bytes 1105928 | tf_op jit(solution)/shard_map/ppermute | solution.py:241
  61.5 6.1 %collective-permute-start.31 = (bf16[3,160,384]{2,1,0:T(8,128)(2,1)S(1)}, bf16[3,160,384]{2,1,0:T(8,128)(2,1)S(1)}, u32[]{:S(2)}, u32[]{:S(2)}) collective-permute-start(bf16[3,160,384]{2,1,0:T(8,128)(2,1)S(1)} %collective-permute-done.15.refs_4_), channel_id=1, source_target_pairs={{0,1},{1,0},{2,3},{3,2},{4,5},{5,4},{6,7},{7,6},{8,9},{9,8},{10,11... | collective-permute-start | bytes 1105928 | tf_op jit(solution)/shard_map/ppermute | solution.py:241
  61.9 5.7 %collective-permute-start.32 = (bf16[3,80,384]{2,1,0:T(8,128)(2,1)S(1)}, bf16[3,80,384]{2,1,0:T(8,128)(2,1)S(1)}, u32[]{:S(2)}, u32[]{:S(2)}) collective-permute-start(bf16[3,80,384]{2,1,0:T(8,128)(2,1)S(1)} %collective-permute-done.27.refs_5_), channel_id=1, source_target_pairs={{0,1},{1,0},{2,3},{3,2},{4,5},{5,4},{6,7},{7,6},{8,9},{9,8},{10,11... | collective-permute-start | bytes 552968 | tf_op jit(solution)/shard_map/ppermute | solution.py:241
  62.0 5.5 %collective-permute-start.33 = (bf16[3,80,384]{2,1,0:T(8,128)(2,1)S(1)}, bf16[3,80,384]{2,1,0:T(8,128)(2,1)S(1)}, u32[]{:S(2)}, u32[]{:S(2)}) collective-permute-start(bf16[3,80,384]{2,1,0:T(8,128)(2,1)S(1)} %collective-permute-done.28.refs_6_), channel_id=1, source_target_pairs={{0,1},{1,0},{2,3},{3,2},{4,5},{5,4},{6,7},{7,6},{8,9},{9,8},{10,11... | collective-permute-start | bytes 552968 | tf_op jit(solution)/shard_map/ppermute | solution.py:241
  73.2 6.1 %collective-permute-start.34 = (bf16[32,640]{1,0:T(8,128)(2,1)S(1)}, bf16[32,640]{1,0:T(8,128)(2,1)S(1)}, u32[]{:S(2)}, u32[]{:S(2)}) collective-permute-start(bf16[32,640]{1,0:T(8,128)(2,1)S(1)} %get-tuple-element.84), channel_id=1, source_target_pairs={{1,9},{3,11},{5,13},{7,15},{8,16},{9,1},{10,18},{11,3},{12,20},{13... | collective-permute-start | bytes 122888 | tf_op jit(solution)/shard_map/ppermute | solution.py:241
  82.5 5.6 %collective-permute-start.35 = (bf16[16,384]{1,0:T(8,128)(2,1)S(1)}, bf16[16,384]{1,0:T(8,128)(2,1)S(1)}, u32[]{:S(2)}, u32[]{:S(2)}) collective-permute-start(bf16[16,384]{1,0:T(8,128)(2,1)S(1)} %get-tuple-element.92), channel_id=1, source_target_pairs={{1,9},{3,11},{5,13},{7,15},{8,16},{9,1},{10,18},{11,3},{12,20},{13... | collective-permute-start | bytes 36872 | tf_op jit(solution)/shard_map/ppermute | solution.py:241
  89.9 4.7 %collective-permute-start.36 = (bf16[32,1536]{1,0:T(8,128)(2,1)S(1)}, bf16[32,1536]{1,0:T(8,128)(2,1)S(1)}, u32[]{:S(2)}, u32[]{:S(2)}) collective-permute-start(bf16[32,1536]{1,0:T(8,128)(2,1)S(1)} %get-tuple-element.96), channel_id=1, source_target_pairs={{0,2},{1,3},{2,0},{3,1},{4,6},{5,7},{6,4},{7,5},{8,10},{9,11},{10,... | collective-permute-start | bytes 294920 | tf_op jit(solution)/shard_map/ppermute | solution.py:241
  94.6 4.0 %collective-permute-start.37 = (bf16[32,1536]{1,0:T(8,128)(2,1)S(1)}, bf16[32,1536]{1,0:T(8,128)(2,1)S(1)}, u32[]{:S(2)}, u32[]{:S(2)}) collective-permute-start(bf16[32,1536]{1,0:T(8,128)(2,1)S(1)} %add_convert_fusion.1), channel_id=1, source_target_pairs={{0,1},{1,5},{2,3},{3,7},{4,0},{5,4},{6,2},{7,6},{8,12},{9,8},{10,1... | collective-permute-start | bytes 294920 | tf_op jit(solution)/shard_map/ppermute | solution.py:241
  96.4 5.9 %collective-permute-start.38 = (bf16[32,1536]{1,0:T(8,128)(2,1)S(1)}, bf16[32,1536]{1,0:T(8,128)(2,1)S(1)}, u32[]{:S(2)}, u32[]{:S(2)}) collective-permute-start(bf16[32,1536]{1,0:T(8,128)(2,1)S(1)} %add_convert_fusion.1), channel_id=1, source_target_pairs={{1,4},{3,6},{4,1},{6,3},{8,13},{10,15},{13,8},{15,10},{17,20},{19,... | collective-permute-start | bytes 294920 | tf_op jit(solution)/shard_map/ppermute | solution.py:241

commit v10 on v9

--- a/solution.py
+++ b/solution.py
@@ -622,20 +622,20 @@
     straight, late, flag, outer, cot_block = after((straight, late, flag, outer, cot_block))
     beside, across = permuted(straight, x_route), permuted(straight, y_route)
     late_straight = jnp.stack(over_z(late))
-    edge = permuted(outer, edge_route)
-    straight, beside, across, late_straight, edge, cot_block, *blocks = after(
-        (straight, beside, across, late_straight, edge, cot_block, *blocks)
+    straight, beside, across, late_straight, outer, cot_block, *blocks = after(
+        (straight, beside, across, late_straight, outer, cot_block, *blocks)
     )
     early = (straight, beside, across) + diagonals(beside, across)
     late_beside, late_across = permuted(late_straight, x_route), permuted(late_straight, y_route)
-    cot_rows = (cot_block, permuted(cot_block, x_route))
-    early, late, cot_rows, mine = (
-        lambda v: (v[:5], v[5:8], v[8:10], v[10:])
-    )(after((*early, late_straight, late_beside, late_across, *cot_rows, *blocks, edge)))
+    edge = permuted(outer, edge_route)
+    early, late, cot_block, mine = (
+        lambda v: (v[:5], v[5:8], v[8], v[9:])
+    )(after((*early, late_straight, late_beside, late_across, cot_block, *blocks, edge)))
     late = tuple(late) + diagonals(late[1], late[2])
     noisy_rows = tuple(mine) + swapped(mine)
     early = tuple(early) + swapped(early)
-    cot_rows = tuple(cot_rows) + swapped(cot_rows)
+    cot_rows = (cot_block, permuted(cot_block, x_route))
+    cot_rows = cot_rows + swapped(cot_rows)
     late_other = swapped(late[:3])
     gain = norm_gain.reshape(1, features)
 

time: 103 us -> 104 us (level)
  waiting for transfers between devices: 38.8 us -> 46.4 us
  starting transfers between devices: 42 us -> 34.7 us
    ppermute x39, waiting for transfers between devices: 38.8 us -> 46.4 us  [permuted(): return lax.ppermute(value, ('sa', 'sb', 'noise'), pairs)]
    ppermute x39, starting transfers between devices: 42 us -> 34.7 us  [permuted(): return lax.ppermute(value, ('sa', 'sb', 'noise'), pairs)]
where the time goes in v10:
time: 104 us; the launch traced here: 103 us
  waiting for transfers between devices  46.4 us (45%)
  starting transfers between devices  34.7 us (33%)
  Pallas kernels  17.4 us (17%)
  other arithmetic  3.63 us (3%)
  between operations  1.12 us (1%)
    ppermute x39, waiting for transfers between devices, permuted(): return lax.ppermute(value, ('sa', 'sb', 'noise'), pairs)  46.4 us
    ppermute x39, starting transfers between devices, permuted(): return lax.ppermute(value, ('sa', 'sb', 'noise'), pairs)  34.7 us
    pallas_call x1, Pallas kernels, stretch_shards(): pl.pallas_call(attention_kernel, out_shape=(shaped(128, 256), shaped(128,...  5.59 us
    pallas_call x1, Pallas kernels, stretch_shards(): pl.pallas_call(forward_kernel, out_shape=(shaped(192, features, dtype=bf1...  5.1 us
    pallas_call x1, Pallas kernels, stretch_shards(): pl.pallas_call(norm_kernel, out_shape=(shaped(128, HID, dtype=bf16), shap...  3.12 us
  transfers between devices with their start and end apart: 39, of which 18 were waited for; matrix products, arithmetic and copies ran while one was open for 3% of the time, Pallas kernels for 5%

profile of v10, /device:TPU:8, one launch (start us, length us, event | category | flops | bytes accessed | tf_op | source)
XLA Modules:
  0.0 103.4 jit_solution(1355650112538856725)
XLA Ops:
  0.0 1.8 %shard_map.100 = (bf16[192,384]{1,0:T(8,128)(2,1)}, bf16[160,384]{1,0:T(8,128)(2,1)}) custom-call(bf16[3,384,384]{2,1,0:T(8,128)(2,1)} %refs_0_.2, bf16[96,1536]{1,0:T(8,128)(2,1)} %refs_1_.2, bf16[384,896]{1,0:T(8,128)(2,1)} %refs_0_.3, bf16[96,1536]{1,0:T(8,128)(2,1)} %refs_1_.3), custom_call_target="tpu_custom_call" | custom-call | tf_op jit(solution)/shard_map/pallas_call | solution.py:567
  1.9 3.0 %collective-permute-start.1 = (bf16[192,384]{1,0:T(8,128)(2,1)}, bf16[192,384]{1,0:T(8,128)(2,1)S(1)}, u32[]{:S(2)}, u32[]{:S(2)}) collective-permute-start(bf16[192,384]{1,0:T(8,128)(2,1)} %get-tuple-element.50), channel_id=1, source_target_pairs={{0,16},{1,17},{2,18},{3,19},{4,20},{5,21},{6,22},{7,23},{8,24},{9,... | collective-permute-start | bytes 442376 | tf_op jit(solution)/shard_map/ppermute | solution.py:241
  4.9 0.5 collective-permute-start.2
  5.3 0.9 convert_element_type.22
  6.3 1.1 %add_convert_fusion = bf16[2,32,1536]{2,1,0:T(8,128)(2,1)S(1)} fusion(bf16[2,32,1536]{2,1,0:T(8,128)(2,1)} %param.11, f32[32,1536]{1,0:T(8,128)S(1)} %convert_element_type.22), kind=kLoop, calls=%fused_computation.1 | loop fusion | flops 294912 | bytes 589824 | tf_op jit(solution)/shard_map/convert_element_type | solution.py:601
  7.4 0.7 and_reduce_fusion
  8.8 1.9 %collective-permute-start.3 = (bf16[32,1536]{1,0:T(8,128)(2,1)S(1)}, bf16[32,1536]{1,0:T(8,128)(2,1)S(1)}, u32[]{:S(2)}, u32[]{:S(2)}) collective-permute-start(bf16[32,1536]{1,0:T(8,128)(2,1)S(1)} %get-tuple-element.97), channel_id=1, source_target_pairs={{0,0},{1,4},{2,2},{3,6},{4,1},{5,5},{6,3},{7,7},{8,9},{9,13},{10,1... | collective-permute-start | bytes 294920 | tf_op jit(solution)/shard_map/ppermute | solution.py:241
  10.7 1.4 %collective-permute-start.4 = (bf16[32,1536]{1,0:T(8,128)(2,1)S(1)}, bf16[32,1536]{1,0:T(8,128)(2,1)S(1)}, u32[]{:S(2)}, u32[]{:S(2)}) collective-permute-start(bf16[32,1536]{1,0:T(8,128)(2,1)S(1)} %get-tuple-element.98), channel_id=1, source_target_pairs={{0,2},{1,6},{2,0},{3,4},{4,3},{5,7},{6,1},{7,5},{8,11},{9,15},{10,... | collective-permute-start | bytes 294920 | tf_op jit(solution)/shard_map/ppermute | solution.py:241
  12.1 1.3 %collective-permute-start.5 = (bf16[32,1536]{1,0:T(8,128)(2,1)S(1)}, bf16[32,1536]{1,0:T(8,128)(2,1)S(1)}, u32[]{:S(2)}, u32[]{:S(2)}) collective-permute-start(bf16[32,1536]{1,0:T(8,128)(2,1)S(1)} %copy-done.5), channel_id=1, source_target_pairs={{0,4},{2,6},{5,1},{7,3},{9,13},{11,15},{12,8},{14,10},{16,20},{18,... | collective-permute-start | bytes 294920 | tf_op jit(solution)/shard_map/ppermute | solution.py:241
  13.4 2.2 %collective-permute-done.1 = bf16[192,384]{1,0:T(8,128)(2,1)S(1)} collective-permute-done((bf16[192,384]{1,0:T(8,128)(2,1)}, bf16[192,384]{1,0:T(8,128)(2,1)S(1)}, u32[]{:S(2)}, u32[]{:S(2)}) %collective-permute-start.1) | collective-permute-done | bytes 147488 | tf_op jit(solution)/shard_map/ppermute | solution.py:241
  15.6 2.8 %collective-permute-done.2 = bf16[192,384]{1,0:T(8,128)(2,1)S(1)} collective-permute-done((bf16[192,384]{1,0:T(8,128)(2,1)}, bf16[192,384]{1,0:T(8,128)(2,1)S(1)}, u32[]{:S(2)}, u32[]{:S(2)}) %collective-permute-start.2) | collective-permute-done | bytes 147488 | tf_op jit(solution)/shard_map/ppermute | solution.py:241
  18.6 1.5 %collective-permute-start.6 = (bf16[3,192,384]{2,1,0:T(8,128)(2,1)S(1)}, bf16[3,192,384]{2,1,0:T(8,128)(2,1)S(1)}, u32[]{:S(2)}, u32[]{:S(2)}) collective-permute-start(bf16[3,192,384]{2,1,0:T(8,128)(2,1)S(1)} %pad_maximum_fusion.refs_2_), channel_id=1, source_target_pairs={{0,2},{1,3},{2,0},{3,1},{4,6},{5,7},{6,4},{7,5},{8,10},{9,11},{10,... | collective-permute-start | bytes 1327112 | tf_op jit(solution)/shard_map/ppermute | solution.py:241
  20.1 1.5 %collective-permute-start.7 = (bf16[3,192,384]{2,1,0:T(8,128)(2,1)S(1)}, bf16[3,192,384]{2,1,0:T(8,128)(2,1)S(1)}, u32[]{:S(2)}, u32[]{:S(2)}) collective-permute-start(bf16[3,192,384]{2,1,0:T(8,128)(2,1)S(1)} %pad_maximum_fusion.refs_2_), channel_id=1, source_target_pairs={{0,4},{1,5},{2,6},{3,7},{4,0},{5,1},{6,2},{7,3},{8,12},{9,13},{10,... | collective-permute-start | bytes 1327112 | tf_op jit(solution)/shard_map/ppermute | solution.py:241
  21.6 1.8 %collective-permute-start.8 = (bf16[160,384]{1,0:T(8,128)(2,1)S(1)}, bf16[160,384]{1,0:T(8,128)(2,1)S(1)}, u32[]{:S(2)}, u32[]{:S(2)}) collective-permute-start(bf16[160,384]{1,0:T(8,128)(2,1)S(1)} %copy-done.8), channel_id=1, source_target_pairs={{0,8},{1,9},{2,10},{3,11},{4,12},{5,13},{6,14},{7,15},{8,0},{9,1},... | collective-permute-start | bytes 368648 | tf_op jit(solution)/shard_map/ppermute | solution.py:241
  23.5 1.7 %collective-permute-start.9 = (bf16[160,384]{1,0:T(8,128)(2,1)S(1)}, bf16[160,384]{1,0:T(8,128)(2,1)S(1)}, u32[]{:S(2)}, u32[]{:S(2)}) collective-permute-start(bf16[160,384]{1,0:T(8,128)(2,1)S(1)} %copy-done.8), channel_id=1, source_target_pairs={{0,16},{1,17},{2,18},{3,19},{4,20},{5,21},{6,22},{7,23},{8,24},{9,... | collective-permute-start | bytes 368648 | tf_op jit(solution)/shard_map/ppermute | solution.py:241
  25.1 2.4 %collective-permute-done.8 = bf16[160,384]{1,0:T(8,128)(2,1)S(1)} collective-permute-done((bf16[160,384]{1,0:T(8,128)(2,1)S(1)}, bf16[160,384]{1,0:T(8,128)(2,1)S(1)}, u32[]{:S(2)}, u32[]{:S(2)}) %collective-permute-start.8) | collective-permute-done | bytes 122912 | tf_op jit(solution)/shard_map/ppermute | solution.py:241
  27.5 5.2 %collective-permute-done.9 = bf16[160,384]{1,0:T(8,128)(2,1)S(1)} collective-permute-done((bf16[160,384]{1,0:T(8,128)(2,1)S(1)}, bf16[160,384]{1,0:T(8,128)(2,1)S(1)}, u32[]{:S(2)}, u32[]{:S(2)}) %collective-permute-start.9) | collective-permute-done | bytes 122912 | tf_op jit(solution)/shard_map/ppermute | solution.py:241
  32.7 2.3 %collective-permute-done.10 = bf16[160,384]{1,0:T(8,128)(2,1)S(1)} collective-permute-done((bf16[160,384]{1,0:T(8,128)(2,1)S(1)}, bf16[160,384]{1,0:T(8,128)(2,1)S(1)}, u32[]{:S(2)}, u32[]{:S(2)}) %collective-permute-start.10) | collective-permute-done | bytes 122912 | tf_op jit(solution)/shard_map/ppermute | solution.py:241
  35.1 1.6 %collective-permute-start.13 = (bf16[3,160,384]{2,1,0:T(8,128)(2,1)S(1)}, bf16[3,160,384]{2,1,0:T(8,128)(2,1)S(1)}, u32[]{:S(2)}, u32[]{:S(2)}) collective-permute-start(bf16[3,160,384]{2,1,0:T(8,128)(2,1)S(1)} %pad_maximum_fusion.1.refs_2_), channel_id=1, source_target_pairs={{0,2},{1,3},{2,0},{3,1},{4,6},{5,7},{6,4},{7,5},{8,10},{9,11},{10,... | collective-permute-start | bytes 1105928 | tf_op jit(solution)/shard_map/ppermute | solution.py:241
  36.9 1.8 %collective-permute-start.11 = (bf16[3,96,384]{2,1,0:T(8,128)(2,1)S(1)}, bf16[3,96,384]{2,1,0:T(8,128)(2,1)S(1)}, u32[]{:S(2)}, u32[]{:S(2)}) collective-permute-start(bf16[3,96,384]{2,1,0:T(8,128)(2,1)S(1)} %slice.48), channel_id=1, source_target_pairs={{0,4},{1,5},{2,6},{3,7},{4,0},{5,1},{6,2},{7,3},{8,12},{9,13},{10,... | collective-permute-start | bytes 663560 | tf_op jit(solution)/shard_map/ppermute | solution.py:241
  38.8 0.6 collective-permute-start.12
  39.4 3.4 %collective-permute-start.15 = (bf16[48,1536]{1,0:T(8,128)(2,1)S(1)}, bf16[48,1536]{1,0:T(8,128)(2,1)S(1)}, u32[]{:S(2)}, u32[]{:S(2)}) collective-permute-start(bf16[48,1536]{1,0:T(8,128)(2,1)S(1)} %pad_maximum_fusion.2), channel_id=1, source_target_pairs={{1,9},{3,11},{5,13},{7,15},{8,16},{9,1},{10,18},{11,3},{12,20},{13... | collective-permute-start | bytes 442376 | tf_op jit(solution)/shard_map/ppermute | solution.py:241
  42.8 3.6 %collective-permute-done.15.edge = bf16[48,1536]{1,0:T(8,128)(2,1)S(1)} collective-permute-done((bf16[48,1536]{1,0:T(8,128)(2,1)S(1)}, bf16[48,1536]{1,0:T(8,128)(2,1)S(1)}, u32[]{:S(2)}, u32[]{:S(2)}) %collective-permute-start.15) | collective-permute-done | bytes 147488 | tf_op jit(solution)/shard_map/ppermute | solution.py:241
  46.4 4.1 %collective-permute-done.11.refs_5_ = bf16[3,96,384]{2,1,0:T(8,128)(2,1)S(1)} collective-permute-done((bf16[3,96,384]{2,1,0:T(8,128)(2,1)S(1)}, bf16[3,96,384]{2,1,0:T(8,128)(2,1)S(1)}, u32[]{:S(2)}, u32[]{:S(2)}) %collective-permute-start.11) | collective-permute-done | bytes 221216 | tf_op jit(solution)/shard_map/ppermute | solution.py:241
  50.6 0.5 collective-permute-start.17
  51.1 0.5 collective-permute-start.24
  51.6 0.3 collective-permute-start.27
  52.0 0.5 collective-permute-start.25
  52.6 3.2 %collective-permute-done.24.cot_beside = bf16[32,1536]{1,0:T(8,128)(2,1)S(1)} collective-permute-done((bf16[32,1536]{1,0:T(8,128)(2,1)S(1)}, bf16[32,1536]{1,0:T(8,128)(2,1)S(1)}, u32[]{:S(2)}, u32[]{:S(2)}) %collective-permute-start.24) | collective-permute-done | bytes 98336 | tf_op jit(solution)/shard_map/ppermute | solution.py:241
  55.9 0.5 collective-permute-start.28
  56.4 0.5 collective-permute-start.20
  56.9 1.1 %collective-permute-done.27.refs_5_ = bf16[3,80,384]{2,1,0:T(8,128)(2,1)S(1)} collective-permute-done((bf16[3,80,384]{2,1,0:T(8,128)(2,1)S(1)}, bf16[3,80,384]{2,1,0:T(8,128)(2,1)S(1)}, u32[]{:S(2)}, u32[]{:S(2)}) %collective-permute-start.27) | collective-permute-done | bytes 184352 | tf_op jit(solution)/shard_map/ppermute | solution.py:241
  58.0 3.6 %collective-permute-done.28.refs_6_ = bf16[3,80,384]{2,1,0:T(8,128)(2,1)S(1)} collective-permute-done((bf16[3,80,384]{2,1,0:T(8,128)(2,1)S(1)}, bf16[3,80,384]{2,1,0:T(8,128)(2,1)S(1)}, u32[]{:S(2)}, u32[]{:S(2)}) %collective-permute-start.28) | collective-permute-done | bytes 184352 | tf_op jit(solution)/shard_map/ppermute | solution.py:241
  61.6 0.5 collective-permute-start.23
  62.2 1.0 collective-permute-done.22.refs_10_
  64.5 5.1 %shard_map.101 = (bf16[192,1536]{1,0:T(8,128)(2,1)S(1)}, f32[128,1536]{1,0:T(8,128)S(1)}, f32[128,1]{1,0:T(8,128)S(1)}, f32[128,384]{1,0:T(8,128)S(1)}, bf16[3,1...) custom-call(bf16[32,1536]{1,0:T(8,128)(2,1)S(1)} %collective-permute-done.3.blocks_even, ...), custom_call_target="tpu_custom_call" | custom-call | tf_op jit(solution)/shard_map/pallas_call | solution.py:642
  69.7 5.6 %shard_map.102 = (f32[128,256]{1,0:T(8,128)S(1)}, f32[128,640]{1,0:T(8,128)S(1)}, bf16[32,640]{1,0:T(8,128)(2,1)S(1)}, bf16[1536,896]{1,0:T(8,128)(2,1)S(1)}, bf16[128,1536]{1,0:T(8,128)(2,1)S(1)}) custom-call(s32[4]{0:T(128)S(1)} %copy-done.4, s32[1]{0:T(128)} %bitcast.3.flag, bf16[192,1536]{1,0:T(8,128)(2,1)S(1)} %get-tuple-element.75.normed, ...), custom_call_target="tpu_custom_call" | custom-call | tf_op jit(solution)/shard_map/pallas_call | solution.py:658
  75.3 2.4 %collective-permute-start.34 = (bf16[32,640]{1,0:T(8,128)(2,1)S(1)}, bf16[32,640]{1,0:T(8,128)(2,1)S(1)}, u32[]{:S(2)}, u32[]{:S(2)}) collective-permute-start(bf16[32,640]{1,0:T(8,128)(2,1)S(1)} %get-tuple-element.82), channel_id=1, source_target_pairs={{1,9},{3,11},{5,13},{7,15},{8,16},{9,1},{10,18},{11,3},{12,20},{13... | collective-permute-start | bytes 122888 | tf_op jit(solution)/shard_map/ppermute | solution.py:241
  77.7 3.5 %collective-permute-done.34.received = bf16[32,640]{1,0:T(8,128)(2,1)S(1)} collective-permute-done((bf16[32,640]{1,0:T(8,128)(2,1)S(1)}, bf16[32,640]{1,0:T(8,128)(2,1)S(1)}, u32[]{:S(2)}, u32[]{:S(2)}) %collective-permute-start.34) | collective-permute-done | bytes 40992 | tf_op jit(solution)/shard_map/ppermute | solution.py:241
  81.2 3.1 %shard_map.103 = (bf16[128,384]{1,0:T(8,128)(2,1)S(1)}, f32[64,1536]{1,0:T(8,128)S(1)}, bf16[16,384]{1,0:T(8,128)(2,1)S(1)}) custom-call(f32[128,256]{1,0:T(8,128)S(1)} %get-tuple-element.80.d_q, f32[128,640]{1,0:T(8,128)S(1)} %get-tuple-element.81.d_kv, bf16[32,640]{1,0:T(8,128)(2,1)S(1)} %collective-permute-done.34.received, ...), custom_call_target="tpu_custom_call" | custom-call | tf_op jit(solution)/shard_map/pallas_call | solution.py:674
  84.3 2.4 %collective-permute-start.35 = (bf16[16,384]{1,0:T(8,128)(2,1)S(1)}, bf16[16,384]{1,0:T(8,128)(2,1)S(1)}, u32[]{:S(2)}, u32[]{:S(2)}) collective-permute-start(bf16[16,384]{1,0:T(8,128)(2,1)S(1)} %get-tuple-element.90), channel_id=1, source_target_pairs={{1,9},{3,11},{5,13},{7,15},{8,16},{9,1},{10,18},{11,3},{12,20},{13... | collective-permute-start | bytes 36872 | tf_op jit(solution)/shard_map/ppermute | solution.py:241
  86.8 3.2 %collective-permute-done.35.received = bf16[16,384]{1,0:T(8,128)(2,1)S(1)} collective-permute-done((bf16[16,384]{1,0:T(8,128)(2,1)S(1)}, bf16[16,384]{1,0:T(8,128)(2,1)S(1)}, u32[]{:S(2)}, u32[]{:S(2)}) %collective-permute-start.35) | collective-permute-done | bytes 12320 | tf_op jit(solution)/shard_map/ppermute | solution.py:241
  89.9 1.8 %shard_map.104 = (f32[32,1536]{1,0:T(8,128)S(1)}, bf16[32,1536]{1,0:T(8,128)(2,1)S(1)}) custom-call(bf16[128,384]{1,0:T(8,128)(2,1)S(1)} %get-tuple-element.89.d_hidden, bf16[16,384]{1,0:T(8,128)(2,1)S(1)} %collective-permute-done.35.received, f32[64,1536]{1,0:T(8,128)S(1)} %get-tuple-element.91.d_resid, ...), custom_call_target="tpu_custom_call" | custom-call | tf_op jit(solution)/shard_map/pallas_call | solution.py:686
  91.7 0.6 collective-permute-start.36
  92.3 4.1 %collective-permute-done.36 = bf16[32,1536]{1,0:T(8,128)(2,1)S(1)} collective-permute-done((bf16[32,1536]{1,0:T(8,128)(2,1)S(1)}, bf16[32,1536]{1,0:T(8,128)(2,1)S(1)}, u32[]{:S(2)}, u32[]{:S(2)}) %collective-permute-start.36) | collective-permute-done | bytes 98336 | tf_op jit(solution)/shard_map/ppermute | solution.py:241
  96.8 1.9 %collective-permute-start.38 = (bf16[32,1536]{1,0:T(8,128)(2,1)S(1)}, bf16[32,1536]{1,0:T(8,128)(2,1)S(1)}, u32[]{:S(2)}, u32[]{:S(2)}) collective-permute-start(bf16[32,1536]{1,0:T(8,128)(2,1)S(1)} %add_convert_fusion.1), channel_id=1, source_target_pairs={{1,4},{3,6},{4,1},{6,3},{8,13},{10,15},{13,8},{15,10},{17,20},{19,... | collective-permute-start | bytes 294920 | tf_op jit(solution)/shard_map/ppermute | solution.py:241
  99.0 3.7 %collective-permute-done.38 = bf16[32,1536]{1,0:T(8,128)(2,1)S(1)} collective-permute-done((bf16[32,1536]{1,0:T(8,128)(2,1)S(1)}, bf16[32,1536]{1,0:T(8,128)(2,1)S(1)}, u32[]{:S(2)}, u32[]{:S(2)}) %collective-permute-start.38) | collective-permute-done | bytes 98336 | tf_op jit(solution)/shard_map/ppermute | solution.py:241
  102.7 0.7 add_multiply_fusion
  (70 shorter events, 3.0 us)
Async XLA Ops:
  0.0 7.4 %copy-start.7 = (s32[16,2]{0,1:T(2,128)S(1)}, s32[16,2]{0,1:T(2,128)}, u32[]{:S(2)}) copy-start(s32[16,2]{0,1:T(2,128)} %param.19) | copy-start | bytes 388
  0.0 12.1 %copy-start.5 = (bf16[32,1536]{1,0:T(8,128)(2,1)S(1)}, bf16[32,1536]{1,0:T(8,128)(2,1)}, u32[]{:S(2)}) copy-start(bf16[32,1536]{1,0:T(8,128)(2,1)} %param.12) | copy-start | bytes 294916
  1.8 19.9 %copy-start.8 = (bf16[160,384]{1,0:T(8,128)(2,1)S(1)}, bf16[160,384]{1,0:T(8,128)(2,1)}, u32[]{:S(2)}) copy-start(bf16[160,384]{1,0:T(8,128)(2,1)} %get-tuple-element.56) | copy-start | bytes 368644
  1.8 7.0 %collective-permute-start = (bf16[192,384]{1,0:T(8,128)(2,1)}, bf16[192,384]{1,0:T(8,128)(2,1)S(1)}, u32[]{:S(2)}, u32[]{:S(2)}) collective-permute-start(bf16[192,384]{1,0:T(8,128)(2,1)} %get-tuple-element.50), channel_id=1, source_target_pairs={{0,8},{1,9},{2,10},{3,11},{4,12},{5,13},{6,14},{7,15},{8,0},{9,1},... | collective-permute-start | bytes 442376 | tf_op jit(solution)/shard_map/ppermute | solution.py:241
  1.9 13.8 %collective-permute-start.1 = (bf16[192,384]{1,0:T(8,128)(2,1)}, bf16[192,384]{1,0:T(8,128)(2,1)S(1)}, u32[]{:S(2)}, u32[]{:S(2)}) collective-permute-start(bf16[192,384]{1,0:T(8,128)(2,1)} %get-tuple-element.50), channel_id=1, source_target_pairs={{0,16},{1,17},{2,18},{3,19},{4,20},{5,21},{6,22},{7,23},{8,24},{9,... | collective-permute-start | bytes 442376 | tf_op jit(solution)/shard_map/ppermute | solution.py:241
  4.9 13.5 %collective-permute-start.2 = (bf16[192,384]{1,0:T(8,128)(2,1)}, bf16[192,384]{1,0:T(8,128)(2,1)S(1)}, u32[]{:S(2)}, u32[]{:S(2)}) collective-permute-start(bf16[192,384]{1,0:T(8,128)(2,1)} %get-tuple-element.50), channel_id=1, source_target_pairs={{0,24},{1,25},{2,26},{3,27},{4,28},{5,29},{6,30},{7,31},{8,16},{9,... | collective-permute-start | bytes 442376 | tf_op jit(solution)/shard_map/ppermute | solution.py:241
  6.2 58.2 %copy-start.6 = (f32[1536]{0:T(1024)S(1)}, f32[1536]{0:T(1024)}, u32[]{:S(2)}) copy-start(f32[1536]{0:T(1024)} %param.15) | copy-start | bytes 18436
  6.3 58.2 %copy-start = (bf16[3,384,384]{2,1,0:T(8,128)(2,1)S(1)}, bf16[3,384,384]{2,1,0:T(8,128)(2,1)}, u32[]{:S(2)}) copy-start(bf16[3,384,384]{2,1,0:T(8,128)(2,1)} %refs_0_.2) | copy-start | bytes 2654212
  6.3 58.2 %copy-start.2 = (bf16[96,1536]{1,0:T(8,128)(2,1)S(1)}, bf16[96,1536]{1,0:T(8,128)(2,1)}, u32[]{:S(2)}) copy-start(bf16[96,1536]{1,0:T(8,128)(2,1)} %refs_1_.2) | copy-start | bytes 884740
  8.8 9.6 %collective-permute-start.3 = (bf16[32,1536]{1,0:T(8,128)(2,1)S(1)}, bf16[32,1536]{1,0:T(8,128)(2,1)S(1)}, u32[]{:S(2)}, u32[]{:S(2)}) collective-permute-start(bf16[32,1536]{1,0:T(8,128)(2,1)S(1)} %get-tuple-element.97), channel_id=1, source_target_pairs={{0,0},{1,4},{2,2},{3,6},{4,1},{5,5},{6,3},{7,7},{8,9},{9,13},{10,1... | collective-permute-start | bytes 294920 | tf_op jit(solution)/shard_map/ppermute | solution.py:241
  10.7 7.7 %collective-permute-start.4 = (bf16[32,1536]{1,0:T(8,128)(2,1)S(1)}, bf16[32,1536]{1,0:T(8,128)(2,1)S(1)}, u32[]{:S(2)}, u32[]{:S(2)}) collective-permute-start(bf16[32,1536]{1,0:T(8,128)(2,1)S(1)} %get-tuple-element.98), channel_id=1, source_target_pairs={{0,2},{1,6},{2,0},{3,4},{4,3},{5,7},{6,1},{7,5},{8,11},{9,15},{10,... | collective-permute-start | bytes 294920 | tf_op jit(solution)/shard_map/ppermute | solution.py:241
  12.1 6.5 %collective-permute-start.5 = (bf16[32,1536]{1,0:T(8,128)(2,1)S(1)}, bf16[32,1536]{1,0:T(8,128)(2,1)S(1)}, u32[]{:S(2)}, u32[]{:S(2)}) collective-permute-start(bf16[32,1536]{1,0:T(8,128)(2,1)S(1)} %copy-done.5), channel_id=1, source_target_pairs={{0,4},{2,6},{5,1},{7,3},{9,13},{11,15},{12,8},{14,10},{16,20},{18,... | collective-permute-start | bytes 294920 | tf_op jit(solution)/shard_map/ppermute | solution.py:241
  18.6 16.4 %collective-permute-start.6 = (bf16[3,192,384]{2,1,0:T(8,128)(2,1)S(1)}, bf16[3,192,384]{2,1,0:T(8,128)(2,1)S(1)}, u32[]{:S(2)}, u32[]{:S(2)}) collective-permute-start(bf16[3,192,384]{2,1,0:T(8,128)(2,1)S(1)} %pad_maximum_fusion.refs_2_), channel_id=1, source_target_pairs={{0,2},{1,3},{2,0},{3,1},{4,6},{5,7},{6,4},{7,5},{8,10},{9,11},{10,... | collective-permute-start | bytes 1327112 | tf_op jit(solution)/shard_map/ppermute | solution.py:241
  20.1 14.9 %collective-permute-start.7 = (bf16[3,192,384]{2,1,0:T(8,128)(2,1)S(1)}, bf16[3,192,384]{2,1,0:T(8,128)(2,1)S(1)}, u32[]{:S(2)}, u32[]{:S(2)}) collective-permute-start(bf16[3,192,384]{2,1,0:T(8,128)(2,1)S(1)} %pad_maximum_fusion.refs_2_), channel_id=1, source_target_pairs={{0,4},{1,5},{2,6},{3,7},{4,0},{5,1},{6,2},{7,3},{8,12},{9,13},{10,... | collective-permute-start | bytes 1327112 | tf_op jit(solution)/shard_map/ppermute | solution.py:241
  21.6 5.9 %collective-permute-start.8 = (bf16[160,384]{1,0:T(8,128)(2,1)S(1)}, bf16[160,384]{1,0:T(8,128)(2,1)S(1)}, u32[]{:S(2)}, u32[]{:S(2)}) collective-permute-start(bf16[160,384]{1,0:T(8,128)(2,1)S(1)} %copy-done.8), channel_id=1, source_target_pairs={{0,8},{1,9},{2,10},{3,11},{4,12},{5,13},{6,14},{7,15},{8,0},{9,1},... | collective-permute-start | bytes 368648 | tf_op jit(solution)/shard_map/ppermute | solution.py:241
  23.5 9.2 %collective-permute-start.9 = (bf16[160,384]{1,0:T(8,128)(2,1)S(1)}, bf16[160,384]{1,0:T(8,128)(2,1)S(1)}, u32[]{:S(2)}, u32[]{:S(2)}) collective-permute-start(bf16[160,384]{1,0:T(8,128)(2,1)S(1)} %copy-done.8), channel_id=1, source_target_pairs={{0,16},{1,17},{2,18},{3,19},{4,20},{5,21},{6,22},{7,23},{8,24},{9,... | collective-permute-start | bytes 368648 | tf_op jit(solution)/shard_map/ppermute | solution.py:241
  25.1 9.8 %collective-permute-start.10 = (bf16[160,384]{1,0:T(8,128)(2,1)S(1)}, bf16[160,384]{1,0:T(8,128)(2,1)S(1)}, u32[]{:S(2)}, u32[]{:S(2)}) collective-permute-start(bf16[160,384]{1,0:T(8,128)(2,1)S(1)} %copy-done.8), channel_id=1, source_target_pairs={{0,24},{1,25},{2,26},{3,27},{4,28},{5,29},{6,30},{7,31},{8,16},{9,... | collective-permute-start | bytes 368648 | tf_op jit(solution)/shard_map/ppermute | solution.py:241
  35.1 15.4 %collective-permute-start.13 = (bf16[3,160,384]{2,1,0:T(8,128)(2,1)S(1)}, bf16[3,160,384]{2,1,0:T(8,128)(2,1)S(1)}, u32[]{:S(2)}, u32[]{:S(2)}) collective-permute-start(bf16[3,160,384]{2,1,0:T(8,128)(2,1)S(1)} %pad_maximum_fusion.1.refs_2_), channel_id=1, source_target_pairs={{0,2},{1,3},{2,0},{3,1},{4,6},{5,7},{6,4},{7,5},{8,10},{9,11},{10,... | collective-permute-start | bytes 1105928 | tf_op jit(solution)/shard_map/ppermute | solution.py:241
  36.6 13.9 %collective-permute-start.14 = (bf16[3,160,384]{2,1,0:T(8,128)(2,1)S(1)}, bf16[3,160,384]{2,1,0:T(8,128)(2,1)S(1)}, u32[]{:S(2)}, u32[]{:S(2)}) collective-permute-start(bf16[3,160,384]{2,1,0:T(8,128)(2,1)S(1)} %pad_maximum_fusion.1.refs_2_), channel_id=1, source_target_pairs={{0,4},{1,5},{2,6},{3,7},{4,0},{5,1},{6,2},{7,3},{8,12},{9,13},{10,... | collective-permute-start | bytes 1105928 | tf_op jit(solution)/shard_map/ppermute | solution.py:241
  36.9 13.6 %collective-permute-start.11 = (bf16[3,96,384]{2,1,0:T(8,128)(2,1)S(1)}, bf16[3,96,384]{2,1,0:T(8,128)(2,1)S(1)}, u32[]{:S(2)}, u32[]{:S(2)}) collective-permute-start(bf16[3,96,384]{2,1,0:T(8,128)(2,1)S(1)} %slice.48), channel_id=1, source_target_pairs={{0,4},{1,5},{2,6},{3,7},{4,0},{5,1},{6,2},{7,3},{8,12},{9,13},{10,... | collective-permute-start | bytes 663560 | tf_op jit(solution)/shard_map/ppermute | solution.py:241
  38.8 11.7 %collective-permute-start.12 = (bf16[3,96,384]{2,1,0:T(8,128)(2,1)S(1)}, bf16[3,96,384]{2,1,0:T(8,128)(2,1)S(1)}, u32[]{:S(2)}, u32[]{:S(2)}) collective-permute-start(bf16[3,96,384]{2,1,0:T(8,128)(2,1)S(1)} %slice.49), channel_id=1, source_target_pairs={{0,2},{1,3},{2,0},{3,1},{4,6},{5,7},{6,4},{7,5},{8,10},{9,11},{10,... | collective-permute-start | bytes 663560 | tf_op jit(solution)/shard_map/ppermute | solution.py:241
  39.4 7.0 %collective-permute-start.15 = (bf16[48,1536]{1,0:T(8,128)(2,1)S(1)}, bf16[48,1536]{1,0:T(8,128)(2,1)S(1)}, u32[]{:S(2)}, u32[]{:S(2)}) collective-permute-start(bf16[48,1536]{1,0:T(8,128)(2,1)S(1)} %pad_maximum_fusion.2), channel_id=1, source_target_pairs={{1,9},{3,11},{5,13},{7,15},{8,16},{9,1},{10,18},{11,3},{12,20},{13... | collective-permute-start | bytes 442376 | tf_op jit(solution)/shard_map/ppermute | solution.py:241
  50.5 1.5 %collective-permute-start.16 = (bf16[32,1536]{1,0:T(8,128)(2,1)S(1)}, bf16[32,1536]{1,0:T(8,128)(2,1)S(1)}, u32[]{:S(2)}, u32[]{:S(2)}) collective-permute-start(bf16[32,1536]{1,0:T(8,128)(2,1)S(1)} %collective-permute-done.3.blocks_even), channel_id=1, source_target_pairs={{0,1},{1,0},{2,3},{3,2},{4,5},{5,4},{6,7},{7,6},{8,9},{9,8},{10,11... | collective-permute-start | bytes 294920 | tf_op jit(solution)/shard_map/ppermute | solution.py:241
  50.6 2.0 %collective-permute-start.17 = (bf16[32,1536]{1,0:T(8,128)(2,1)S(1)}, bf16[32,1536]{1,0:T(8,128)(2,1)S(1)}, u32[]{:S(2)}, u32[]{:S(2)}) collective-permute-start(bf16[32,1536]{1,0:T(8,128)(2,1)S(1)} %collective-permute-done.4.blocks_odd), channel_id=1, source_target_pairs={{0,1},{1,0},{2,3},{3,2},{4,5},{5,4},{6,7},{7,6},{8,9},{9,8},{10,11... | collective-permute-start | bytes 294920 | tf_op jit(solution)/shard_map/ppermute | solution.py:241
  51.1 4.8 %collective-permute-start.24 = (bf16[32,1536]{1,0:T(8,128)(2,1)S(1)}, bf16[32,1536]{1,0:T(8,128)(2,1)S(1)}, u32[]{:S(2)}, u32[]{:S(2)}) collective-permute-start(bf16[32,1536]{1,0:T(8,128)(2,1)S(1)} %broadcast_select_fusion.cot_block), channel_id=1, source_target_pairs={{0,2},{1,3},{2,0},{3,1},{4,6},{5,7},{6,4},{7,5},{8,10},{9,11},{10,... | collective-permute-start | bytes 294920 | tf_op jit(solution)/shard_map/ppermute | solution.py:241
  51.6 6.4 %collective-permute-start.27 = (bf16[3,80,384]{2,1,0:T(8,128)(2,1)S(1)}, bf16[3,80,384]{2,1,0:T(8,128)(2,1)S(1)}, u32[]{:S(2)}, u32[]{:S(2)}) collective-permute-start(bf16[3,80,384]{2,1,0:T(8,128)(2,1)S(1)} %slice.50), channel_id=1, source_target_pairs={{0,4},{1,5},{2,6},{3,7},{4,0},{5,1},{6,2},{7,3},{8,12},{9,13},{10,... | collective-permute-start | bytes 552968 | tf_op jit(solution)/shard_map/ppermute | solution.py:241
  52.0 11.6 %collective-permute-start.19 = (bf16[3,192,384]{2,1,0:T(8,128)(2,1)S(1)}, bf16[3,192,384]{2,1,0:T(8,128)(2,1)S(1)}, u32[]{:S(2)}, u32[]{:S(2)}) collective-permute-start(bf16[3,192,384]{2,1,0:T(8,128)(2,1)S(1)} %pad_maximum_fusion.refs_2_), channel_id=1, source_target_pairs={{0,1},{1,0},{2,3},{3,2},{4,5},{5,4},{6,7},{7,6},{8,9},{9,8},{10,11... | collective-permute-start | bytes 1327112 | tf_op jit(solution)/shard_map/ppermute | solution.py:241
  52.0 4.4 %collective-permute-start.25 = (bf16[32,1536]{1,0:T(8,128)(2,1)S(1)}, bf16[32,1536]{1,0:T(8,128)(2,1)S(1)}, u32[]{:S(2)}, u32[]{:S(2)}) collective-permute-start(bf16[32,1536]{1,0:T(8,128)(2,1)S(1)} %broadcast_select_fusion.cot_block), channel_id=1, source_target_pairs={{0,1},{1,0},{2,3},{3,2},{4,5},{5,4},{6,7},{7,6},{8,9},{9,8},{10,11... | collective-permute-start | bytes 294920 | tf_op jit(solution)/shard_map/ppermute | solution.py:241
  52.5 17.1 %copy-start.1 = (bf16[384,896]{1,0:T(8,128)(2,1)S(1)}, bf16[384,896]{1,0:T(8,128)(2,1)}, u32[]{:S(2)}) copy-start(bf16[384,896]{1,0:T(8,128)(2,1)} %refs_0_.3) | copy-start | bytes 2064388
  52.5 17.1 %copy-start.3 = (bf16[96,1536]{1,0:T(8,128)(2,1)S(1)}, bf16[96,1536]{1,0:T(8,128)(2,1)}, u32[]{:S(2)}) copy-start(bf16[96,1536]{1,0:T(8,128)(2,1)} %refs_1_.3) | copy-start | bytes 884740
  52.5 17.1 %copy-start.4 = (s32[4]{0:T(128)S(1)}, s32[4]{0:T(128)}, u32[]{:S(2)}) copy-start(s32[4]{0:T(128)} %band.1) | copy-start | bytes 52
  52.6 3.8 %collective-permute-start.18 = (bf16[48,1536]{1,0:T(8,128)(2,1)S(1)}, bf16[48,1536]{1,0:T(8,128)(2,1)S(1)}, u32[]{:S(2)}, u32[]{:S(2)}) collective-permute-start(bf16[48,1536]{1,0:T(8,128)(2,1)S(1)} %collective-permute-done.15.edge), channel_id=1, source_target_pairs={{0,1},{1,0},{2,3},{3,2},{4,5},{5,4},{6,7},{7,6},{8,9},{9,8},{10,11... | collective-permute-start | bytes 442376 | tf_op jit(solution)/shard_map/ppermute | solution.py:241
  55.9 5.8 %collective-permute-start.28 = (bf16[3,80,384]{2,1,0:T(8,128)(2,1)S(1)}, bf16[3,80,384]{2,1,0:T(8,128)(2,1)S(1)}, u32[]{:S(2)}, u32[]{:S(2)}) collective-permute-start(bf16[3,80,384]{2,1,0:T(8,128)(2,1)S(1)} %slice.51), channel_id=1, source_target_pairs={{0,2},{1,3},{2,0},{3,1},{4,6},{5,7},{6,4},{7,5},{8,10},{9,11},{10,... | collective-permute-start | bytes 552968 | tf_op jit(solution)/shard_map/ppermute | solution.py:241
  56.4 5.2 %collective-permute-start.26 = (bf16[32,1536]{1,0:T(8,128)(2,1)S(1)}, bf16[32,1536]{1,0:T(8,128)(2,1)S(1)}, u32[]{:S(2)}, u32[]{:S(2)}) collective-permute-start(bf16[32,1536]{1,0:T(8,128)(2,1)S(1)} %collective-permute-done.24.cot_beside), channel_id=1, source_target_pairs={{0,1},{1,0},{2,3},{3,2},{4,5},{5,4},{6,7},{7,6},{8,9},{9,8},{10,11... | collective-permute-start | bytes 294920 | tf_op jit(solution)/shard_map/ppermute | solution.py:241
  56.4 7.5 %collective-permute-start.20 = (bf16[3,192,384]{2,1,0:T(8,128)(2,1)S(1)}, bf16[3,192,384]{2,1,0:T(8,128)(2,1)S(1)}, u32[]{:S(2)}, u32[]{:S(2)}) collective-permute-start(bf16[3,192,384]{2,1,0:T(8,128)(2,1)S(1)} %collective-permute-done.6.refs_3_), channel_id=1, source_target_pairs={{0,1},{1,0},{2,3},{3,2},{4,5},{5,4},{6,7},{7,6},{8,9},{9,8},{10,11... | collective-permute-start | bytes 1327112 | tf_op jit(solution)/shard_map/ppermute | solution.py:241
  58.0 6.1 %collective-permute-start.21 = (bf16[3,192,384]{2,1,0:T(8,128)(2,1)S(1)}, bf16[3,192,384]{2,1,0:T(8,128)(2,1)S(1)}, u32[]{:S(2)}, u32[]{:S(2)}) collective-permute-start(bf16[3,192,384]{2,1,0:T(8,128)(2,1)S(1)} %collective-permute-done.7.refs_4_), channel_id=1, source_target_pairs={{0,1},{1,0},{2,3},{3,2},{4,5},{5,4},{6,7},{7,6},{8,9},{9,8},{10,11... | collective-permute-start | bytes 1327112 | tf_op jit(solution)/shard_map/ppermute | solution.py:241
  61.6 1.5 %collective-permute-start.22 = (bf16[3,96,384]{2,1,0:T(8,128)(2,1)S(1)}, bf16[3,96,384]{2,1,0:T(8,128)(2,1)S(1)}, u32[]{:S(2)}, u32[]{:S(2)}) collective-permute-start(bf16[3,96,384]{2,1,0:T(8,128)(2,1)S(1)} %collective-permute-done.11.refs_5_), channel_id=1, source_target_pairs={{0,1},{1,0},{2,3},{3,2},{4,5},{5,4},{6,7},{7,6},{8,9},{9,8},{10,11... | collective-permute-start | bytes 663560 | tf_op jit(solution)/shard_map/ppermute | solution.py:241
  61.6 1.8 %collective-permute-start.23 = (bf16[3,96,384]{2,1,0:T(8,128)(2,1)S(1)}, bf16[3,96,384]{2,1,0:T(8,128)(2,1)S(1)}, u32[]{:S(2)}, u32[]{:S(2)}) collective-permute-start(bf16[3,96,384]{2,1,0:T(8,128)(2,1)S(1)} %collective-permute-done.12.refs_6_), channel_id=1, source_target_pairs={{0,1},{1,0},{2,3},{3,2},{4,5},{5,4},{6,7},{7,6},{8,9},{9,8},{10,11... | collective-permute-start | bytes 663560 | tf_op jit(solution)/shard_map/ppermute | solution.py:241
  63.1 6.5 %collective-permute-start.30 = (bf16[3,160,384]{2,1,0:T(8,128)(2,1)S(1)}, bf16[3,160,384]{2,1,0:T(8,128)(2,1)S(1)}, u32[]{:S(2)}, u32[]{:S(2)}) collective-permute-start(bf16[3,160,384]{2,1,0:T(8,128)(2,1)S(1)} %collective-permute-done.13.refs_3_), channel_id=1, source_target_pairs={{0,1},{1,0},{2,3},{3,2},{4,5},{5,4},{6,7},{7,6},{8,9},{9,8},{10,11... | collective-permute-start | bytes 1105928 | tf_op jit(solution)/shard_map/ppermute | solution.py:241
  63.4 6.2 %collective-permute-start.29 = (bf16[3,160,384]{2,1,0:T(8,128)(2,1)S(1)}, bf16[3,160,384]{2,1,0:T(8,128)(2,1)S(1)}, u32[]{:S(2)}, u32[]{:S(2)}) collective-permute-start(bf16[3,160,384]{2,1,0:T(8,128)(2,1)S(1)} %pad_maximum_fusion.1.refs_2_), channel_id=1, source_target_pairs={{0,1},{1,0},{2,3},{3,2},{4,5},{5,4},{6,7},{7,6},{8,9},{9,8},{10,11... | collective-permute-start | bytes 1105928 | tf_op jit(solution)/shard_map/ppermute | solution.py:241
  63.6 6.0 %collective-permute-start.31 = (bf16[3,160,384]{2,1,0:T(8,128)(2,1)S(1)}, bf16[3,160,384]{2,1,0:T(8,128)(2,1)S(1)}, u32[]{:S(2)}, u32[]{:S(2)}) collective-permute-start(bf16[3,160,384]{2,1,0:T(8,128)(2,1)S(1)} %collective-permute-done.14.refs_4_), channel_id=1, source_target_pairs={{0,1},{1,0},{2,3},{3,2},{4,5},{5,4},{6,7},{7,6},{8,9},{9,8},{10,11... | collective-permute-start | bytes 1105928 | tf_op jit(solution)/shard_map/ppermute | solution.py:241
  64.0 5.7 %collective-permute-start.32 = (bf16[3,80,384]{2,1,0:T(8,128)(2,1)S(1)}, bf16[3,80,384]{2,1,0:T(8,128)(2,1)S(1)}, u32[]{:S(2)}, u32[]{:S(2)}) collective-permute-start(bf16[3,80,384]{2,1,0:T(8,128)(2,1)S(1)} %collective-permute-done.27.refs_5_), channel_id=1, source_target_pairs={{0,1},{1,0},{2,3},{3,2},{4,5},{5,4},{6,7},{7,6},{8,9},{9,8},{10,11... | collective-permute-start | bytes 552968 | tf_op jit(solution)/shard_map/ppermute | solution.py:241
  64.2 5.5 %collective-permute-start.33 = (bf16[3,80,384]{2,1,0:T(8,128)(2,1)S(1)}, bf16[3,80,384]{2,1,0:T(8,128)(2,1)S(1)}, u32[]{:S(2)}, u32[]{:S(2)}) collective-permute-start(bf16[3,80,384]{2,1,0:T(8,128)(2,1)S(1)} %collective-permute-done.28.refs_6_), channel_id=1, source_target_pairs={{0,1},{1,0},{2,3},{3,2},{4,5},{5,4},{6,7},{7,6},{8,9},{9,8},{10,11... | collective-permute-start | bytes 552968 | tf_op jit(solution)/shard_map/ppermute | solution.py:241
  75.3 5.9 %collective-permute-start.34 = (bf16[32,640]{1,0:T(8,128)(2,1)S(1)}, bf16[32,640]{1,0:T(8,128)(2,1)S(1)}, u32[]{:S(2)}, u32[]{:S(2)}) collective-permute-start(bf16[32,640]{1,0:T(8,128)(2,1)S(1)} %get-tuple-element.82), channel_id=1, source_target_pairs={{1,9},{3,11},{5,13},{7,15},{8,16},{9,1},{10,18},{11,3},{12,20},{13... | collective-permute-start | bytes 122888 | tf_op jit(solution)/shard_map/ppermute | solution.py:241
  84.3 5.6 %collective-permute-start.35 = (bf16[16,384]{1,0:T(8,128)(2,1)S(1)}, bf16[16,384]{1,0:T(8,128)(2,1)S(1)}, u32[]{:S(2)}, u32[]{:S(2)}) collective-permute-start(bf16[16,384]{1,0:T(8,128)(2,1)S(1)} %get-tuple-element.90), channel_id=1, source_target_pairs={{1,9},{3,11},{5,13},{7,15},{8,16},{9,1},{10,18},{11,3},{12,20},{13... | collective-permute-start | bytes 36872 | tf_op jit(solution)/shard_map/ppermute | solution.py:241
  91.7 4.7 %collective-permute-start.36 = (bf16[32,1536]{1,0:T(8,128)(2,1)S(1)}, bf16[32,1536]{1,0:T(8,128)(2,1)S(1)}, u32[]{:S(2)}, u32[]{:S(2)}) collective-permute-start(bf16[32,1536]{1,0:T(8,128)(2,1)S(1)} %get-tuple-element.94), channel_id=1, source_target_pairs={{0,2},{1,3},{2,0},{3,1},{4,6},{5,7},{6,4},{7,5},{8,10},{9,11},{10,... | collective-permute-start | bytes 294920 | tf_op jit(solution)/shard_map/ppermute | solution.py:241
  96.4 2.6 %collective-permute-start.37 = (bf16[32,1536]{1,0:T(8,128)(2,1)S(1)}, bf16[32,1536]{1,0:T(8,128)(2,1)S(1)}, u32[]{:S(2)}, u32[]{:S(2)}) collective-permute-start(bf16[32,1536]{1,0:T(8,128)(2,1)S(1)} %add_convert_fusion.1), channel_id=1, source_target_pairs={{0,1},{1,5},{2,3},{3,7},{4,0},{5,4},{6,2},{7,6},{8,12},{9,8},{10,1... | collective-permute-start | bytes 294920 | tf_op jit(solution)/shard_map/ppermute | solution.py:241
  96.8 5.9 %collective-permute-start.38 = (bf16[32,1536]{1,0:T(8,128)(2,1)S(1)}, bf16[32,1536]{1,0:T(8,128)(2,1)S(1)}, u32[]{:S(2)}, u32[]{:S(2)}) collective-permute-start(bf16[32,1536]{1,0:T(8,128)(2,1)S(1)} %add_convert_fusion.1), channel_id=1, source_target_pairs={{1,4},{3,6},{4,1},{6,3},{8,13},{10,15},{13,8},{15,10},{17,20},{19,... | collective-permute-start | bytes 294920 | tf_op jit(solution)/shard_map/ppermute | solution.py:241

commit v11 on v9

--- a/solution.py
+++ b/solution.py
@@ -628,14 +628,15 @@
     )
     early = (straight, beside, across) + diagonals(beside, across)
     late_beside, late_across = permuted(late_straight, x_route), permuted(late_straight, y_route)
+    moved = swapped((straight, *blocks))
+    early, late, cot_block, mine, moved = (
+        lambda v: (v[:5], v[5:8], v[8], v[9:12], v[12:])
+    )(after((*early, late_straight, late_beside, late_across, cot_block, *blocks, edge, *moved)))
+    late = tuple(late) + diagonals(late[1], late[2])
+    noisy_rows = tuple(mine) + tuple(moved[1:]) + swapped(mine[2:])
+    early = tuple(early) + tuple(moved[:1]) + swapped(early[1:])
     cot_rows = (cot_block, permuted(cot_block, x_route))
-    early, late, cot_rows, mine = (
-        lambda v: (v[:5], v[5:8], v[8:10], v[10:])
-    )(after((*early, late_straight, late_beside, late_across, *cot_rows, *blocks, edge)))
-    late = tuple(late) + diagonals(late[1], late[2])
-    noisy_rows = tuple(mine) + swapped(mine)
-    early = tuple(early) + swapped(early)
-    cot_rows = tuple(cot_rows) + swapped(cot_rows)
+    cot_rows = cot_rows + swapped(cot_rows)
     late_other = swapped(late[:3])
     gain = norm_gain.reshape(1, features)
 

time: 103 us -> 106 us (1.029)
  waiting for transfers between devices: 38.8 us -> 44.4 us
  starting transfers between devices: 42 us -> 39.3 us
    ppermute x39, waiting for transfers between devices: 38.8 us -> 44.4 us  [permuted(): return lax.ppermute(value, ('sa', 'sb', 'noise'), pairs)]
    ppermute x39, starting transfers between devices: 42 us -> 39.3 us  [permuted(): return lax.ppermute(value, ('sa', 'sb', 'noise'), pairs)]
  transfers between devices with their start and end apart: 39 -> 39, of which waited for: 18 -> 17; matrix products, arithmetic and copies ran while one was open for 3% -> 3% of each run, Pallas kernels for 5% -> 5%
where the time goes in v11:
time: 106 us
  waiting for transfers between devices  44.4 us (42%)
  starting transfers between devices  39.3 us (37%)
  Pallas kernels  17.4 us (16%)
  other arithmetic  3.63 us (3%)
  between operations  1.1 us (1%)
    ppermute x39, waiting for transfers between devices, permuted(): return lax.ppermute(value, ('sa', 'sb', 'noise'), pairs)  44.4 us
    ppermute x39, starting transfers between devices, permuted(): return lax.ppermute(value, ('sa', 'sb', 'noise'), pairs)  39.3 us
    pallas_call x1, Pallas kernels, stretch_shards(): pl.pallas_call(attention_kernel, out_shape=(shaped(128, 256), shaped(128,...  5.59 us
    pallas_call x1, Pallas kernels, stretch_shards(): pl.pallas_call(forward_kernel, out_shape=(shaped(192, features, dtype=bf1...  5.1 us
    pallas_call x1, Pallas kernels, stretch_shards(): pl.pallas_call(norm_kernel, out_shape=(shaped(128, HID, dtype=bf16), shap...  3.12 us
  transfers between devices with their start and end apart: 39, of which 17 were waited for; matrix products, arithmetic and copies ran while one was open for 3% of the time, Pallas kernels for 5%

profile of v11, /device:TPU:8, one launch (start us, length us, event | category | flops | bytes accessed | tf_op | source)
XLA Modules:
  0.0 106.0 jit_solution(12491324182774303684)
XLA Ops:
  0.0 1.8 %shard_map.100 = (bf16[192,384]{1,0:T(8,128)(2,1)}, bf16[160,384]{1,0:T(8,128)(2,1)}) custom-call(bf16[3,384,384]{2,1,0:T(8,128)(2,1)} %refs_0_.2, bf16[96,1536]{1,0:T(8,128)(2,1)} %refs_1_.2, bf16[384,896]{1,0:T(8,128)(2,1)} %refs_0_.3, bf16[96,1536]{1,0:T(8,128)(2,1)} %refs_1_.3), custom_call_target="tpu_custom_call" | custom-call | tf_op jit(solution)/shard_map/pallas_call | solution.py:567
  1.9 3.0 %collective-permute-start.1 = (bf16[192,384]{1,0:T(8,128)(2,1)}, bf16[192,384]{1,0:T(8,128)(2,1)S(1)}, u32[]{:S(2)}, u32[]{:S(2)}) collective-permute-start(bf16[192,384]{1,0:T(8,128)(2,1)} %get-tuple-element.53), channel_id=1, source_target_pairs={{0,16},{1,17},{2,18},{3,19},{4,20},{5,21},{6,22},{7,23},{8,24},{9,... | collective-permute-start | bytes 442376 | tf_op jit(solution)/shard_map/ppermute | solution.py:241
  4.9 0.5 collective-permute-start.2
  5.3 0.9 convert_element_type.22
  6.3 1.1 %add_convert_fusion = bf16[2,32,1536]{2,1,0:T(8,128)(2,1)S(1)} fusion(bf16[2,32,1536]{2,1,0:T(8,128)(2,1)} %param.11, f32[32,1536]{1,0:T(8,128)S(1)} %convert_element_type.22), kind=kLoop, calls=%fused_computation.1 | loop fusion | flops 294912 | bytes 589824 | tf_op jit(solution)/shard_map/convert_element_type | solution.py:601
  7.4 0.7 and_reduce_fusion
  8.8 1.9 %collective-permute-start.3 = (bf16[32,1536]{1,0:T(8,128)(2,1)S(1)}, bf16[32,1536]{1,0:T(8,128)(2,1)S(1)}, u32[]{:S(2)}, u32[]{:S(2)}) collective-permute-start(bf16[32,1536]{1,0:T(8,128)(2,1)S(1)} %get-tuple-element.103), channel_id=1, source_target_pairs={{0,0},{1,4},{2,2},{3,6},{4,1},{5,5},{6,3},{7,7},{8,9},{9,13},{10,1... | collective-permute-start | bytes 294920 | tf_op jit(solution)/shard_map/ppermute | solution.py:241
  10.7 1.4 %collective-permute-start.4 = (bf16[32,1536]{1,0:T(8,128)(2,1)S(1)}, bf16[32,1536]{1,0:T(8,128)(2,1)S(1)}, u32[]{:S(2)}, u32[]{:S(2)}) collective-permute-start(bf16[32,1536]{1,0:T(8,128)(2,1)S(1)} %get-tuple-element.104), channel_id=1, source_target_pairs={{0,2},{1,6},{2,0},{3,4},{4,3},{5,7},{6,1},{7,5},{8,11},{9,15},{10,... | collective-permute-start | bytes 294920 | tf_op jit(solution)/shard_map/ppermute | solution.py:241
  12.1 1.3 %collective-permute-start.5 = (bf16[32,1536]{1,0:T(8,128)(2,1)S(1)}, bf16[32,1536]{1,0:T(8,128)(2,1)S(1)}, u32[]{:S(2)}, u32[]{:S(2)}) collective-permute-start(bf16[32,1536]{1,0:T(8,128)(2,1)S(1)} %copy-done.5), channel_id=1, source_target_pairs={{0,4},{2,6},{5,1},{7,3},{9,13},{11,15},{12,8},{14,10},{16,20},{18,... | collective-permute-start | bytes 294920 | tf_op jit(solution)/shard_map/ppermute | solution.py:241
  13.4 2.2 %collective-permute-done.1 = bf16[192,384]{1,0:T(8,128)(2,1)S(1)} collective-permute-done((bf16[192,384]{1,0:T(8,128)(2,1)}, bf16[192,384]{1,0:T(8,128)(2,1)S(1)}, u32[]{:S(2)}, u32[]{:S(2)}) %collective-permute-start.1) | collective-permute-done | bytes 147488 | tf_op jit(solution)/shard_map/ppermute | solution.py:241
  15.6 2.8 %collective-permute-done.2 = bf16[192,384]{1,0:T(8,128)(2,1)S(1)} collective-permute-done((bf16[192,384]{1,0:T(8,128)(2,1)}, bf16[192,384]{1,0:T(8,128)(2,1)S(1)}, u32[]{:S(2)}, u32[]{:S(2)}) %collective-permute-start.2) | collective-permute-done | bytes 147488 | tf_op jit(solution)/shard_map/ppermute | solution.py:241
  18.6 1.5 %collective-permute-start.6 = (bf16[3,192,384]{2,1,0:T(8,128)(2,1)S(1)}, bf16[3,192,384]{2,1,0:T(8,128)(2,1)S(1)}, u32[]{:S(2)}, u32[]{:S(2)}) collective-permute-start(bf16[3,192,384]{2,1,0:T(8,128)(2,1)S(1)} %pad_maximum_fusion.refs_2_), channel_id=1, source_target_pairs={{0,2},{1,3},{2,0},{3,1},{4,6},{5,7},{6,4},{7,5},{8,10},{9,11},{10,... | collective-permute-start | bytes 1327112 | tf_op jit(solution)/shard_map/ppermute | solution.py:241
  20.1 1.5 %collective-permute-start.7 = (bf16[3,192,384]{2,1,0:T(8,128)(2,1)S(1)}, bf16[3,192,384]{2,1,0:T(8,128)(2,1)S(1)}, u32[]{:S(2)}, u32[]{:S(2)}) collective-permute-start(bf16[3,192,384]{2,1,0:T(8,128)(2,1)S(1)} %pad_maximum_fusion.refs_2_), channel_id=1, source_target_pairs={{0,4},{1,5},{2,6},{3,7},{4,0},{5,1},{6,2},{7,3},{8,12},{9,13},{10,... | collective-permute-start | bytes 1327112 | tf_op jit(solution)/shard_map/ppermute | solution.py:241
  21.6 1.8 %collective-permute-start.8 = (bf16[160,384]{1,0:T(8,128)(2,1)S(1)}, bf16[160,384]{1,0:T(8,128)(2,1)S(1)}, u32[]{:S(2)}, u32[]{:S(2)}) collective-permute-start(bf16[160,384]{1,0:T(8,128)(2,1)S(1)} %copy-done.8), channel_id=1, source_target_pairs={{0,8},{1,9},{2,10},{3,11},{4,12},{5,13},{6,14},{7,15},{8,0},{9,1},... | collective-permute-start | bytes 368648 | tf_op jit(solution)/shard_map/ppermute | solution.py:241
  23.5 1.7 %collective-permute-start.9 = (bf16[160,384]{1,0:T(8,128)(2,1)S(1)}, bf16[160,384]{1,0:T(8,128)(2,1)S(1)}, u32[]{:S(2)}, u32[]{:S(2)}) collective-permute-start(bf16[160,384]{1,0:T(8,128)(2,1)S(1)} %copy-done.8), channel_id=1, source_target_pairs={{0,16},{1,17},{2,18},{3,19},{4,20},{5,21},{6,22},{7,23},{8,24},{9,... | collective-permute-start | bytes 368648 | tf_op jit(solution)/shard_map/ppermute | solution.py:241
  25.1 2.4 %collective-permute-done.8 = bf16[160,384]{1,0:T(8,128)(2,1)S(1)} collective-permute-done((bf16[160,384]{1,0:T(8,128)(2,1)S(1)}, bf16[160,384]{1,0:T(8,128)(2,1)S(1)}, u32[]{:S(2)}, u32[]{:S(2)}) %collective-permute-start.8) | collective-permute-done | bytes 122912 | tf_op jit(solution)/shard_map/ppermute | solution.py:241
  27.5 3.6 %collective-permute-start.11 = (bf16[48,1536]{1,0:T(8,128)(2,1)S(1)}, bf16[48,1536]{1,0:T(8,128)(2,1)S(1)}, u32[]{:S(2)}, u32[]{:S(2)}) collective-permute-start(bf16[48,1536]{1,0:T(8,128)(2,1)S(1)} %pad_maximum_fusion.2), channel_id=1, source_target_pairs={{1,9},{3,11},{5,13},{7,15},{8,16},{9,1},{10,18},{11,3},{12,20},{13... | collective-permute-start | bytes 442376 | tf_op jit(solution)/shard_map/ppermute | solution.py:241
  31.1 1.6 %collective-permute-done.9 = bf16[160,384]{1,0:T(8,128)(2,1)S(1)} collective-permute-done((bf16[160,384]{1,0:T(8,128)(2,1)S(1)}, bf16[160,384]{1,0:T(8,128)(2,1)S(1)}, u32[]{:S(2)}, u32[]{:S(2)}) %collective-permute-start.9) | collective-permute-done | bytes 122912 | tf_op jit(solution)/shard_map/ppermute | solution.py:241
  32.7 2.3 %collective-permute-done.10 = bf16[160,384]{1,0:T(8,128)(2,1)S(1)} collective-permute-done((bf16[160,384]{1,0:T(8,128)(2,1)S(1)}, bf16[160,384]{1,0:T(8,128)(2,1)S(1)}, u32[]{:S(2)}, u32[]{:S(2)}) %collective-permute-start.10) | collective-permute-done | bytes 122912 | tf_op jit(solution)/shard_map/ppermute | solution.py:241
  35.1 1.5 %collective-permute-done.11.edge = bf16[48,1536]{1,0:T(8,128)(2,1)S(1)} collective-permute-done((bf16[48,1536]{1,0:T(8,128)(2,1)S(1)}, bf16[48,1536]{1,0:T(8,128)(2,1)S(1)}, u32[]{:S(2)}, u32[]{:S(2)}) %collective-permute-start.11) | collective-permute-done | bytes 147488 | tf_op jit(solution)/shard_map/ppermute | solution.py:241
  36.6 1.5 %collective-permute-start.14 = (bf16[3,160,384]{2,1,0:T(8,128)(2,1)S(1)}, bf16[3,160,384]{2,1,0:T(8,128)(2,1)S(1)}, u32[]{:S(2)}, u32[]{:S(2)}) collective-permute-start(bf16[3,160,384]{2,1,0:T(8,128)(2,1)S(1)} %pad_maximum_fusion.1.refs_2_), channel_id=1, source_target_pairs={{0,2},{1,3},{2,0},{3,1},{4,6},{5,7},{6,4},{7,5},{8,10},{9,11},{10,... | collective-permute-start | bytes 1105928 | tf_op jit(solution)/shard_map/ppermute | solution.py:241
  38.4 0.5 collective-permute-start.18
  39.0 0.7 collective-permute-done.17.other_even
  39.7 1.7 %collective-permute-start.12 = (bf16[3,96,384]{2,1,0:T(8,128)(2,1)S(1)}, bf16[3,96,384]{2,1,0:T(8,128)(2,1)S(1)}, u32[]{:S(2)}, u32[]{:S(2)}) collective-permute-start(bf16[3,96,384]{2,1,0:T(8,128)(2,1)S(1)} %slice.48), channel_id=1, source_target_pairs={{0,4},{1,5},{2,6},{3,7},{4,0},{5,1},{6,2},{7,3},{8,12},{9,13},{10,... | collective-permute-start | bytes 663560 | tf_op jit(solution)/shard_map/ppermute | solution.py:241
  41.5 0.6 collective-permute-start.13
  42.0 11.5 %collective-permute-done.12.refs_5_ = bf16[3,96,384]{2,1,0:T(8,128)(2,1)S(1)} collective-permute-done((bf16[3,96,384]{2,1,0:T(8,128)(2,1)S(1)}, bf16[3,96,384]{2,1,0:T(8,128)(2,1)S(1)}, u32[]{:S(2)}, u32[]{:S(2)}) %collective-permute-start.12) | collective-permute-done | bytes 221216 | tf_op jit(solution)/shard_map/ppermute | solution.py:241
  53.6 0.4 collective-permute-start.27
  53.9 0.9 collective-permute-start.24
  55.1 1.2 %collective-permute-start.28 = (bf16[3,80,384]{2,1,0:T(8,128)(2,1)S(1)}, bf16[3,80,384]{2,1,0:T(8,128)(2,1)S(1)}, u32[]{:S(2)}, u32[]{:S(2)}) collective-permute-start(bf16[3,80,384]{2,1,0:T(8,128)(2,1)S(1)} %slice.51), channel_id=1, source_target_pairs={{0,2},{1,3},{2,0},{3,1},{4,6},{5,7},{6,4},{7,5},{8,10},{9,11},{10,... | collective-permute-start | bytes 552968 | tf_op jit(solution)/shard_map/ppermute | solution.py:241
  56.3 3.2 %collective-permute-done.24.cot_beside = bf16[32,1536]{1,0:T(8,128)(2,1)S(1)} collective-permute-done((bf16[32,1536]{1,0:T(8,128)(2,1)S(1)}, bf16[32,1536]{1,0:T(8,128)(2,1)S(1)}, u32[]{:S(2)}, u32[]{:S(2)}) %collective-permute-start.24) | collective-permute-done | bytes 98336 | tf_op jit(solution)/shard_map/ppermute | solution.py:241
  59.5 0.5 collective-permute-start.21
  60.1 0.4 collective-permute-start.23
  60.6 2.5 %collective-permute-done.28.refs_6_ = bf16[3,80,384]{2,1,0:T(8,128)(2,1)S(1)} collective-permute-done((bf16[3,80,384]{2,1,0:T(8,128)(2,1)S(1)}, bf16[3,80,384]{2,1,0:T(8,128)(2,1)S(1)}, u32[]{:S(2)}, u32[]{:S(2)}) %collective-permute-start.28) | collective-permute-done | bytes 184352 | tf_op jit(solution)/shard_map/ppermute | solution.py:241
  63.1 1.3 %collective-permute-done.26.other_beside = bf16[32,1536]{1,0:T(8,128)(2,1)S(1)} collective-permute-done((bf16[32,1536]{1,0:T(8,128)(2,1)S(1)}, bf16[32,1536]{1,0:T(8,128)(2,1)S(1)}, u32[]{:S(2)}, u32[]{:S(2)}) %collective-permute-start.26) | collective-permute-done | bytes 98336 | tf_op jit(solution)/shard_map/ppermute | solution.py:241
  65.6 5.1 %shard_map.101 = (bf16[192,1536]{1,0:T(8,128)(2,1)S(1)}, f32[128,1536]{1,0:T(8,128)S(1)}, f32[128,1]{1,0:T(8,128)S(1)}, f32[128,384]{1,0:T(8,128)S(1)}, bf16[3,1...) custom-call(bf16[32,1536]{1,0:T(8,128)(2,1)S(1)} %collective-permute-done.3.blocks_even, ...), custom_call_target="tpu_custom_call" | custom-call | tf_op jit(solution)/shard_map/pallas_call | solution.py:643
  70.8 5.6 %shard_map.102 = (f32[128,256]{1,0:T(8,128)S(1)}, f32[128,640]{1,0:T(8,128)S(1)}, bf16[32,640]{1,0:T(8,128)(2,1)S(1)}, bf16[1536,896]{1,0:T(8,128)(2,1)S(1)}, bf16[128,1536]{1,0:T(8,128)(2,1)S(1)}) custom-call(s32[4]{0:T(128)S(1)} %copy-done.4, s32[1]{0:T(128)} %bitcast.3.flag, bf16[192,1536]{1,0:T(8,128)(2,1)S(1)} %get-tuple-element.81.normed, ...), custom_call_target="tpu_custom_call" | custom-call | tf_op jit(solution)/shard_map/pallas_call | solution.py:659
  76.4 3.5 %collective-permute-start.34 = (bf16[32,640]{1,0:T(8,128)(2,1)S(1)}, bf16[32,640]{1,0:T(8,128)(2,1)S(1)}, u32[]{:S(2)}, u32[]{:S(2)}) collective-permute-start(bf16[32,640]{1,0:T(8,128)(2,1)S(1)} %get-tuple-element.88), channel_id=1, source_target_pairs={{1,9},{3,11},{5,13},{7,15},{8,16},{9,1},{10,18},{11,3},{12,20},{13... | collective-permute-start | bytes 122888 | tf_op jit(solution)/shard_map/ppermute | solution.py:241
  79.9 2.4 %collective-permute-done.34.received = bf16[32,640]{1,0:T(8,128)(2,1)S(1)} collective-permute-done((bf16[32,640]{1,0:T(8,128)(2,1)S(1)}, bf16[32,640]{1,0:T(8,128)(2,1)S(1)}, u32[]{:S(2)}, u32[]{:S(2)}) %collective-permute-start.34) | collective-permute-done | bytes 40992 | tf_op jit(solution)/shard_map/ppermute | solution.py:241
  82.3 3.1 %shard_map.103 = (bf16[128,384]{1,0:T(8,128)(2,1)S(1)}, f32[64,1536]{1,0:T(8,128)S(1)}, bf16[16,384]{1,0:T(8,128)(2,1)S(1)}) custom-call(f32[128,256]{1,0:T(8,128)S(1)} %get-tuple-element.86.d_q, f32[128,640]{1,0:T(8,128)S(1)} %get-tuple-element.87.d_kv, bf16[32,640]{1,0:T(8,128)(2,1)S(1)} %collective-permute-done.34.received, ...), custom_call_target="tpu_custom_call" | custom-call | tf_op jit(solution)/shard_map/pallas_call | solution.py:675
  85.4 3.5 %collective-permute-start.35 = (bf16[16,384]{1,0:T(8,128)(2,1)S(1)}, bf16[16,384]{1,0:T(8,128)(2,1)S(1)}, u32[]{:S(2)}, u32[]{:S(2)}) collective-permute-start(bf16[16,384]{1,0:T(8,128)(2,1)S(1)} %get-tuple-element.96), channel_id=1, source_target_pairs={{1,9},{3,11},{5,13},{7,15},{8,16},{9,1},{10,18},{11,3},{12,20},{13... | collective-permute-start | bytes 36872 | tf_op jit(solution)/shard_map/ppermute | solution.py:241
  88.9 2.1 %collective-permute-done.35.received = bf16[16,384]{1,0:T(8,128)(2,1)S(1)} collective-permute-done((bf16[16,384]{1,0:T(8,128)(2,1)S(1)}, bf16[16,384]{1,0:T(8,128)(2,1)S(1)}, u32[]{:S(2)}, u32[]{:S(2)}) %collective-permute-start.35) | collective-permute-done | bytes 12320 | tf_op jit(solution)/shard_map/ppermute | solution.py:241
  91.0 1.8 %shard_map.104 = (f32[32,1536]{1,0:T(8,128)S(1)}, bf16[32,1536]{1,0:T(8,128)(2,1)S(1)}) custom-call(bf16[128,384]{1,0:T(8,128)(2,1)S(1)} %get-tuple-element.95.d_hidden, bf16[16,384]{1,0:T(8,128)(2,1)S(1)} %collective-permute-done.35.received, f32[64,1536]{1,0:T(8,128)S(1)} %get-tuple-element.97.d_resid, ...), custom_call_target="tpu_custom_call" | custom-call | tf_op jit(solution)/shard_map/pallas_call | solution.py:687
  92.8 1.0 collective-permute-start.36
  93.8 3.7 %collective-permute-done.36 = bf16[32,1536]{1,0:T(8,128)(2,1)S(1)} collective-permute-done((bf16[32,1536]{1,0:T(8,128)(2,1)S(1)}, bf16[32,1536]{1,0:T(8,128)(2,1)S(1)}, u32[]{:S(2)}, u32[]{:S(2)}) %collective-permute-start.36) | collective-permute-done | bytes 98336 | tf_op jit(solution)/shard_map/ppermute | solution.py:241
  97.6 1.8 %collective-permute-start.37 = (bf16[32,1536]{1,0:T(8,128)(2,1)S(1)}, bf16[32,1536]{1,0:T(8,128)(2,1)S(1)}, u32[]{:S(2)}, u32[]{:S(2)}) collective-permute-start(bf16[32,1536]{1,0:T(8,128)(2,1)S(1)} %add_convert_fusion.1), channel_id=1, source_target_pairs={{0,1},{1,5},{2,3},{3,7},{4,0},{5,4},{6,2},{7,6},{8,12},{9,8},{10,1... | collective-permute-start | bytes 294920 | tf_op jit(solution)/shard_map/ppermute | solution.py:241
  99.3 1.9 %collective-permute-start.38 = (bf16[32,1536]{1,0:T(8,128)(2,1)S(1)}, bf16[32,1536]{1,0:T(8,128)(2,1)S(1)}, u32[]{:S(2)}, u32[]{:S(2)}) collective-permute-start(bf16[32,1536]{1,0:T(8,128)(2,1)S(1)} %add_convert_fusion.1), channel_id=1, source_target_pairs={{1,4},{3,6},{4,1},{6,3},{8,13},{10,15},{13,8},{15,10},{17,20},{19,... | collective-permute-start | bytes 294920 | tf_op jit(solution)/shard_map/ppermute | solution.py:241
  101.6 3.7 %collective-permute-done.38 = bf16[32,1536]{1,0:T(8,128)(2,1)S(1)} collective-permute-done((bf16[32,1536]{1,0:T(8,128)(2,1)S(1)}, bf16[32,1536]{1,0:T(8,128)(2,1)S(1)}, u32[]{:S(2)}, u32[]{:S(2)}) %collective-permute-start.38) | collective-permute-done | bytes 98336 | tf_op jit(solution)/shard_map/ppermute | solution.py:241
  105.3 0.7 add_multiply_fusion
  (70 shorter events, 2.7 us)
Async XLA Ops:
  0.0 7.4 %copy-start.7 = (s32[16,2]{0,1:T(2,128)S(1)}, s32[16,2]{0,1:T(2,128)}, u32[]{:S(2)}) copy-start(s32[16,2]{0,1:T(2,128)} %param.19) | copy-start | bytes 388
  0.0 12.1 %copy-start.5 = (bf16[32,1536]{1,0:T(8,128)(2,1)S(1)}, bf16[32,1536]{1,0:T(8,128)(2,1)}, u32[]{:S(2)}) copy-start(bf16[32,1536]{1,0:T(8,128)(2,1)} %param.12) | copy-start | bytes 294916
  1.8 19.9 %copy-start.8 = (bf16[160,384]{1,0:T(8,128)(2,1)S(1)}, bf16[160,384]{1,0:T(8,128)(2,1)}, u32[]{:S(2)}) copy-start(bf16[160,384]{1,0:T(8,128)(2,1)} %get-tuple-element.59) | copy-start | bytes 368644
  1.8 7.0 %collective-permute-start = (bf16[192,384]{1,0:T(8,128)(2,1)}, bf16[192,384]{1,0:T(8,128)(2,1)S(1)}, u32[]{:S(2)}, u32[]{:S(2)}) collective-permute-start(bf16[192,384]{1,0:T(8,128)(2,1)} %get-tuple-element.53), channel_id=1, source_target_pairs={{0,8},{1,9},{2,10},{3,11},{4,12},{5,13},{6,14},{7,15},{8,0},{9,1},... | collective-permute-start | bytes 442376 | tf_op jit(solution)/shard_map/ppermute | solution.py:241
  1.9 13.8 %collective-permute-start.1 = (bf16[192,384]{1,0:T(8,128)(2,1)}, bf16[192,384]{1,0:T(8,128)(2,1)S(1)}, u32[]{:S(2)}, u32[]{:S(2)}) collective-permute-start(bf16[192,384]{1,0:T(8,128)(2,1)} %get-tuple-element.53), channel_id=1, source_target_pairs={{0,16},{1,17},{2,18},{3,19},{4,20},{5,21},{6,22},{7,23},{8,24},{9,... | collective-permute-start | bytes 442376 | tf_op jit(solution)/shard_map/ppermute | solution.py:241
  4.9 13.5 %collective-permute-start.2 = (bf16[192,384]{1,0:T(8,128)(2,1)}, bf16[192,384]{1,0:T(8,128)(2,1)S(1)}, u32[]{:S(2)}, u32[]{:S(2)}) collective-permute-start(bf16[192,384]{1,0:T(8,128)(2,1)} %get-tuple-element.53), channel_id=1, source_target_pairs={{0,24},{1,25},{2,26},{3,27},{4,28},{5,29},{6,30},{7,31},{8,16},{9,... | collective-permute-start | bytes 442376 | tf_op jit(solution)/shard_map/ppermute | solution.py:241
  6.2 59.4 %copy-start.6 = (f32[1536]{0:T(1024)S(1)}, f32[1536]{0:T(1024)}, u32[]{:S(2)}) copy-start(f32[1536]{0:T(1024)} %param.15) | copy-start | bytes 18436
  6.3 59.4 %copy-start = (bf16[3,384,384]{2,1,0:T(8,128)(2,1)S(1)}, bf16[3,384,384]{2,1,0:T(8,128)(2,1)}, u32[]{:S(2)}) copy-start(bf16[3,384,384]{2,1,0:T(8,128)(2,1)} %refs_0_.2) | copy-start | bytes 2654212
  6.3 59.4 %copy-start.2 = (bf16[96,1536]{1,0:T(8,128)(2,1)S(1)}, bf16[96,1536]{1,0:T(8,128)(2,1)}, u32[]{:S(2)}) copy-start(bf16[96,1536]{1,0:T(8,128)(2,1)} %refs_1_.2) | copy-start | bytes 884740
  8.8 9.6 %collective-permute-start.3 = (bf16[32,1536]{1,0:T(8,128)(2,1)S(1)}, bf16[32,1536]{1,0:T(8,128)(2,1)S(1)}, u32[]{:S(2)}, u32[]{:S(2)}) collective-permute-start(bf16[32,1536]{1,0:T(8,128)(2,1)S(1)} %get-tuple-element.103), channel_id=1, source_target_pairs={{0,0},{1,4},{2,2},{3,6},{4,1},{5,5},{6,3},{7,7},{8,9},{9,13},{10,1... | collective-permute-start | bytes 294920 | tf_op jit(solution)/shard_map/ppermute | solution.py:241
  10.7 7.7 %collective-permute-start.4 = (bf16[32,1536]{1,0:T(8,128)(2,1)S(1)}, bf16[32,1536]{1,0:T(8,128)(2,1)S(1)}, u32[]{:S(2)}, u32[]{:S(2)}) collective-permute-start(bf16[32,1536]{1,0:T(8,128)(2,1)S(1)} %get-tuple-element.104), channel_id=1, source_target_pairs={{0,2},{1,6},{2,0},{3,4},{4,3},{5,7},{6,1},{7,5},{8,11},{9,15},{10,... | collective-permute-start | bytes 294920 | tf_op jit(solution)/shard_map/ppermute | solution.py:241
  12.1 6.5 %collective-permute-start.5 = (bf16[32,1536]{1,0:T(8,128)(2,1)S(1)}, bf16[32,1536]{1,0:T(8,128)(2,1)S(1)}, u32[]{:S(2)}, u32[]{:S(2)}) collective-permute-start(bf16[32,1536]{1,0:T(8,128)(2,1)S(1)} %copy-done.5), channel_id=1, source_target_pairs={{0,4},{2,6},{5,1},{7,3},{9,13},{11,15},{12,8},{14,10},{16,20},{18,... | collective-permute-start | bytes 294920 | tf_op jit(solution)/shard_map/ppermute | solution.py:241
  18.6 18.0 %collective-permute-start.6 = (bf16[3,192,384]{2,1,0:T(8,128)(2,1)S(1)}, bf16[3,192,384]{2,1,0:T(8,128)(2,1)S(1)}, u32[]{:S(2)}, u32[]{:S(2)}) collective-permute-start(bf16[3,192,384]{2,1,0:T(8,128)(2,1)S(1)} %pad_maximum_fusion.refs_2_), channel_id=1, source_target_pairs={{0,2},{1,3},{2,0},{3,1},{4,6},{5,7},{6,4},{7,5},{8,10},{9,11},{10,... | collective-permute-start | bytes 1327112 | tf_op jit(solution)/shard_map/ppermute | solution.py:241
  20.1 16.5 %collective-permute-start.7 = (bf16[3,192,384]{2,1,0:T(8,128)(2,1)S(1)}, bf16[3,192,384]{2,1,0:T(8,128)(2,1)S(1)}, u32[]{:S(2)}, u32[]{:S(2)}) collective-permute-start(bf16[3,192,384]{2,1,0:T(8,128)(2,1)S(1)} %pad_maximum_fusion.refs_2_), channel_id=1, source_target_pairs={{0,4},{1,5},{2,6},{3,7},{4,0},{5,1},{6,2},{7,3},{8,12},{9,13},{10,... | collective-permute-start | bytes 1327112 | tf_op jit(solution)/shard_map/ppermute | solution.py:241
  21.6 5.9 %collective-permute-start.8 = (bf16[160,384]{1,0:T(8,128)(2,1)S(1)}, bf16[160,384]{1,0:T(8,128)(2,1)S(1)}, u32[]{:S(2)}, u32[]{:S(2)}) collective-permute-start(bf16[160,384]{1,0:T(8,128)(2,1)S(1)} %copy-done.8), channel_id=1, source_target_pairs={{0,8},{1,9},{2,10},{3,11},{4,12},{5,13},{6,14},{7,15},{8,0},{9,1},... | collective-permute-start | bytes 368648 | tf_op jit(solution)/shard_map/ppermute | solution.py:241
  23.5 9.2 %collective-permute-start.9 = (bf16[160,384]{1,0:T(8,128)(2,1)S(1)}, bf16[160,384]{1,0:T(8,128)(2,1)S(1)}, u32[]{:S(2)}, u32[]{:S(2)}) collective-permute-start(bf16[160,384]{1,0:T(8,128)(2,1)S(1)} %copy-done.8), channel_id=1, source_target_pairs={{0,16},{1,17},{2,18},{3,19},{4,20},{5,21},{6,22},{7,23},{8,24},{9,... | collective-permute-start | bytes 368648 | tf_op jit(solution)/shard_map/ppermute | solution.py:241
  25.1 9.9 %collective-permute-start.10 = (bf16[160,384]{1,0:T(8,128)(2,1)S(1)}, bf16[160,384]{1,0:T(8,128)(2,1)S(1)}, u32[]{:S(2)}, u32[]{:S(2)}) collective-permute-start(bf16[160,384]{1,0:T(8,128)(2,1)S(1)} %copy-done.8), channel_id=1, source_target_pairs={{0,24},{1,25},{2,26},{3,27},{4,28},{5,29},{6,30},{7,31},{8,16},{9,... | collective-permute-start | bytes 368648 | tf_op jit(solution)/shard_map/ppermute | solution.py:241
  27.5 9.1 %collective-permute-start.11 = (bf16[48,1536]{1,0:T(8,128)(2,1)S(1)}, bf16[48,1536]{1,0:T(8,128)(2,1)S(1)}, u32[]{:S(2)}, u32[]{:S(2)}) collective-permute-start(bf16[48,1536]{1,0:T(8,128)(2,1)S(1)} %pad_maximum_fusion.2), channel_id=1, source_target_pairs={{1,9},{3,11},{5,13},{7,15},{8,16},{9,1},{10,18},{11,3},{12,20},{13... | collective-permute-start | bytes 442376 | tf_op jit(solution)/shard_map/ppermute | solution.py:241
  36.6 16.9 %collective-permute-start.16 = (bf16[3,192,384]{2,1,0:T(8,128)(2,1)S(1)}, bf16[3,192,384]{2,1,0:T(8,128)(2,1)S(1)}, u32[]{:S(2)}, u32[]{:S(2)}) collective-permute-start(bf16[3,192,384]{2,1,0:T(8,128)(2,1)S(1)} %pad_maximum_fusion.refs_2_), channel_id=1, source_target_pairs={{0,1},{1,0},{2,3},{3,2},{4,5},{5,4},{6,7},{7,6},{8,9},{9,8},{10,11... | collective-permute-start | bytes 1327112 | tf_op jit(solution)/shard_map/ppermute | solution.py:241
  36.6 16.9 %collective-permute-start.14 = (bf16[3,160,384]{2,1,0:T(8,128)(2,1)S(1)}, bf16[3,160,384]{2,1,0:T(8,128)(2,1)S(1)}, u32[]{:S(2)}, u32[]{:S(2)}) collective-permute-start(bf16[3,160,384]{2,1,0:T(8,128)(2,1)S(1)} %pad_maximum_fusion.1.refs_2_), channel_id=1, source_target_pairs={{0,2},{1,3},{2,0},{3,1},{4,6},{5,7},{6,4},{7,5},{8,10},{9,11},{10,... | collective-permute-start | bytes 1105928 | tf_op jit(solution)/shard_map/ppermute | solution.py:241
  38.1 15.4 %collective-permute-start.15 = (bf16[3,160,384]{2,1,0:T(8,128)(2,1)S(1)}, bf16[3,160,384]{2,1,0:T(8,128)(2,1)S(1)}, u32[]{:S(2)}, u32[]{:S(2)}) collective-permute-start(bf16[3,160,384]{2,1,0:T(8,128)(2,1)S(1)} %pad_maximum_fusion.1.refs_2_), channel_id=1, source_target_pairs={{0,4},{1,5},{2,6},{3,7},{4,0},{5,1},{6,2},{7,3},{8,12},{9,13},{10,... | collective-permute-start | bytes 1105928 | tf_op jit(solution)/shard_map/ppermute | solution.py:241
  38.4 1.3 %collective-permute-start.17 = (bf16[32,1536]{1,0:T(8,128)(2,1)S(1)}, bf16[32,1536]{1,0:T(8,128)(2,1)S(1)}, u32[]{:S(2)}, u32[]{:S(2)}) collective-permute-start(bf16[32,1536]{1,0:T(8,128)(2,1)S(1)} %collective-permute-done.3.blocks_even), channel_id=1, source_target_pairs={{0,1},{1,0},{2,3},{3,2},{4,5},{5,4},{6,7},{7,6},{8,9},{9,8},{10,11... | collective-permute-start | bytes 294920 | tf_op jit(solution)/shard_map/ppermute | solution.py:241
  38.4 3.0 %collective-permute-start.18 = (bf16[32,1536]{1,0:T(8,128)(2,1)S(1)}, bf16[32,1536]{1,0:T(8,128)(2,1)S(1)}, u32[]{:S(2)}, u32[]{:S(2)}) collective-permute-start(bf16[32,1536]{1,0:T(8,128)(2,1)S(1)} %collective-permute-done.4.blocks_odd), channel_id=1, source_target_pairs={{0,1},{1,0},{2,3},{3,2},{4,5},{5,4},{6,7},{7,6},{8,9},{9,8},{10,11... | collective-permute-start | bytes 294920 | tf_op jit(solution)/shard_map/ppermute | solution.py:241
  39.7 13.8 %collective-permute-start.12 = (bf16[3,96,384]{2,1,0:T(8,128)(2,1)S(1)}, bf16[3,96,384]{2,1,0:T(8,128)(2,1)S(1)}, u32[]{:S(2)}, u32[]{:S(2)}) collective-permute-start(bf16[3,96,384]{2,1,0:T(8,128)(2,1)S(1)} %slice.48), channel_id=1, source_target_pairs={{0,4},{1,5},{2,6},{3,7},{4,0},{5,1},{6,2},{7,3},{8,12},{9,13},{10,... | collective-permute-start | bytes 663560 | tf_op jit(solution)/shard_map/ppermute | solution.py:241
  41.5 12.1 %collective-permute-start.13 = (bf16[3,96,384]{2,1,0:T(8,128)(2,1)S(1)}, bf16[3,96,384]{2,1,0:T(8,128)(2,1)S(1)}, u32[]{:S(2)}, u32[]{:S(2)}) collective-permute-start(bf16[3,96,384]{2,1,0:T(8,128)(2,1)S(1)} %slice.49), channel_id=1, source_target_pairs={{0,2},{1,3},{2,0},{3,1},{4,6},{5,7},{6,4},{7,5},{8,10},{9,11},{10,... | collective-permute-start | bytes 663560 | tf_op jit(solution)/shard_map/ppermute | solution.py:241
  53.6 6.5 %collective-permute-start.27 = (bf16[3,80,384]{2,1,0:T(8,128)(2,1)S(1)}, bf16[3,80,384]{2,1,0:T(8,128)(2,1)S(1)}, u32[]{:S(2)}, u32[]{:S(2)}) collective-permute-start(bf16[3,80,384]{2,1,0:T(8,128)(2,1)S(1)} %slice.50), channel_id=1, source_target_pairs={{0,4},{1,5},{2,6},{3,7},{4,0},{5,1},{6,2},{7,3},{8,12},{9,13},{10,... | collective-permute-start | bytes 552968 | tf_op jit(solution)/shard_map/ppermute | solution.py:241
  53.9 6.1 %collective-permute-start.19 = (bf16[48,1536]{1,0:T(8,128)(2,1)S(1)}, bf16[48,1536]{1,0:T(8,128)(2,1)S(1)}, u32[]{:S(2)}, u32[]{:S(2)}) collective-permute-start(bf16[48,1536]{1,0:T(8,128)(2,1)S(1)} %collective-permute-done.11.edge), channel_id=1, source_target_pairs={{0,1},{1,0},{2,3},{3,2},{4,5},{5,4},{6,7},{7,6},{8,9},{9,8},{10,11... | collective-permute-start | bytes 442376 | tf_op jit(solution)/shard_map/ppermute | solution.py:241
  53.9 5.6 %collective-permute-start.24 = (bf16[32,1536]{1,0:T(8,128)(2,1)S(1)}, bf16[32,1536]{1,0:T(8,128)(2,1)S(1)}, u32[]{:S(2)}, u32[]{:S(2)}) collective-permute-start(bf16[32,1536]{1,0:T(8,128)(2,1)S(1)} %broadcast_select_fusion.cot_block), channel_id=1, source_target_pairs={{0,2},{1,3},{2,0},{3,1},{4,6},{5,7},{6,4},{7,5},{8,10},{9,11},{10,... | collective-permute-start | bytes 294920 | tf_op jit(solution)/shard_map/ppermute | solution.py:241
  54.8 4.7 %collective-permute-start.25 = (bf16[32,1536]{1,0:T(8,128)(2,1)S(1)}, bf16[32,1536]{1,0:T(8,128)(2,1)S(1)}, u32[]{:S(2)}, u32[]{:S(2)}) collective-permute-start(bf16[32,1536]{1,0:T(8,128)(2,1)S(1)} %broadcast_select_fusion.cot_block), channel_id=1, source_target_pairs={{0,1},{1,0},{2,3},{3,2},{4,5},{5,4},{6,7},{7,6},{8,9},{9,8},{10,11... | collective-permute-start | bytes 294920 | tf_op jit(solution)/shard_map/ppermute | solution.py:241
  55.1 15.7 %copy-start.1 = (bf16[384,896]{1,0:T(8,128)(2,1)S(1)}, bf16[384,896]{1,0:T(8,128)(2,1)}, u32[]{:S(2)}) copy-start(bf16[384,896]{1,0:T(8,128)(2,1)} %refs_0_.3) | copy-start | bytes 2064388
  55.1 15.7 %copy-start.3 = (bf16[96,1536]{1,0:T(8,128)(2,1)S(1)}, bf16[96,1536]{1,0:T(8,128)(2,1)}, u32[]{:S(2)}) copy-start(bf16[96,1536]{1,0:T(8,128)(2,1)} %refs_1_.3) | copy-start | bytes 884740
  55.1 15.7 %copy-start.4 = (s32[4]{0:T(128)S(1)}, s32[4]{0:T(128)}, u32[]{:S(2)}) copy-start(s32[4]{0:T(128)} %band.1) | copy-start | bytes 52
  55.1 8.0 %collective-permute-start.28 = (bf16[3,80,384]{2,1,0:T(8,128)(2,1)S(1)}, bf16[3,80,384]{2,1,0:T(8,128)(2,1)S(1)}, u32[]{:S(2)}, u32[]{:S(2)}) collective-permute-start(bf16[3,80,384]{2,1,0:T(8,128)(2,1)S(1)} %slice.51), channel_id=1, source_target_pairs={{0,2},{1,3},{2,0},{3,1},{4,6},{5,7},{6,4},{7,5},{8,10},{9,11},{10,... | collective-permute-start | bytes 552968 | tf_op jit(solution)/shard_map/ppermute | solution.py:241
  59.5 5.5 %collective-permute-start.20 = (bf16[3,192,384]{2,1,0:T(8,128)(2,1)S(1)}, bf16[3,192,384]{2,1,0:T(8,128)(2,1)S(1)}, u32[]{:S(2)}, u32[]{:S(2)}) collective-permute-start(bf16[3,192,384]{2,1,0:T(8,128)(2,1)S(1)} %collective-permute-done.6.refs_3_), channel_id=1, source_target_pairs={{0,1},{1,0},{2,3},{3,2},{4,5},{5,4},{6,7},{7,6},{8,9},{9,8},{10,11... | collective-permute-start | bytes 1327112 | tf_op jit(solution)/shard_map/ppermute | solution.py:241
  59.5 5.9 %collective-permute-start.21 = (bf16[3,192,384]{2,1,0:T(8,128)(2,1)S(1)}, bf16[3,192,384]{2,1,0:T(8,128)(2,1)S(1)}, u32[]{:S(2)}, u32[]{:S(2)}) collective-permute-start(bf16[3,192,384]{2,1,0:T(8,128)(2,1)S(1)} %collective-permute-done.7.refs_4_), channel_id=1, source_target_pairs={{0,1},{1,0},{2,3},{3,2},{4,5},{5,4},{6,7},{7,6},{8,9},{9,8},{10,11... | collective-permute-start | bytes 1327112 | tf_op jit(solution)/shard_map/ppermute | solution.py:241
  60.1 4.5 %collective-permute-start.22 = (bf16[3,96,384]{2,1,0:T(8,128)(2,1)S(1)}, bf16[3,96,384]{2,1,0:T(8,128)(2,1)S(1)}, u32[]{:S(2)}, u32[]{:S(2)}) collective-permute-start(bf16[3,96,384]{2,1,0:T(8,128)(2,1)S(1)} %collective-permute-done.12.refs_5_), channel_id=1, source_target_pairs={{0,1},{1,0},{2,3},{3,2},{4,5},{5,4},{6,7},{7,6},{8,9},{9,8},{10,11... | collective-permute-start | bytes 663560 | tf_op jit(solution)/shard_map/ppermute | solution.py:241
  60.1 4.8 %collective-permute-start.23 = (bf16[3,96,384]{2,1,0:T(8,128)(2,1)S(1)}, bf16[3,96,384]{2,1,0:T(8,128)(2,1)S(1)}, u32[]{:S(2)}, u32[]{:S(2)}) collective-permute-start(bf16[3,96,384]{2,1,0:T(8,128)(2,1)S(1)} %collective-permute-done.13.refs_6_), channel_id=1, source_target_pairs={{0,1},{1,0},{2,3},{3,2},{4,5},{5,4},{6,7},{7,6},{8,9},{9,8},{10,11... | collective-permute-start | bytes 663560 | tf_op jit(solution)/shard_map/ppermute | solution.py:241
  63.1 1.3 %collective-permute-start.26 = (bf16[32,1536]{1,0:T(8,128)(2,1)S(1)}, bf16[32,1536]{1,0:T(8,128)(2,1)S(1)}, u32[]{:S(2)}, u32[]{:S(2)}) collective-permute-start(bf16[32,1536]{1,0:T(8,128)(2,1)S(1)} %collective-permute-done.24.cot_beside), channel_id=1, source_target_pairs={{0,1},{1,0},{2,3},{3,2},{4,5},{5,4},{6,7},{7,6},{8,9},{9,8},{10,11... | collective-permute-start | bytes 294920 | tf_op jit(solution)/shard_map/ppermute | solution.py:241
  64.4 6.3 %collective-permute-start.30 = (bf16[3,160,384]{2,1,0:T(8,128)(2,1)S(1)}, bf16[3,160,384]{2,1,0:T(8,128)(2,1)S(1)}, u32[]{:S(2)}, u32[]{:S(2)}) collective-permute-start(bf16[3,160,384]{2,1,0:T(8,128)(2,1)S(1)} %collective-permute-done.14.refs_3_), channel_id=1, source_target_pairs={{0,1},{1,0},{2,3},{3,2},{4,5},{5,4},{6,7},{7,6},{8,9},{9,8},{10,11... | collective-permute-start | bytes 1105928 | tf_op jit(solution)/shard_map/ppermute | solution.py:241
  64.6 6.2 %collective-permute-start.29 = (bf16[3,160,384]{2,1,0:T(8,128)(2,1)S(1)}, bf16[3,160,384]{2,1,0:T(8,128)(2,1)S(1)}, u32[]{:S(2)}, u32[]{:S(2)}) collective-permute-start(bf16[3,160,384]{2,1,0:T(8,128)(2,1)S(1)} %pad_maximum_fusion.1.refs_2_), channel_id=1, source_target_pairs={{0,1},{1,0},{2,3},{3,2},{4,5},{5,4},{6,7},{7,6},{8,9},{9,8},{10,11... | collective-permute-start | bytes 1105928 | tf_op jit(solution)/shard_map/ppermute | solution.py:241
  64.9 5.8 %collective-permute-start.31 = (bf16[3,160,384]{2,1,0:T(8,128)(2,1)S(1)}, bf16[3,160,384]{2,1,0:T(8,128)(2,1)S(1)}, u32[]{:S(2)}, u32[]{:S(2)}) collective-permute-start(bf16[3,160,384]{2,1,0:T(8,128)(2,1)S(1)} %collective-permute-done.15.refs_4_), channel_id=1, source_target_pairs={{0,1},{1,0},{2,3},{3,2},{4,5},{5,4},{6,7},{7,6},{8,9},{9,8},{10,11... | collective-permute-start | bytes 1105928 | tf_op jit(solution)/shard_map/ppermute | solution.py:241
  65.1 5.7 %collective-permute-start.32 = (bf16[3,80,384]{2,1,0:T(8,128)(2,1)S(1)}, bf16[3,80,384]{2,1,0:T(8,128)(2,1)S(1)}, u32[]{:S(2)}, u32[]{:S(2)}) collective-permute-start(bf16[3,80,384]{2,1,0:T(8,128)(2,1)S(1)} %collective-permute-done.27.refs_5_), channel_id=1, source_target_pairs={{0,1},{1,0},{2,3},{3,2},{4,5},{5,4},{6,7},{7,6},{8,9},{9,8},{10,11... | collective-permute-start | bytes 552968 | tf_op jit(solution)/shard_map/ppermute | solution.py:241
  65.4 5.3 %collective-permute-start.33 = (bf16[3,80,384]{2,1,0:T(8,128)(2,1)S(1)}, bf16[3,80,384]{2,1,0:T(8,128)(2,1)S(1)}, u32[]{:S(2)}, u32[]{:S(2)}) collective-permute-start(bf16[3,80,384]{2,1,0:T(8,128)(2,1)S(1)} %collective-permute-done.28.refs_6_), channel_id=1, source_target_pairs={{0,1},{1,0},{2,3},{3,2},{4,5},{5,4},{6,7},{7,6},{8,9},{9,8},{10,11... | collective-permute-start | bytes 552968 | tf_op jit(solution)/shard_map/ppermute | solution.py:241
  76.4 5.9 %collective-permute-start.34 = (bf16[32,640]{1,0:T(8,128)(2,1)S(1)}, bf16[32,640]{1,0:T(8,128)(2,1)S(1)}, u32[]{:S(2)}, u32[]{:S(2)}) collective-permute-start(bf16[32,640]{1,0:T(8,128)(2,1)S(1)} %get-tuple-element.88), channel_id=1, source_target_pairs={{1,9},{3,11},{5,13},{7,15},{8,16},{9,1},{10,18},{11,3},{12,20},{13... | collective-permute-start | bytes 122888 | tf_op jit(solution)/shard_map/ppermute | solution.py:241
  85.4 5.6 %collective-permute-start.35 = (bf16[16,384]{1,0:T(8,128)(2,1)S(1)}, bf16[16,384]{1,0:T(8,128)(2,1)S(1)}, u32[]{:S(2)}, u32[]{:S(2)}) collective-permute-start(bf16[16,384]{1,0:T(8,128)(2,1)S(1)} %get-tuple-element.96), channel_id=1, source_target_pairs={{1,9},{3,11},{5,13},{7,15},{8,16},{9,1},{10,18},{11,3},{12,20},{13... | collective-permute-start | bytes 36872 | tf_op jit(solution)/shard_map/ppermute | solution.py:241
  92.8 4.7 %collective-permute-start.36 = (bf16[32,1536]{1,0:T(8,128)(2,1)S(1)}, bf16[32,1536]{1,0:T(8,128)(2,1)S(1)}, u32[]{:S(2)}, u32[]{:S(2)}) collective-permute-start(bf16[32,1536]{1,0:T(8,128)(2,1)S(1)} %get-tuple-element.100), channel_id=1, source_target_pairs={{0,2},{1,3},{2,0},{3,1},{4,6},{5,7},{6,4},{7,5},{8,10},{9,11},{10,... | collective-permute-start | bytes 294920 | tf_op jit(solution)/shard_map/ppermute | solution.py:241
  97.6 4.0 %collective-permute-start.37 = (bf16[32,1536]{1,0:T(8,128)(2,1)S(1)}, bf16[32,1536]{1,0:T(8,128)(2,1)S(1)}, u32[]{:S(2)}, u32[]{:S(2)}) collective-permute-start(bf16[32,1536]{1,0:T(8,128)(2,1)S(1)} %add_convert_fusion.1), channel_id=1, source_target_pairs={{0,1},{1,5},{2,3},{3,7},{4,0},{5,4},{6,2},{7,6},{8,12},{9,8},{10,1... | collective-permute-start | bytes 294920 | tf_op jit(solution)/shard_map/ppermute | solution.py:241
  99.3 5.9 %collective-permute-start.38 = (bf16[32,1536]{1,0:T(8,128)(2,1)S(1)}, bf16[32,1536]{1,0:T(8,128)(2,1)S(1)}, u32[]{:S(2)}, u32[]{:S(2)}) collective-permute-start(bf16[32,1536]{1,0:T(8,128)(2,1)S(1)} %add_convert_fusion.1), channel_id=1, source_target_pairs={{1,4},{3,6},{4,1},{6,3},{8,13},{10,15},{13,8},{15,10},{17,20},{19,... | collective-permute-start | bytes 294920 | tf_op jit(solution)/shard_map/ppermute | solution.py:241

commit v12 on v9

--- a/solution.py
+++ b/solution.py
@@ -696,12 +696,10 @@
 
     received = permuted(send, x_route)
     partial = (keep + received.astype(f32)).astype(bf16)
-    first_sum = permuted(
-        partial, routes(n_sa, lambda z, y, x, c: (z, 1 - y, x, c) if y != c ^ (z & 1) else (z, y, x, 1 - c))
-    )
-    second_sum = permuted(partial, routes(n_sa, lambda z, y, x, c: (z, 1 - y, x, 1 - c) if y != c ^ (z & 1) else None))
-    other = jnp.where(y == m, partial, second_sum)
-    return (first_sum.astype(f32) + other.astype(f32)) * 0.25
+    received = permuted(partial, y_route)
+    total = (partial.astype(f32) + received.astype(f32)) * 0.25
+    swapped_total = permuted(total, core_route)
+    return jnp.where(y == m, total, swapped_total)
 
 
 def solution(mesh):

time: 103 us -> 103 us (level); the launches traced: 103 us -> 102 us
  starting transfers between devices: 42 us -> 40.1 us
    ppermute x39, starting transfers between devices: 42 us -> 40.1 us  [permuted(): return lax.ppermute(value, ('sa', 'sb', 'noise'), pairs)]
where the time goes in v12:
time: 103 us; the launch traced here: 102 us
  starting transfers between devices  40.1 us (39%)
  waiting for transfers between devices  39.1 us (38%)
  Pallas kernels  17.4 us (17%)
  other arithmetic  3.65 us (4%)
  between operations  1.1 us (1%)
    ppermute x39, starting transfers between devices, permuted(): return lax.ppermute(value, ('sa', 'sb', 'noise'), pairs)  40.1 us
    ppermute x39, waiting for transfers between devices, permuted(): return lax.ppermute(value, ('sa', 'sb', 'noise'), pairs)  39.1 us
    pallas_call x1, Pallas kernels, stretch_shards(): pl.pallas_call(attention_kernel, out_shape=(shaped(128, 256), shaped(128,...  5.59 us
    pallas_call x1, Pallas kernels, stretch_shards(): pl.pallas_call(forward_kernel, out_shape=(shaped(192, features, dtype=bf1...  5.1 us
    pallas_call x1, Pallas kernels, stretch_shards(): pl.pallas_call(norm_kernel, out_shape=(shaped(128, HID, dtype=bf16), shap...  3.12 us
  transfers between devices with their start and end apart: 39, of which 18 were waited for; matrix products, arithmetic and copies ran while one was open for 3% of the time, Pallas kernels for 5%

profile of v12, /device:TPU:8, one launch (start us, length us, event | category | flops | bytes accessed | tf_op | source)
XLA Modules:
  0.0 101.5 jit_solution(11258081101895949240)
XLA Ops:
  0.0 1.8 %shard_map.100 = (bf16[192,384]{1,0:T(8,128)(2,1)}, bf16[160,384]{1,0:T(8,128)(2,1)}) custom-call(bf16[3,384,384]{2,1,0:T(8,128)(2,1)} %refs_0_.2, bf16[96,1536]{1,0:T(8,128)(2,1)} %refs_1_.2, bf16[384,896]{1,0:T(8,128)(2,1)} %refs_0_.3, bf16[96,1536]{1,0:T(8,128)(2,1)} %refs_1_.3), custom_call_target="tpu_custom_call" | custom-call | tf_op jit(solution)/shard_map/pallas_call | solution.py:567
  1.9 3.0 %collective-permute-start.1 = (bf16[192,384]{1,0:T(8,128)(2,1)}, bf16[192,384]{1,0:T(8,128)(2,1)S(1)}, u32[]{:S(2)}, u32[]{:S(2)}) collective-permute-start(bf16[192,384]{1,0:T(8,128)(2,1)} %get-tuple-element.51), channel_id=1, source_target_pairs={{0,16},{1,17},{2,18},{3,19},{4,20},{5,21},{6,22},{7,23},{8,24},{9,... | collective-permute-start | bytes 442376 | tf_op jit(solution)/shard_map/ppermute | solution.py:241
  4.9 0.5 collective-permute-start.2
  5.3 0.9 convert_element_type.22
  6.3 1.1 %add_convert_fusion = bf16[2,32,1536]{2,1,0:T(8,128)(2,1)S(1)} fusion(bf16[2,32,1536]{2,1,0:T(8,128)(2,1)} %param.11, f32[32,1536]{1,0:T(8,128)S(1)} %convert_element_type.22), kind=kLoop, calls=%fused_computation.1 | loop fusion | flops 294912 | bytes 589824 | tf_op jit(solution)/shard_map/convert_element_type | solution.py:601
  7.4 0.7 and_reduce_fusion
  8.8 1.9 %collective-permute-start.3 = (bf16[32,1536]{1,0:T(8,128)(2,1)S(1)}, bf16[32,1536]{1,0:T(8,128)(2,1)S(1)}, u32[]{:S(2)}, u32[]{:S(2)}) collective-permute-start(bf16[32,1536]{1,0:T(8,128)(2,1)S(1)} %get-tuple-element.99), channel_id=1, source_target_pairs={{0,0},{1,4},{2,2},{3,6},{4,1},{5,5},{6,3},{7,7},{8,9},{9,13},{10,1... | collective-permute-start | bytes 294920 | tf_op jit(solution)/shard_map/ppermute | solution.py:241
  10.7 1.4 %collective-permute-start.4 = (bf16[32,1536]{1,0:T(8,128)(2,1)S(1)}, bf16[32,1536]{1,0:T(8,128)(2,1)S(1)}, u32[]{:S(2)}, u32[]{:S(2)}) collective-permute-start(bf16[32,1536]{1,0:T(8,128)(2,1)S(1)} %get-tuple-element.100), channel_id=1, source_target_pairs={{0,2},{1,6},{2,0},{3,4},{4,3},{5,7},{6,1},{7,5},{8,11},{9,15},{10,... | collective-permute-start | bytes 294920 | tf_op jit(solution)/shard_map/ppermute | solution.py:241
  12.1 1.3 %collective-permute-start.5 = (bf16[32,1536]{1,0:T(8,128)(2,1)S(1)}, bf16[32,1536]{1,0:T(8,128)(2,1)S(1)}, u32[]{:S(2)}, u32[]{:S(2)}) collective-permute-start(bf16[32,1536]{1,0:T(8,128)(2,1)S(1)} %copy-done.5), channel_id=1, source_target_pairs={{0,4},{2,6},{5,1},{7,3},{9,13},{11,15},{12,8},{14,10},{16,20},{18,... | collective-permute-start | bytes 294920 | tf_op jit(solution)/shard_map/ppermute | solution.py:241
  13.4 2.2 %collective-permute-done.1 = bf16[192,384]{1,0:T(8,128)(2,1)S(1)} collective-permute-done((bf16[192,384]{1,0:T(8,128)(2,1)}, bf16[192,384]{1,0:T(8,128)(2,1)S(1)}, u32[]{:S(2)}, u32[]{:S(2)}) %collective-permute-start.1) | collective-permute-done | bytes 147488 | tf_op jit(solution)/shard_map/ppermute | solution.py:241
  15.6 2.8 %collective-permute-done.2 = bf16[192,384]{1,0:T(8,128)(2,1)S(1)} collective-permute-done((bf16[192,384]{1,0:T(8,128)(2,1)}, bf16[192,384]{1,0:T(8,128)(2,1)S(1)}, u32[]{:S(2)}, u32[]{:S(2)}) %collective-permute-start.2) | collective-permute-done | bytes 147488 | tf_op jit(solution)/shard_map/ppermute | solution.py:241
  18.6 1.5 %collective-permute-start.6 = (bf16[3,192,384]{2,1,0:T(8,128)(2,1)S(1)}, bf16[3,192,384]{2,1,0:T(8,128)(2,1)S(1)}, u32[]{:S(2)}, u32[]{:S(2)}) collective-permute-start(bf16[3,192,384]{2,1,0:T(8,128)(2,1)S(1)} %pad_maximum_fusion.refs_2_), channel_id=1, source_target_pairs={{0,2},{1,3},{2,0},{3,1},{4,6},{5,7},{6,4},{7,5},{8,10},{9,11},{10,... | collective-permute-start | bytes 1327112 | tf_op jit(solution)/shard_map/ppermute | solution.py:241
  20.1 1.5 %collective-permute-start.7 = (bf16[3,192,384]{2,1,0:T(8,128)(2,1)S(1)}, bf16[3,192,384]{2,1,0:T(8,128)(2,1)S(1)}, u32[]{:S(2)}, u32[]{:S(2)}) collective-permute-start(bf16[3,192,384]{2,1,0:T(8,128)(2,1)S(1)} %pad_maximum_fusion.refs_2_), channel_id=1, source_target_pairs={{0,4},{1,5},{2,6},{3,7},{4,0},{5,1},{6,2},{7,3},{8,12},{9,13},{10,... | collective-permute-start | bytes 1327112 | tf_op jit(solution)/shard_map/ppermute | solution.py:241
  21.6 1.8 %collective-permute-start.8 = (bf16[160,384]{1,0:T(8,128)(2,1)S(1)}, bf16[160,384]{1,0:T(8,128)(2,1)S(1)}, u32[]{:S(2)}, u32[]{:S(2)}) collective-permute-start(bf16[160,384]{1,0:T(8,128)(2,1)S(1)} %copy-done.8), channel_id=1, source_target_pairs={{0,8},{1,9},{2,10},{3,11},{4,12},{5,13},{6,14},{7,15},{8,0},{9,1},... | collective-permute-start | bytes 368648 | tf_op jit(solution)/shard_map/ppermute | solution.py:241
  23.5 1.7 %collective-permute-start.9 = (bf16[160,384]{1,0:T(8,128)(2,1)S(1)}, bf16[160,384]{1,0:T(8,128)(2,1)S(1)}, u32[]{:S(2)}, u32[]{:S(2)}) collective-permute-start(bf16[160,384]{1,0:T(8,128)(2,1)S(1)} %copy-done.8), channel_id=1, source_target_pairs={{0,16},{1,17},{2,18},{3,19},{4,20},{5,21},{6,22},{7,23},{8,24},{9,... | collective-permute-start | bytes 368648 | tf_op jit(solution)/shard_map/ppermute | solution.py:241
  25.1 2.4 %collective-permute-done.8 = bf16[160,384]{1,0:T(8,128)(2,1)S(1)} collective-permute-done((bf16[160,384]{1,0:T(8,128)(2,1)S(1)}, bf16[160,384]{1,0:T(8,128)(2,1)S(1)}, u32[]{:S(2)}, u32[]{:S(2)}) %collective-permute-start.8) | collective-permute-done | bytes 122912 | tf_op jit(solution)/shard_map/ppermute | solution.py:241
  27.5 3.6 %collective-permute-start.11 = (bf16[48,1536]{1,0:T(8,128)(2,1)S(1)}, bf16[48,1536]{1,0:T(8,128)(2,1)S(1)}, u32[]{:S(2)}, u32[]{:S(2)}) collective-permute-start(bf16[48,1536]{1,0:T(8,128)(2,1)S(1)} %pad_maximum_fusion.2), channel_id=1, source_target_pairs={{1,9},{3,11},{5,13},{7,15},{8,16},{9,1},{10,18},{11,3},{12,20},{13... | collective-permute-start | bytes 442376 | tf_op jit(solution)/shard_map/ppermute | solution.py:241
  31.1 1.6 %collective-permute-done.9 = bf16[160,384]{1,0:T(8,128)(2,1)S(1)} collective-permute-done((bf16[160,384]{1,0:T(8,128)(2,1)S(1)}, bf16[160,384]{1,0:T(8,128)(2,1)S(1)}, u32[]{:S(2)}, u32[]{:S(2)}) %collective-permute-start.9) | collective-permute-done | bytes 122912 | tf_op jit(solution)/shard_map/ppermute | solution.py:241
  32.7 2.3 %collective-permute-done.10 = bf16[160,384]{1,0:T(8,128)(2,1)S(1)} collective-permute-done((bf16[160,384]{1,0:T(8,128)(2,1)S(1)}, bf16[160,384]{1,0:T(8,128)(2,1)S(1)}, u32[]{:S(2)}, u32[]{:S(2)}) %collective-permute-start.10) | collective-permute-done | bytes 122912 | tf_op jit(solution)/shard_map/ppermute | solution.py:241
  35.1 1.5 %collective-permute-done.11.edge = bf16[48,1536]{1,0:T(8,128)(2,1)S(1)} collective-permute-done((bf16[48,1536]{1,0:T(8,128)(2,1)S(1)}, bf16[48,1536]{1,0:T(8,128)(2,1)S(1)}, u32[]{:S(2)}, u32[]{:S(2)}) %collective-permute-start.11) | collective-permute-done | bytes 147488 | tf_op jit(solution)/shard_map/ppermute | solution.py:241
  36.6 1.5 %collective-permute-start.14 = (bf16[3,160,384]{2,1,0:T(8,128)(2,1)S(1)}, bf16[3,160,384]{2,1,0:T(8,128)(2,1)S(1)}, u32[]{:S(2)}, u32[]{:S(2)}) collective-permute-start(bf16[3,160,384]{2,1,0:T(8,128)(2,1)S(1)} %pad_maximum_fusion.1.refs_2_), channel_id=1, source_target_pairs={{0,2},{1,3},{2,0},{3,1},{4,6},{5,7},{6,4},{7,5},{8,10},{9,11},{10,... | collective-permute-start | bytes 1105928 | tf_op jit(solution)/shard_map/ppermute | solution.py:241
  38.4 1.8 %collective-permute-start.12 = (bf16[3,96,384]{2,1,0:T(8,128)(2,1)S(1)}, bf16[3,96,384]{2,1,0:T(8,128)(2,1)S(1)}, u32[]{:S(2)}, u32[]{:S(2)}) collective-permute-start(bf16[3,96,384]{2,1,0:T(8,128)(2,1)S(1)} %slice.48), channel_id=1, source_target_pairs={{0,4},{1,5},{2,6},{3,7},{4,0},{5,1},{6,2},{7,3},{8,12},{9,13},{10,... | collective-permute-start | bytes 663560 | tf_op jit(solution)/shard_map/ppermute | solution.py:241
  40.2 0.6 collective-permute-start.13
  40.8 1.5 %collective-permute-start.16 = (bf16[32,1536]{1,0:T(8,128)(2,1)S(1)}, bf16[32,1536]{1,0:T(8,128)(2,1)S(1)}, u32[]{:S(2)}, u32[]{:S(2)}) collective-permute-start(bf16[32,1536]{1,0:T(8,128)(2,1)S(1)} %broadcast_select_fusion.3.cot_block), channel_id=1, source_target_pairs={{0,2},{1,3},{2,0},{3,1},{4,6},{5,7},{6,4},{7,5},{8,10},{9,11},{10,... | collective-permute-start | bytes 294920 | tf_op jit(solution)/shard_map/ppermute | solution.py:241
  42.3 9.1 %collective-permute-done.16.cot_beside = bf16[32,1536]{1,0:T(8,128)(2,1)S(1)} collective-permute-done((bf16[32,1536]{1,0:T(8,128)(2,1)S(1)}, bf16[32,1536]{1,0:T(8,128)(2,1)S(1)}, u32[]{:S(2)}, u32[]{:S(2)}) %collective-permute-start.16) | collective-permute-done | bytes 98336 | tf_op jit(solution)/shard_map/ppermute | solution.py:241
  51.5 0.5 collective-permute-start.18
  52.1 0.4 collective-permute-start.20
  53.0 1.6 %collective-permute-start.28 = (bf16[3,80,384]{2,1,0:T(8,128)(2,1)S(1)}, bf16[3,80,384]{2,1,0:T(8,128)(2,1)S(1)}, u32[]{:S(2)}, u32[]{:S(2)}) collective-permute-start(bf16[3,80,384]{2,1,0:T(8,128)(2,1)S(1)} %slice.51), channel_id=1, source_target_pairs={{0,2},{1,3},{2,0},{3,1},{4,6},{5,7},{6,4},{7,5},{8,10},{9,11},{10,... | collective-permute-start | bytes 552968 | tf_op jit(solution)/shard_map/ppermute | solution.py:241
  54.8 1.1 %collective-permute-done.26.other_beside = bf16[32,1536]{1,0:T(8,128)(2,1)S(1)} collective-permute-done((bf16[32,1536]{1,0:T(8,128)(2,1)S(1)}, bf16[32,1536]{1,0:T(8,128)(2,1)S(1)}, u32[]{:S(2)}, u32[]{:S(2)}) %collective-permute-start.26) | collective-permute-done | bytes 98336 | tf_op jit(solution)/shard_map/ppermute | solution.py:241
  56.4 2.8 %collective-permute-done.27.refs_5_ = bf16[3,80,384]{2,1,0:T(8,128)(2,1)S(1)} collective-permute-done((bf16[3,80,384]{2,1,0:T(8,128)(2,1)S(1)}, bf16[3,80,384]{2,1,0:T(8,128)(2,1)S(1)}, u32[]{:S(2)}, u32[]{:S(2)}) %collective-permute-start.27) | collective-permute-done | bytes 184352 | tf_op jit(solution)/shard_map/ppermute | solution.py:241
  59.3 0.7 collective-permute-done.28.refs_6_
  59.9 0.8 collective-permute-done.23.refs_10_
  60.9 0.5 collective-permute-done.24.refs_11_
  61.5 0.4 collective-permute-start.31
  62.5 5.1 %shard_map.101 = (bf16[192,1536]{1,0:T(8,128)(2,1)S(1)}, f32[128,1536]{1,0:T(8,128)S(1)}, f32[128,1]{1,0:T(8,128)S(1)}, f32[128,384]{1,0:T(8,128)S(1)}, bf16[3,1...) custom-call(bf16[32,1536]{1,0:T(8,128)(2,1)S(1)} %collective-permute-done.3.blocks_even, ...), custom_call_target="tpu_custom_call" | custom-call | tf_op jit(solution)/shard_map/pallas_call | solution.py:642
  67.6 5.6 %shard_map.102 = (f32[128,256]{1,0:T(8,128)S(1)}, f32[128,640]{1,0:T(8,128)S(1)}, bf16[32,640]{1,0:T(8,128)(2,1)S(1)}, bf16[1536,896]{1,0:T(8,128)(2,1)S(1)}, bf16[128,1536]{1,0:T(8,128)(2,1)S(1)}) custom-call(s32[4]{0:T(128)S(1)} %copy-done.4, s32[1]{0:T(128)} %bitcast.3.flag, bf16[192,1536]{1,0:T(8,128)(2,1)S(1)} %get-tuple-element.76.normed, ...), custom_call_target="tpu_custom_call" | custom-call | tf_op jit(solution)/shard_map/pallas_call | solution.py:658
  73.2 4.1 %collective-permute-start.34 = (bf16[32,640]{1,0:T(8,128)(2,1)S(1)}, bf16[32,640]{1,0:T(8,128)(2,1)S(1)}, u32[]{:S(2)}, u32[]{:S(2)}) collective-permute-start(bf16[32,640]{1,0:T(8,128)(2,1)S(1)} %get-tuple-element.84), channel_id=1, source_target_pairs={{1,9},{3,11},{5,13},{7,15},{8,16},{9,1},{10,18},{11,3},{12,20},{13... | collective-permute-start | bytes 122888 | tf_op jit(solution)/shard_map/ppermute | solution.py:241
  77.4 2.0 %collective-permute-done.34.received = bf16[32,640]{1,0:T(8,128)(2,1)S(1)} collective-permute-done((bf16[32,640]{1,0:T(8,128)(2,1)S(1)}, bf16[32,640]{1,0:T(8,128)(2,1)S(1)}, u32[]{:S(2)}, u32[]{:S(2)}) %collective-permute-start.34) | collective-permute-done | bytes 40992 | tf_op jit(solution)/shard_map/ppermute | solution.py:241
  79.4 3.1 %shard_map.103 = (bf16[128,384]{1,0:T(8,128)(2,1)S(1)}, f32[64,1536]{1,0:T(8,128)S(1)}, bf16[16,384]{1,0:T(8,128)(2,1)S(1)}) custom-call(f32[128,256]{1,0:T(8,128)S(1)} %get-tuple-element.82.d_q, f32[128,640]{1,0:T(8,128)S(1)} %get-tuple-element.83.d_kv, bf16[32,640]{1,0:T(8,128)(2,1)S(1)} %collective-permute-done.34.received, ...), custom_call_target="tpu_custom_call" | custom-call | tf_op jit(solution)/shard_map/pallas_call | solution.py:674
  82.5 3.9 %collective-permute-start.35 = (bf16[16,384]{1,0:T(8,128)(2,1)S(1)}, bf16[16,384]{1,0:T(8,128)(2,1)S(1)}, u32[]{:S(2)}, u32[]{:S(2)}) collective-permute-start(bf16[16,384]{1,0:T(8,128)(2,1)S(1)} %get-tuple-element.92), channel_id=1, source_target_pairs={{1,9},{3,11},{5,13},{7,15},{8,16},{9,1},{10,18},{11,3},{12,20},{13... | collective-permute-start | bytes 36872 | tf_op jit(solution)/shard_map/ppermute | solution.py:241
  86.4 1.7 %collective-permute-done.35.received = bf16[16,384]{1,0:T(8,128)(2,1)S(1)} collective-permute-done((bf16[16,384]{1,0:T(8,128)(2,1)S(1)}, bf16[16,384]{1,0:T(8,128)(2,1)S(1)}, u32[]{:S(2)}, u32[]{:S(2)}) %collective-permute-start.35) | collective-permute-done | bytes 12320 | tf_op jit(solution)/shard_map/ppermute | solution.py:241
  88.1 1.8 %shard_map.104 = (f32[32,1536]{1,0:T(8,128)S(1)}, bf16[32,1536]{1,0:T(8,128)(2,1)S(1)}) custom-call(bf16[128,384]{1,0:T(8,128)(2,1)S(1)} %get-tuple-element.91.d_hidden, bf16[16,384]{1,0:T(8,128)(2,1)S(1)} %collective-permute-done.35.received, f32[64,1536]{1,0:T(8,128)S(1)} %get-tuple-element.93.d_resid, ...), custom_call_target="tpu_custom_call" | custom-call | tf_op jit(solution)/shard_map/pallas_call | solution.py:686
  89.9 1.5 %collective-permute-start.36 = (bf16[32,1536]{1,0:T(8,128)(2,1)S(1)}, bf16[32,1536]{1,0:T(8,128)(2,1)S(1)}, u32[]{:S(2)}, u32[]{:S(2)}) collective-permute-start(bf16[32,1536]{1,0:T(8,128)(2,1)S(1)} %get-tuple-element.96), channel_id=1, source_target_pairs={{0,2},{1,3},{2,0},{3,1},{4,6},{5,7},{6,4},{7,5},{8,10},{9,11},{10,... | collective-permute-start | bytes 294920 | tf_op jit(solution)/shard_map/ppermute | solution.py:241
  91.4 3.2 %collective-permute-done.36 = bf16[32,1536]{1,0:T(8,128)(2,1)S(1)} collective-permute-done((bf16[32,1536]{1,0:T(8,128)(2,1)S(1)}, bf16[32,1536]{1,0:T(8,128)(2,1)S(1)}, u32[]{:S(2)}, u32[]{:S(2)}) %collective-permute-start.36) | collective-permute-done | bytes 98336 | tf_op jit(solution)/shard_map/ppermute | solution.py:241
  94.6 1.8 %collective-permute-start.37 = (bf16[32,1536]{1,0:T(8,128)(2,1)S(1)}, bf16[32,1536]{1,0:T(8,128)(2,1)S(1)}, u32[]{:S(2)}, u32[]{:S(2)}) collective-permute-start(bf16[32,1536]{1,0:T(8,128)(2,1)S(1)} %add_convert_fusion.1), channel_id=1, source_target_pairs={{0,4},{1,5},{2,6},{3,7},{4,0},{5,1},{6,2},{7,3},{8,12},{9,13},{10,... | collective-permute-start | bytes 294920 | tf_op jit(solution)/shard_map/ppermute | solution.py:241
  96.4 2.9 %collective-permute-done.37 = bf16[32,1536]{1,0:T(8,128)(2,1)S(1)} collective-permute-done((bf16[32,1536]{1,0:T(8,128)(2,1)S(1)}, bf16[32,1536]{1,0:T(8,128)(2,1)S(1)}, u32[]{:S(2)}, u32[]{:S(2)}) %collective-permute-start.37) | collective-permute-done | bytes 98336 | tf_op jit(solution)/shard_map/ppermute | solution.py:241
  99.4 1.4 %collective-permute-done.38 = f32[32,1536]{1,0:T(8,128)S(1)} collective-permute-done((f32[32,1536]{1,0:T(8,128)S(1)}, f32[32,1536]{1,0:T(8,128)S(1)}, u32[]{:S(2)}, u32[]{:S(2)}) %collective-permute-start.38) | collective-permute-done | bytes 196640 | tf_op jit(solution)/shard_map/ppermute | solution.py:241
  100.8 0.7 broadcast_select_fusion.2
  (71 shorter events, 2.9 us)
Async XLA Ops:
  0.0 7.4 %copy-start.7 = (s32[16,2]{0,1:T(2,128)S(1)}, s32[16,2]{0,1:T(2,128)}, u32[]{:S(2)}) copy-start(s32[16,2]{0,1:T(2,128)} %param.19) | copy-start | bytes 388
  0.0 12.1 %copy-start.5 = (bf16[32,1536]{1,0:T(8,128)(2,1)S(1)}, bf16[32,1536]{1,0:T(8,128)(2,1)}, u32[]{:S(2)}) copy-start(bf16[32,1536]{1,0:T(8,128)(2,1)} %param.12) | copy-start | bytes 294916
  1.8 19.9 %copy-start.8 = (bf16[160,384]{1,0:T(8,128)(2,1)S(1)}, bf16[160,384]{1,0:T(8,128)(2,1)}, u32[]{:S(2)}) copy-start(bf16[160,384]{1,0:T(8,128)(2,1)} %get-tuple-element.57) | copy-start | bytes 368644
  1.8 7.0 %collective-permute-start = (bf16[192,384]{1,0:T(8,128)(2,1)}, bf16[192,384]{1,0:T(8,128)(2,1)S(1)}, u32[]{:S(2)}, u32[]{:S(2)}) collective-permute-start(bf16[192,384]{1,0:T(8,128)(2,1)} %get-tuple-element.51), channel_id=1, source_target_pairs={{0,8},{1,9},{2,10},{3,11},{4,12},{5,13},{6,14},{7,15},{8,0},{9,1},... | collective-permute-start | bytes 442376 | tf_op jit(solution)/shard_map/ppermute | solution.py:241
  1.9 13.8 %collective-permute-start.1 = (bf16[192,384]{1,0:T(8,128)(2,1)}, bf16[192,384]{1,0:T(8,128)(2,1)S(1)}, u32[]{:S(2)}, u32[]{:S(2)}) collective-permute-start(bf16[192,384]{1,0:T(8,128)(2,1)} %get-tuple-element.51), channel_id=1, source_target_pairs={{0,16},{1,17},{2,18},{3,19},{4,20},{5,21},{6,22},{7,23},{8,24},{9,... | collective-permute-start | bytes 442376 | tf_op jit(solution)/shard_map/ppermute | solution.py:241
  4.9 13.5 %collective-permute-start.2 = (bf16[192,384]{1,0:T(8,128)(2,1)}, bf16[192,384]{1,0:T(8,128)(2,1)S(1)}, u32[]{:S(2)}, u32[]{:S(2)}) collective-permute-start(bf16[192,384]{1,0:T(8,128)(2,1)} %get-tuple-element.51), channel_id=1, source_target_pairs={{0,24},{1,25},{2,26},{3,27},{4,28},{5,29},{6,30},{7,31},{8,16},{9,... | collective-permute-start | bytes 442376 | tf_op jit(solution)/shard_map/ppermute | solution.py:241
  6.2 56.2 %copy-start.6 = (f32[1536]{0:T(1024)S(1)}, f32[1536]{0:T(1024)}, u32[]{:S(2)}) copy-start(f32[1536]{0:T(1024)} %param.15) | copy-start | bytes 18436
  6.3 56.2 %copy-start = (bf16[3,384,384]{2,1,0:T(8,128)(2,1)S(1)}, bf16[3,384,384]{2,1,0:T(8,128)(2,1)}, u32[]{:S(2)}) copy-start(bf16[3,384,384]{2,1,0:T(8,128)(2,1)} %refs_0_.2) | copy-start | bytes 2654212
  6.3 56.2 %copy-start.2 = (bf16[96,1536]{1,0:T(8,128)(2,1)S(1)}, bf16[96,1536]{1,0:T(8,128)(2,1)}, u32[]{:S(2)}) copy-start(bf16[96,1536]{1,0:T(8,128)(2,1)} %refs_1_.2) | copy-start | bytes 884740
  8.8 9.6 %collective-permute-start.3 = (bf16[32,1536]{1,0:T(8,128)(2,1)S(1)}, bf16[32,1536]{1,0:T(8,128)(2,1)S(1)}, u32[]{:S(2)}, u32[]{:S(2)}) collective-permute-start(bf16[32,1536]{1,0:T(8,128)(2,1)S(1)} %get-tuple-element.99), channel_id=1, source_target_pairs={{0,0},{1,4},{2,2},{3,6},{4,1},{5,5},{6,3},{7,7},{8,9},{9,13},{10,1... | collective-permute-start | bytes 294920 | tf_op jit(solution)/shard_map/ppermute | solution.py:241
  10.7 7.7 %collective-permute-start.4 = (bf16[32,1536]{1,0:T(8,128)(2,1)S(1)}, bf16[32,1536]{1,0:T(8,128)(2,1)S(1)}, u32[]{:S(2)}, u32[]{:S(2)}) collective-permute-start(bf16[32,1536]{1,0:T(8,128)(2,1)S(1)} %get-tuple-element.100), channel_id=1, source_target_pairs={{0,2},{1,6},{2,0},{3,4},{4,3},{5,7},{6,1},{7,5},{8,11},{9,15},{10,... | collective-permute-start | bytes 294920 | tf_op jit(solution)/shard_map/ppermute | solution.py:241
  12.1 6.5 %collective-permute-start.5 = (bf16[32,1536]{1,0:T(8,128)(2,1)S(1)}, bf16[32,1536]{1,0:T(8,128)(2,1)S(1)}, u32[]{:S(2)}, u32[]{:S(2)}) collective-permute-start(bf16[32,1536]{1,0:T(8,128)(2,1)S(1)} %copy-done.5), channel_id=1, source_target_pairs={{0,4},{2,6},{5,1},{7,3},{9,13},{11,15},{12,8},{14,10},{16,20},{18,... | collective-permute-start | bytes 294920 | tf_op jit(solution)/shard_map/ppermute | solution.py:241
  18.6 18.0 %collective-permute-start.6 = (bf16[3,192,384]{2,1,0:T(8,128)(2,1)S(1)}, bf16[3,192,384]{2,1,0:T(8,128)(2,1)S(1)}, u32[]{:S(2)}, u32[]{:S(2)}) collective-permute-start(bf16[3,192,384]{2,1,0:T(8,128)(2,1)S(1)} %pad_maximum_fusion.refs_2_), channel_id=1, source_target_pairs={{0,2},{1,3},{2,0},{3,1},{4,6},{5,7},{6,4},{7,5},{8,10},{9,11},{10,... | collective-permute-start | bytes 1327112 | tf_op jit(solution)/shard_map/ppermute | solution.py:241
  20.1 16.5 %collective-permute-start.7 = (bf16[3,192,384]{2,1,0:T(8,128)(2,1)S(1)}, bf16[3,192,384]{2,1,0:T(8,128)(2,1)S(1)}, u32[]{:S(2)}, u32[]{:S(2)}) collective-permute-start(bf16[3,192,384]{2,1,0:T(8,128)(2,1)S(1)} %pad_maximum_fusion.refs_2_), channel_id=1, source_target_pairs={{0,4},{1,5},{2,6},{3,7},{4,0},{5,1},{6,2},{7,3},{8,12},{9,13},{10,... | collective-permute-start | bytes 1327112 | tf_op jit(solution)/shard_map/ppermute | solution.py:241
  21.6 5.9 %collective-permute-start.8 = (bf16[160,384]{1,0:T(8,128)(2,1)S(1)}, bf16[160,384]{1,0:T(8,128)(2,1)S(1)}, u32[]{:S(2)}, u32[]{:S(2)}) collective-permute-start(bf16[160,384]{1,0:T(8,128)(2,1)S(1)} %copy-done.8), channel_id=1, source_target_pairs={{0,8},{1,9},{2,10},{3,11},{4,12},{5,13},{6,14},{7,15},{8,0},{9,1},... | collective-permute-start | bytes 368648 | tf_op jit(solution)/shard_map/ppermute | solution.py:241
  23.5 9.2 %collective-permute-start.9 = (bf16[160,384]{1,0:T(8,128)(2,1)S(1)}, bf16[160,384]{1,0:T(8,128)(2,1)S(1)}, u32[]{:S(2)}, u32[]{:S(2)}) collective-permute-start(bf16[160,384]{1,0:T(8,128)(2,1)S(1)} %copy-done.8), channel_id=1, source_target_pairs={{0,16},{1,17},{2,18},{3,19},{4,20},{5,21},{6,22},{7,23},{8,24},{9,... | collective-permute-start | bytes 368648 | tf_op jit(solution)/shard_map/ppermute | solution.py:241
  25.1 9.9 %collective-permute-start.10 = (bf16[160,384]{1,0:T(8,128)(2,1)S(1)}, bf16[160,384]{1,0:T(8,128)(2,1)S(1)}, u32[]{:S(2)}, u32[]{:S(2)}) collective-permute-start(bf16[160,384]{1,0:T(8,128)(2,1)S(1)} %copy-done.8), channel_id=1, source_target_pairs={{0,24},{1,25},{2,26},{3,27},{4,28},{5,29},{6,30},{7,31},{8,16},{9,... | collective-permute-start | bytes 368648 | tf_op jit(solution)/shard_map/ppermute | solution.py:241
  27.5 9.1 %collective-permute-start.11 = (bf16[48,1536]{1,0:T(8,128)(2,1)S(1)}, bf16[48,1536]{1,0:T(8,128)(2,1)S(1)}, u32[]{:S(2)}, u32[]{:S(2)}) collective-permute-start(bf16[48,1536]{1,0:T(8,128)(2,1)S(1)} %pad_maximum_fusion.2), channel_id=1, source_target_pairs={{1,9},{3,11},{5,13},{7,15},{8,16},{9,1},{10,18},{11,3},{12,20},{13... | collective-permute-start | bytes 442376 | tf_op jit(solution)/shard_map/ppermute | solution.py:241
  36.6 14.8 %collective-permute-start.14 = (bf16[3,160,384]{2,1,0:T(8,128)(2,1)S(1)}, bf16[3,160,384]{2,1,0:T(8,128)(2,1)S(1)}, u32[]{:S(2)}, u32[]{:S(2)}) collective-permute-start(bf16[3,160,384]{2,1,0:T(8,128)(2,1)S(1)} %pad_maximum_fusion.1.refs_2_), channel_id=1, source_target_pairs={{0,2},{1,3},{2,0},{3,1},{4,6},{5,7},{6,4},{7,5},{8,10},{9,11},{10,... | collective-permute-start | bytes 1105928 | tf_op jit(solution)/shard_map/ppermute | solution.py:241
  38.1 13.4 %collective-permute-start.15 = (bf16[3,160,384]{2,1,0:T(8,128)(2,1)S(1)}, bf16[3,160,384]{2,1,0:T(8,128)(2,1)S(1)}, u32[]{:S(2)}, u32[]{:S(2)}) collective-permute-start(bf16[3,160,384]{2,1,0:T(8,128)(2,1)S(1)} %pad_maximum_fusion.1.refs_2_), channel_id=1, source_target_pairs={{0,4},{1,5},{2,6},{3,7},{4,0},{5,1},{6,2},{7,3},{8,12},{9,13},{10,... | collective-permute-start | bytes 1105928 | tf_op jit(solution)/shard_map/ppermute | solution.py:241
  38.4 13.0 %collective-permute-start.12 = (bf16[3,96,384]{2,1,0:T(8,128)(2,1)S(1)}, bf16[3,96,384]{2,1,0:T(8,128)(2,1)S(1)}, u32[]{:S(2)}, u32[]{:S(2)}) collective-permute-start(bf16[3,96,384]{2,1,0:T(8,128)(2,1)S(1)} %slice.48), channel_id=1, source_target_pairs={{0,4},{1,5},{2,6},{3,7},{4,0},{5,1},{6,2},{7,3},{8,12},{9,13},{10,... | collective-permute-start | bytes 663560 | tf_op jit(solution)/shard_map/ppermute | solution.py:241
  40.2 11.2 %collective-permute-start.13 = (bf16[3,96,384]{2,1,0:T(8,128)(2,1)S(1)}, bf16[3,96,384]{2,1,0:T(8,128)(2,1)S(1)}, u32[]{:S(2)}, u32[]{:S(2)}) collective-permute-start(bf16[3,96,384]{2,1,0:T(8,128)(2,1)S(1)} %slice.49), channel_id=1, source_target_pairs={{0,2},{1,3},{2,0},{3,1},{4,6},{5,7},{6,4},{7,5},{8,10},{9,11},{10,... | collective-permute-start | bytes 663560 | tf_op jit(solution)/shard_map/ppermute | solution.py:241
  40.8 10.6 %collective-permute-start.16 = (bf16[32,1536]{1,0:T(8,128)(2,1)S(1)}, bf16[32,1536]{1,0:T(8,128)(2,1)S(1)}, u32[]{:S(2)}, u32[]{:S(2)}) collective-permute-start(bf16[32,1536]{1,0:T(8,128)(2,1)S(1)} %broadcast_select_fusion.3.cot_block), channel_id=1, source_target_pairs={{0,2},{1,3},{2,0},{3,1},{4,6},{5,7},{6,4},{7,5},{8,10},{9,11},{10,... | collective-permute-start | bytes 294920 | tf_op jit(solution)/shard_map/ppermute | solution.py:241
  51.5 1.4 %collective-permute-start.17 = (bf16[32,1536]{1,0:T(8,128)(2,1)S(1)}, bf16[32,1536]{1,0:T(8,128)(2,1)S(1)}, u32[]{:S(2)}, u32[]{:S(2)}) collective-permute-start(bf16[32,1536]{1,0:T(8,128)(2,1)S(1)} %collective-permute-done.3.blocks_even), channel_id=1, source_target_pairs={{0,1},{1,0},{2,3},{3,2},{4,5},{5,4},{6,7},{7,6},{8,9},{9,8},{10,11... | collective-permute-start | bytes 294920 | tf_op jit(solution)/shard_map/ppermute | solution.py:241
  51.5 1.4 %collective-permute-start.18 = (bf16[32,1536]{1,0:T(8,128)(2,1)S(1)}, bf16[32,1536]{1,0:T(8,128)(2,1)S(1)}, u32[]{:S(2)}, u32[]{:S(2)}) collective-permute-start(bf16[32,1536]{1,0:T(8,128)(2,1)S(1)} %collective-permute-done.4.blocks_odd), channel_id=1, source_target_pairs={{0,1},{1,0},{2,3},{3,2},{4,5},{5,4},{6,7},{7,6},{8,9},{9,8},{10,11... | collective-permute-start | bytes 294920 | tf_op jit(solution)/shard_map/ppermute | solution.py:241
  52.0 2.6 %collective-permute-start.25 = (bf16[32,1536]{1,0:T(8,128)(2,1)S(1)}, bf16[32,1536]{1,0:T(8,128)(2,1)S(1)}, u32[]{:S(2)}, u32[]{:S(2)}) collective-permute-start(bf16[32,1536]{1,0:T(8,128)(2,1)S(1)} %broadcast_select_fusion.3.cot_block), channel_id=1, source_target_pairs={{0,1},{1,0},{2,3},{3,2},{4,5},{5,4},{6,7},{7,6},{8,9},{9,8},{10,11... | collective-permute-start | bytes 294920 | tf_op jit(solution)/shard_map/ppermute | solution.py:241
  52.1 9.4 %collective-permute-start.20 = (bf16[3,192,384]{2,1,0:T(8,128)(2,1)S(1)}, bf16[3,192,384]{2,1,0:T(8,128)(2,1)S(1)}, u32[]{:S(2)}, u32[]{:S(2)}) collective-permute-start(bf16[3,192,384]{2,1,0:T(8,128)(2,1)S(1)} %pad_maximum_fusion.refs_2_), channel_id=1, source_target_pairs={{0,1},{1,0},{2,3},{3,2},{4,5},{5,4},{6,7},{7,6},{8,9},{9,8},{10,11... | collective-permute-start | bytes 1327112 | tf_op jit(solution)/shard_map/ppermute | solution.py:241
  52.6 6.7 %collective-permute-start.27 = (bf16[3,80,384]{2,1,0:T(8,128)(2,1)S(1)}, bf16[3,80,384]{2,1,0:T(8,128)(2,1)S(1)}, u32[]{:S(2)}, u32[]{:S(2)}) collective-permute-start(bf16[3,80,384]{2,1,0:T(8,128)(2,1)S(1)} %slice.50), channel_id=1, source_target_pairs={{0,4},{1,5},{2,6},{3,7},{4,0},{5,1},{6,2},{7,3},{8,12},{9,13},{10,... | collective-permute-start | bytes 552968 | tf_op jit(solution)/shard_map/ppermute | solution.py:241
  52.7 14.9 %copy-start.1 = (bf16[384,896]{1,0:T(8,128)(2,1)S(1)}, bf16[384,896]{1,0:T(8,128)(2,1)}, u32[]{:S(2)}) copy-start(bf16[384,896]{1,0:T(8,128)(2,1)} %refs_0_.3) | copy-start | bytes 2064388
  52.8 14.9 %copy-start.3 = (bf16[96,1536]{1,0:T(8,128)(2,1)S(1)}, bf16[96,1536]{1,0:T(8,128)(2,1)}, u32[]{:S(2)}) copy-start(bf16[96,1536]{1,0:T(8,128)(2,1)} %refs_1_.3) | copy-start | bytes 884740
  52.8 14.9 %copy-start.4 = (s32[4]{0:T(128)S(1)}, s32[4]{0:T(128)}, u32[]{:S(2)}) copy-start(s32[4]{0:T(128)} %band.1) | copy-start | bytes 52
  52.8 3.3 %collective-permute-start.19 = (bf16[48,1536]{1,0:T(8,128)(2,1)S(1)}, bf16[48,1536]{1,0:T(8,128)(2,1)S(1)}, u32[]{:S(2)}, u32[]{:S(2)}) collective-permute-start(bf16[48,1536]{1,0:T(8,128)(2,1)S(1)} %collective-permute-done.11.edge), channel_id=1, source_target_pairs={{0,1},{1,0},{2,3},{3,2},{4,5},{5,4},{6,7},{7,6},{8,9},{9,8},{10,11... | collective-permute-start | bytes 442376 | tf_op jit(solution)/shard_map/ppermute | solution.py:241
  53.0 6.9 %collective-permute-start.28 = (bf16[3,80,384]{2,1,0:T(8,128)(2,1)S(1)}, bf16[3,80,384]{2,1,0:T(8,128)(2,1)S(1)}, u32[]{:S(2)}, u32[]{:S(2)}) collective-permute-start(bf16[3,80,384]{2,1,0:T(8,128)(2,1)S(1)} %slice.51), channel_id=1, source_target_pairs={{0,2},{1,3},{2,0},{3,1},{4,6},{5,7},{6,4},{7,5},{8,10},{9,11},{10,... | collective-permute-start | bytes 552968 | tf_op jit(solution)/shard_map/ppermute | solution.py:241
  54.6 1.3 %collective-permute-start.26 = (bf16[32,1536]{1,0:T(8,128)(2,1)S(1)}, bf16[32,1536]{1,0:T(8,128)(2,1)S(1)}, u32[]{:S(2)}, u32[]{:S(2)}) collective-permute-start(bf16[32,1536]{1,0:T(8,128)(2,1)S(1)} %collective-permute-done.16.cot_beside), channel_id=1, source_target_pairs={{0,1},{1,0},{2,3},{3,2},{4,5},{5,4},{6,7},{7,6},{8,9},{9,8},{10,11... | collective-permute-start | bytes 294920 | tf_op jit(solution)/shard_map/ppermute | solution.py:241
  55.9 6.0 %collective-permute-start.21 = (bf16[3,192,384]{2,1,0:T(8,128)(2,1)S(1)}, bf16[3,192,384]{2,1,0:T(8,128)(2,1)S(1)}, u32[]{:S(2)}, u32[]{:S(2)}) collective-permute-start(bf16[3,192,384]{2,1,0:T(8,128)(2,1)S(1)} %collective-permute-done.6.refs_3_), channel_id=1, source_target_pairs={{0,1},{1,0},{2,3},{3,2},{4,5},{5,4},{6,7},{7,6},{8,9},{9,8},{10,11... | collective-permute-start | bytes 1327112 | tf_op jit(solution)/shard_map/ppermute | solution.py:241
  56.1 6.0 %collective-permute-start.22 = (bf16[3,192,384]{2,1,0:T(8,128)(2,1)S(1)}, bf16[3,192,384]{2,1,0:T(8,128)(2,1)S(1)}, u32[]{:S(2)}, u32[]{:S(2)}) collective-permute-start(bf16[3,192,384]{2,1,0:T(8,128)(2,1)S(1)} %collective-permute-done.7.refs_4_), channel_id=1, source_target_pairs={{0,1},{1,0},{2,3},{3,2},{4,5},{5,4},{6,7},{7,6},{8,9},{9,8},{10,11... | collective-permute-start | bytes 1327112 | tf_op jit(solution)/shard_map/ppermute | solution.py:241
  59.2 1.5 %collective-permute-start.23 = (bf16[3,96,384]{2,1,0:T(8,128)(2,1)S(1)}, bf16[3,96,384]{2,1,0:T(8,128)(2,1)S(1)}, u32[]{:S(2)}, u32[]{:S(2)}) collective-permute-start(bf16[3,96,384]{2,1,0:T(8,128)(2,1)S(1)} %collective-permute-done.12.refs_5_), channel_id=1, source_target_pairs={{0,1},{1,0},{2,3},{3,2},{4,5},{5,4},{6,7},{7,6},{8,9},{9,8},{10,11... | collective-permute-start | bytes 663560 | tf_op jit(solution)/shard_map/ppermute | solution.py:241
  59.9 1.5 %collective-permute-start.24 = (bf16[3,96,384]{2,1,0:T(8,128)(2,1)S(1)}, bf16[3,96,384]{2,1,0:T(8,128)(2,1)S(1)}, u32[]{:S(2)}, u32[]{:S(2)}) collective-permute-start(bf16[3,96,384]{2,1,0:T(8,128)(2,1)S(1)} %collective-permute-done.13.refs_6_), channel_id=1, source_target_pairs={{0,1},{1,0},{2,3},{3,2},{4,5},{5,4},{6,7},{7,6},{8,9},{9,8},{10,11... | collective-permute-start | bytes 663560 | tf_op jit(solution)/shard_map/ppermute | solution.py:241
  60.7 6.9 %collective-permute-start.30 = (bf16[3,160,384]{2,1,0:T(8,128)(2,1)S(1)}, bf16[3,160,384]{2,1,0:T(8,128)(2,1)S(1)}, u32[]{:S(2)}, u32[]{:S(2)}) collective-permute-start(bf16[3,160,384]{2,1,0:T(8,128)(2,1)S(1)} %collective-permute-done.14.refs_3_), channel_id=1, source_target_pairs={{0,1},{1,0},{2,3},{3,2},{4,5},{5,4},{6,7},{7,6},{8,9},{9,8},{10,11... | collective-permute-start | bytes 1105928 | tf_op jit(solution)/shard_map/ppermute | solution.py:241
  61.4 6.2 %collective-permute-start.29 = (bf16[3,160,384]{2,1,0:T(8,128)(2,1)S(1)}, bf16[3,160,384]{2,1,0:T(8,128)(2,1)S(1)}, u32[]{:S(2)}, u32[]{:S(2)}) collective-permute-start(bf16[3,160,384]{2,1,0:T(8,128)(2,1)S(1)} %pad_maximum_fusion.1.refs_2_), channel_id=1, source_target_pairs={{0,1},{1,0},{2,3},{3,2},{4,5},{5,4},{6,7},{7,6},{8,9},{9,8},{10,11... | collective-permute-start | bytes 1105928 | tf_op jit(solution)/shard_map/ppermute | solution.py:241
  61.5 6.1 %collective-permute-start.31 = (bf16[3,160,384]{2,1,0:T(8,128)(2,1)S(1)}, bf16[3,160,384]{2,1,0:T(8,128)(2,1)S(1)}, u32[]{:S(2)}, u32[]{:S(2)}) collective-permute-start(bf16[3,160,384]{2,1,0:T(8,128)(2,1)S(1)} %collective-permute-done.15.refs_4_), channel_id=1, source_target_pairs={{0,1},{1,0},{2,3},{3,2},{4,5},{5,4},{6,7},{7,6},{8,9},{9,8},{10,11... | collective-permute-start | bytes 1105928 | tf_op jit(solution)/shard_map/ppermute | solution.py:241
  61.9 5.7 %collective-permute-start.32 = (bf16[3,80,384]{2,1,0:T(8,128)(2,1)S(1)}, bf16[3,80,384]{2,1,0:T(8,128)(2,1)S(1)}, u32[]{:S(2)}, u32[]{:S(2)}) collective-permute-start(bf16[3,80,384]{2,1,0:T(8,128)(2,1)S(1)} %collective-permute-done.27.refs_5_), channel_id=1, source_target_pairs={{0,1},{1,0},{2,3},{3,2},{4,5},{5,4},{6,7},{7,6},{8,9},{9,8},{10,11... | collective-permute-start | bytes 552968 | tf_op jit(solution)/shard_map/ppermute | solution.py:241
  62.0 5.5 %collective-permute-start.33 = (bf16[3,80,384]{2,1,0:T(8,128)(2,1)S(1)}, bf16[3,80,384]{2,1,0:T(8,128)(2,1)S(1)}, u32[]{:S(2)}, u32[]{:S(2)}) collective-permute-start(bf16[3,80,384]{2,1,0:T(8,128)(2,1)S(1)} %collective-permute-done.28.refs_6_), channel_id=1, source_target_pairs={{0,1},{1,0},{2,3},{3,2},{4,5},{5,4},{6,7},{7,6},{8,9},{9,8},{10,11... | collective-permute-start | bytes 552968 | tf_op jit(solution)/shard_map/ppermute | solution.py:241
  73.2 6.1 %collective-permute-start.34 = (bf16[32,640]{1,0:T(8,128)(2,1)S(1)}, bf16[32,640]{1,0:T(8,128)(2,1)S(1)}, u32[]{:S(2)}, u32[]{:S(2)}) collective-permute-start(bf16[32,640]{1,0:T(8,128)(2,1)S(1)} %get-tuple-element.84), channel_id=1, source_target_pairs={{1,9},{3,11},{5,13},{7,15},{8,16},{9,1},{10,18},{11,3},{12,20},{13... | collective-permute-start | bytes 122888 | tf_op jit(solution)/shard_map/ppermute | solution.py:241
  82.5 5.6 %collective-permute-start.35 = (bf16[16,384]{1,0:T(8,128)(2,1)S(1)}, bf16[16,384]{1,0:T(8,128)(2,1)S(1)}, u32[]{:S(2)}, u32[]{:S(2)}) collective-permute-start(bf16[16,384]{1,0:T(8,128)(2,1)S(1)} %get-tuple-element.92), channel_id=1, source_target_pairs={{1,9},{3,11},{5,13},{7,15},{8,16},{9,1},{10,18},{11,3},{12,20},{13... | collective-permute-start | bytes 36872 | tf_op jit(solution)/shard_map/ppermute | solution.py:241
  89.9 4.7 %collective-permute-start.36 = (bf16[32,1536]{1,0:T(8,128)(2,1)S(1)}, bf16[32,1536]{1,0:T(8,128)(2,1)S(1)}, u32[]{:S(2)}, u32[]{:S(2)}) collective-permute-start(bf16[32,1536]{1,0:T(8,128)(2,1)S(1)} %get-tuple-element.96), channel_id=1, source_target_pairs={{0,2},{1,3},{2,0},{3,1},{4,6},{5,7},{6,4},{7,5},{8,10},{9,11},{10,... | collective-permute-start | bytes 294920 | tf_op jit(solution)/shard_map/ppermute | solution.py:241
  94.6 4.7 %collective-permute-start.37 = (bf16[32,1536]{1,0:T(8,128)(2,1)S(1)}, bf16[32,1536]{1,0:T(8,128)(2,1)S(1)}, u32[]{:S(2)}, u32[]{:S(2)}) collective-permute-start(bf16[32,1536]{1,0:T(8,128)(2,1)S(1)} %add_convert_fusion.1), channel_id=1, source_target_pairs={{0,4},{1,5},{2,6},{3,7},{4,0},{5,1},{6,2},{7,3},{8,12},{9,13},{10,... | collective-permute-start | bytes 294920 | tf_op jit(solution)/shard_map/ppermute | solution.py:241
  99.3 1.5 %collective-permute-start.38 = (f32[32,1536]{1,0:T(8,128)S(1)}, f32[32,1536]{1,0:T(8,128)S(1)}, u32[]{:S(2)}, u32[]{:S(2)}) collective-permute-start(f32[32,1536]{1,0:T(8,128)S(1)} %add_multiply_fusion), channel_id=1, source_target_pairs={{0,1},{1,0},{2,3},{3,2},{4,5},{5,4},{6,7},{7,6},{8,9},{9,8},{10,11... | collective-permute-start | bytes 589832 | tf_op jit(solution)/shard_map/ppermute | solution.py:241
